TPU v7x, 128 devices: a whole 4x4x4 slice. The times are simulated.
128 devices in a mesh: dp: 16 (over x, z), fsdp: 8 (over y, core).
Axes of the slice: x: 4, y: 4, z: 4, core: 2. Of those that a mesh axis runs over, the one named last changes fastest.
Arguments:
- grad_shards: bfloat16 [16, 8192, 6144], P('dp', None, 'fsdp'), may hold values from -36 to 36
- hadamard_signs: int32 [6144], P('fsdp'), may hold values from 0 to 1
- scale_index: int32 [24, 8192], P('fsdp'), may hold values from 0 to 15
- scale_table: float32 [16], replicated, may hold values from 0.004 to 0.2
- master: float32 [8192, 6144], P('dp', 'fsdp'), may hold values from -6 to 6
- mean_moment: float32 [8192, 6144], P('dp', 'fsdp'), may hold values from -3 to 3
- var_moment: float32 [8192, 6144], P('dp', 'fsdp'), may hold values from 0.01 to 1
Outputs:
- new_master: float32 [8192, 6144], P('dp', 'fsdp')
- new_mean: float32 [8192, 6144], P('dp', 'fsdp')
- new_var: float32 [8192, 6144], P('dp', 'fsdp')
- weights: bfloat16 [8192, 6144], P('dp')
All inputs are finite; a program needn't handle non-finite values.
Results may differ from a plain program's by a relative error of at most 0.0019.
Values may be sent and summed in bfloat16 or wider, within the bound.
No kernel may reach another device: no remote copies, remote signals or barrier semaphores. Data moves between devices by JAX's collectives and lax.ppermute only.
A program may use at most 192 MiB of HBM per device.

v0:
```python
import math

import jax
import jax.numpy as jnp
from jax import lax
from jax.sharding import PartitionSpec as P

D = 6144
ROWS = 8192
TILE = 256


def hadamard(length, dtype):
    row_index = lax.broadcasted_iota(jnp.int32, (length, length), 0)
    col_index = lax.broadcasted_iota(jnp.int32, (length, length), 1)
    common_bits = row_index & col_index
    parity = jnp.zeros((length, length), jnp.int32)
    for bit_pos in range(length.bit_length() - 1):
        parity = parity ^ common_bits >> bit_pos & 1
    return (1 - 2 * parity).astype(dtype)


def lookup(table, index):
    levels = jnp.arange(table.shape[0], dtype=jnp.int32)
    hits = index[..., None] == levels
    return jnp.sum(jnp.where(hits, table, jnp.zeros_like(table)), axis=-1)


def encode(grad_rows, sign_low, scales, hmat_low):
    count, width = grad_rows.shape
    length = hmat_low.shape[0]
    tiles = width // length
    signed = grad_rows * sign_low
    rotated = jnp.dot(
        signed.reshape(count * tiles, length), hmat_low, preferred_element_type=jnp.float32
    )
    rotated = rotated.reshape(count, tiles, length) * (1.0 / math.sqrt(length))
    coded = jnp.clip(rotated / scales[:, :, None], -127.0, 127.0)
    return coded.astype(jnp.bfloat16)


def global_squares(values):
    return lax.psum(jnp.sum(values * values), ("dp", "fsdp"))


def on_device(
    grad_shards, hadamard_signs, scale_index, scale_table, master, mean_moment, var_moment
):
    local = grad_shards[0]
    total_rows, width = local.shape
    groups = lax.axis_size("dp")
    owned = total_rows // groups
    tiles = width // TILE
    hmat_low = hadamard(TILE, jnp.bfloat16)
    hmat_high = hadamard(TILE, jnp.float32)
    sign_low = (2 * hadamard_signs - 1).astype(jnp.bfloat16)
    sign_high = (2 * hadamard_signs - 1).astype(jnp.float32)
    all_scales = jnp.transpose(lookup(scale_table, scale_index))
    coded = encode(local, sign_low, all_scales, hmat_low)
    summed = lax.psum_scatter(
        coded.astype(jnp.float32).reshape(lax.axis_size("dp") * owned, width),
        "dp",
        scatter_dimension=0,
        tiled=True,
    )
    first_row = lax.axis_index("dp") * owned
    own_scales = lax.dynamic_slice_in_dim(all_scales, first_row, owned, 0)
    dequant = summed.reshape(owned, tiles, TILE) * own_scales[:, :, None]
    plain = jnp.dot(
        dequant.reshape(-1, TILE),
        hmat_high,
        precision=lax.Precision.HIGHEST,
        preferred_element_type=jnp.float32,
    )
    plain = (plain * (1.0 / math.sqrt(TILE))).reshape(owned, width) * sign_high
    squares = global_squares(plain)
    limit = 4.0 * math.sqrt(ROWS * D)
    grad = plain * (limit / jnp.maximum(jnp.sqrt(squares), limit))
    new_mean = 0.9 * mean_moment + 0.1 * grad
    new_var = 0.95 * var_moment + 0.05 * grad * grad
    update = new_mean / (1.0 - 0.9**10) / (jnp.sqrt(new_var / (1.0 - 0.95**10)) + 1e-08)
    new_master = master - 0.02 * (update + 0.1 * master)
    weights = lax.all_gather(new_master.astype(jnp.bfloat16), "fsdp", axis=1, tiled=True)
    return (new_master, new_mean, new_var, weights)


def solution(mesh):
    return jax.shard_map(
        on_device,
        mesh=mesh,
        in_specs=(
            P("dp", None, "fsdp"),
            P("fsdp"),
            P("fsdp", None),
            P(),
            P("dp", "fsdp"),
            P("dp", "fsdp"),
            P("dp", "fsdp"),
        ),
        out_specs=(P("dp", "fsdp"), P("dp", "fsdp"), P("dp", "fsdp"), P("dp", None)),
        check_vma=False,
    )
```

profile of v0, /device:TPU:1, one launch (start us, length us, event | category | flops | bytes accessed | tf_op | source)
XLA Modules:
  0.0 366.4 jit_solution(14899868575472121637)
XLA Ops:
  7.2 0.0 reduce-scatter.2.cloned.1.call-start
  7.2 0.7 fusion.8
  7.9 0.0 copy-start.2
  7.9 0.0 copy-start.3
  7.9 16.8 %copy.16 = bf16[1,8192,768]{1,2,0:T(8,128)(2,1)} copy(bf16[1,8192,768]{2,1,0:T(8,128)(2,1)} %param.7) | data formatting | bytes 25165824 | tf_op args[0]
  24.7 0.0 copy-done.2
  24.7 0.0 copy-done.3
  24.7 0.4 select_reduce_fusion
  25.1 16.4 %clamp_convert_fusion = bf16[8192,3,256]{0,2,1:T(8,128)(2,1)} fusion(f32[8192,3]{0,1:T(4,128)S(1)} %bitcast.11, bf16[8192,3,256]{0,2,1:T(8,128)(2,1)} %bitcast.10, bf16[3,256]{1,0:T(4,128)(2,1)S(1)} %mul.111), kind=kOutput, calls=%fused_computation | convolution fusion | flops 3273326592 | bytes 25265664 | tf_op jit(solution)/shard_map/dot_general | solution.py:34
  41.5 14.1 %bitcast_convert_fusion = f32[8192,768]{0,1:T(8,128)} fusion(bf16[8192,3,256]{0,2,1:T(8,128)(2,1)} %clamp_convert_fusion), kind=kLoop, calls=%fused_computation.1 | loop fusion | flops 6291456 | bytes 37748736 | tf_op jit(solution)/shard_map/reshape | solution.py:61
  55.7 24.7 %copy.18 = f32[8192,768]{1,0:T(8,128)} copy(f32[8192,768]{0,1:T(8,128)} %bitcast_convert_fusion) | data formatting | bytes 50331648 | tf_op jit(solution)/shard_map/reshape | solution.py:61
  80.3 0.0 reduce-scatter.2.cloned.1.call-update
  80.3 0.0 all-gather.2.cloned.1.call-start
  80.4 0.1 copy.19
  80.6 0.2 mul.118
  80.8 0.3 mul.126
  81.1 1.7 mul.127
  82.8 0.0 copy-start
  82.8 154.2 %reduce-scatter.2.cloned.1.call-done = f32[512,768]{1,0:T(8,128)} async-done(((f32[8192,768]{1,0:T(8,128)}), f32[512,768]{1,0:T(8,128)}) %reduce-scatter.2.cloned.1.call-update) | async-done | bytes 1572880 | tf_op jit(solution)/shard_map/reduce_scatter | solution.py:60
  237.0 1.6 reshape.41
  238.6 0.0 copy-done
  238.7 3.4 multiply_reduce_fusion
  242.1 0.0 copy-start.1
  242.1 1.8 reshape.42
  243.9 64.8 %psum.7 = f32[]{:T(128)} all-reduce(f32[]{:T(128)} %get-tuple-element.10), channel_id=1, replica_groups=mesh['dp'=16,'fsdp'=8] {'dp','fsdp'}, use_global_device_ids=true, to_apply=%region_3.4 | all-reduce | flops 1 | bytes 8 | tf_op jit(solution)/shard_map/psum | solution.py:43
  309.5 0.0 copy-done.1
  309.5 5.1 %fusion.26 = (bf16[512,768]{1,0:T(8,128)(2,1)}, f32[512,768]{1,0:T(8,128)}, f32[512,768]{1,0:T(8,128)}, f32[512,768]{1,0:T(8,128)}) fusion(f32[512,768]{1,0:T(8,128)S(1)} %copy-done.1, f32[]{:T(128)S(6)} %div.28, f32[512,768]{1,0:T(8,128)S(1)} %reshape.42, f32[768]{0:T(1024)S(1)} %get-tuple-element.8, f32[512,768]{1,0:T(8,128)} %param.12, f32[512,768]{1,0:T(8,128)} %param.13), kind=kLoop, calls=%fused_computation.39 | loop fusion | flops 7077888 | bytes 11799556 | tf_op jit(solution)/shard_map/convert_element_type | solution.py:83
  314.6 0.0 all-gather.2.cloned.1.call-update
  314.6 38.7 %all-gather.2.cloned.1.call-done = bf16[512,6144]{1,0:T(8,128)(2,1)} async-done(((bf16[512,768]{1,0:T(8,128)(2,1)}), bf16[512,6144]{1,0:T(8,128)(2,1)}) %all-gather.2.cloned.1.call-update) | async-done | bytes 6291472 | tf_op jit(solution)/shard_map/all_gather | solution.py:83
  353.3 6.2 %copy.22 = bf16[512,6144]{1,0:T(8,128)(2,1)} copy(bf16[512,6144]{1,0:T(8,128)(2,1)} %all-gather.2.cloned.1.call-done) | data formatting | bytes 12582912
  (3 shorter events, 0.0 us)
Async XLA Ops:
  7.2 229.9 %reduce-scatter.2.cloned.1.call-start = ((), (), s32[]{:S(2)}) async-start(), calls=%async_computation.1 | async-start | bytes 26738688 | tf_op jit(solution)/shard_map/reduce_scatter | solution.py:60
  7.9 16.8 %copy-start.2 = (s32[3,8192]{1,0:T(4,128)S(1)}, s32[3,8192]{1,0:T(4,128)}, u32[]{:S(2)}) copy-start(s32[3,8192]{1,0:T(4,128)} %param.9) | copy-start | bytes 294916
  7.9 16.8 %copy-start.3 = (f32[16]{0:T(128)S(1)}, f32[16]{0:T(128)}, u32[]{:S(2)}) copy-start(f32[16]{0:T(128)} %param.10) | copy-start | bytes 196
  80.3 273.0 %all-gather.2.cloned.1.call-start = ((), (), s32[]{:S(2)}) async-start(), calls=%async_computation.2 | async-start | bytes 7077888 | tf_op jit(solution)/shard_map/all_gather | solution.py:83
  82.8 155.9 %copy-start = (f32[1536,256]{1,0:T(8,128)S(1)}, f32[1536,256]{1,0:T(8,128)}, u32[]{:S(2)}) copy-start(f32[1536,256]{1,0:T(8,128)} %mul.127) | copy-start | bytes 4718596
  242.1 67.4 %copy-start.1 = (f32[512,768]{1,0:T(8,128)S(1)}, f32[512,768]{1,0:T(8,128)}, u32[]{:S(2)}) copy-start(f32[512,768]{1,0:T(8,128)} %param.11) | copy-start | bytes 4718596
Sparse Core Ops, SparseCore 0:
  80.5 156.5 reduce-scatter.1
  314.7 38.5 all-gather.1
where the time goes:
time: 368 us; the launch traced here: 366 us
  waiting for transfers between devices  193 us (52%)
  blocking collectives  64.8 us (18%)
  local copies, waits for them, and re-layouts  53.5 us (15%)
  other arithmetic  20.4 us (6%)
  matrix products  19.8 us (5%)
  between operations  14.9 us (4%)
    reduce_scatter x1, waiting for transfers between devices, on_device(): lax.psum_scatter(coded.astype(jnp.float32).reshape(lax.axis_size('dp') *...  154 us
    psum x1, blocking collectives, global_squares(): return lax.psum(jnp.sum(values * values), ('dp', 'fsdp'))  64.8 us
    all_gather x1, waiting for transfers between devices, on_device(): lax.all_gather(new_master.astype(jnp.bfloat16), 'fsdp', axis=1, tiled=True)  38.7 us
    reshape x1, local copies, waits for them, and re-layouts, on_device(): coded.astype(jnp.float32).reshape(lax.axis_size('dp') * owned, width)  24.7 us
    unnamed x10, local copies, waits for them, and re-layouts  23 us
    dot_general x1, matrix products, encode(): jnp.dot(signed.reshape(count * tiles, length), hmat_low, preferred_elemen...  16.4 us
    reshape x1, other arithmetic, on_device(): coded.astype(jnp.float32).reshape(lax.axis_size('dp') * owned, width)  14.1 us
  transfers between devices with their start and end apart: 2, of which 2 were waited for; matrix products, arithmetic and copies ran while one was open for 1% of the time, Pallas kernels for 0%

commit v1 on v0

v1 whole, which is shorter than its diff:
```python
import functools
import math

import jax
import jax.numpy as jnp
from jax import lax
from jax.experimental import pallas as pl
from jax.experimental.pallas import tpu as pltpu
from jax.sharding import PartitionSpec as P

D = 6144
ROWS = 8192
TILE = 256
WIDTH = 768
TILES = WIDTH // TILE
SIDE = 4
BLOCK = 256
RING0, RING1 = (2, 1), (3, 0)
LIMIT = 4.0 * math.sqrt(ROWS * D)
VMEM_BYTES = 32 * 1024 * 1024


def hadamard(length):
    row_index = lax.broadcasted_iota(jnp.int32, (length, length), 0)
    col_index = lax.broadcasted_iota(jnp.int32, (length, length), 1)
    common_bits = row_index & col_index
    parity = jnp.zeros((length, length), jnp.int32)
    for bit_pos in range(length.bit_length() - 1):
        parity = parity ^ common_bits >> bit_pos & 1
    return 1 - 2 * parity


def hop(value, axis, step):
    if axis == "x":
        pairs = [(i, (i // 4 + step) % 4 * 4 + i % 4) for i in range(16)]
    elif axis == "z":
        pairs = [(i, i // 4 * 4 + (i % 4 + step) % 4) for i in range(16)]
    elif axis == "y":
        pairs = [(i, (i // 2 + step) % 4 * 2 + i % 2) for i in range(8)]
    else:
        pairs = [(i, i ^ 1) for i in range(8)]
    return lax.ppermute(value, "dp" if axis in "xz" else "fsdp", pairs)


def row_scales(index_ref, table_ref):
    index = index_ref[...]
    scale = jnp.zeros(index.shape, jnp.float32)
    for level in range(table_ref.shape[0]):
        scale = jnp.where(index == level, table_ref[level], scale)
    ones = jnp.ones((8 - index.shape[0], index.shape[1]), jnp.float32)
    return jnp.concatenate([scale, ones], axis=0).T


def encode_kernel(count, place_ref, table_ref, grad_ref, index_ref, hmat_ref, *refs):
    arrived, out_ref = refs[:count], refs[count]
    steps = 1.0 / (math.sqrt(TILE) * row_scales(index_ref, table_ref))
    for tile in range(TILES):
        cols = slice(tile * TILE, (tile + 1) * TILE)
        rotated = jnp.dot(grad_ref[:, cols], hmat_ref[cols, :], preferred_element_type=jnp.float32)
        code = jnp.clip(rotated * steps[:, tile : tile + 1], -127.0, 127.0).astype(jnp.bfloat16)
        if count:
            total = code.astype(jnp.float32)
            for ref in arrived:
                total = total + ref[:, cols].astype(jnp.float32)
            code = total.astype(out_ref.dtype)
        out_ref[:, cols] = code


def encode(place, table, grad, index, hmat, half, near, ring, arrived=(), dtype=jnp.bfloat16):
    count = len(ring)

    def block(j, place_ref):
        far = ring[0] + j * (ring[1] - ring[0])
        first, second = place_ref[half], place_ref[1 - half]
        first, second = (first + near) % SIDE, (second + far) % SIDE
        x, z = (first, second) if half == 0 else (second, first)
        return (x * SIDE + z) * 2 + half

    whole = pl.BlockSpec((BLOCK, WIDTH), lambda j, place_ref: (j, 0))
    return pl.pallas_call(
        functools.partial(encode_kernel, len(arrived)),
        out_shape=jax.ShapeDtypeStruct((count * BLOCK, WIDTH), dtype),
        grid_spec=pltpu.PrefetchScalarGridSpec(
            num_scalar_prefetch=1,
            grid=(count,),
            in_specs=[
                pl.BlockSpec(memory_space=pltpu.SMEM),
                pl.BlockSpec((BLOCK, WIDTH), lambda j, place_ref: (block(j, place_ref), 0)),
                pl.BlockSpec((TILES, BLOCK), lambda j, place_ref: (0, block(j, place_ref))),
                pl.BlockSpec((WIDTH, TILE), lambda j, place_ref: (0, 0)),
            ]
            + [whole] * len(arrived),
            out_specs=whole,
        ),
        compiler_params=pltpu.CompilerParams(vmem_limit_bytes=VMEM_BYTES),
        cost_estimate=pl.CostEstimate(
            flops=2 * count * BLOCK * WIDTH * TILE,
            bytes_accessed=count * BLOCK * WIDTH * 2 * (2 + len(arrived)),
            transcendentals=0,
        ),
    )(place, table, grad, index, hmat, *arrived)


def first_axis(place, table, grad, index, hmat, half):
    axis = "xz"[half]
    code = functools.partial(encode, place, table, grad, index, hmat, half)
    up_far = hop(code(2, RING0), axis, 1)
    down_far = hop(code(2, RING1), axis, -1)
    up_own = hop(code(1, RING1), axis, 1)
    down_own = hop(code(-1, RING0), axis, -1)
    up_sum = hop(code(1, RING0, (up_far,)), axis, 1)
    down_sum = hop(code(-1, RING1, (down_far,)), axis, -1)
    sum0 = code(0, RING0, (up_sum, down_own), jnp.float32)
    sum1 = code(0, RING1, (up_own, down_sum), jnp.float32)
    by_offset = {}
    for ring, total in ((RING0, sum0), (RING1, sum1)):
        for j, far in enumerate(ring):
            by_offset[far] = total[j * BLOCK : (j + 1) * BLOCK]
    return by_offset


def second_axis(blocks, half):
    axis = "zx"[half]
    low, mid = slice(0, BLOCK // 2), slice(BLOCK // 2, BLOCK)
    send = lambda v, step: hop(v.astype(jnp.bfloat16), axis, step)
    up_far = send(blocks[2][low], 1)
    down_far = send(blocks[2][mid], -1)
    up_own = send(blocks[1][mid], 1)
    down_own = send(blocks[3][low], -1)
    up_sum = send(blocks[1][low] + up_far.astype(jnp.float32), 1)
    down_sum = send(blocks[3][mid] + down_far.astype(jnp.float32), -1)
    return blocks[0], (up_sum, down_own), (up_own, down_sum)


def decode_kernel(place_ref, table_ref, own_ref, up0_ref, down0_ref, up1_ref, down1_ref, index_ref, hmat_ref, plain_ref, square_ref):
    half_rows = BLOCK // 2
    scales = row_scales(index_ref, table_ref)
    f32 = jnp.float32
    square = jnp.zeros((8, 128), f32)
    for part, (up_ref, down_ref) in enumerate(((up0_ref, down0_ref), (up1_ref, down1_ref))):
        rows = slice(part * half_rows, (part + 1) * half_rows)
        total = own_ref[rows, :] + up_ref[...].astype(f32) + down_ref[...].astype(f32)
        for tile in range(TILES):
            cols = slice(tile * TILE, (tile + 1) * TILE)
            value = total[:, cols] * scales[rows, tile : tile + 1]
            plain = jnp.zeros((half_rows, TILE), f32)
            for _ in range(3):
                piece = value.astype(jnp.bfloat16)
                plain = plain + jnp.dot(piece, hmat_ref[:, cols], preferred_element_type=f32)
                value = value - piece.astype(f32)
            plain = plain * (1.0 / math.sqrt(TILE))
            plain_ref[rows, cols] = plain
            square = square + jnp.sum((plain * plain).reshape(-1, 8, TILE), axis=0).reshape(8, 2, 128).sum(axis=1)
    square_ref[...] = square


def decode(place, table, terms, index, hmat_t, half):
    own, (up0, down0), (up1, down1) = terms
    block = lambda j, place_ref: (0, (place_ref[0] * SIDE + place_ref[1]) * 2 + half)
    full = pl.BlockSpec((BLOCK, WIDTH), lambda j, place_ref: (0, 0))
    part = pl.BlockSpec((BLOCK // 2, WIDTH), lambda j, place_ref: (0, 0))
    return pl.pallas_call(
        decode_kernel,
        out_shape=(
            jax.ShapeDtypeStruct((BLOCK, WIDTH), jnp.float32),
            jax.ShapeDtypeStruct((8, 128), jnp.float32),
        ),
        grid_spec=pltpu.PrefetchScalarGridSpec(
            num_scalar_prefetch=1,
            grid=(1,),
            in_specs=[
                pl.BlockSpec(memory_space=pltpu.SMEM),
                full,
                part,
                part,
                part,
                part,
                pl.BlockSpec((TILES, BLOCK), block),
                pl.BlockSpec((TILE, WIDTH), lambda j, place_ref: (0, 0)),
            ],
            out_specs=(full, pl.BlockSpec((8, 128), lambda j, place_ref: (0, 0))),
        ),
        compiler_params=pltpu.CompilerParams(vmem_limit_bytes=VMEM_BYTES),
    )(place, table, own, up0, down0, up1, down1, index, hmat_t)


def total_squares(square):
    for axis in "xzy":
        square = square + hop(square, axis, 1) + (hop(square, axis, 2) + hop(square, axis, 3))
    return square + hop(square, "core", 1)


def updated(plain, square, master, mean, var):
    factor = LIMIT / jnp.maximum(jnp.sqrt(jnp.sum(square)), LIMIT)
    grad = plain * factor
    new_mean = 0.9 * mean + 0.1 * grad
    new_var = 0.95 * var + 0.05 * grad * grad
    update = new_mean / (1.0 - 0.9**10) / (jnp.sqrt(new_var / (1.0 - 0.95**10)) + 1e-08)
    return master - 0.02 * (update + 0.1 * master), new_mean, new_var


def weights_kernel(square_ref, plain0_ref, plain1_ref, master_ref, mean_ref, var_ref, out_ref):
    for half, plain_ref in enumerate((plain0_ref, plain1_ref)):
        rows = slice(half * BLOCK, (half + 1) * BLOCK)
        new_master, _, _ = updated(plain_ref[...], square_ref[...], master_ref[rows, :], mean_ref[rows, :], var_ref[rows, :])
        out_ref[rows, :] = new_master.astype(jnp.bfloat16)


def state_kernel(square_ref, plain0_ref, plain1_ref, master_ref, mean_ref, var_ref, *out_refs):
    for half, plain_ref in enumerate((plain0_ref, plain1_ref)):
        rows = slice(half * BLOCK, (half + 1) * BLOCK)
        values = updated(plain_ref[...], square_ref[...], master_ref[rows, :], mean_ref[rows, :], var_ref[rows, :])
        for ref, value in zip(out_refs, values, strict=True):
            ref[rows, :] = value


def adamw(kernel, out_shape, square, plains, master, mean, var):
    step = WIDTH // 6
    half = pl.BlockSpec((BLOCK, step), lambda j: (0, j))
    full = pl.BlockSpec((2 * BLOCK, step), lambda j: (0, j))
    return pl.pallas_call(
        kernel,
        out_shape=out_shape,
        grid=(6,),
        in_specs=[pl.BlockSpec((8, 128), lambda j: (0, 0)), half, half, full, full, full],
        out_specs=jax.tree.map(lambda _: full, out_shape),
        compiler_params=pltpu.CompilerParams(vmem_limit_bytes=VMEM_BYTES),
        cost_estimate=pl.CostEstimate(flops=20 * 512 * 768, bytes_accessed=10 * 512 * 768 * 4, transcendentals=512 * 768),
    )(square, *plains, master, mean, var)


def gather_columns(low):
    fsdp = lax.axis_index("fsdp")
    chip, core = fsdp // 2, fsdp % 2
    moved = [low, hop(low, "y", 1), hop(low, "y", -1), hop(low, "y", 2)]
    other = [hop(v, "core", 1) for v in moved]
    out = jnp.zeros((low.shape[0], D), low.dtype)
    for mine, theirs, step in zip(moved, other, (0, 1, -1, 2), strict=True):
        source = (chip - step) % SIDE * 2
        out = lax.dynamic_update_slice(out, mine, (0, (source + core) * WIDTH))
        out = lax.dynamic_update_slice(out, theirs, (0, (source + 1 - core) * WIDTH))
    return out


def on_device(grad_shards, hadamard_signs, scale_index, scale_table, master, mean_moment, var_moment):
    grad = grad_shards[0]
    dp = lax.axis_index("dp")
    place = jnp.stack([dp // SIDE, dp % SIDE]).astype(jnp.int32)
    sign = 2 * hadamard_signs - 1
    hmat = hadamard(TILE)
    hmat_in = (jnp.tile(hmat, (TILES, 1)) * sign[:, None]).astype(jnp.bfloat16)
    hmat_out = (jnp.tile(hmat, (1, TILES)) * sign[None, :]).astype(jnp.bfloat16)
    plains, squares = [], []
    firsts = [first_axis(place, scale_table, grad, scale_index, hmat_in, half) for half in (0, 1)]
    for half in (0, 1):
        terms = second_axis(firsts[half], half)
        plain, square = decode(place, scale_table, terms, scale_index, hmat_out, half)
        plains.append(plain)
        squares.append(square)
    square = total_squares(squares[0] + squares[1])
    state = jax.ShapeDtypeStruct((2 * BLOCK, WIDTH), jnp.float32)
    low = adamw(weights_kernel, jax.ShapeDtypeStruct((2 * BLOCK, WIDTH), jnp.bfloat16), square, plains, master, mean_moment, var_moment)
    new_master, new_mean, new_var = adamw(state_kernel, (state,) * 3, square, plains, master, mean_moment, var_moment)
    return new_master, new_mean, new_var, gather_columns(low)


def solution(mesh):
    return jax.shard_map(
        on_device,
        mesh=mesh,
        in_specs=(
            P("dp", None, "fsdp"),
            P("fsdp"),
            P("fsdp", None),
            P(),
            P("dp", "fsdp"),
            P("dp", "fsdp"),
            P("dp", "fsdp"),
        ),
        out_specs=(P("dp", "fsdp"), P("dp", "fsdp"), P("dp", "fsdp"), P("dp", None)),
        check_vma=False,
    )
```

time: 368 us -> 211 us (0.57)
  waiting for transfers between devices: 193 us -> 55.4 us
  starting transfers between devices: 0.08 us -> 70.5 us
  blocking collectives: 64.8 us -> 0 us
  Pallas kernels: 0 us -> 50.1 us
  local copies, waits for them, and re-layouts: 53.5 us -> 31.4 us
  matrix products: 19.8 us -> 0 us
  other arithmetic: 20.4 us -> 1.56 us
  between operations: 14.9 us -> 1.21 us
    reduce_scatter x1 -> x0, waiting for transfers between devices: 154 us -> none  [on_device(): lax.psum_scatter(coded.astype(jnp.float32).reshape(lax.axis_size('dp') *...]
    ppermute x0 -> x41, starting transfers between devices: none -> 70.5 us  [hop(): return lax.ppermute(value, 'dp' if axis in 'xz' else 'fsdp', pairs)]
    psum x1 -> x0, blocking collectives: 64.8 us -> none  [global_squares(): return lax.psum(jnp.sum(values * values), ('dp', 'fsdp'))]
    ppermute x0 -> x41, waiting for transfers between devices: none -> 55.4 us  [hop(): return lax.ppermute(value, 'dp' if axis in 'xz' else 'fsdp', pairs)]
    pallas_call x0 -> x20, Pallas kernels: none -> 50.1 us  [the longest x16 37.6 us: encode(): pl.pallas_call(functools.partial(encode_kernel, len(arrived)), out_shape=...]
    all_gather x1 -> x0, waiting for transfers between devices: 38.7 us -> none  [on_device(): lax.all_gather(new_master.astype(jnp.bfloat16), 'fsdp', axis=1, tiled=True)]
    reshape x3 -> x0, local copies, waits for them, and re-layouts: 28.1 us -> none  [the longest x1 24.7 us: on_device(): coded.astype(jnp.float32).reshape(lax.axis_size('dp') * owned, width)]
    dot_general x2 -> x0, matrix products: 19.8 us -> none  [the longest x1 16.4 us: encode(): jnp.dot(signed.reshape(count * tiles, length), hmat_low, preferred_elemen...]
  transfers between devices with their start and end apart: 2 -> 41, of which waited for: 2 -> 20; matrix products, arithmetic and copies ran while one was open for 1% -> 5% of each run, Pallas kernels for 0% -> 20%
where the time goes in v1:
time: 211 us; the launch traced here: 210 us
  starting transfers between devices  70.5 us (33%)
  waiting for transfers between devices  55.4 us (26%)
  Pallas kernels  50.1 us (24%)
  local copies, waits for them, and re-layouts  31.4 us (15%)
    ppermute x41, starting transfers between devices, hop(): return lax.ppermute(value, 'dp' if axis in 'xz' else 'fsdp', pairs)  70.5 us
    ppermute x41, waiting for transfers between devices, hop(): return lax.ppermute(value, 'dp' if axis in 'xz' else 'fsdp', pairs)  55.4 us
    pallas_call x16, Pallas kernels, encode(): pl.pallas_call(functools.partial(encode_kernel, len(arrived)), out_shape=...  37.6 us
    unnamed x38, local copies, waits for them, and re-layouts  20.6 us
    pallas_call x2, Pallas kernels, adamw(): pl.pallas_call(kernel, out_shape=out_shape, grid=(6,), in_specs=[pl.Block...  8.69 us
  transfers between devices with their start and end apart: 41, of which 20 were waited for; matrix products, arithmetic and copies ran while one was open for 5% of the time, Pallas kernels for 20%

profile of v1, /device:TPU:1, one launch (start us, length us, event | category | flops | bytes accessed | tf_op | source)
XLA Modules:
  0.0 210.1 jit_solution(12192034343450984967)
XLA Ops:
  2.0 4.6 %copy-done = bf16[1,8192,768]{2,1,0:T(8,128)(2,1)S(1)} copy-done((bf16[1,8192,768]{2,1,0:T(8,128)(2,1)S(1)}, bf16[1,8192,768]{2,1,0:T(8,128)(2,1)}, u32[]{:S(2)}) %copy-start) | copy-done | bytes 12582936
  10.1 2.5 %collective-permute-start.15 = (bf16[512,768]{1,0:T(8,128)(2,1)S(1)}, bf16[512,768]{1,0:T(8,128)(2,1)S(1)}, u32[]{:S(2)}, u32[]{:S(2)}) collective-permute-start(bf16[512,768]{1,0:T(8,128)(2,1)S(1)} %shard_map.115), channel_id=1, source_target_pairs={{0,8},{8,16},{16,24},{24,0},{32,40},{40,48},{48,56},{56,32},{64,72... | collective-permute-start | bytes 2359304 | tf_op jit(solution)/shard_map/ppermute | solution.py:42
  29.0 3.0 %collective-permute-done.15.refs_0_ = bf16[512,768]{1,0:T(8,128)(2,1)S(1)} collective-permute-done((bf16[512,768]{1,0:T(8,128)(2,1)S(1)}, bf16[512,768]{1,0:T(8,128)(2,1)S(1)}, u32[]{:S(2)}, u32[]{:S(2)}) %collective-permute-start.15) | collective-permute-done | bytes 786464 | tf_op jit(solution)/shard_map/ppermute | solution.py:42
  34.8 2.8 %shard_map.113 = bf16[512,768]{1,0:T(8,128)(2,1)} custom-call(s32[2]{0:T(128)S(1)} %pad_add_fusion.place_ref, f32[16]{0:T(128)S(1)} %copy-done.15, bf16[8192,768]{1,0:T(8,128)(2,1)S(1)} %bitcast.15, s32[3,8192]{1,0:T(4,128)S(1)} %copy-done.2, bf16[768,256]{1,0:T(8,128)(2,1)S(1)} %fusion.hmat_ref, bf16[512,768]{1,0:T(8,128)(2,1)S(1)} %collective-permute-done.13.refs_0_), custom_call_target="tpu_custom_call" | custom-call | flops 201326592 | bytes 2359296 | tf_op jit(solution)/shard_map/pallas_call | solution.py:80
  37.6 12.4 %collective-permute-done.17.refs_1_ = bf16[512,768]{1,0:T(8,128)(2,1)S(1)} collective-permute-done((bf16[512,768]{1,0:T(8,128)(2,1)S(1)}, bf16[512,768]{1,0:T(8,128)(2,1)S(1)}, u32[]{:S(2)}, u32[]{:S(2)}) %collective-permute-start.17) | collective-permute-done | bytes 786464 | tf_op jit(solution)/shard_map/ppermute | solution.py:42
  50.0 3.3 %collective-permute-start.14 = (bf16[512,768]{1,0:T(8,128)(2,1)}, bf16[512,768]{1,0:T(8,128)(2,1)}, u32[]{:S(2)}, u32[]{:S(2)}) collective-permute-start(bf16[512,768]{1,0:T(8,128)(2,1)} %shard_map.113), channel_id=1, source_target_pairs={{0,24},{8,0},{16,8},{24,16},{32,56},{40,32},{48,40},{56,48},{64,88... | collective-permute-start | bytes 2359304 | tf_op jit(solution)/shard_map/ppermute | solution.py:42
  53.3 2.7 %shard_map.108 = bf16[512,768]{1,0:T(8,128)(2,1)} custom-call(s32[2]{0:T(128)S(1)} %pad_add_fusion.place_ref, f32[16]{0:T(128)S(1)} %copy-done.15, bf16[8192,768]{1,0:T(8,128)(2,1)S(1)} %bitcast.16, s32[3,8192]{1,0:T(4,128)S(1)} %copy-done.2, bf16[768,256]{1,0:T(8,128)(2,1)S(1)} %fusion.hmat_ref), custom_call_target="tpu_custom_call" | custom-call | flops 201326592 | bytes 1572864 | tf_op jit(solution)/shard_map/pallas_call | solution.py:80
  56.0 2.5 %collective-permute-start.5 = (bf16[512,768]{1,0:T(8,128)(2,1)}, bf16[512,768]{1,0:T(8,128)(2,1)}, u32[]{:S(2)}, u32[]{:S(2)}) collective-permute-start(bf16[512,768]{1,0:T(8,128)(2,1)} %shard_map.108), channel_id=1, source_target_pairs={{0,96},{8,104},{16,112},{24,120},{32,0},{40,8},{48,16},{56,24},{64... | collective-permute-start | bytes 2359304 | tf_op jit(solution)/shard_map/ppermute | solution.py:42
  58.5 2.8 %shard_map.107 = bf16[512,768]{1,0:T(8,128)(2,1)} custom-call(s32[2]{0:T(128)S(1)} %pad_add_fusion.place_ref, f32[16]{0:T(128)S(1)} %copy-done.15, bf16[8192,768]{1,0:T(8,128)(2,1)S(1)} %bitcast.17, s32[3,8192]{1,0:T(4,128)S(1)} %copy-done.2, bf16[768,256]{1,0:T(8,128)(2,1)S(1)} %fusion.hmat_ref, bf16[512,768]{1,0:T(8,128)(2,1)S(1)} %collective-permute-done.3.refs_0_), custom_call_target="tpu_custom_call" | custom-call | flops 201326592 | bytes 2359296 | tf_op jit(solution)/shard_map/pallas_call | solution.py:80
  61.3 2.7 %shard_map.102 = bf16[512,768]{1,0:T(8,128)(2,1)} custom-call(s32[2]{0:T(128)S(1)} %pad_add_fusion.place_ref, f32[16]{0:T(128)S(1)} %copy-done.15, bf16[8192,768]{1,0:T(8,128)(2,1)S(1)} %bitcast.18, s32[3,8192]{1,0:T(4,128)S(1)} %copy-done.2, bf16[768,256]{1,0:T(8,128)(2,1)S(1)} %fusion.hmat_ref), custom_call_target="tpu_custom_call" | custom-call | flops 201326592 | bytes 1572864 | tf_op jit(solution)/shard_map/pallas_call | solution.py:80
  64.0 2.8 %shard_map.104 = bf16[512,768]{1,0:T(8,128)(2,1)} custom-call(s32[2]{0:T(128)S(1)} %pad_add_fusion.place_ref, f32[16]{0:T(128)S(1)} %copy-done.15, bf16[8192,768]{1,0:T(8,128)(2,1)S(1)} %bitcast.19, s32[3,8192]{1,0:T(4,128)S(1)} %copy-done.2, bf16[768,256]{1,0:T(8,128)(2,1)S(1)} %fusion.hmat_ref, bf16[512,768]{1,0:T(8,128)(2,1)S(1)} %collective-permute-done.1.refs_0_), custom_call_target="tpu_custom_call" | custom-call | flops 201326592 | bytes 2359296 | tf_op jit(solution)/shard_map/pallas_call | solution.py:80
  68.8 2.6 %collective-permute-start.2 = (bf16[512,768]{1,0:T(8,128)(2,1)}, bf16[512,768]{1,0:T(8,128)(2,1)}, u32[]{:S(2)}, u32[]{:S(2)}) collective-permute-start(bf16[512,768]{1,0:T(8,128)(2,1)} %shard_map.104), channel_id=1, source_target_pairs={{0,96},{8,104},{16,112},{24,120},{32,0},{40,8},{48,16},{56,24},{64... | collective-permute-start | bytes 2359304 | tf_op jit(solution)/shard_map/ppermute | solution.py:42
  74.6 4.6 %copy-done.1 = bf16[1,8192,768]{2,1,0:T(8,128)(2,1)S(1)} copy-done((bf16[1,8192,768]{2,1,0:T(8,128)(2,1)S(1)}, bf16[1,8192,768]{2,1,0:T(8,128)(2,1)}, u32[]{:S(2)}) %copy-start.1) | copy-done | bytes 12582936
  82.7 2.6 %shard_map.114 = f32[512,768]{1,0:T(8,128)S(1)} custom-call(s32[2]{0:T(128)S(1)} %pad_add_fusion.place_ref, f32[16]{0:T(128)S(1)} %copy-done.16, bf16[8192,768]{1,0:T(8,128)(2,1)S(1)} %bitcast.21, s32[3,8192]{1,0:T(4,128)S(1)} %copy-done.3, bf16[768,256]{1,0:T(8,128)(2,1)S(1)} %fusion.hmat_ref, bf16[512,768]{1,0:T(8,128)(2,1)S(1)} %collective-permute-done.12.refs_0_, ...), custom_call_target="tpu_custom_call" | custom-call | flops 201326592 | bytes 3145728 | tf_op jit(solution)/shard_map/pallas_call | solution.py:80
  85.3 2.7 %collective-permute-start.22 = (bf16[128,768]{1,0:T(8,128)(2,1)S(1)}, bf16[128,768]{1,0:T(8,128)(2,1)S(1)}, u32[]{:S(2)}, u32[]{:S(2)}) collective-permute-start(bf16[128,768]{1,0:T(8,128)(2,1)S(1)} %get-tuple-element.18), channel_id=1, source_target_pairs={{0,96},{8,104},{16,112},{24,120},{32,0},{40,8},{48,16},{56,24},{64... | collective-permute-start | bytes 589832 | tf_op jit(solution)/shard_map/ppermute | solution.py:42
  88.0 2.7 %shard_map.109 = f32[512,768]{1,0:T(8,128)S(1)} custom-call(s32[2]{0:T(128)S(1)} %pad_add_fusion.place_ref, f32[16]{0:T(128)S(1)} %copy-done.16, bf16[8192,768]{1,0:T(8,128)(2,1)S(1)} %bitcast.22, s32[3,8192]{1,0:T(4,128)S(1)} %copy-done.3, bf16[768,256]{1,0:T(8,128)(2,1)S(1)} %fusion.hmat_ref, bf16[512,768]{1,0:T(8,128)(2,1)} %collective-permute-done.4.refs_0_, ...), custom_call_target="tpu_custom_call" | custom-call | flops 201326592 | bytes 3145728 | tf_op jit(solution)/shard_map/pallas_call | solution.py:80
  90.9 5.6 %collective-permute-done.refs_0_ = bf16[512,768]{1,0:T(8,128)(2,1)S(1)} collective-permute-done((bf16[512,768]{1,0:T(8,128)(2,1)}, bf16[512,768]{1,0:T(8,128)(2,1)S(1)}, u32[]{:S(2)}, u32[]{:S(2)}) %collective-permute-start) | collective-permute-done | bytes 786464 | tf_op jit(solution)/shard_map/ppermute | solution.py:42
  96.6 2.6 %shard_map.105 = f32[512,768]{1,0:T(8,128)S(1)} custom-call(s32[2]{0:T(128)S(1)} %pad_add_fusion.place_ref, f32[16]{0:T(128)S(1)} %copy-done.16, bf16[8192,768]{1,0:T(8,128)(2,1)S(1)} %bitcast.23, s32[3,8192]{1,0:T(4,128)S(1)} %copy-done.3, bf16[768,256]{1,0:T(8,128)(2,1)S(1)} %fusion.hmat_ref, bf16[512,768]{1,0:T(8,128)(2,1)S(1)} %collective-permute-done.refs_0_, ...), custom_call_target="tpu_custom_call" | custom-call | flops 201326592 | bytes 3145728 | tf_op jit(solution)/shard_map/pallas_call | solution.py:80
  103.7 3.0 %collective-permute-done.6 = bf16[128,768]{1,0:T(8,128)(2,1)S(1)} collective-permute-done((bf16[128,768]{1,0:T(8,128)(2,1)S(1)}, bf16[128,768]{1,0:T(8,128)(2,1)S(1)}, u32[]{:S(2)}, u32[]{:S(2)}) %collective-permute-start.6) | collective-permute-done | bytes 196640 | tf_op jit(solution)/shard_map/ppermute | solution.py:42
  106.8 2.7 %collective-permute-start.23 = (bf16[128,768]{1,0:T(8,128)(2,1)S(1)}, bf16[128,768]{1,0:T(8,128)(2,1)S(1)}, u32[]{:S(2)}, u32[]{:S(2)}) collective-permute-start(bf16[128,768]{1,0:T(8,128)(2,1)S(1)} %fusion.1), channel_id=1, source_target_pairs={{0,96},{8,104},{16,112},{24,120},{32,0},{40,8},{48,16},{56,24},{64... | collective-permute-start | bytes 589832 | tf_op jit(solution)/shard_map/ppermute | solution.py:42
  109.5 3.2 %collective-permute-done.19.up0_ref = bf16[128,768]{1,0:T(8,128)(2,1)S(1)} collective-permute-done((bf16[128,768]{1,0:T(8,128)(2,1)S(1)}, bf16[128,768]{1,0:T(8,128)(2,1)S(1)}, u32[]{:S(2)}, u32[]{:S(2)}) %collective-permute-start.19) | collective-permute-done | bytes 196640 | tf_op jit(solution)/shard_map/ppermute | solution.py:42
  115.8 3.0 %collective-permute-done.7.up0_ref = bf16[128,768]{1,0:T(8,128)(2,1)S(1)} collective-permute-done((bf16[128,768]{1,0:T(8,128)(2,1)S(1)}, bf16[128,768]{1,0:T(8,128)(2,1)S(1)}, u32[]{:S(2)}, u32[]{:S(2)}) %collective-permute-start.7) | collective-permute-done | bytes 196640 | tf_op jit(solution)/shard_map/ppermute | solution.py:42
  120.9 2.5 %collective-permute-start.26 = (f32[8,128]{1,0:T(8,128)S(1)}, f32[8,128]{1,0:T(8,128)S(1)}, u32[]{:S(2)}, u32[]{:S(2)}) collective-permute-start(f32[8,128]{1,0:T(8,128)S(1)} %add.123), channel_id=1, source_target_pairs={{0,96},{8,104},{16,112},{24,120},{32,0},{40,8},{48,16},{56,24},{64... | collective-permute-start | bytes 12296 | tf_op jit(solution)/shard_map/ppermute | solution.py:42
  125.5 2.5 %collective-permute-start.29 = (f32[8,128]{1,0:T(8,128)S(1)}, f32[8,128]{1,0:T(8,128)S(1)}, u32[]{:S(2)}, u32[]{:S(2)}) collective-permute-start(f32[8,128]{1,0:T(8,128)S(1)} %add_add_fusion.2), channel_id=1, source_target_pairs={{0,24},{8,0},{16,8},{24,16},{32,56},{40,32},{48,40},{56,48},{64,88... | collective-permute-start | bytes 12296 | tf_op jit(solution)/shard_map/ppermute | solution.py:42
  130.9 2.6 %collective-permute-start.31 = (f32[8,128]{1,0:T(8,128)S(1)}, f32[8,128]{1,0:T(8,128)S(1)}, u32[]{:S(2)}, u32[]{:S(2)}) collective-permute-start(f32[8,128]{1,0:T(8,128)S(1)} %add_add_fusion.1), channel_id=1, source_target_pairs={{0,4},{1,5},{2,6},{3,7},{4,0},{5,1},{6,2},{7,3},{8,12},{9,13},{10,... | collective-permute-start | bytes 12296 | tf_op jit(solution)/shard_map/ppermute | solution.py:42
  136.0 12.0 %collective-permute-start.33 = (f32[8,128]{1,0:T(8,128)S(1)}, f32[8,128]{1,0:T(8,128)S(1)}, u32[]{:S(2)}, u32[]{:S(2)}) collective-permute-start(f32[8,128]{1,0:T(8,128)S(1)} %add_add_fusion), channel_id=1, source_target_pairs={{0,1},{1,0},{2,3},{3,2},{4,5},{5,4},{6,7},{7,6},{8,9},{9,8},{10,11... | collective-permute-start | bytes 12296 | tf_op jit(solution)/shard_map/ppermute | solution.py:42
  148.8 3.9 %shard_map.121 = bf16[512,768]{1,0:T(8,128)(2,1)S(1)} custom-call(f32[8,128]{1,0:T(8,128)S(1)} %add.133.square_ref, f32[256,768]{1,0:T(8,128)S(1)} %get-tuple-element.13.plain0_ref, f32[256,768]{1,0:T(8,128)S(1)} %get-tuple-element.14.plain1_ref, f32[512,768]{1,0:T(8,128)S(1)} %copy-done.4, f32[512,768]{1,0:T(8,128)S(1)} %copy-done.5, f32[512,768]{1,0:T(8,128)S(1)} %copy-done.7), custom_call_target="tpu_custom_call" | custom-call | flops 7864320 | bytes 15728640 | tf_op jit(solution)/shard_map/pallas_call | solution.py:221
  152.8 2.7 %collective-permute-start.37 = (bf16[512,768]{1,0:T(8,128)(2,1)S(1)}, bf16[512,768]{1,0:T(8,128)(2,1)}, u32[]{:S(2)}, u32[]{:S(2)}) collective-permute-start(bf16[512,768]{1,0:T(8,128)(2,1)S(1)} %shard_map.121), channel_id=1, source_target_pairs={{0,6},{1,7},{2,0},{3,1},{4,2},{5,3},{6,4},{7,5},{8,14},{9,15},{10,... | collective-permute-start | bytes 2359304 | tf_op jit(solution)/shard_map/ppermute | solution.py:42
  157.2 15.7 %collective-permute-done.35 = bf16[512,768]{1,0:T(8,128)(2,1)} collective-permute-done((bf16[512,768]{1,0:T(8,128)(2,1)S(1)}, bf16[512,768]{1,0:T(8,128)(2,1)}, u32[]{:S(2)}, u32[]{:S(2)}) %collective-permute-start.35) | collective-permute-done | bytes 786464 | tf_op jit(solution)/shard_map/ppermute | solution.py:42
  174.1 16.0 %collective-permute-start.38 = (bf16[512,768]{1,0:T(8,128)(2,1)}, bf16[512,768]{1,0:T(8,128)(2,1)}, u32[]{:S(2)}, u32[]{:S(2)}) collective-permute-start(bf16[512,768]{1,0:T(8,128)(2,1)} %collective-permute-done.37), channel_id=1, source_target_pairs={{0,1},{1,0},{2,3},{3,2},{4,5},{5,4},{6,7},{7,6},{8,9},{9,8},{10,11... | collective-permute-start | bytes 2359304 | tf_op jit(solution)/shard_map/ppermute | solution.py:42
  195.2 4.8 %shard_map.120 = (f32[512,768]{1,0:T(8,128)}, f32[512,768]{1,0:T(8,128)}, f32[512,768]{1,0:T(8,128)}) custom-call(f32[8,128]{1,0:T(8,128)S(1)} %add.133.square_ref, f32[256,768]{1,0:T(8,128)S(1)} %copy-done.12, f32[256,768]{1,0:T(8,128)S(1)} %copy-done.10, f32[512,768]{1,0:T(8,128)S(1)} %copy-done.4, f32[512,768]{1,0:T(8,128)S(1)} %copy-done.6, ...), custom_call_target="tpu_custom_call" | custom-call | flops 7864320 | bytes 15728640 | tf_op jit(solution)/shard_map/pallas_call | solution.py:221
  207.4 2.7 %copy-done.17 = bf16[512,6144]{1,0:T(8,128)(2,1)} copy-done((bf16[512,6144]{1,0:T(8,128)(2,1)}, bf16[512,6144]{1,0:T(8,128)(2,1)S(1)}, u32[]{:S(2)}) %copy-start.17) | copy-done | bytes 6291480
  (142 shorter events, 66.2 us)
Async XLA Ops:
  10.1 21.9 %collective-permute-start.15 = (bf16[512,768]{1,0:T(8,128)(2,1)S(1)}, bf16[512,768]{1,0:T(8,128)(2,1)S(1)}, u32[]{:S(2)}, u32[]{:S(2)}) collective-permute-start(bf16[512,768]{1,0:T(8,128)(2,1)S(1)} %shard_map.115), channel_id=1, source_target_pairs={{0,8},{8,16},{16,24},{24,0},{32,40},{40,48},{48,56},{56,32},{64,72... | collective-permute-start | bytes 2359304 | tf_op jit(solution)/shard_map/ppermute | solution.py:42
  14.6 19.4 %collective-permute-start.13 = (bf16[512,768]{1,0:T(8,128)(2,1)S(1)}, bf16[512,768]{1,0:T(8,128)(2,1)S(1)}, u32[]{:S(2)}, u32[]{:S(2)}) collective-permute-start(bf16[512,768]{1,0:T(8,128)(2,1)S(1)} %shard_map.112), channel_id=1, source_target_pairs={{0,24},{8,0},{16,8},{24,16},{32,56},{40,32},{48,40},{56,48},{64,88... | collective-permute-start | bytes 2359304 | tf_op jit(solution)/shard_map/ppermute | solution.py:42
  18.8 31.2 %collective-permute-start.17 = (bf16[512,768]{1,0:T(8,128)(2,1)S(1)}, bf16[512,768]{1,0:T(8,128)(2,1)S(1)}, u32[]{:S(2)}, u32[]{:S(2)}) collective-permute-start(bf16[512,768]{1,0:T(8,128)(2,1)S(1)} %shard_map.117), channel_id=1, source_target_pairs={{0,24},{8,0},{16,8},{24,16},{32,56},{40,32},{48,40},{56,48},{64,88... | collective-permute-start | bytes 2359304 | tf_op jit(solution)/shard_map/ppermute | solution.py:42
  22.3 33.7 %collective-permute-start.3 = (bf16[512,768]{1,0:T(8,128)(2,1)S(1)}, bf16[512,768]{1,0:T(8,128)(2,1)S(1)}, u32[]{:S(2)}, u32[]{:S(2)}) collective-permute-start(bf16[512,768]{1,0:T(8,128)(2,1)S(1)} %shard_map.106), channel_id=1, source_target_pairs={{0,32},{8,40},{16,48},{24,56},{32,64},{40,72},{48,80},{56,88},{64,... | collective-permute-start | bytes 2359304 | tf_op jit(solution)/shard_map/ppermute | solution.py:42
  25.5 35.7 %collective-permute-start.1 = (bf16[512,768]{1,0:T(8,128)(2,1)S(1)}, bf16[512,768]{1,0:T(8,128)(2,1)S(1)}, u32[]{:S(2)}, u32[]{:S(2)}) collective-permute-start(bf16[512,768]{1,0:T(8,128)(2,1)S(1)} %shard_map.103), channel_id=1, source_target_pairs={{0,96},{8,104},{16,112},{24,120},{32,0},{40,8},{48,16},{56,24},{64... | collective-permute-start | bytes 2359304 | tf_op jit(solution)/shard_map/ppermute | solution.py:42
  32.0 34.8 %collective-permute-start.12 = (bf16[512,768]{1,0:T(8,128)(2,1)S(1)}, bf16[512,768]{1,0:T(8,128)(2,1)S(1)}, u32[]{:S(2)}, u32[]{:S(2)}) collective-permute-start(bf16[512,768]{1,0:T(8,128)(2,1)S(1)} %shard_map.111), channel_id=1, source_target_pairs={{0,8},{8,16},{16,24},{24,0},{32,40},{40,48},{48,56},{56,32},{64,72... | collective-permute-start | bytes 2359304 | tf_op jit(solution)/shard_map/ppermute | solution.py:42
  34.1 33.8 %collective-permute-start.16 = (bf16[512,768]{1,0:T(8,128)(2,1)S(1)}, bf16[512,768]{1,0:T(8,128)(2,1)S(1)}, u32[]{:S(2)}, u32[]{:S(2)}) collective-permute-start(bf16[512,768]{1,0:T(8,128)(2,1)S(1)} %shard_map.116), channel_id=1, source_target_pairs={{0,8},{8,16},{16,24},{24,0},{32,40},{40,48},{48,56},{56,32},{64,72... | collective-permute-start | bytes 2359304 | tf_op jit(solution)/shard_map/ppermute | solution.py:42
  50.0 32.6 %collective-permute-start.14 = (bf16[512,768]{1,0:T(8,128)(2,1)}, bf16[512,768]{1,0:T(8,128)(2,1)}, u32[]{:S(2)}, u32[]{:S(2)}) collective-permute-start(bf16[512,768]{1,0:T(8,128)(2,1)} %shard_map.113), channel_id=1, source_target_pairs={{0,24},{8,0},{16,8},{24,16},{32,56},{40,32},{48,40},{56,48},{64,88... | collective-permute-start | bytes 2359304 | tf_op jit(solution)/shard_map/ppermute | solution.py:42
  56.0 29.3 %collective-permute-start.5 = (bf16[512,768]{1,0:T(8,128)(2,1)}, bf16[512,768]{1,0:T(8,128)(2,1)}, u32[]{:S(2)}, u32[]{:S(2)}) collective-permute-start(bf16[512,768]{1,0:T(8,128)(2,1)} %shard_map.108), channel_id=1, source_target_pairs={{0,96},{8,104},{16,112},{24,120},{32,0},{40,8},{48,16},{56,24},{64... | collective-permute-start | bytes 2359304 | tf_op jit(solution)/shard_map/ppermute | solution.py:42
  61.3 26.8 %collective-permute-start.4 = (bf16[512,768]{1,0:T(8,128)(2,1)}, bf16[512,768]{1,0:T(8,128)(2,1)}, u32[]{:S(2)}, u32[]{:S(2)}) collective-permute-start(bf16[512,768]{1,0:T(8,128)(2,1)} %shard_map.107), channel_id=1, source_target_pairs={{0,32},{8,40},{16,48},{24,56},{32,64},{40,72},{48,80},{56,88},{64,... | collective-permute-start | bytes 2359304 | tf_op jit(solution)/shard_map/ppermute | solution.py:42
  66.8 29.7 %collective-permute-start = (bf16[512,768]{1,0:T(8,128)(2,1)}, bf16[512,768]{1,0:T(8,128)(2,1)S(1)}, u32[]{:S(2)}, u32[]{:S(2)}) collective-permute-start(bf16[512,768]{1,0:T(8,128)(2,1)} %shard_map.102), channel_id=1, source_target_pairs={{0,32},{8,40},{16,48},{24,56},{32,64},{40,72},{48,80},{56,88},{64,... | collective-permute-start | bytes 2359304 | tf_op jit(solution)/shard_map/ppermute | solution.py:42
  68.8 27.7 %collective-permute-start.2 = (bf16[512,768]{1,0:T(8,128)(2,1)}, bf16[512,768]{1,0:T(8,128)(2,1)}, u32[]{:S(2)}, u32[]{:S(2)}) collective-permute-start(bf16[512,768]{1,0:T(8,128)(2,1)} %shard_map.104), channel_id=1, source_target_pairs={{0,96},{8,104},{16,112},{24,120},{32,0},{40,8},{48,16},{56,24},{64... | collective-permute-start | bytes 2359304 | tf_op jit(solution)/shard_map/ppermute | solution.py:42
  82.6 18.1 %collective-permute-start.18 = (bf16[128,768]{1,0:T(8,128)(2,1)S(1)}, bf16[128,768]{1,0:T(8,128)(2,1)S(1)}, u32[]{:S(2)}, u32[]{:S(2)}) collective-permute-start(bf16[128,768]{1,0:T(8,128)(2,1)S(1)} %get-tuple-element.20), channel_id=1, source_target_pairs={{0,32},{8,40},{16,48},{24,56},{32,64},{40,72},{48,80},{56,88},{64,... | collective-permute-start | bytes 589832 | tf_op jit(solution)/shard_map/ppermute | solution.py:42
  85.3 15.5 %collective-permute-start.22 = (bf16[128,768]{1,0:T(8,128)(2,1)S(1)}, bf16[128,768]{1,0:T(8,128)(2,1)S(1)}, u32[]{:S(2)}, u32[]{:S(2)}) collective-permute-start(bf16[128,768]{1,0:T(8,128)(2,1)S(1)} %get-tuple-element.18), channel_id=1, source_target_pairs={{0,96},{8,104},{16,112},{24,120},{32,0},{40,8},{48,16},{56,24},{64... | collective-permute-start | bytes 589832 | tf_op jit(solution)/shard_map/ppermute | solution.py:42
  88.0 18.7 %collective-permute-start.21 = (bf16[128,768]{1,0:T(8,128)(2,1)S(1)}, bf16[128,768]{1,0:T(8,128)(2,1)S(1)}, u32[]{:S(2)}, u32[]{:S(2)}) collective-permute-start(bf16[128,768]{1,0:T(8,128)(2,1)S(1)} %get-tuple-element.19), channel_id=1, source_target_pairs={{0,32},{8,40},{16,48},{24,56},{32,64},{40,72},{48,80},{56,88},{64,... | collective-permute-start | bytes 589832 | tf_op jit(solution)/shard_map/ppermute | solution.py:42
  96.5 13.0 %collective-permute-start.20 = (bf16[128,768]{1,0:T(8,128)(2,1)S(1)}, bf16[128,768]{1,0:T(8,128)(2,1)S(1)}, u32[]{:S(2)}, u32[]{:S(2)}) collective-permute-start(bf16[128,768]{1,0:T(8,128)(2,1)S(1)} %slice.110), channel_id=1, source_target_pairs={{0,96},{8,104},{16,112},{24,120},{32,0},{40,8},{48,16},{56,24},{64... | collective-permute-start | bytes 589832 | tf_op jit(solution)/shard_map/ppermute | solution.py:42
  100.7 6.0 %collective-permute-start.6 = (bf16[128,768]{1,0:T(8,128)(2,1)S(1)}, bf16[128,768]{1,0:T(8,128)(2,1)S(1)}, u32[]{:S(2)}, u32[]{:S(2)}) collective-permute-start(bf16[128,768]{1,0:T(8,128)(2,1)S(1)} %get-tuple-element.23), channel_id=1, source_target_pairs={{0,8},{8,16},{16,24},{24,0},{32,40},{40,48},{48,56},{56,32},{64,72... | collective-permute-start | bytes 589832 | tf_op jit(solution)/shard_map/ppermute | solution.py:42
  100.8 14.1 %collective-permute-start.9 = (bf16[128,768]{1,0:T(8,128)(2,1)S(1)}, bf16[128,768]{1,0:T(8,128)(2,1)S(1)}, u32[]{:S(2)}, u32[]{:S(2)}) collective-permute-start(bf16[128,768]{1,0:T(8,128)(2,1)S(1)} %get-tuple-element.22), channel_id=1, source_target_pairs={{0,8},{8,16},{16,24},{24,0},{32,40},{40,48},{48,56},{56,32},{64,72... | collective-permute-start | bytes 589832 | tf_op jit(solution)/shard_map/ppermute | solution.py:42
  101.4 13.5 %collective-permute-start.8 = (bf16[128,768]{1,0:T(8,128)(2,1)S(1)}, bf16[128,768]{1,0:T(8,128)(2,1)S(1)}, u32[]{:S(2)}, u32[]{:S(2)}) collective-permute-start(bf16[128,768]{1,0:T(8,128)(2,1)S(1)} %slice.111), channel_id=1, source_target_pairs={{0,24},{8,0},{16,8},{24,16},{32,56},{40,32},{48,40},{56,48},{64,88... | collective-permute-start | bytes 589832 | tf_op jit(solution)/shard_map/ppermute | solution.py:42
  106.7 6.0 %collective-permute-start.19 = (bf16[128,768]{1,0:T(8,128)(2,1)S(1)}, bf16[128,768]{1,0:T(8,128)(2,1)S(1)}, u32[]{:S(2)}, u32[]{:S(2)}) collective-permute-start(bf16[128,768]{1,0:T(8,128)(2,1)S(1)} %fusion.2), channel_id=1, source_target_pairs={{0,32},{8,40},{16,48},{24,56},{32,64},{40,72},{48,80},{56,88},{64,... | collective-permute-start | bytes 589832 | tf_op jit(solution)/shard_map/ppermute | solution.py:42
  106.8 6.2 %collective-permute-start.23 = (bf16[128,768]{1,0:T(8,128)(2,1)S(1)}, bf16[128,768]{1,0:T(8,128)(2,1)S(1)}, u32[]{:S(2)}, u32[]{:S(2)}) collective-permute-start(bf16[128,768]{1,0:T(8,128)(2,1)S(1)} %fusion.1), channel_id=1, source_target_pairs={{0,96},{8,104},{16,112},{24,120},{32,0},{40,8},{48,16},{56,24},{64... | collective-permute-start | bytes 589832 | tf_op jit(solution)/shard_map/ppermute | solution.py:42
  109.5 6.3 %collective-permute-start.11 = (bf16[128,768]{1,0:T(8,128)(2,1)S(1)}, bf16[128,768]{1,0:T(8,128)(2,1)S(1)}, u32[]{:S(2)}, u32[]{:S(2)}) collective-permute-start(bf16[128,768]{1,0:T(8,128)(2,1)S(1)} %fusion.3), channel_id=1, source_target_pairs={{0,24},{8,0},{16,8},{24,16},{32,56},{40,32},{48,40},{56,48},{64,88... | collective-permute-start | bytes 589832 | tf_op jit(solution)/shard_map/ppermute | solution.py:42
  112.7 6.0 %collective-permute-start.7 = (bf16[128,768]{1,0:T(8,128)(2,1)S(1)}, bf16[128,768]{1,0:T(8,128)(2,1)S(1)}, u32[]{:S(2)}, u32[]{:S(2)}) collective-permute-start(bf16[128,768]{1,0:T(8,128)(2,1)S(1)} %fusion.4), channel_id=1, source_target_pairs={{0,8},{8,16},{16,24},{24,0},{32,40},{40,48},{48,56},{56,32},{64,72... | collective-permute-start | bytes 589832 | tf_op jit(solution)/shard_map/ppermute | solution.py:42
  129.6 5.0 %collective-permute-start.30 = (f32[8,128]{1,0:T(8,128)S(1)}, f32[8,128]{1,0:T(8,128)S(1)}, u32[]{:S(2)}, u32[]{:S(2)}) collective-permute-start(f32[8,128]{1,0:T(8,128)S(1)} %add_add_fusion.1), channel_id=1, source_target_pairs={{0,2},{1,3},{2,4},{3,5},{4,6},{5,7},{6,0},{7,1},{8,10},{9,11},{10,... | collective-permute-start | bytes 12296 | tf_op jit(solution)/shard_map/ppermute | solution.py:42
  136.0 12.8 %collective-permute-start.33 = (f32[8,128]{1,0:T(8,128)S(1)}, f32[8,128]{1,0:T(8,128)S(1)}, u32[]{:S(2)}, u32[]{:S(2)}) collective-permute-start(f32[8,128]{1,0:T(8,128)S(1)} %add_add_fusion), channel_id=1, source_target_pairs={{0,1},{1,0},{2,3},{3,2},{4,5},{5,4},{6,7},{7,6},{8,9},{9,8},{10,11... | collective-permute-start | bytes 12296 | tf_op jit(solution)/shard_map/ppermute | solution.py:42
  152.7 20.2 %collective-permute-start.35 = (bf16[512,768]{1,0:T(8,128)(2,1)S(1)}, bf16[512,768]{1,0:T(8,128)(2,1)}, u32[]{:S(2)}, u32[]{:S(2)}) collective-permute-start(bf16[512,768]{1,0:T(8,128)(2,1)S(1)} %shard_map.121), channel_id=1, source_target_pairs={{0,2},{1,3},{2,4},{3,5},{4,6},{5,7},{6,0},{7,1},{8,10},{9,11},{10,... | collective-permute-start | bytes 2359304 | tf_op jit(solution)/shard_map/ppermute | solution.py:42
  152.8 21.3 %collective-permute-start.37 = (bf16[512,768]{1,0:T(8,128)(2,1)S(1)}, bf16[512,768]{1,0:T(8,128)(2,1)}, u32[]{:S(2)}, u32[]{:S(2)}) collective-permute-start(bf16[512,768]{1,0:T(8,128)(2,1)S(1)} %shard_map.121), channel_id=1, source_target_pairs={{0,6},{1,7},{2,0},{3,1},{4,2},{5,3},{6,4},{7,5},{8,14},{9,15},{10,... | collective-permute-start | bytes 2359304 | tf_op jit(solution)/shard_map/ppermute | solution.py:42
  155.5 45.4 %collective-permute-start.39 = (bf16[512,768]{1,0:T(8,128)(2,1)S(1)}, bf16[512,768]{1,0:T(8,128)(2,1)S(1)}, u32[]{:S(2)}, u32[]{:S(2)}) collective-permute-start(bf16[512,768]{1,0:T(8,128)(2,1)S(1)} %shard_map.121), channel_id=1, source_target_pairs={{0,4},{1,5},{2,6},{3,7},{4,0},{5,1},{6,2},{7,3},{8,12},{9,13},{10,... | collective-permute-start | bytes 2359304 | tf_op jit(solution)/shard_map/ppermute | solution.py:42
  156.3 44.7 %collective-permute-start.34 = (bf16[512,768]{1,0:T(8,128)(2,1)S(1)}, bf16[512,768]{1,0:T(8,128)(2,1)}, u32[]{:S(2)}, u32[]{:S(2)}) collective-permute-start(bf16[512,768]{1,0:T(8,128)(2,1)S(1)} %shard_map.121), channel_id=1, source_target_pairs={{0,1},{1,0},{2,3},{3,2},{4,5},{5,4},{6,7},{7,6},{8,9},{9,8},{10,11... | collective-permute-start | bytes 2359304 | tf_op jit(solution)/shard_map/ppermute | solution.py:42
  172.9 30.5 %collective-permute-start.36 = (bf16[512,768]{1,0:T(8,128)(2,1)}, bf16[512,768]{1,0:T(8,128)(2,1)}, u32[]{:S(2)}, u32[]{:S(2)}) collective-permute-start(bf16[512,768]{1,0:T(8,128)(2,1)} %collective-permute-done.35), channel_id=1, source_target_pairs={{0,1},{1,0},{2,3},{3,2},{4,5},{5,4},{6,7},{7,6},{8,9},{9,8},{10,11... | collective-permute-start | bytes 2359304 | tf_op jit(solution)/shard_map/ppermute | solution.py:42
  174.1 31.8 %collective-permute-start.38 = (bf16[512,768]{1,0:T(8,128)(2,1)}, bf16[512,768]{1,0:T(8,128)(2,1)}, u32[]{:S(2)}, u32[]{:S(2)}) collective-permute-start(bf16[512,768]{1,0:T(8,128)(2,1)} %collective-permute-done.37), channel_id=1, source_target_pairs={{0,1},{1,0},{2,3},{3,2},{4,5},{5,4},{6,7},{7,6},{8,9},{9,8},{10,11... | collective-permute-start | bytes 2359304 | tf_op jit(solution)/shard_map/ppermute | solution.py:42
  200.9 6.4 %collective-permute-start.40 = (bf16[512,768]{1,0:T(8,128)(2,1)S(1)}, bf16[512,768]{1,0:T(8,128)(2,1)S(1)}, u32[]{:S(2)}, u32[]{:S(2)}) collective-permute-start(bf16[512,768]{1,0:T(8,128)(2,1)S(1)} %collective-permute-done.39), channel_id=1, source_target_pairs={{0,1},{1,0},{2,3},{3,2},{4,5},{5,4},{6,7},{7,6},{8,9},{9,8},{10,11... | collective-permute-start | bytes 2359304 | tf_op jit(solution)/shard_map/ppermute | solution.py:42
  (28 other events, 355.4 us)

commit v2 on v0

v2 whole, which is shorter than its diff:
```python
import functools
import math

import jax
import jax.numpy as jnp
import ml_dtypes
import numpy as np
from jax import lax
from jax.experimental import pallas as pl
from jax.experimental.pallas import tpu as pltpu
from jax.sharding import PartitionSpec as P

D = 6144
ROWS = 8192
TILE = 256
WIDTH = 768
TILES = WIDTH // TILE
SIDE = 4
BLOCK = 512
PART = 256
STEP = 128
RING0, RING1 = (2, 1), (3, 0)
LIMIT = 4.0 * math.sqrt(ROWS * D)
VMEM_BYTES = 24 * 1024 * 1024


def hadamard(length):
    index = np.arange(length)
    common_bits = index[:, None] & index[None, :]
    parity = np.zeros((length, length), np.int32)
    for bit_pos in range(length.bit_length() - 1):
        parity = parity ^ common_bits >> bit_pos & 1
    return (1 - 2 * parity).astype(ml_dtypes.bfloat16)


def hop(value, axis, step):
    pairs = []
    for device in range(128):
        x, z, core = device // 32, device // 8 % SIDE, device % 2
        if (axis == "first") == (core == 0):
            x = (x + step) % SIDE
        else:
            z = (z + step) % SIDE
        pairs.append((device, (x * SIDE + z) * 8 + device % 8))
    return lax.ppermute(value, ("dp", "fsdp"), pairs)


def in_hbm(value):
    return pltpu.with_memory_space_constraint(value, pltpu.HBM)


def row_scales(index_refs, table_ref, inverse):
    index = jnp.concatenate([ref[...] for ref in index_refs], axis=1)
    scale = jnp.zeros(index.shape, jnp.float32)
    for level in range(table_ref.shape[0]):
        scale = jnp.where(index == level, table_ref[level], scale)
    if inverse:
        scale = 1.0 / (math.sqrt(TILE) * scale)
    ones = jnp.ones((8 - index.shape[0], index.shape[1]), jnp.float32)
    return jnp.concatenate([scale, ones], axis=0).T


def encode_kernel(counts, place_ref, table_ref, sign_ref, hmat_ref, *refs):
    jobs = len(counts)
    inputs, out_refs = iter(refs[:-jobs]), refs[-jobs:]
    grad_refs, index_refs, arrived_refs = [], [], []
    for count in counts:
        grad_refs.append(next(inputs))
        index_refs.append(next(inputs))
        arrived_refs.append([next(inputs) for _ in range(count)])
    steps = row_scales(index_refs, table_ref, True)
    sign = (2 * sign_ref[...] - 1).astype(jnp.bfloat16)
    for tile in range(TILES):
        cols = slice(tile * TILE, (tile + 1) * TILE)
        signed = jnp.concatenate([ref[:, cols] for ref in grad_refs], axis=0) * sign[:, cols]
        rotated = jnp.dot(signed, hmat_ref[...], preferred_element_type=jnp.float32)
        codes = jnp.clip(rotated * steps[:, tile : tile + 1], -127.0, 127.0).astype(jnp.bfloat16)
        for job in range(jobs):
            code = codes[job * PART : (job + 1) * PART]
            if arrived_refs[job]:
                total = code.astype(jnp.float32)
                for ref in arrived_refs[job]:
                    total = total + ref[:, cols].astype(jnp.float32)
                code = total.astype(out_refs[job].dtype)
            out_refs[job][:, cols] = code


def block_at(place_ref, near, far):
    place = place_ref[0]
    x, z, core = place // (2 * SIDE), place // 2 % SIDE, place % 2
    x, z = x + jnp.where(core == 0, near, far), z + jnp.where(core == 0, far, near)
    return lax.rem(x, SIDE) * SIDE + lax.rem(z, SIDE)


def encode(place, table, sign, grad, index, hmat, grid, jobs):
    in_specs = [
        pl.BlockSpec(memory_space=pltpu.SMEM),
        pl.BlockSpec((1, WIDTH), lambda *_: (0, 0)),
        pl.BlockSpec((TILE, TILE), lambda *_: (0, 0)),
    ]
    operands, out_specs, out_shape = [table, sign, hmat], [], []
    parts = BLOCK // PART
    for near, far, arrived, spec, shape, dtype in jobs:
        rows = functools.partial(lambda near, far, i, j, place_ref: block_at(place_ref, near, far(i)) * parts + j, near, far)
        in_specs.append(pl.BlockSpec((PART, WIDTH), functools.partial(lambda rows, *at: (rows(*at), 0), rows)))
        in_specs.append(pl.BlockSpec((TILES, PART), functools.partial(lambda rows, *at: (0, rows(*at)), rows)))
        operands += [grad, index]
        for value, its_spec in arrived:
            in_specs.append(its_spec)
            operands.append(value)
        out_specs.append(spec)
        out_shape.append(jax.ShapeDtypeStruct(shape, dtype))
    blocks = len(jobs) * grid[0] * parts
    return pl.pallas_call(
        functools.partial(encode_kernel, [len(job[2]) for job in jobs]),
        out_shape=out_shape,
        grid_spec=pltpu.PrefetchScalarGridSpec(num_scalar_prefetch=1, grid=grid, in_specs=in_specs, out_specs=out_specs),
        compiler_params=pltpu.CompilerParams(vmem_limit_bytes=VMEM_BYTES),
        cost_estimate=pl.CostEstimate(flops=2 * blocks * PART * WIDTH * TILE, bytes_accessed=blocks * PART * WIDTH * 6, transcendentals=0),
    )(place, *operands)


def paired(ring):
    return lambda i: ring[0] + i * (ring[1] - ring[0])


def reduce_scatter(place, table, sign, grad, index, hmat, beside):
    code = functools.partial(encode, place, table, sign, grad, index, hmat)
    pair = ((2, BLOCK, WIDTH), jnp.bfloat16)
    both = pl.BlockSpec((None, PART, WIDTH), lambda i, j, place_ref: (i, j, 0))
    grid = (2, BLOCK // PART)

    def round_of(*plan):
        jobs = [(near, paired(ring), [(v, both) for v in arrived], both, *pair) for _, near, ring, arrived in plan]
        codes = code(grid, jobs)
        return [hop(v, "first", step) for v, (step, *_) in zip(codes, plan, strict=True)], codes

    (up_far, down_far), far_codes = round_of((1, 2, RING0, ()), (-1, 2, RING1, ()))
    packed = lax.all_gather(beside(far_codes[0]), "fsdp")
    (up_own, down_own), _ = round_of((1, 1, RING1, ()), (-1, 3, RING0, ()))
    (up_sum, down_sum), _ = round_of((1, 1, RING0, (up_far,)), (-1, 3, RING1, (down_far,)))
    jobs = []
    single = pl.BlockSpec((PART, WIDTH), lambda i, j, place_ref: (j, 0))
    for ring, values in ((RING0, (up_sum, down_own)), (RING1, (up_own, down_sum))):
        for slot, offset in enumerate(ring):
            spec = pl.BlockSpec((None, PART, WIDTH), functools.partial(lambda slot, i, j, place_ref: (slot, j, 0), slot))
            dtype = jnp.bfloat16 if offset else jnp.float32
            far_of = functools.partial(lambda offset, i: offset, offset)
            jobs.append((0, far_of, [(v, spec) for v in values], single, (BLOCK, WIDTH), dtype))
    sums = dict(zip(RING0 + RING1, code((1, BLOCK // PART), jobs), strict=True))
    return [sums[0]] + [in_hbm(hop(sums[k], "second", k)) for k in (2, 1, 3)], packed


def decode_kernel(place_ref, table_ref, sign_ref, hmat_ref, own_ref, two_ref, one_ref, three_ref, index_ref, after_ref, plain_ref, low_ref, square_ref, sum_ref):
    del after_ref
    f32 = jnp.float32
    first = pl.program_id(0) == 0

    @pl.when(first)
    def _():
        sum_ref[...] = jnp.zeros_like(sum_ref)

    scales = row_scales([index_ref], table_ref, False) * (1.0 / math.sqrt(TILE))
    sign = (2 * sign_ref[...] - 1).astype(f32)
    square = sum_ref[...]
    for tile in range(TILES):
        cols = slice(tile * TILE, (tile + 1) * TILE)
        value = own_ref[:, cols] + two_ref[:, cols].astype(f32) + one_ref[:, cols].astype(f32) + three_ref[:, cols].astype(f32)
        plain = jnp.zeros(value.shape, f32)
        for _ in range(3):
            piece = value.astype(jnp.bfloat16)
            plain = plain + jnp.dot(piece, hmat_ref[...], preferred_element_type=f32)
            value = value - piece.astype(f32)
        plain = plain * scales[:, tile : tile + 1] * sign[:, cols]
        plain_ref[:, cols] = plain

        @pl.when(first)
        def _():
            low_ref[:, cols] = plain.astype(jnp.bfloat16)

        parts = jnp.sum((plain * plain).reshape(-1, 8, TILE), axis=0)
        square = square + parts[:, :128] + parts[:, 128:]
    sum_ref[...] = square
    square_ref[...] = jnp.broadcast_to(square, square_ref.shape)


def decode(place, table, sign, terms, index, hmat, packed, copies):
    parts = BLOCK // PART
    single = pl.BlockSpec((PART, WIDTH), lambda j, place_ref: (j, 0))
    return pl.pallas_call(
        decode_kernel,
        out_shape=(
            jax.ShapeDtypeStruct((BLOCK, WIDTH), jnp.float32),
            pltpu.HBM((PART, WIDTH), jnp.bfloat16),
            pltpu.HBM((copies, 8, 128), jnp.float32),
        ),
        grid_spec=pltpu.PrefetchScalarGridSpec(
            num_scalar_prefetch=1,
            grid=(parts,),
            in_specs=[
                pl.BlockSpec(memory_space=pltpu.SMEM),
                pl.BlockSpec((1, WIDTH), lambda j, place_ref: (0, 0)),
                pl.BlockSpec((TILE, TILE), lambda j, place_ref: (0, 0)),
                *[single] * 4,
                pl.BlockSpec((TILES, PART), lambda j, place_ref: (0, block_at(place_ref, 0, 0) * parts + j)),
                pl.BlockSpec((1, 1, 16, 128), lambda j, place_ref: (0, 0, 0, 0)),
            ],
            out_specs=(
                single,
                pl.BlockSpec((PART, WIDTH), lambda j, place_ref: (0, 0)),
                pl.BlockSpec((copies, 8, 128), lambda j, place_ref: (0, 0, 0)),
            ),
            scratch_shapes=[pltpu.VMEM((8, 128), jnp.float32)],
        ),
        compiler_params=pltpu.CompilerParams(vmem_limit_bytes=VMEM_BYTES),
        cost_estimate=pl.CostEstimate(flops=6 * 512 * WIDTH * TILE, bytes_accessed=512 * WIDTH * 14, transcendentals=0),
    )(place, table, sign, hmat, *terms, index, packed)


def total_squares(square):
    square = jnp.sum(lax.all_to_all(square, "fsdp", 0, 0), axis=0)
    copies = jnp.broadcast_to(square, (lax.axis_size("dp"), *square.shape))
    return lax.all_to_all(copies, "dp", 0, 0)


MEAN_SCALE = 0.02 / (1.0 - 0.9**10)
VAR_SCALE = 1.0 / (1.0 - 0.95**10)


def clip_factor(square_ref):
    square = jnp.sum(square_ref[...], axis=0)
    square = jnp.sum(jnp.sum(square, axis=0, keepdims=True), axis=1, keepdims=True)
    return LIMIT / jnp.maximum(jnp.sqrt(square), LIMIT)


def stepped(master, new_mean, new_var):
    spread = new_var * VAR_SCALE
    spread = spread * lax.rsqrt(spread)
    return 0.998 * master - new_mean * MEAN_SCALE / (spread + 1e-08)


def weights_kernel(square_ref, plain_ref, master_ref, mean_ref, var_ref, out_ref):
    grad = plain_ref[...] * clip_factor(square_ref)
    new_mean = 0.9 * mean_ref[...] + 0.1 * grad
    new_var = 0.95 * var_ref[...] + 0.05 * grad * grad
    out_ref[...] = stepped(master_ref[...], new_mean, new_var).astype(jnp.bfloat16)


def state_kernel(square_ref, plain_ref, master_ref, mean_ref, var_ref, new_master_ref, new_mean_ref, new_var_ref):
    grad = plain_ref[...] * clip_factor(square_ref)
    new_mean = 0.9 * mean_ref[...] + 0.1 * grad
    new_var = 0.95 * var_ref[...] + 0.05 * grad * grad
    new_mean_ref[...] = new_mean
    new_var_ref[...] = new_var
    new_master_ref[...] = stepped(master_ref[...], new_mean, new_var)


def adamw(kernel, out_shape, square, plain, master, mean, var, skip):
    rows = pl.BlockSpec((STEP, WIDTH), lambda j: (j + skip, 0))
    count = BLOCK // STEP - skip
    return pl.pallas_call(
        kernel,
        out_shape=out_shape,
        grid=(count,),
        in_specs=[pl.BlockSpec(square.shape, lambda j: (0, 0, 0))] + [rows] * 4,
        out_specs=jax.tree.map(lambda _: pl.BlockSpec((STEP, WIDTH), lambda j: (j, 0)), out_shape),
        compiler_params=pltpu.CompilerParams(vmem_limit_bytes=VMEM_BYTES),
        cost_estimate=pl.CostEstimate(flops=20 * count * STEP * WIDTH, bytes_accessed=24 * count * STEP * WIDTH, transcendentals=count * STEP * WIDTH),
    )(square, plain, master, mean, var)


def pack_kernel(master_ref, mean_ref, var_ref, after_ref, out_ref):
    del after_ref
    master = master_ref[...]
    high = master.astype(jnp.bfloat16)
    out_ref[0] = high
    out_ref[1] = (master - high.astype(jnp.float32)).astype(jnp.bfloat16)
    out_ref[2] = mean_ref[...].astype(jnp.bfloat16)
    out_ref[3] = var_ref[...].astype(jnp.bfloat16)


def pack(master, mean, var, after):
    rows = pl.BlockSpec((STEP, WIDTH), lambda j: (j, 0))
    return pl.pallas_call(
        pack_kernel,
        out_shape=pltpu.HBM((4, PART, WIDTH), jnp.bfloat16),
        grid=(PART // STEP,),
        in_specs=[rows] * 3 + [pl.BlockSpec((1, 16, 128), lambda j: (0, 0, 0))],
        out_specs=pl.BlockSpec((4, STEP, WIDTH), lambda j: (0, j, 0)),
        compiler_params=pltpu.CompilerParams(vmem_limit_bytes=VMEM_BYTES),
        cost_estimate=pl.CostEstimate(flops=PART * WIDTH * 4, bytes_accessed=PART * WIDTH * 20, transcendentals=0),
    )(master, mean, var, after)


def wide_kernel(square_ref, packed_ref, plain_ref, out_ref):
    f32 = jnp.float32
    master = packed_ref[0, 0].astype(f32) + packed_ref[0, 1].astype(f32)
    grad = plain_ref[0].astype(f32) * clip_factor(square_ref)
    new_mean = 0.9 * packed_ref[0, 2].astype(f32) + 0.1 * grad
    new_var = 0.95 * packed_ref[0, 3].astype(f32) + 0.05 * grad * grad
    out_ref[...] = stepped(master, new_mean, new_var).astype(jnp.bfloat16)


def wide(square, packed, plain):
    sources = packed.shape[0]
    return pl.pallas_call(
        wide_kernel,
        out_shape=pltpu.HBM((BLOCK, D), jnp.bfloat16),
        grid=(sources,),
        in_specs=[
            pl.BlockSpec(square.shape, lambda j: (0, 0, 0)),
            pl.BlockSpec((1, 4, PART, WIDTH), lambda j: (j, 0, 0, 0)),
            pl.BlockSpec((1, PART, WIDTH), lambda j: (j, 0, 0)),
        ],
        out_specs=pl.BlockSpec((PART, WIDTH), lambda j: (0, j)),
        compiler_params=pltpu.CompilerParams(vmem_limit_bytes=VMEM_BYTES),
        cost_estimate=pl.CostEstimate(flops=20 * PART * D, bytes_accessed=12 * PART * D, transcendentals=PART * D),
    )(square, packed, plain)


def fill_kernel(rows_ref, given_ref, out_ref):
    del given_ref
    for j in range(rows_ref.shape[0]):
        out_ref[:, j * WIDTH : (j + 1) * WIDTH] = rows_ref[j]


def fill(rows, weights):
    count = 4
    sources = rows.shape[0] // count
    return pl.pallas_call(
        fill_kernel,
        out_shape=jax.ShapeDtypeStruct(weights.shape, weights.dtype),
        grid=(count,),
        in_specs=[pl.BlockSpec((sources, PART, WIDTH), lambda i: (i, 0, 0)), pl.BlockSpec(memory_space=pl.ANY)],
        out_specs=pl.BlockSpec((PART, sources * WIDTH), lambda i: (1, i)),
        input_output_aliases={1: 0},
        compiler_params=pltpu.CompilerParams(vmem_limit_bytes=VMEM_BYTES),
        cost_estimate=pl.CostEstimate(flops=0, bytes_accessed=4 * PART * D, transcendentals=0),
    )(rows, weights)


def on_device(grad_shards, hadamard_signs, scale_index, scale_table, master, mean_moment, var_moment):
    grad, scale_index, master, mean_moment, var_moment = map(in_hbm, (grad_shards[0], scale_index, master, mean_moment, var_moment))
    place = (lax.axis_index("dp") * 2 + (lax.axis_index("fsdp") & 1)).reshape(1)
    sign = in_hbm(hadamard_signs.reshape(1, WIDTH))
    hmat = in_hbm(jnp.asarray(hadamard(TILE)))
    terms, packed = reduce_scatter(place, scale_table, sign, grad, scale_index, hmat, functools.partial(pack, master, mean_moment, var_moment))
    packed = in_hbm(packed)
    plain, low, square = decode(place, scale_table, sign, terms, scale_index, hmat, packed, lax.axis_size("fsdp"))
    low = in_hbm(lax.all_gather(low, "fsdp"))
    square = total_squares(square)
    state = (square, plain, master, mean_moment, var_moment)
    rest = adamw(weights_kernel, pltpu.HBM((BLOCK - PART, WIDTH), jnp.bfloat16), *state, PART // STEP)
    rest = in_hbm(lax.all_gather(rest, "fsdp"))
    weights = fill(rest, wide(square, packed, low))
    new_state = adamw(state_kernel, (jax.ShapeDtypeStruct(master.shape, jnp.float32),) * 3, *state, 0)
    return *new_state, weights


def solution(mesh):
    return jax.shard_map(
        on_device,
        mesh=mesh,
        in_specs=(
            P("dp", None, "fsdp"),
            P("fsdp"),
            P("fsdp", None),
            P(),
            P("dp", "fsdp"),
            P("dp", "fsdp"),
            P("dp", "fsdp"),
        ),
        out_specs=(P("dp", "fsdp"), P("dp", "fsdp"), P("dp", "fsdp"), P("dp", None)),
        check_vma=False,
    )
```

time: 368 us -> 176 us (0.48)
  waiting for transfers between devices: 193 us -> 71.8 us
  local copies, waits for them, and re-layouts: 53.5 us -> 2.83 us
  Pallas kernels: 0 us -> 49.7 us
  blocking collectives: 64.8 us -> 21.3 us
  other arithmetic: 20.4 us -> 0.01 us
  matrix products: 19.8 us -> 0 us
  starting transfers between devices: 0.08 us -> 15.7 us
    reduce_scatter x1 -> x0, waiting for transfers between devices: 154 us -> none  [on_device(): lax.psum_scatter(coded.astype(jnp.float32).reshape(lax.axis_size('dp') *...]
    psum x1 -> x0, blocking collectives: 64.8 us -> none  [global_squares(): return lax.psum(jnp.sum(values * values), ('dp', 'fsdp'))]
    ppermute x0 -> x9, waiting for transfers between devices: none -> 56 us  [hop(): return lax.ppermute(value, ('dp', 'fsdp'), pairs)]
    pallas_call x0 -> x10, Pallas kernels: none -> 49.7 us  [the longest x4 18.1 us: encode(): pl.pallas_call(functools.partial(encode_kernel, [len(job[2]) for job in j...]
    reshape x3 -> x1, local copies, waits for them, and re-layouts: 28.1 us -> 1.28 us  [on_device(): sign = in_hbm(hadamard_signs.reshape(1, WIDTH))]
    all_gather x1 -> x3, waiting for transfers between devices: 38.7 us -> 15.7 us  [the longest x1 15.7 us: on_device(): rest = in_hbm(lax.all_gather(rest, 'fsdp'))]
    unnamed x10 -> x8, local copies, waits for them, and re-layouts: 23 us -> 1.54 us
    all_to_all x0 -> x2, blocking collectives: none -> 21.3 us  [the longest x1 11.1 us: total_squares(): square = jnp.sum(lax.all_to_all(square, 'fsdp', 0, 0), axis=0)]
  transfers between devices with their start and end apart: 2 -> 12, of which waited for: 2 -> 8; matrix products, arithmetic and copies ran while one was open for 1% -> 0% of each run, Pallas kernels for 0% -> 19%
where the time goes in v2:
time: 176 us; the launch traced here: 175 us
  waiting for transfers between devices  71.8 us (41%)
  Pallas kernels  49.7 us (28%)
  blocking collectives  21.3 us (12%)
  starting transfers between devices  15.7 us (9%)
  between operations  13.8 us (8%)
  local copies, waits for them, and re-layouts  2.83 us (2%)
    ppermute x9, waiting for transfers between devices, hop(): return lax.ppermute(value, ('dp', 'fsdp'), pairs)  56 us
    pallas_call x4, Pallas kernels, encode(): pl.pallas_call(functools.partial(encode_kernel, [len(job[2]) for job in j...  18.1 us
    all_gather x1, waiting for transfers between devices, on_device(): rest = in_hbm(lax.all_gather(rest, 'fsdp'))  15.7 us
    ppermute x9, starting transfers between devices, hop(): return lax.ppermute(value, ('dp', 'fsdp'), pairs)  15.6 us
    pallas_call x1, Pallas kernels, wide(): pl.pallas_call(wide_kernel, out_shape=pltpu.HBM((BLOCK, D), jnp.bfloat16)...  12.4 us
    all_to_all x1, blocking collectives, total_squares(): square = jnp.sum(lax.all_to_all(square, 'fsdp', 0, 0), axis=0)  11.1 us
    all_to_all x1, blocking collectives, total_squares(): return lax.all_to_all(copies, 'dp', 0, 0)  10.2 us
    pallas_call x2, Pallas kernels, adamw(): pl.pallas_call(kernel, out_shape=out_shape, grid=(count,), in_specs=[pl.B...  8.19 us
  transfers between devices with their start and end apart: 12, of which 8 were waited for; matrix products, arithmetic and copies ran while one was open for 0% of the time, Pallas kernels for 19%

profile of v2, /device:TPU:1, one launch (start us, length us, event | category | flops | bytes accessed | tf_op | source)
XLA Modules:
  0.0 175.2 jit_solution(624893853852814334)
XLA Ops:
  7.2 1.3 reshape.15.sign_ref
  8.5 0.7 copy-done
  9.2 4.9 %shard_map.111 = (bf16[2,512,768]{2,1,0:T(8,128)(2,1)S(1)}, bf16[2,512,768]{2,1,0:T(8,128)(2,1)}) custom-call(s32[1]{0:T(128)} %bitcast.place_ref, f32[16]{0:T(128)S(1)} %copy-done, s32[1,768]{1,0:T(1,128)} %reshape.15.sign_ref, bf16[256,256]{1,0:T(8,128)(2,1)} %constant.17.clone.hmat_ref, bf16[8192,768]{1,0:T(8,128)(2,1)} %bitcast.5, s32[3,8192]{1,0:T(4,128)} %index_ref.1, ...), custom_call_target="tpu_custom_call" | custom-call | flops 805306368 | bytes 9437184 | tf_op jit(solution)/shard_map/pallas_call | solution.py:114
  14.1 2.6 %shard_map.115 = bf16[4,256,768]{2,1,0:T(8,128)(2,1)} custom-call(f32[512,768]{1,0:T(8,128)} %master_ref.5, f32[512,768]{1,0:T(8,128)} %mean_ref.5, f32[512,768]{1,0:T(8,128)} %var_ref.5, bf16[2,512,768]{2,1,0:T(8,128)(2,1)S(1)} %get-tuple-element.20.after_ref), custom_call_target="tpu_custom_call" | custom-call | flops 786432 | bytes 3932160 | tf_op jit(solution)/shard_map/pallas_call | solution.py:284
  16.7 0.0 all-gather.11.cloned.1.call-start
  16.7 4.7 %collective-permute-start.1 = (bf16[2,512,768]{2,1,0:T(8,128)(2,1)}, bf16[2,512,768]{2,1,0:T(8,128)(2,1)S(1)}, u32[]{:S(2)}, u32[]{:S(2)}) collective-permute-start(bf16[2,512,768]{2,1,0:T(8,128)(2,1)} %get-tuple-element.21), channel_id=1, source_target_pairs={{0,96},{1,25},{2,98},{3,27},{4,100},{5,29},{6,102},{7,31},{8,104},... | collective-permute-start | bytes 4718600 | tf_op jit(solution)/shard_map/ppermute | solution.py:45
  21.4 4.2 %shard_map.113 = (bf16[2,512,768]{2,1,0:T(8,128)(2,1)S(1)}, bf16[2,512,768]{2,1,0:T(8,128)(2,1)S(1)}) custom-call(s32[1]{0:T(128)} %bitcast.place_ref, f32[16]{0:T(128)S(1)} %copy-done.1, s32[1,768]{1,0:T(1,128)} %reshape.15.sign_ref, bf16[256,256]{1,0:T(8,128)(2,1)} %constant.17.clone.hmat_ref, bf16[8192,768]{1,0:T(8,128)(2,1)} %bitcast.7, ...), custom_call_target="tpu_custom_call" | custom-call | flops 805306368 | bytes 9437184 | tf_op jit(solution)/shard_map/pallas_call | solution.py:114
  25.6 2.7 %collective-permute-start.3 = (bf16[2,512,768]{2,1,0:T(8,128)(2,1)S(1)}, bf16[2,512,768]{2,1,0:T(8,128)(2,1)S(1)}, u32[]{:S(2)}, u32[]{:S(2)}) collective-permute-start(bf16[2,512,768]{2,1,0:T(8,128)(2,1)S(1)} %get-tuple-element.23), channel_id=1, source_target_pairs={{0,96},{1,25},{2,98},{3,27},{4,100},{5,29},{6,102},{7,31},{8,104},... | collective-permute-start | bytes 4718600 | tf_op jit(solution)/shard_map/ppermute | solution.py:45
  28.3 10.8 %collective-permute-done.1.refs_5_ = bf16[2,512,768]{2,1,0:T(8,128)(2,1)S(1)} collective-permute-done((bf16[2,512,768]{2,1,0:T(8,128)(2,1)}, bf16[2,512,768]{2,1,0:T(8,128)(2,1)S(1)}, u32[]{:S(2)}, u32[]{:S(2)}) %collective-permute-start.1) | collective-permute-done | bytes 1572896 | tf_op jit(solution)/shard_map/ppermute | solution.py:45
  39.1 3.2 %collective-permute-done.refs_2_ = bf16[2,512,768]{2,1,0:T(8,128)(2,1)S(1)} collective-permute-done((bf16[2,512,768]{2,1,0:T(8,128)(2,1)S(1)}, bf16[2,512,768]{2,1,0:T(8,128)(2,1)S(1)}, u32[]{:S(2)}, u32[]{:S(2)}) %collective-permute-start) | collective-permute-done | bytes 1572896 | tf_op jit(solution)/shard_map/ppermute | solution.py:45
  42.3 4.5 %shard_map.112 = (bf16[2,512,768]{2,1,0:T(8,128)(2,1)S(1)}, bf16[2,512,768]{2,1,0:T(8,128)(2,1)S(1)}) custom-call(s32[1]{0:T(128)} %bitcast.place_ref, f32[16]{0:T(128)S(1)} %copy-done.1, s32[1,768]{1,0:T(1,128)} %reshape.15.sign_ref, bf16[256,256]{1,0:T(8,128)(2,1)} %constant.17.clone.hmat_ref, bf16[8192,768]{1,0:T(8,128)(2,1)} %bitcast.9, ...), custom_call_target="tpu_custom_call" | custom-call | flops 805306368 | bytes 9437184 | tf_op jit(solution)/shard_map/pallas_call | solution.py:114
  46.8 0.1 collective-permute-start.2
  46.9 2.7 %collective-permute-start.5 = (bf16[2,512,768]{2,1,0:T(8,128)(2,1)S(1)}, bf16[2,512,768]{2,1,0:T(8,128)(2,1)S(1)}, u32[]{:S(2)}, u32[]{:S(2)}) collective-permute-start(bf16[2,512,768]{2,1,0:T(8,128)(2,1)S(1)} %get-tuple-element.25), channel_id=1, source_target_pairs={{0,96},{1,25},{2,98},{3,27},{4,100},{5,29},{6,102},{7,31},{8,104},... | collective-permute-start | bytes 4718600 | tf_op jit(solution)/shard_map/ppermute | solution.py:45
  49.5 6.3 %collective-permute-done.3.refs_3_.refs_7_ = bf16[2,512,768]{2,1,0:T(8,128)(2,1)S(1)} collective-permute-done((bf16[2,512,768]{2,1,0:T(8,128)(2,1)S(1)}, bf16[2,512,768]{2,1,0:T(8,128)(2,1)S(1)}, u32[]{:S(2)}, u32[]{:S(2)}) %collective-permute-start.3) | collective-permute-done | bytes 1572896 | tf_op jit(solution)/shard_map/ppermute | solution.py:45
  55.8 3.3 %collective-permute-done.4.refs_10_.refs_14_ = bf16[2,512,768]{2,1,0:T(8,128)(2,1)S(1)} collective-permute-done((bf16[2,512,768]{2,1,0:T(8,128)(2,1)S(1)}, bf16[2,512,768]{2,1,0:T(8,128)(2,1)S(1)}, u32[]{:S(2)}, u32[]{:S(2)}) %collective-permute-start.4) | collective-permute-done | bytes 1572896 | tf_op jit(solution)/shard_map/ppermute | solution.py:45
  59.1 16.9 %collective-permute-done.2.refs_2_.refs_6_ = bf16[2,512,768]{2,1,0:T(8,128)(2,1)S(1)} collective-permute-done((bf16[2,512,768]{2,1,0:T(8,128)(2,1)S(1)}, bf16[2,512,768]{2,1,0:T(8,128)(2,1)S(1)}, u32[]{:S(2)}, u32[]{:S(2)}) %collective-permute-start.2) | collective-permute-done | bytes 1572896 | tf_op jit(solution)/shard_map/ppermute | solution.py:45
  76.0 4.5 %shard_map.114 = (bf16[512,768]{1,0:T(8,128)(2,1)S(1)}, bf16[512,768]{1,0:T(8,128)(2,1)S(1)}, bf16[512,768]{1,0:T(8,128)(2,1)S(1)}, f32[512,768]{1,0:T(8,128)S(1)}) custom-call(s32[1]{0:T(128)} %bitcast.place_ref, f32[16]{0:T(128)S(1)} %copy-done.1, s32[1,768]{1,0:T(1,128)} %reshape.15.sign_ref, bf16[256,256]{1,0:T(8,128)(2,1)} %constant.17.clone.hmat_ref, ...), custom_call_target="tpu_custom_call" | custom-call | flops 805306368 | bytes 9437184 | tf_op jit(solution)/shard_map/pallas_call | solution.py:114
  80.4 2.8 %collective-permute-start.6 = (bf16[512,768]{1,0:T(8,128)(2,1)S(1)}, bf16[512,768]{1,0:T(8,128)(2,1)S(1)}, u32[]{:S(2)}, u32[]{:S(2)}) collective-permute-start(bf16[512,768]{1,0:T(8,128)(2,1)S(1)} %get-tuple-element.27), channel_id=1, source_target_pairs={{0,16},{1,65},{2,18},{3,67},{4,20},{5,69},{6,22},{7,71},{8,24},{9,... | collective-permute-start | bytes 2359304 | tf_op jit(solution)/shard_map/ppermute | solution.py:45
  83.3 0.3 collective-permute-start.7
  83.6 2.4 %collective-permute-start.8 = (bf16[512,768]{1,0:T(8,128)(2,1)S(1)}, bf16[512,768]{1,0:T(8,128)(2,1)}, u32[]{:S(2)}, u32[]{:S(2)}) collective-permute-start(bf16[512,768]{1,0:T(8,128)(2,1)S(1)} %get-tuple-element.29), channel_id=1, source_target_pairs={{0,24},{1,97},{2,26},{3,99},{4,28},{5,101},{6,30},{7,103},{8,0},{9... | collective-permute-start | bytes 2359304 | tf_op jit(solution)/shard_map/ppermute | solution.py:45
  85.9 7.3 %collective-permute-done.6.two_ref = bf16[512,768]{1,0:T(8,128)(2,1)S(1)} collective-permute-done((bf16[512,768]{1,0:T(8,128)(2,1)S(1)}, bf16[512,768]{1,0:T(8,128)(2,1)S(1)}, u32[]{:S(2)}, u32[]{:S(2)}) %collective-permute-start.6) | collective-permute-done | bytes 786464 | tf_op jit(solution)/shard_map/ppermute | solution.py:45
  93.2 8.4 %collective-permute-done.7.one_ref = bf16[512,768]{1,0:T(8,128)(2,1)S(1)} collective-permute-done((bf16[512,768]{1,0:T(8,128)(2,1)S(1)}, bf16[512,768]{1,0:T(8,128)(2,1)S(1)}, u32[]{:S(2)}, u32[]{:S(2)}) %collective-permute-start.7) | collective-permute-done | bytes 786464 | tf_op jit(solution)/shard_map/ppermute | solution.py:45
  101.6 0.9 copy-done.3
  102.5 4.2 %shard_map.116 = (f32[512,768]{1,0:T(8,128)S(1)}, bf16[256,768]{1,0:T(8,128)(2,1)}, f32[8,8,128]{2,1,0:T(8,128)}) custom-call(s32[1]{0:T(128)} %bitcast.place_ref, f32[16]{0:T(128)S(1)} %copy-done.1, s32[1,768]{1,0:T(1,128)} %reshape.15.sign_ref, bf16[256,256]{1,0:T(8,128)(2,1)} %constant.17.clone.hmat_ref, f32[512,768]{1,0:T(8,128)S(1)} %get-tuple-element.26.own_ref, ...), custom_call_target="tpu_custom_call" | custom-call | flops 603979776 | bytes 5505024 | tf_op jit(solution)/shard_map/pallas_call | solution.py:190
  106.7 0.0 all-gather.9.cloned.1.call-start
  106.8 11.1 %all_to_all.10 = f32[8,8,128]{2,1,0:T(8,128)S(1)} all-to-all(f32[8,8,128]{2,1,0:T(8,128)} %get-tuple-element.30), channel_id=1, replica_groups=mesh['dp'=16,'fsdp'=8] {'fsdp'}, dimensions={0} | all-to-all | bytes 65536 | tf_op jit(solution)/shard_map/all_to_all | solution.py:221
  117.9 10.2 %all_to_all.11.square_ref = f32[16,8,128]{2,1,0:T(8,128)S(1)} all-to-all(f32[16,8,128]{2,1,0:T(8,128)S(1)} %broadcast_in_dim.3), channel_id=1, replica_groups=mesh['dp'=16,'fsdp'=8] {'dp'}, dimensions={0} | all-to-all | bytes 131072 | tf_op jit(solution)/shard_map/all_to_all | solution.py:223
  128.1 2.9 %shard_map.118 = bf16[256,768]{1,0:T(8,128)(2,1)} custom-call(f32[16,8,128]{2,1,0:T(8,128)S(1)} %all_to_all.11.square_ref, f32[512,768]{1,0:T(8,128)S(1)} %get-tuple-element.31.plain_ref, f32[512,768]{1,0:T(8,128)} %master_ref.5, f32[512,768]{1,0:T(8,128)} %mean_ref.5, f32[512,768]{1,0:T(8,128)} %var_ref.5), custom_call_target="tpu_custom_call" | custom-call | flops 3932160 | bytes 4718592 | tf_op jit(solution)/shard_map/pallas_call | solution.py:261
  131.0 5.3 %shard_map.117 = (f32[512,768]{1,0:T(8,128)}, f32[512,768]{1,0:T(8,128)}, f32[512,768]{1,0:T(8,128)}) custom-call(f32[16,8,128]{2,1,0:T(8,128)S(1)} %all_to_all.11.square_ref, f32[512,768]{1,0:T(8,128)S(1)} %get-tuple-element.31.plain_ref, f32[512,768]{1,0:T(8,128)} %master_ref.5, f32[512,768]{1,0:T(8,128)} %mean_ref.5, f32[512,768]{1,0:T(8,128)} %var_ref.5), custom_call_target="tpu_custom_call" | custom-call | flops 7864320 | bytes 9437184 | tf_op jit(solution)/shard_map/pallas_call | solution.py:261
  136.3 12.4 %shard_map.119.given_ref = bf16[512,6144]{1,0:T(8,128)(2,1)} custom-call(f32[16,8,128]{2,1,0:T(8,128)S(1)} %all_to_all.11.square_ref, bf16[8,4,256,768]{3,2,1,0:T(8,128)(2,1)} %bitcast.16, bf16[8,256,768]{2,1,0:T(8,128)(2,1)} %bitcast.17), custom_call_target="tpu_custom_call" | custom-call | flops 31457280 | bytes 18874368 | tf_op jit(solution)/shard_map/pallas_call | solution.py:306
  148.8 15.7 %all-gather.9.cloned.1.call-done = bf16[2048,768]{1,0:T(8,128)(2,1)} async-done(((bf16[256,768]{1,0:T(8,128)(2,1)}), bf16[2048,768]{1,0:T(8,128)(2,1)}) %all-gather.9.cloned.1.call-update) | async-done | bytes 3145744 | tf_op jit(solution)/shard_map/all_gather | solution.py:354
  164.5 4.2 %shard_map.120 = bf16[512,6144]{1,0:T(8,128)(2,1)} custom-call(bf16[8,256,768]{2,1,0:T(8,128)(2,1)} %bitcast.18, bf16[512,6144]{1,0:T(8,128)(2,1)} %shard_map.119.given_ref), custom_call_target="tpu_custom_call", output_to_operand_aliasing={{}: (1, {})} | custom-call | bytes 6291456 | tf_op jit(solution)/shard_map/pallas_call | solution.py:330
  (18 shorter events, 0.1 us)
Async XLA Ops:
  7.2 95.3 %all-gather.7.cloned.1.call-start = ((), (), s32[]{:S(2)}) async-start(), calls=%async_computation.2 | async-start | bytes 14155776 | tf_op jit(solution)/shard_map/all_gather | solution.py:139
  8.5 0.7 copy-start
  16.6 4.7 %copy-start.1 = (f32[16]{0:T(128)S(1)}, f32[16]{0:T(128)}, u32[]{:S(2)}) copy-start(f32[16]{0:T(128)} %table_ref.9) | copy-start | bytes 196
  16.7 119.7 %all-gather.11.cloned.1.call-start = ((), (), s32[]{:S(2)}) async-start(), calls=%async_computation.4 | async-start | bytes 3538944 | tf_op jit(solution)/shard_map/all_gather | solution.py:350
  16.7 22.3 %collective-permute-start.1 = (bf16[2,512,768]{2,1,0:T(8,128)(2,1)}, bf16[2,512,768]{2,1,0:T(8,128)(2,1)S(1)}, u32[]{:S(2)}, u32[]{:S(2)}) collective-permute-start(bf16[2,512,768]{2,1,0:T(8,128)(2,1)} %get-tuple-element.21), channel_id=1, source_target_pairs={{0,96},{1,25},{2,98},{3,27},{4,100},{5,29},{6,102},{7,31},{8,104},... | collective-permute-start | bytes 4718600 | tf_op jit(solution)/shard_map/ppermute | solution.py:45
  21.4 20.9 %collective-permute-start = (bf16[2,512,768]{2,1,0:T(8,128)(2,1)S(1)}, bf16[2,512,768]{2,1,0:T(8,128)(2,1)S(1)}, u32[]{:S(2)}, u32[]{:S(2)}) collective-permute-start(bf16[2,512,768]{2,1,0:T(8,128)(2,1)S(1)} %get-tuple-element.20.after_ref), channel_id=1, source_target_pairs={{0,32},{1,9},{2,34},{3,11},{4,36},{5,13},{6,38},{7,15},{8,40},{9,1... | collective-permute-start | bytes 4718600 | tf_op jit(solution)/shard_map/ppermute | solution.py:45
  25.6 30.2 %collective-permute-start.3 = (bf16[2,512,768]{2,1,0:T(8,128)(2,1)S(1)}, bf16[2,512,768]{2,1,0:T(8,128)(2,1)S(1)}, u32[]{:S(2)}, u32[]{:S(2)}) collective-permute-start(bf16[2,512,768]{2,1,0:T(8,128)(2,1)S(1)} %get-tuple-element.23), channel_id=1, source_target_pairs={{0,96},{1,25},{2,98},{3,27},{4,100},{5,29},{6,102},{7,31},{8,104},... | collective-permute-start | bytes 4718600 | tf_op jit(solution)/shard_map/ppermute | solution.py:45
  28.3 30.8 %collective-permute-start.4 = (bf16[2,512,768]{2,1,0:T(8,128)(2,1)S(1)}, bf16[2,512,768]{2,1,0:T(8,128)(2,1)S(1)}, u32[]{:S(2)}, u32[]{:S(2)}) collective-permute-start(bf16[2,512,768]{2,1,0:T(8,128)(2,1)S(1)} %get-tuple-element.24), channel_id=1, source_target_pairs={{0,32},{1,9},{2,34},{3,11},{4,36},{5,13},{6,38},{7,15},{8,40},{9,1... | collective-permute-start | bytes 4718600 | tf_op jit(solution)/shard_map/ppermute | solution.py:45
  46.8 29.2 %collective-permute-start.2 = (bf16[2,512,768]{2,1,0:T(8,128)(2,1)S(1)}, bf16[2,512,768]{2,1,0:T(8,128)(2,1)S(1)}, u32[]{:S(2)}, u32[]{:S(2)}) collective-permute-start(bf16[2,512,768]{2,1,0:T(8,128)(2,1)S(1)} %get-tuple-element.22), channel_id=1, source_target_pairs={{0,32},{1,9},{2,34},{3,11},{4,36},{5,13},{6,38},{7,15},{8,40},{9,1... | collective-permute-start | bytes 4718600 | tf_op jit(solution)/shard_map/ppermute | solution.py:45
  46.9 29.1 %collective-permute-start.5 = (bf16[2,512,768]{2,1,0:T(8,128)(2,1)S(1)}, bf16[2,512,768]{2,1,0:T(8,128)(2,1)S(1)}, u32[]{:S(2)}, u32[]{:S(2)}) collective-permute-start(bf16[2,512,768]{2,1,0:T(8,128)(2,1)S(1)} %get-tuple-element.25), channel_id=1, source_target_pairs={{0,96},{1,25},{2,98},{3,27},{4,100},{5,29},{6,102},{7,31},{8,104},... | collective-permute-start | bytes 4718600 | tf_op jit(solution)/shard_map/ppermute | solution.py:45
  80.4 12.8 %collective-permute-start.6 = (bf16[512,768]{1,0:T(8,128)(2,1)S(1)}, bf16[512,768]{1,0:T(8,128)(2,1)S(1)}, u32[]{:S(2)}, u32[]{:S(2)}) collective-permute-start(bf16[512,768]{1,0:T(8,128)(2,1)S(1)} %get-tuple-element.27), channel_id=1, source_target_pairs={{0,16},{1,65},{2,18},{3,67},{4,20},{5,69},{6,22},{7,71},{8,24},{9,... | collective-permute-start | bytes 2359304 | tf_op jit(solution)/shard_map/ppermute | solution.py:45
  83.3 18.3 %collective-permute-start.7 = (bf16[512,768]{1,0:T(8,128)(2,1)S(1)}, bf16[512,768]{1,0:T(8,128)(2,1)S(1)}, u32[]{:S(2)}, u32[]{:S(2)}) collective-permute-start(bf16[512,768]{1,0:T(8,128)(2,1)S(1)} %get-tuple-element.28), channel_id=1, source_target_pairs={{0,8},{1,33},{2,10},{3,35},{4,12},{5,37},{6,14},{7,39},{8,16},{9,4... | collective-permute-start | bytes 2359304 | tf_op jit(solution)/shard_map/ppermute | solution.py:45
  83.6 18.9 %collective-permute-start.8 = (bf16[512,768]{1,0:T(8,128)(2,1)S(1)}, bf16[512,768]{1,0:T(8,128)(2,1)}, u32[]{:S(2)}, u32[]{:S(2)}) collective-permute-start(bf16[512,768]{1,0:T(8,128)(2,1)S(1)} %get-tuple-element.29), channel_id=1, source_target_pairs={{0,24},{1,97},{2,26},{3,99},{4,28},{5,101},{6,30},{7,103},{8,0},{9... | collective-permute-start | bytes 2359304 | tf_op jit(solution)/shard_map/ppermute | solution.py:45
  93.2 8.4 %copy-start.2 = (bf16[512,768]{1,0:T(8,128)(2,1)}, bf16[512,768]{1,0:T(8,128)(2,1)S(1)}, u32[]{:S(2)}) copy-start(bf16[512,768]{1,0:T(8,128)(2,1)S(1)} %collective-permute-done.6.two_ref) | copy-start | bytes 2359300
  101.6 0.9 copy-start.3
  106.7 57.8 %all-gather.9.cloned.1.call-start = ((), (), s32[]{:S(2)}) async-start(), calls=%async_computation.3 | async-start | bytes 3538944 | tf_op jit(solution)/shard_map/all_gather | solution.py:354
Sparse Core Ops, SparseCore 0:
  16.8 70.9 all-gather.6
  106.8 28.0 all-gather.10
  136.6 27.7 all-gather.8

commit v3 on v2

v3 whole, which is shorter than its diff:
```python
import functools
import math

import jax
import jax.numpy as jnp
import ml_dtypes
import numpy as np
from jax import lax
from jax.experimental import pallas as pl
from jax.experimental.pallas import tpu as pltpu
from jax.sharding import PartitionSpec as P

D = 6144
ROWS = 8192
TILE = 256
WIDTH = 768
TILES = WIDTH // TILE
SIDE = 4
BLOCK = 512
PART = 256
STEP = 128
RING0, RING1 = (2, 1), (3, 0)
LIMIT = 4.0 * math.sqrt(ROWS * D)
VMEM_BYTES = 14 * 1024 * 1024


def hadamard(length):
    index = np.arange(length)
    common_bits = index[:, None] & index[None, :]
    parity = np.zeros((length, length), np.int32)
    for bit_pos in range(length.bit_length() - 1):
        parity = parity ^ common_bits >> bit_pos & 1
    return (1 - 2 * parity).astype(ml_dtypes.bfloat16)


def hop(value, axis, step):
    pairs = []
    for device in range(128):
        x, z, core = device // 32, device // 8 % SIDE, device % 2
        if (axis == "first") == (core == 0):
            x = (x + step) % SIDE
        else:
            z = (z + step) % SIDE
        pairs.append((device, (x * SIDE + z) * 8 + device % 8))
    return lax.ppermute(value, ("dp", "fsdp"), pairs)


def in_hbm(value):
    return pltpu.with_memory_space_constraint(value, pltpu.HBM)


def row_scales(index_refs, table_ref, inverse):
    index = jnp.concatenate([ref[...] for ref in index_refs], axis=1)
    scale = jnp.zeros(index.shape, jnp.float32)
    for level in range(table_ref.shape[0]):
        scale = jnp.where(index == level, table_ref[level], scale)
    if inverse:
        scale = 1.0 / (math.sqrt(TILE) * scale)
    ones = jnp.ones((8 - index.shape[0], index.shape[1]), jnp.float32)
    return jnp.concatenate([scale, ones], axis=0).T


def encode_kernel(counts, ordered, place_ref, table_ref, sign_ref, hmat_ref, *refs):
    jobs = len(counts)
    inputs, out_refs = iter(refs[int(ordered) : -jobs]), refs[-jobs:]
    grad_refs, index_refs, arrived_refs = [], [], []
    for count in counts:
        grad_refs.append(next(inputs))
        index_refs.append(next(inputs))
        arrived_refs.append([next(inputs) for _ in range(count)])
    steps = row_scales(index_refs, table_ref, True)
    sign = (2 * sign_ref[...] - 1).astype(jnp.bfloat16)
    for tile in range(TILES):
        cols = slice(tile * TILE, (tile + 1) * TILE)
        signed = jnp.concatenate([ref[:, cols] for ref in grad_refs], axis=0) * sign[:, cols]
        rotated = jnp.dot(signed, hmat_ref[...], preferred_element_type=jnp.float32)
        codes = jnp.clip(rotated * steps[:, tile : tile + 1], -127.0, 127.0).astype(jnp.bfloat16)
        for job in range(jobs):
            code = codes[job * PART : (job + 1) * PART]
            if arrived_refs[job]:
                total = code.astype(jnp.float32)
                for ref in arrived_refs[job]:
                    total = total + ref[:, cols].astype(jnp.float32)
                code = total.astype(out_refs[job].dtype)
            out_refs[job][:, cols] = code


def block_at(place_ref, near, far):
    place = place_ref[0]
    x, z, core = place // (2 * SIDE), place // 2 % SIDE, place % 2
    x, z = x + jnp.where(core == 0, near, far), z + jnp.where(core == 0, far, near)
    return lax.rem(x, SIDE) * SIDE + lax.rem(z, SIDE)


def encode(place, table, sign, grad, index, hmat, grid, jobs, after=None):
    in_specs = [
        pl.BlockSpec(memory_space=pltpu.SMEM),
        pl.BlockSpec((1, WIDTH), lambda *_: (0, 0)),
        pl.BlockSpec((TILE, TILE), lambda *_: (0, 0)),
    ]
    operands, out_specs, out_shape = [table, sign, hmat], [], []
    if after is not None:
        in_specs.append(pl.BlockSpec((8, 128), lambda *_: (0, 0)))
        operands.append(after)
    parts = BLOCK // PART
    for near, far, arrived, spec, shape, dtype in jobs:
        rows = functools.partial(lambda near, far, i, j, place_ref: block_at(place_ref, near, far(i)) * parts + j, near, far)
        in_specs.append(pl.BlockSpec((PART, WIDTH), functools.partial(lambda rows, *at: (rows(*at), 0), rows)))
        in_specs.append(pl.BlockSpec((TILES, PART), functools.partial(lambda rows, *at: (0, rows(*at)), rows)))
        operands += [grad, index]
        for value, its_spec in arrived:
            in_specs.append(its_spec)
            operands.append(value)
        out_specs.append(spec)
        out_shape.append(jax.ShapeDtypeStruct(shape, dtype))
    blocks = len(jobs) * grid[0] * parts
    return pl.pallas_call(
        functools.partial(encode_kernel, [len(job[2]) for job in jobs], after is not None),
        out_shape=out_shape,
        grid_spec=pltpu.PrefetchScalarGridSpec(num_scalar_prefetch=1, grid=grid, in_specs=in_specs, out_specs=out_specs),
        compiler_params=pltpu.CompilerParams(vmem_limit_bytes=VMEM_BYTES),
        cost_estimate=pl.CostEstimate(flops=2 * blocks * PART * WIDTH * TILE, bytes_accessed=blocks * PART * WIDTH * 6, transcendentals=0),
    )(place, *operands)


def paired(ring):
    return lambda i: ring[0] + i * (ring[1] - ring[0])


def reduce_scatter(place, table, sign, grad, index, hmat, staged):
    code = functools.partial(encode, place, table, sign, grad, index, hmat)
    pair = ((2, BLOCK, WIDTH), jnp.bfloat16)
    both = pl.BlockSpec((None, PART, WIDTH), lambda i, j, place_ref: (i, j, 0))
    grid = (2, BLOCK // PART)

    def round_of(*plan):
        jobs = [(near, paired(ring), [(v, both) for v in arrived], both, *pair) for _, near, ring, arrived in plan]
        codes = code(grid, jobs)
        return [hop(v, "first", step) for v, (step, *_) in zip(codes, plan, strict=True)]

    up_far, down_far = round_of((1, 2, RING0, ()), (-1, 2, RING1, ()))
    up_own, down_own = round_of((1, 1, RING1, ()), (-1, 3, RING0, ()))
    single = pl.BlockSpec((PART, WIDTH), lambda i, j, place_ref: (j, 0))
    low = ((BLOCK, WIDTH), jnp.bfloat16)

    def of_slot(slot):
        return pl.BlockSpec((None, PART, WIDTH), lambda i, j, place_ref: (slot, j, 0))

    def sums_of(slot):
        plan = ((1, 1, RING0[slot], up_far), (-1, 3, RING1[slot], down_far))
        jobs = [(near, lambda i, far=far: far, [(v, of_slot(slot))], single, *low) for _, near, far, v in plan]
        return [hop(v, "first", step) for v, (step, *_) in zip(code((1, BLOCK // PART), jobs, staged), plan, strict=True)]

    def own_of(slot, up_sum, down_sum):
        plan = ((RING0[slot], up_sum, down_own), (RING1[slot], down_sum, up_own))
        jobs = []
        for far, whole, part in plan:
            shape = low if far else ((BLOCK, WIDTH), jnp.float32)
            jobs.append((0, lambda i, far=far: far, [(whole, single), (part, of_slot(slot))], single, *shape))
        values = code((1, BLOCK // PART), jobs)
        return [in_hbm(hop(v, "second", far)) if far else v for v, (far, *_) in zip(values, plan, strict=True)]

    early, late = sums_of(0), sums_of(1)
    two, three = own_of(0, *early)
    one, own = own_of(1, *late)
    return [own, two, one, three]


def decode_kernel(place_ref, table_ref, sign_ref, hmat_ref, own_ref, two_ref, one_ref, three_ref, index_ref, plain_ref, square_ref, sum_ref):
    f32 = jnp.float32

    @pl.when(pl.program_id(0) == 0)
    def _():
        sum_ref[...] = jnp.zeros_like(sum_ref)

    scales = row_scales([index_ref], table_ref, False) * (1.0 / math.sqrt(TILE))
    sign = (2 * sign_ref[...] - 1).astype(f32)
    square = sum_ref[...]
    for tile in range(TILES):
        cols = slice(tile * TILE, (tile + 1) * TILE)
        value = own_ref[:, cols] + two_ref[:, cols].astype(f32) + one_ref[:, cols].astype(f32) + three_ref[:, cols].astype(f32)
        plain = jnp.zeros(value.shape, f32)
        for _ in range(3):
            piece = value.astype(jnp.bfloat16)
            plain = plain + jnp.dot(piece, hmat_ref[...], preferred_element_type=f32)
            value = value - piece.astype(f32)
        plain = plain * scales[:, tile : tile + 1] * sign[:, cols]
        plain_ref[:, cols] = plain
        parts = jnp.sum((plain * plain).reshape(-1, 8, TILE), axis=0)
        square = square + parts[:, :128] + parts[:, 128:]
    sum_ref[...] = square
    square_ref[...] = jnp.broadcast_to(square, square_ref.shape)


def decode(place, table, sign, terms, index, hmat, copies):
    parts = BLOCK // PART
    single = pl.BlockSpec((PART, WIDTH), lambda j, place_ref: (j, 0))
    return pl.pallas_call(
        decode_kernel,
        out_shape=(
            jax.ShapeDtypeStruct((BLOCK, WIDTH), jnp.float32),
            pltpu.HBM((copies, 8, 128), jnp.float32),
        ),
        grid_spec=pltpu.PrefetchScalarGridSpec(
            num_scalar_prefetch=1,
            grid=(parts,),
            in_specs=[
                pl.BlockSpec(memory_space=pltpu.SMEM),
                pl.BlockSpec((1, WIDTH), lambda j, place_ref: (0, 0)),
                pl.BlockSpec((TILE, TILE), lambda j, place_ref: (0, 0)),
                *[single] * 4,
                pl.BlockSpec((TILES, PART), lambda j, place_ref: (0, block_at(place_ref, 0, 0) * parts + j)),
            ],
            out_specs=(
                single,
                pl.BlockSpec((copies, 8, 128), lambda j, place_ref: (0, 0, 0)),
            ),
            scratch_shapes=[pltpu.VMEM((8, 128), jnp.float32)],
        ),
        compiler_params=pltpu.CompilerParams(vmem_limit_bytes=VMEM_BYTES),
        cost_estimate=pl.CostEstimate(flops=6 * 512 * WIDTH * TILE, bytes_accessed=512 * WIDTH * 14, transcendentals=0),
    )(place, table, sign, hmat, *terms, index)


def total_squares(square):
    square = jnp.sum(lax.all_to_all(square, "fsdp", 0, 0), axis=0)
    copies = jnp.broadcast_to(square, (lax.axis_size("dp"), *square.shape))
    return lax.all_to_all(copies, "dp", 0, 0)


MEAN_SCALE = 0.02 / (1.0 - 0.9**10)
VAR_SCALE = 1.0 / (1.0 - 0.95**10)


def clip_factor(square_ref):
    square = jnp.sum(square_ref[...], axis=0)
    square = jnp.sum(jnp.sum(square, axis=0, keepdims=True), axis=1, keepdims=True)
    return LIMIT / jnp.maximum(jnp.sqrt(square), LIMIT)


def stepped(master, new_mean, new_var):
    spread = new_var * VAR_SCALE
    spread = spread * lax.rsqrt(spread)
    return 0.998 * master - new_mean * MEAN_SCALE / (spread + 1e-08)


def weights_kernel(square_ref, plain_ref, master_ref, mean_ref, var_ref, out_ref):
    grad = plain_ref[...] * clip_factor(square_ref)
    new_mean = 0.9 * mean_ref[...] + 0.1 * grad
    new_var = 0.95 * var_ref[...] + 0.05 * grad * grad
    out_ref[...] = stepped(master_ref[...], new_mean, new_var).astype(jnp.bfloat16)


def state_kernel(square_ref, plain_ref, master_ref, mean_ref, var_ref, new_master_ref, new_mean_ref, new_var_ref):
    grad = plain_ref[...] * clip_factor(square_ref)
    new_mean = 0.9 * mean_ref[...] + 0.1 * grad
    new_var = 0.95 * var_ref[...] + 0.05 * grad * grad
    new_mean_ref[...] = new_mean
    new_var_ref[...] = new_var
    new_master_ref[...] = stepped(master_ref[...], new_mean, new_var)


def adamw(kernel, out_shape, square, plain, master, mean, var):
    rows = pl.BlockSpec((STEP, WIDTH), lambda j: (j, 0))
    return pl.pallas_call(
        kernel,
        out_shape=out_shape,
        grid=(BLOCK // STEP,),
        in_specs=[pl.BlockSpec(square.shape, lambda j: (0, 0, 0))] + [rows] * 4,
        out_specs=jax.tree.map(lambda _: rows, out_shape),
        compiler_params=pltpu.CompilerParams(vmem_limit_bytes=VMEM_BYTES),
        cost_estimate=pl.CostEstimate(flops=20 * BLOCK * WIDTH, bytes_accessed=24 * BLOCK * WIDTH, transcendentals=BLOCK * WIDTH),
    )(square, plain, master, mean, var)


def stage_kernel(*refs):
    for source, target in zip(refs[:3], refs[3:6], strict=True):
        target[...] = source[...]
    refs[6][...] = jnp.zeros_like(refs[6])


def stage(*state):
    rows = pl.BlockSpec((STEP, WIDTH), lambda j: (j, 0))
    return pl.pallas_call(
        stage_kernel,
        out_shape=[pltpu.VMEM(v.shape, v.dtype) for v in state] + [jax.ShapeDtypeStruct((8, 128), jnp.float32)],
        grid=(BLOCK // STEP,),
        in_specs=[rows] * 3,
        out_specs=[rows] * 3 + [pl.BlockSpec((8, 128), lambda j: (0, 0))],
        compiler_params=pltpu.CompilerParams(vmem_limit_bytes=VMEM_BYTES),
        cost_estimate=pl.CostEstimate(flops=0, bytes_accessed=24 * BLOCK * WIDTH, transcendentals=0),
    )(*state)


def after(value, first):
    anywhere = pl.BlockSpec(memory_space=pl.ANY)
    return pl.pallas_call(
        lambda *_: None,
        out_shape=jax.ShapeDtypeStruct(value.shape, value.dtype),
        in_specs=[anywhere, anywhere],
        out_specs=anywhere,
        input_output_aliases={0: 0},
        compiler_params=pltpu.CompilerParams(vmem_limit_bytes=VMEM_BYTES),
    )(value, first)


def fill_kernel(places, at_ref, *refs):
    count = len(places)
    out_ref, tile_ref, sems = refs[-3:]
    tile_ref[...] = jnp.zeros_like(tile_ref)
    chip, core = at_ref[0] // 2, at_ref[0] % 2
    copies = []
    for j, (step, swapped) in enumerate(places):
        source = (chip + SIDE - step + 2 * step * core) % SIDE
        column = pl.multiple_of((source * 2 + (1 - core if swapped else core)) * WIDTH, WIDTH)
        target = out_ref.at[:, pl.ds(column, WIDTH)]
        copies.append(pltpu.make_async_copy(refs[j], target, sems.at[j]))
    for copy in copies:
        copy.start()
    for copy in copies:
        copy.wait()


def fill(at, places, blocks, weights=None):
    anywhere = pl.BlockSpec(memory_space=pl.ANY)
    whole = pl.BlockSpec(blocks[0].shape, lambda: (0, 0))
    given = [] if weights is None else [weights]
    return pl.pallas_call(
        functools.partial(fill_kernel, places),
        out_shape=(pltpu.HBM((BLOCK, D), jnp.bfloat16), jax.ShapeDtypeStruct((8, 128), jnp.float32)),
        in_specs=[pl.BlockSpec(memory_space=pltpu.SMEM)] + [whole] * len(blocks) + [anywhere] * len(given),
        out_specs=(anywhere, pl.BlockSpec((8, 128), lambda: (0, 0))),
        scratch_shapes=[pltpu.SemaphoreType.DMA((len(blocks),))],
        input_output_aliases={len(blocks) + 1: 0} if given else {},
        compiler_params=pltpu.CompilerParams(vmem_limit_bytes=VMEM_BYTES),
        cost_estimate=pl.CostEstimate(flops=0, bytes_accessed=4 * len(blocks) * blocks[0].size, transcendentals=0),
    )(at, *blocks, *given)


def along_y(value):
    pairs = [(y * 2 + core, (y + 1 - 2 * core) % SIDE * 2 + core) for y in range(SIDE) for core in range(2)]
    return lax.ppermute(value, "fsdp", pairs)


def to_other_core(value):
    return lax.ppermute(value, "fsdp", [(i, i ^ 1) for i in range(8)])


def gather(low, state):
    at = lax.axis_index("fsdp").reshape(1)
    one = along_y(low)
    other = to_other_core(low)
    one_other = along_y(other)
    one = after(one, state)
    two = along_y(one)
    one_swapped = to_other_core(one)
    other_swapped = to_other_core(one_other)
    near = ((0, False), (0, True), (1, False), (1, True), (-1, True), (-1, False))
    weights, filled = fill(at, near, (low, other, one, one_other, one_swapped, other_swapped))
    two = after(two, filled)
    two_swapped = to_other_core(two)
    return fill(at, ((2, False), (2, True)), (two, two_swapped), weights)[0]


def on_device(grad_shards, hadamard_signs, scale_index, scale_table, master, mean_moment, var_moment):
    grad, scale_index, master, mean_moment, var_moment = map(in_hbm, (grad_shards[0], scale_index, master, mean_moment, var_moment))
    scale_table = in_hbm(scale_table)
    place = (lax.axis_index("dp") * 2 + (lax.axis_index("fsdp") & 1)).reshape(1)
    sign = in_hbm(hadamard_signs.reshape(1, WIDTH))
    hmat = in_hbm(jnp.asarray(hadamard(TILE)))
    *state, staged = stage(master, mean_moment, var_moment)
    terms = reduce_scatter(place, scale_table, sign, grad, scale_index, hmat, staged)
    plain, square = decode(place, scale_table, sign, terms, scale_index, hmat, lax.axis_size("fsdp"))
    square = total_squares(square)
    low = adamw(weights_kernel, jax.ShapeDtypeStruct((BLOCK, WIDTH), jnp.bfloat16), square, plain, *state)
    new_state = adamw(state_kernel, (jax.ShapeDtypeStruct(master.shape, jnp.float32),) * 3, square, plain, *state)
    return *new_state, gather(low, new_state[0])


def solution(mesh):
    return jax.shard_map(
        on_device,
        mesh=mesh,
        in_specs=(
            P("dp", None, "fsdp"),
            P("fsdp"),
            P("fsdp", None),
            P(),
            P("dp", "fsdp"),
            P("dp", "fsdp"),
            P("dp", "fsdp"),
        ),
        out_specs=(P("dp", "fsdp"), P("dp", "fsdp"), P("dp", "fsdp"), P("dp", None)),
        check_vma=False,
    )
```

time: 176 us -> 163 us (0.926)
  Pallas kernels: 49.7 us -> 34.1 us
  between operations: 13.8 us -> 0.75 us
  waiting for transfers between devices: 71.8 us -> 60.2 us
  starting transfers between devices: 15.7 us -> 27.1 us
  blocking collectives: 21.3 us -> 31.9 us
  local copies, waits for them, and re-layouts: 2.83 us -> 8.67 us
    ppermute x0 -> x7, waiting for transfers between devices: none -> 22.1 us  [the longest x3 17.3 us: along_y(): return lax.ppermute(value, 'fsdp', pairs)]
    ppermute x9 -> x11, waiting for transfers between devices: 56 us -> 38.1 us  [hop(): return lax.ppermute(value, ('dp', 'fsdp'), pairs)]
    all_gather x3 -> x0, waiting for transfers between devices: 15.7 us -> none  [the longest x1 15.7 us: on_device(): rest = in_hbm(lax.all_gather(rest, 'fsdp'))]
    pallas_call x5 -> x7, Pallas kernels: 27.4 us -> 11.8 us  [the longest x2 4.71 us: adamw(): pl.pallas_call(kernel, out_shape=out_shape, grid=(BLOCK // STEP,), in_spe...]
    ppermute x0 -> x7, starting transfers between devices: none -> 10.4 us  [the longest x4 8.58 us: to_other_core(): return lax.ppermute(value, 'fsdp', [(i, i ^ 1) for i in range(8)])]
    all_to_all x1, blocking collectives: 11.1 us -> 19.4 us  [total_squares(): square = jnp.sum(lax.all_to_all(square, 'fsdp', 0, 0), axis=0)]
    unnamed x8 -> x16, local copies, waits for them, and re-layouts: 1.54 us -> 7.38 us
    all_to_all x1, blocking collectives: 10.2 us -> 12.6 us  [total_squares(): return lax.all_to_all(copies, 'dp', 0, 0)]
  transfers between devices with their start and end apart: 12 -> 18, of which waited for: 8 -> 13; matrix products, arithmetic and copies ran while one was open for 0% -> 0% of each run, Pallas kernels for 19% -> 14%
where the time goes in v3:
time: 163 us
  waiting for transfers between devices  60.2 us (37%)
  Pallas kernels  34.1 us (21%)
  blocking collectives  31.9 us (20%)
  starting transfers between devices  27.1 us (17%)
  local copies, waits for them, and re-layouts  8.67 us (5%)
    ppermute x11, waiting for transfers between devices, hop(): return lax.ppermute(value, ('dp', 'fsdp'), pairs)  38.1 us
    all_to_all x1, blocking collectives, total_squares(): square = jnp.sum(lax.all_to_all(square, 'fsdp', 0, 0), axis=0)  19.4 us
    pallas_call x6, Pallas kernels, encode(): pl.pallas_call(functools.partial(encode_kernel, [len(job[2]) for job in j...  19 us
    ppermute x3, waiting for transfers between devices, along_y(): return lax.ppermute(value, 'fsdp', pairs)  17.3 us
    ppermute x11, starting transfers between devices, hop(): return lax.ppermute(value, ('dp', 'fsdp'), pairs)  16.8 us
    all_to_all x1, blocking collectives, total_squares(): return lax.all_to_all(copies, 'dp', 0, 0)  12.6 us
    ppermute x4, starting transfers between devices, to_other_core(): return lax.ppermute(value, 'fsdp', [(i, i ^ 1) for i in range(8)])  8.58 us
    unnamed x16, local copies, waits for them, and re-layouts  7.38 us
  transfers between devices with their start and end apart: 18, of which 13 were waited for; matrix products, arithmetic and copies ran while one was open for 0% of the time, Pallas kernels for 14%

profile of v3, /device:TPU:1, one launch (start us, length us, event | category | flops | bytes accessed | tf_op | source)
XLA Modules:
  0.0 162.8 jit_solution(16684511538185907827)
XLA Ops:
  1.9 4.1 %shard_map.112 = (bf16[2,512,768]{2,1,0:T(8,128)(2,1)S(1)}, bf16[2,512,768]{2,1,0:T(8,128)(2,1)S(1)}) custom-call(s32[1]{0:T(128)} %bitcast.place_ref, f32[16]{0:T(128)} %table_ref.13, s32[1,768]{1,0:T(1,128)} %reshape.18.sign_ref, bf16[256,256]{1,0:T(8,128)(2,1)} %constant.17.clone.hmat_ref, bf16[8192,768]{1,0:T(8,128)(2,1)} %bitcast.3, ...), custom_call_target="tpu_custom_call" | custom-call | flops 805306368 | bytes 9437184 | tf_op jit(solution)/shard_map/pallas_call | solution.py:117
  6.1 2.5 %collective-permute-start = (bf16[2,512,768]{2,1,0:T(8,128)(2,1)S(1)}, bf16[2,512,768]{2,1,0:T(8,128)(2,1)S(1)}, u32[]{:S(2)}, u32[]{:S(2)}) collective-permute-start(bf16[2,512,768]{2,1,0:T(8,128)(2,1)S(1)} %get-tuple-element.29), channel_id=1, source_target_pairs={{0,32},{1,9},{2,34},{3,11},{4,36},{5,13},{6,38},{7,15},{8,40},{9,1... | collective-permute-start | bytes 4718600 | tf_op jit(solution)/shard_map/ppermute | solution.py:45
  8.6 2.2 %collective-permute-start.1 = (bf16[2,512,768]{2,1,0:T(8,128)(2,1)S(1)}, bf16[2,512,768]{2,1,0:T(8,128)(2,1)S(1)}, u32[]{:S(2)}, u32[]{:S(2)}) collective-permute-start(bf16[2,512,768]{2,1,0:T(8,128)(2,1)S(1)} %get-tuple-element.30), channel_id=1, source_target_pairs={{0,96},{1,25},{2,98},{3,27},{4,100},{5,29},{6,102},{7,31},{8,104},... | collective-permute-start | bytes 4718600 | tf_op jit(solution)/shard_map/ppermute | solution.py:45
  10.8 4.1 %shard_map.114 = (bf16[2,512,768]{2,1,0:T(8,128)(2,1)S(1)}, bf16[2,512,768]{2,1,0:T(8,128)(2,1)S(1)}) custom-call(s32[1]{0:T(128)} %bitcast.place_ref, f32[16]{0:T(128)} %table_ref.13, s32[1,768]{1,0:T(1,128)} %reshape.18.sign_ref, bf16[256,256]{1,0:T(8,128)(2,1)} %constant.17.clone.hmat_ref, bf16[8192,768]{1,0:T(8,128)(2,1)} %bitcast.5, ...), custom_call_target="tpu_custom_call" | custom-call | flops 805306368 | bytes 9437184 | tf_op jit(solution)/shard_map/pallas_call | solution.py:117
  16.5 3.1 %shard_map.111 = (f32[512,768]{1,0:T(8,128)S(1)}, f32[512,768]{1,0:T(8,128)S(1)}, f32[512,768]{1,0:T(8,128)S(1)}, f32[8,128]{1,0:T(8,128)S(1)}) custom-call(f32[512,768]{1,0:T(8,128)} %refs_0_.1, f32[512,768]{1,0:T(8,128)} %refs_1_.5, f32[512,768]{1,0:T(8,128)} %refs_2_.3), custom_call_target="tpu_custom_call" | custom-call | bytes 9437184 | tf_op jit(solution)/shard_map/pallas_call | solution.py:284
  20.7 8.1 %collective-permute-done.refs_3_ = bf16[2,512,768]{2,1,0:T(8,128)(2,1)S(1)} collective-permute-done((bf16[2,512,768]{2,1,0:T(8,128)(2,1)S(1)}, bf16[2,512,768]{2,1,0:T(8,128)(2,1)S(1)}, u32[]{:S(2)}, u32[]{:S(2)}) %collective-permute-start) | collective-permute-done | bytes 1572896 | tf_op jit(solution)/shard_map/ppermute | solution.py:45
  28.8 2.6 %shard_map.116 = (bf16[512,768]{1,0:T(8,128)(2,1)S(1)}, bf16[512,768]{1,0:T(8,128)(2,1)S(1)}) custom-call(s32[1]{0:T(128)} %bitcast.place_ref, f32[16]{0:T(128)} %table_ref.13, s32[1,768]{1,0:T(1,128)} %reshape.18.sign_ref, bf16[256,256]{1,0:T(8,128)(2,1)} %constant.17.clone.hmat_ref, f32[8,128]{1,0:T(8,128)S(1)} %get-tuple-element.28.refs_0_, ...), custom_call_target="tpu_custom_call" | custom-call | flops 402653184 | bytes 4718592 | tf_op jit(solution)/shard_map/pallas_call | solution.py:117
  32.4 1.9 %collective-permute-start.7 = (bf16[512,768]{1,0:T(8,128)(2,1)S(1)}, bf16[512,768]{1,0:T(8,128)(2,1)S(1)}, u32[]{:S(2)}, u32[]{:S(2)}) collective-permute-start(bf16[512,768]{1,0:T(8,128)(2,1)S(1)} %get-tuple-element.37), channel_id=1, source_target_pairs={{0,96},{1,25},{2,98},{3,27},{4,100},{5,29},{6,102},{7,31},{8,104},... | collective-permute-start | bytes 2359304 | tf_op jit(solution)/shard_map/ppermute | solution.py:45
  34.3 2.5 %shard_map.113 = (bf16[512,768]{1,0:T(8,128)(2,1)S(1)}, bf16[512,768]{1,0:T(8,128)(2,1)S(1)}) custom-call(s32[1]{0:T(128)} %bitcast.place_ref, f32[16]{0:T(128)} %table_ref.13, s32[1,768]{1,0:T(1,128)} %reshape.18.sign_ref, bf16[256,256]{1,0:T(8,128)(2,1)} %constant.17.clone.hmat_ref, f32[8,128]{1,0:T(8,128)S(1)} %get-tuple-element.28.refs_0_, ...), custom_call_target="tpu_custom_call" | custom-call | flops 402653184 | bytes 4718592 | tf_op jit(solution)/shard_map/pallas_call | solution.py:117
  36.9 8.3 %collective-permute-done.3.refs_3_ = bf16[2,512,768]{2,1,0:T(8,128)(2,1)S(1)} collective-permute-done((bf16[2,512,768]{2,1,0:T(8,128)(2,1)S(1)}, bf16[2,512,768]{2,1,0:T(8,128)(2,1)S(1)}, u32[]{:S(2)}, u32[]{:S(2)}) %collective-permute-start.3) | collective-permute-done | bytes 1572896 | tf_op jit(solution)/shard_map/ppermute | solution.py:45
  45.2 3.2 %collective-permute-start.4 = (bf16[512,768]{1,0:T(8,128)(2,1)S(1)}, bf16[512,768]{1,0:T(8,128)(2,1)S(1)}, u32[]{:S(2)}, u32[]{:S(2)}) collective-permute-start(bf16[512,768]{1,0:T(8,128)(2,1)S(1)} %get-tuple-element.33), channel_id=1, source_target_pairs={{0,96},{1,25},{2,98},{3,27},{4,100},{5,29},{6,102},{7,31},{8,104},... | collective-permute-start | bytes 2359304 | tf_op jit(solution)/shard_map/ppermute | solution.py:45
  48.4 5.7 %collective-permute-done.6.refs_2_ = bf16[512,768]{1,0:T(8,128)(2,1)S(1)} collective-permute-done((bf16[512,768]{1,0:T(8,128)(2,1)S(1)}, bf16[512,768]{1,0:T(8,128)(2,1)S(1)}, u32[]{:S(2)}, u32[]{:S(2)}) %collective-permute-start.6) | collective-permute-done | bytes 786464 | tf_op jit(solution)/shard_map/ppermute | solution.py:45
  54.1 2.8 %shard_map.117 = (bf16[512,768]{1,0:T(8,128)(2,1)S(1)}, bf16[512,768]{1,0:T(8,128)(2,1)S(1)}) custom-call(s32[1]{0:T(128)} %bitcast.place_ref, f32[16]{0:T(128)} %table_ref.13, s32[1,768]{1,0:T(1,128)} %reshape.18.sign_ref, bf16[256,256]{1,0:T(8,128)(2,1)} %constant.17.clone.hmat_ref, bf16[8192,768]{1,0:T(8,128)(2,1)} %bitcast.11, s32[3,8192]{1,0:T(4,128)} %index_ref.1, ...), custom_call_target="tpu_custom_call" | custom-call | flops 402653184 | bytes 4718592 | tf_op jit(solution)/shard_map/pallas_call | solution.py:117
  56.9 2.5 %collective-permute-start.8 = (bf16[512,768]{1,0:T(8,128)(2,1)S(1)}, bf16[512,768]{1,0:T(8,128)(2,1)S(1)}, u32[]{:S(2)}, u32[]{:S(2)}) collective-permute-start(bf16[512,768]{1,0:T(8,128)(2,1)S(1)} %get-tuple-element.38), channel_id=1, source_target_pairs={{0,16},{1,65},{2,18},{3,67},{4,20},{5,69},{6,22},{7,71},{8,24},{9,... | collective-permute-start | bytes 2359304 | tf_op jit(solution)/shard_map/ppermute | solution.py:45
  60.3 2.2 %collective-permute-done.2.refs_2_ = bf16[512,768]{1,0:T(8,128)(2,1)S(1)} collective-permute-done((bf16[512,768]{1,0:T(8,128)(2,1)S(1)}, bf16[512,768]{1,0:T(8,128)(2,1)S(1)}, u32[]{:S(2)}, u32[]{:S(2)}) %collective-permute-start.2) | collective-permute-done | bytes 786464 | tf_op jit(solution)/shard_map/ppermute | solution.py:45
  62.5 2.8 %shard_map.115 = (bf16[512,768]{1,0:T(8,128)(2,1)S(1)}, f32[512,768]{1,0:T(8,128)S(1)}) custom-call(s32[1]{0:T(128)} %bitcast.place_ref, f32[16]{0:T(128)} %table_ref.13, s32[1,768]{1,0:T(1,128)} %reshape.18.sign_ref, bf16[256,256]{1,0:T(8,128)(2,1)} %constant.17.clone.hmat_ref, bf16[8192,768]{1,0:T(8,128)(2,1)} %bitcast.13, s32[3,8192]{1,0:T(4,128)} %index_ref.1, ...), custom_call_target="tpu_custom_call" | custom-call | flops 402653184 | bytes 4718592 | tf_op jit(solution)/shard_map/pallas_call | solution.py:117
  66.3 5.7 %collective-permute-done.8.two_ref = bf16[512,768]{1,0:T(8,128)(2,1)S(1)} collective-permute-done((bf16[512,768]{1,0:T(8,128)(2,1)S(1)}, bf16[512,768]{1,0:T(8,128)(2,1)S(1)}, u32[]{:S(2)}, u32[]{:S(2)}) %collective-permute-start.8) | collective-permute-done | bytes 786464 | tf_op jit(solution)/shard_map/ppermute | solution.py:45
  72.0 7.7 %collective-permute-done.10.three_ref = bf16[512,768]{1,0:T(8,128)(2,1)S(1)} collective-permute-done((bf16[512,768]{1,0:T(8,128)(2,1)S(1)}, bf16[512,768]{1,0:T(8,128)(2,1)S(1)}, u32[]{:S(2)}, u32[]{:S(2)}) %collective-permute-start.10) | collective-permute-done | bytes 786464 | tf_op jit(solution)/shard_map/ppermute | solution.py:45
  81.0 3.3 %shard_map.118 = (f32[512,768]{1,0:T(8,128)S(1)}, f32[8,8,128]{2,1,0:T(8,128)}) custom-call(s32[1]{0:T(128)} %bitcast.place_ref, f32[16]{0:T(128)} %table_ref.13, s32[1,768]{1,0:T(1,128)} %reshape.18.sign_ref, bf16[256,256]{1,0:T(8,128)(2,1)} %constant.17.clone.hmat_ref, f32[512,768]{1,0:T(8,128)S(1)} %get-tuple-element.35.own_ref, ...), custom_call_target="tpu_custom_call" | custom-call | flops 603979776 | bytes 5505024 | tf_op jit(solution)/shard_map/pallas_call | solution.py:198
  85.5 19.4 %all_to_all.10 = f32[8,8,128]{2,1,0:T(8,128)S(1)} all-to-all(f32[8,8,128]{2,1,0:T(8,128)} %get-tuple-element.41), channel_id=1, replica_groups=mesh['dp'=16,'fsdp'=8] {'fsdp'}, dimensions={0} | all-to-all | bytes 65536 | tf_op jit(solution)/shard_map/all_to_all | solution.py:226
  104.8 12.6 %all_to_all.11.square_ref = f32[16,8,128]{2,1,0:T(8,128)S(1)} all-to-all(f32[16,8,128]{2,1,0:T(8,128)S(1)} %broadcast_in_dim.3), channel_id=1, replica_groups=mesh['dp'=16,'fsdp'=8] {'dp'}, dimensions={0} | all-to-all | bytes 131072 | tf_op jit(solution)/shard_map/all_to_all | solution.py:228
  122.0 2.2 %collective-permute-start.13 = (bf16[512,768]{1,0:T(8,128)(2,1)S(1)}, bf16[512,768]{1,0:T(8,128)(2,1)S(1)}, u32[]{:S(2)}, u32[]{:S(2)}) collective-permute-start(bf16[512,768]{1,0:T(8,128)(2,1)S(1)} %shard_map.120.refs_0_), channel_id=1, source_target_pairs={{0,1},{1,0},{2,3},{3,2},{4,5},{5,4},{6,7},{7,6},{8,9},{9,8},{10,11... | collective-permute-start | bytes 2359304 | tf_op jit(solution)/shard_map/ppermute | solution.py:346
  127.1 2.9 %shard_map.119 = (f32[512,768]{1,0:T(8,128)}, f32[512,768]{1,0:T(8,128)}, f32[512,768]{1,0:T(8,128)}) custom-call(f32[16,8,128]{2,1,0:T(8,128)S(1)} %all_to_all.11.square_ref, f32[512,768]{1,0:T(8,128)S(1)} %copy-done.3, f32[512,768]{1,0:T(8,128)S(1)} %get-tuple-element.43.master_ref, f32[512,768]{1,0:T(8,128)S(1)} %get-tuple-element.44.mean_ref, ...), custom_call_target="tpu_custom_call" | custom-call | flops 7864320 | bytes 9437184 | tf_op jit(solution)/shard_map/pallas_call | solution.py:265
  130.0 5.4 %collective-permute-done.11.__0_ = bf16[512,768]{1,0:T(8,128)(2,1)S(1)} collective-permute-done((bf16[512,768]{1,0:T(8,128)(2,1)S(1)}, bf16[512,768]{1,0:T(8,128)(2,1)S(1)}, u32[]{:S(2)}, u32[]{:S(2)}) %collective-permute-start.11) | collective-permute-done | bytes 786464 | tf_op jit(solution)/shard_map/ppermute | solution.py:342
  136.8 2.1 %collective-permute-start.15 = (bf16[512,768]{1,0:T(8,128)(2,1)S(1)}, bf16[512,768]{1,0:T(8,128)(2,1)S(1)}, u32[]{:S(2)}, u32[]{:S(2)}) collective-permute-start(bf16[512,768]{1,0:T(8,128)(2,1)S(1)} %shard_map.121.refs_2_), channel_id=1, source_target_pairs={{0,1},{1,0},{2,3},{3,2},{4,5},{5,4},{6,7},{7,6},{8,9},{9,8},{10,11... | collective-permute-start | bytes 2359304 | tf_op jit(solution)/shard_map/ppermute | solution.py:346
  139.0 4.9 %collective-permute-done.14.refs_3_ = bf16[512,768]{1,0:T(8,128)(2,1)S(1)} collective-permute-done((bf16[512,768]{1,0:T(8,128)(2,1)S(1)}, bf16[512,768]{1,0:T(8,128)(2,1)S(1)}, u32[]{:S(2)}, u32[]{:S(2)}) %collective-permute-start.14) | collective-permute-done | bytes 786464 | tf_op jit(solution)/shard_map/ppermute | solution.py:342
  143.8 2.1 %collective-permute-start.16 = (bf16[512,768]{1,0:T(8,128)(2,1)S(1)}, bf16[512,768]{1,0:T(8,128)(2,1)S(1)}, u32[]{:S(2)}, u32[]{:S(2)}) collective-permute-start(bf16[512,768]{1,0:T(8,128)(2,1)S(1)} %collective-permute-done.14.refs_3_), channel_id=1, source_target_pairs={{0,1},{1,0},{2,3},{3,2},{4,5},{5,4},{6,7},{7,6},{8,9},{9,8},{10,11... | collective-permute-start | bytes 2359304 | tf_op jit(solution)/shard_map/ppermute | solution.py:346
  146.0 1.9 %collective-permute-done.16.refs_5_ = bf16[512,768]{1,0:T(8,128)(2,1)S(1)} collective-permute-done((bf16[512,768]{1,0:T(8,128)(2,1)S(1)}, bf16[512,768]{1,0:T(8,128)(2,1)S(1)}, u32[]{:S(2)}, u32[]{:S(2)}) %collective-permute-start.16) | collective-permute-done | bytes 786464 | tf_op jit(solution)/shard_map/ppermute | solution.py:346
  147.9 2.2 %shard_map.122 = (bf16[512,6144]{1,0:T(8,128)(2,1)}, f32[8,128]{1,0:T(8,128)S(1)}) custom-call(s32[1]{0:T(128)} %bitcast.2.at_ref, bf16[512,768]{1,0:T(8,128)(2,1)S(1)} %shard_map.120.refs_0_, bf16[512,768]{1,0:T(8,128)(2,1)S(1)} %collective-permute-done.13.refs_1_, bf16[512,768]{1,0:T(8,128)(2,1)S(1)} %shard_map.121.refs_2_, ...), custom_call_target="tpu_custom_call" | custom-call | bytes 9437184 | tf_op jit(solution)/shard_map/pallas_call | solution.py:328
  150.1 7.0 %collective-permute-done.12.__0_ = bf16[512,768]{1,0:T(8,128)(2,1)S(1)} collective-permute-done((bf16[512,768]{1,0:T(8,128)(2,1)S(1)}, bf16[512,768]{1,0:T(8,128)(2,1)S(1)}, u32[]{:S(2)}, u32[]{:S(2)}) %collective-permute-start.12) | collective-permute-done | bytes 786464 | tf_op jit(solution)/shard_map/ppermute | solution.py:342
  157.1 2.1 %collective-permute-start.17 = (bf16[512,768]{1,0:T(8,128)(2,1)S(1)}, bf16[512,768]{1,0:T(8,128)(2,1)S(1)}, u32[]{:S(2)}, u32[]{:S(2)}) collective-permute-start(bf16[512,768]{1,0:T(8,128)(2,1)S(1)} %shard_map.123.refs_0_), channel_id=1, source_target_pairs={{0,1},{1,0},{2,3},{3,2},{4,5},{5,4},{6,7},{7,6},{8,9},{9,8},{10,11... | collective-permute-start | bytes 2359304 | tf_op jit(solution)/shard_map/ppermute | solution.py:346
  159.2 1.9 %collective-permute-done.17.refs_1_ = bf16[512,768]{1,0:T(8,128)(2,1)S(1)} collective-permute-done((bf16[512,768]{1,0:T(8,128)(2,1)S(1)}, bf16[512,768]{1,0:T(8,128)(2,1)S(1)}, u32[]{:S(2)}, u32[]{:S(2)}) %collective-permute-start.17) | collective-permute-done | bytes 786464 | tf_op jit(solution)/shard_map/ppermute | solution.py:346
  (39 shorter events, 19.8 us)
Async XLA Ops:
  6.1 22.8 %collective-permute-start = (bf16[2,512,768]{2,1,0:T(8,128)(2,1)S(1)}, bf16[2,512,768]{2,1,0:T(8,128)(2,1)S(1)}, u32[]{:S(2)}, u32[]{:S(2)}) collective-permute-start(bf16[2,512,768]{2,1,0:T(8,128)(2,1)S(1)} %get-tuple-element.29), channel_id=1, source_target_pairs={{0,32},{1,9},{2,34},{3,11},{4,36},{5,13},{6,38},{7,15},{8,40},{9,1... | collective-permute-start | bytes 4718600 | tf_op jit(solution)/shard_map/ppermute | solution.py:45
  8.6 20.2 %collective-permute-start.1 = (bf16[2,512,768]{2,1,0:T(8,128)(2,1)S(1)}, bf16[2,512,768]{2,1,0:T(8,128)(2,1)S(1)}, u32[]{:S(2)}, u32[]{:S(2)}) collective-permute-start(bf16[2,512,768]{2,1,0:T(8,128)(2,1)S(1)} %get-tuple-element.30), channel_id=1, source_target_pairs={{0,96},{1,25},{2,98},{3,27},{4,100},{5,29},{6,102},{7,31},{8,104},... | collective-permute-start | bytes 4718600 | tf_op jit(solution)/shard_map/ppermute | solution.py:45
  14.9 30.3 %collective-permute-start.3 = (bf16[2,512,768]{2,1,0:T(8,128)(2,1)S(1)}, bf16[2,512,768]{2,1,0:T(8,128)(2,1)S(1)}, u32[]{:S(2)}, u32[]{:S(2)}) collective-permute-start(bf16[2,512,768]{2,1,0:T(8,128)(2,1)S(1)} %get-tuple-element.32), channel_id=1, source_target_pairs={{0,96},{1,25},{2,98},{3,27},{4,100},{5,29},{6,102},{7,31},{8,104},... | collective-permute-start | bytes 4718600 | tf_op jit(solution)/shard_map/ppermute | solution.py:45
  16.4 32.0 %collective-permute-start.5 = (bf16[2,512,768]{2,1,0:T(8,128)(2,1)S(1)}, bf16[2,512,768]{2,1,0:T(8,128)(2,1)S(1)}, u32[]{:S(2)}, u32[]{:S(2)}) collective-permute-start(bf16[2,512,768]{2,1,0:T(8,128)(2,1)S(1)} %get-tuple-element.34), channel_id=1, source_target_pairs={{0,32},{1,9},{2,34},{3,11},{4,36},{5,13},{6,38},{7,15},{8,40},{9,1... | collective-permute-start | bytes 4718600 | tf_op jit(solution)/shard_map/ppermute | solution.py:45
  19.6 1.1 copy-start
  31.4 22.7 %collective-permute-start.6 = (bf16[512,768]{1,0:T(8,128)(2,1)S(1)}, bf16[512,768]{1,0:T(8,128)(2,1)S(1)}, u32[]{:S(2)}, u32[]{:S(2)}) collective-permute-start(bf16[512,768]{1,0:T(8,128)(2,1)S(1)} %get-tuple-element.36), channel_id=1, source_target_pairs={{0,32},{1,9},{2,34},{3,11},{4,36},{5,13},{6,38},{7,15},{8,40},{9,1... | collective-permute-start | bytes 2359304 | tf_op jit(solution)/shard_map/ppermute | solution.py:45
  32.4 21.7 %collective-permute-start.7 = (bf16[512,768]{1,0:T(8,128)(2,1)S(1)}, bf16[512,768]{1,0:T(8,128)(2,1)S(1)}, u32[]{:S(2)}, u32[]{:S(2)}) collective-permute-start(bf16[512,768]{1,0:T(8,128)(2,1)S(1)} %get-tuple-element.37), channel_id=1, source_target_pairs={{0,96},{1,25},{2,98},{3,27},{4,100},{5,29},{6,102},{7,31},{8,104},... | collective-permute-start | bytes 2359304 | tf_op jit(solution)/shard_map/ppermute | solution.py:45
  36.8 25.7 %collective-permute-start.2 = (bf16[512,768]{1,0:T(8,128)(2,1)S(1)}, bf16[512,768]{1,0:T(8,128)(2,1)S(1)}, u32[]{:S(2)}, u32[]{:S(2)}) collective-permute-start(bf16[512,768]{1,0:T(8,128)(2,1)S(1)} %get-tuple-element.31), channel_id=1, source_target_pairs={{0,32},{1,9},{2,34},{3,11},{4,36},{5,13},{6,38},{7,15},{8,40},{9,1... | collective-permute-start | bytes 2359304 | tf_op jit(solution)/shard_map/ppermute | solution.py:45
  45.2 17.3 %collective-permute-start.4 = (bf16[512,768]{1,0:T(8,128)(2,1)S(1)}, bf16[512,768]{1,0:T(8,128)(2,1)S(1)}, u32[]{:S(2)}, u32[]{:S(2)}) collective-permute-start(bf16[512,768]{1,0:T(8,128)(2,1)S(1)} %get-tuple-element.33), channel_id=1, source_target_pairs={{0,96},{1,25},{2,98},{3,27},{4,100},{5,29},{6,102},{7,31},{8,104},... | collective-permute-start | bytes 2359304 | tf_op jit(solution)/shard_map/ppermute | solution.py:45
  56.9 15.1 %collective-permute-start.8 = (bf16[512,768]{1,0:T(8,128)(2,1)S(1)}, bf16[512,768]{1,0:T(8,128)(2,1)S(1)}, u32[]{:S(2)}, u32[]{:S(2)}) collective-permute-start(bf16[512,768]{1,0:T(8,128)(2,1)S(1)} %get-tuple-element.38), channel_id=1, source_target_pairs={{0,16},{1,65},{2,18},{3,67},{4,20},{5,69},{6,22},{7,71},{8,24},{9,... | collective-permute-start | bytes 2359304 | tf_op jit(solution)/shard_map/ppermute | solution.py:45
  59.5 20.3 %collective-permute-start.10 = (bf16[512,768]{1,0:T(8,128)(2,1)S(1)}, bf16[512,768]{1,0:T(8,128)(2,1)S(1)}, u32[]{:S(2)}, u32[]{:S(2)}) collective-permute-start(bf16[512,768]{1,0:T(8,128)(2,1)S(1)} %get-tuple-element.40), channel_id=1, source_target_pairs={{0,24},{1,97},{2,26},{3,99},{4,28},{5,101},{6,30},{7,103},{8,0},{9... | collective-permute-start | bytes 2359304 | tf_op jit(solution)/shard_map/ppermute | solution.py:45
  65.3 14.8 %collective-permute-start.9 = (bf16[512,768]{1,0:T(8,128)(2,1)S(1)}, bf16[512,768]{1,0:T(8,128)(2,1)S(1)}, u32[]{:S(2)}, u32[]{:S(2)}) collective-permute-start(bf16[512,768]{1,0:T(8,128)(2,1)S(1)} %get-tuple-element.39), channel_id=1, source_target_pairs={{0,8},{1,33},{2,10},{3,35},{4,12},{5,37},{6,14},{7,39},{8,16},{9,4... | collective-permute-start | bytes 2359304 | tf_op jit(solution)/shard_map/ppermute | solution.py:45
  72.0 8.1 %copy-start.5 = (bf16[512,768]{1,0:T(8,128)(2,1)}, bf16[512,768]{1,0:T(8,128)(2,1)S(1)}, u32[]{:S(2)}) copy-start(bf16[512,768]{1,0:T(8,128)(2,1)S(1)} %collective-permute-done.8.two_ref) | copy-start | bytes 2359300
  79.7 0.9 copy-start.6
  80.1 0.9 copy-start.7
  84.3 1.1 copy-start.2
  117.4 1.4 copy-start.1
  118.8 1.4 copy-start.3
  122.0 4.1 %collective-permute-start.13 = (bf16[512,768]{1,0:T(8,128)(2,1)S(1)}, bf16[512,768]{1,0:T(8,128)(2,1)S(1)}, u32[]{:S(2)}, u32[]{:S(2)}) collective-permute-start(bf16[512,768]{1,0:T(8,128)(2,1)S(1)} %shard_map.120.refs_0_), channel_id=1, source_target_pairs={{0,1},{1,0},{2,3},{3,2},{4,5},{5,4},{6,7},{7,6},{8,9},{9,8},{10,11... | collective-permute-start | bytes 2359304 | tf_op jit(solution)/shard_map/ppermute | solution.py:346
  124.3 11.1 %collective-permute-start.11 = (bf16[512,768]{1,0:T(8,128)(2,1)S(1)}, bf16[512,768]{1,0:T(8,128)(2,1)S(1)}, u32[]{:S(2)}, u32[]{:S(2)}) collective-permute-start(bf16[512,768]{1,0:T(8,128)(2,1)S(1)} %shard_map.120.refs_0_), channel_id=1, source_target_pairs={{0,2},{1,7},{2,4},{3,1},{4,6},{5,3},{6,0},{7,5},{8,10},{9,15},{10,... | collective-permute-start | bytes 2359304 | tf_op jit(solution)/shard_map/ppermute | solution.py:342
  126.2 17.6 %collective-permute-start.14 = (bf16[512,768]{1,0:T(8,128)(2,1)S(1)}, bf16[512,768]{1,0:T(8,128)(2,1)S(1)}, u32[]{:S(2)}, u32[]{:S(2)}) collective-permute-start(bf16[512,768]{1,0:T(8,128)(2,1)S(1)} %collective-permute-done.13.refs_1_), channel_id=1, source_target_pairs={{0,2},{1,7},{2,4},{3,1},{4,6},{5,3},{6,0},{7,5},{8,10},{9,15},{10,... | collective-permute-start | bytes 2359304 | tf_op jit(solution)/shard_map/ppermute | solution.py:342
  135.4 1.4 copy-start.4
  136.8 9.2 %collective-permute-start.15 = (bf16[512,768]{1,0:T(8,128)(2,1)S(1)}, bf16[512,768]{1,0:T(8,128)(2,1)S(1)}, u32[]{:S(2)}, u32[]{:S(2)}) collective-permute-start(bf16[512,768]{1,0:T(8,128)(2,1)S(1)} %shard_map.121.refs_2_), channel_id=1, source_target_pairs={{0,1},{1,0},{2,3},{3,2},{4,5},{5,4},{6,7},{7,6},{8,9},{9,8},{10,11... | collective-permute-start | bytes 2359304 | tf_op jit(solution)/shard_map/ppermute | solution.py:346
  143.8 4.1 %collective-permute-start.16 = (bf16[512,768]{1,0:T(8,128)(2,1)S(1)}, bf16[512,768]{1,0:T(8,128)(2,1)S(1)}, u32[]{:S(2)}, u32[]{:S(2)}) collective-permute-start(bf16[512,768]{1,0:T(8,128)(2,1)S(1)} %collective-permute-done.14.refs_3_), channel_id=1, source_target_pairs={{0,1},{1,0},{2,3},{3,2},{4,5},{5,4},{6,7},{7,6},{8,9},{9,8},{10,11... | collective-permute-start | bytes 2359304 | tf_op jit(solution)/shard_map/ppermute | solution.py:346
  146.0 11.1 %collective-permute-start.12 = (bf16[512,768]{1,0:T(8,128)(2,1)S(1)}, bf16[512,768]{1,0:T(8,128)(2,1)S(1)}, u32[]{:S(2)}, u32[]{:S(2)}) collective-permute-start(bf16[512,768]{1,0:T(8,128)(2,1)S(1)} %shard_map.121.refs_2_), channel_id=1, source_target_pairs={{0,2},{1,7},{2,4},{3,1},{4,6},{5,3},{6,0},{7,5},{8,10},{9,15},{10,... | collective-permute-start | bytes 2359304 | tf_op jit(solution)/shard_map/ppermute | solution.py:342
  157.1 4.0 %collective-permute-start.17 = (bf16[512,768]{1,0:T(8,128)(2,1)S(1)}, bf16[512,768]{1,0:T(8,128)(2,1)S(1)}, u32[]{:S(2)}, u32[]{:S(2)}) collective-permute-start(bf16[512,768]{1,0:T(8,128)(2,1)S(1)} %shard_map.123.refs_0_), channel_id=1, source_target_pairs={{0,1},{1,0},{2,3},{3,2},{4,5},{5,4},{6,7},{7,6},{8,9},{9,8},{10,11... | collective-permute-start | bytes 2359304 | tf_op jit(solution)/shard_map/ppermute | solution.py:346

commit v4 on v3

--- a/solution.py
+++ b/solution.py
@@ -47,6 +47,10 @@
 
 def in_hbm(value):
     return pltpu.with_memory_space_constraint(value, pltpu.HBM)
+
+
+def in_vmem(value):
+    return pltpu.with_memory_space_constraint(value, pltpu.VMEM)
 
 
 def row_scales(index_refs, table_ref, inverse):
@@ -119,7 +123,7 @@
         out_shape=out_shape,
         grid_spec=pltpu.PrefetchScalarGridSpec(num_scalar_prefetch=1, grid=grid, in_specs=in_specs, out_specs=out_specs),
         compiler_params=pltpu.CompilerParams(vmem_limit_bytes=VMEM_BYTES),
-        cost_estimate=pl.CostEstimate(flops=2 * blocks * PART * WIDTH * TILE, bytes_accessed=blocks * PART * WIDTH * 6, transcendentals=0),
+        cost_estimate=pl.CostEstimate(flops=0, bytes_accessed=0, transcendentals=0),
     )(place, *operands)
 
 
@@ -151,18 +155,21 @@
         jobs = [(near, lambda i, far=far: far, [(v, of_slot(slot))], single, *low) for _, near, far, v in plan]
         return [hop(v, "first", step) for v, (step, *_) in zip(code((1, BLOCK // PART), jobs, staged), plan, strict=True)]
 
-    def own_of(slot, up_sum, down_sum):
-        plan = ((RING0[slot], up_sum, down_own), (RING1[slot], down_sum, up_own))
-        jobs = []
-        for far, whole, part in plan:
+    def own_of(slot, *rings):
+        plan, jobs = [], []
+        for ring, whole in rings:
+            far, part = (RING0[slot], down_own) if ring == 0 else (RING1[slot], up_own)
             shape = low if far else ((BLOCK, WIDTH), jnp.float32)
             jobs.append((0, lambda i, far=far: far, [(whole, single), (part, of_slot(slot))], single, *shape))
+            plan.append(far)
         values = code((1, BLOCK // PART), jobs)
-        return [in_hbm(hop(v, "second", far)) if far else v for v, (far, *_) in zip(values, plan, strict=True)]
-
-    early, late = sums_of(0), sums_of(1)
-    two, three = own_of(0, *early)
-    one, own = own_of(1, *late)
+        return [in_vmem(hop(v, "second", far)) if far else v for v, far in zip(values, plan, strict=True)]
+
+    early_up, early_down = sums_of(0)
+    late_up, late_down = sums_of(1)
+    two, three = own_of(0, (0, early_up), (1, early_down))
+    (one,) = own_of(1, (0, late_up))
+    (own,) = own_of(1, (1, late_down))
     return [own, two, one, three]
 
 
@@ -198,7 +205,7 @@
     return pl.pallas_call(
         decode_kernel,
         out_shape=(
-            jax.ShapeDtypeStruct((BLOCK, WIDTH), jnp.float32),
+            pltpu.HBM((BLOCK, WIDTH), jnp.float32),
             pltpu.HBM((copies, 8, 128), jnp.float32),
         ),
         grid_spec=pltpu.PrefetchScalarGridSpec(
@@ -218,7 +225,7 @@
             scratch_shapes=[pltpu.VMEM((8, 128), jnp.float32)],
         ),
         compiler_params=pltpu.CompilerParams(vmem_limit_bytes=VMEM_BYTES),
-        cost_estimate=pl.CostEstimate(flops=6 * 512 * WIDTH * TILE, bytes_accessed=512 * WIDTH * 14, transcendentals=0),
+        cost_estimate=pl.CostEstimate(flops=0, bytes_accessed=0, transcendentals=0),
     )(place, table, sign, hmat, *terms, index)
 
 
@@ -269,14 +276,14 @@
         in_specs=[pl.BlockSpec(square.shape, lambda j: (0, 0, 0))] + [rows] * 4,
         out_specs=jax.tree.map(lambda _: rows, out_shape),
         compiler_params=pltpu.CompilerParams(vmem_limit_bytes=VMEM_BYTES),
-        cost_estimate=pl.CostEstimate(flops=20 * BLOCK * WIDTH, bytes_accessed=24 * BLOCK * WIDTH, transcendentals=BLOCK * WIDTH),
+        cost_estimate=pl.CostEstimate(flops=0, bytes_accessed=0, transcendentals=0),
     )(square, plain, master, mean, var)
 
 
 def stage_kernel(*refs):
-    for source, target in zip(refs[:3], refs[3:6], strict=True):
+    for source, target in zip(refs[:2], refs[2:4], strict=True):
         target[...] = source[...]
-    refs[6][...] = jnp.zeros_like(refs[6])
+    refs[4][...] = jnp.zeros_like(refs[4])
 
 
 def stage(*state):
@@ -285,10 +292,10 @@
         stage_kernel,
         out_shape=[pltpu.VMEM(v.shape, v.dtype) for v in state] + [jax.ShapeDtypeStruct((8, 128), jnp.float32)],
         grid=(BLOCK // STEP,),
-        in_specs=[rows] * 3,
-        out_specs=[rows] * 3 + [pl.BlockSpec((8, 128), lambda j: (0, 0))],
-        compiler_params=pltpu.CompilerParams(vmem_limit_bytes=VMEM_BYTES),
-        cost_estimate=pl.CostEstimate(flops=0, bytes_accessed=24 * BLOCK * WIDTH, transcendentals=0),
+        in_specs=[rows] * 2,
+        out_specs=[rows] * 2 + [pl.BlockSpec((8, 128), lambda j: (0, 0))],
+        compiler_params=pltpu.CompilerParams(vmem_limit_bytes=VMEM_BYTES),
+        cost_estimate=pl.CostEstimate(flops=0, bytes_accessed=0, transcendentals=0),
     )(*state)
 
 
@@ -310,10 +317,10 @@
     tile_ref[...] = jnp.zeros_like(tile_ref)
     chip, core = at_ref[0] // 2, at_ref[0] % 2
     copies = []
-    for j, (step, swapped) in enumerate(places):
+    for j, (step, swapped, row) in enumerate(places):
         source = (chip + SIDE - step + 2 * step * core) % SIDE
         column = pl.multiple_of((source * 2 + (1 - core if swapped else core)) * WIDTH, WIDTH)
-        target = out_ref.at[:, pl.ds(column, WIDTH)]
+        target = out_ref.at[pl.ds(row, refs[j].shape[0]), pl.ds(column, WIDTH)]
         copies.append(pltpu.make_async_copy(refs[j], target, sems.at[j]))
     for copy in copies:
         copy.start()
@@ -323,17 +330,16 @@
 
 def fill(at, places, blocks, weights=None):
     anywhere = pl.BlockSpec(memory_space=pl.ANY)
-    whole = pl.BlockSpec(blocks[0].shape, lambda: (0, 0))
     given = [] if weights is None else [weights]
     return pl.pallas_call(
         functools.partial(fill_kernel, places),
         out_shape=(pltpu.HBM((BLOCK, D), jnp.bfloat16), jax.ShapeDtypeStruct((8, 128), jnp.float32)),
-        in_specs=[pl.BlockSpec(memory_space=pltpu.SMEM)] + [whole] * len(blocks) + [anywhere] * len(given),
+        in_specs=[pl.BlockSpec(memory_space=pltpu.SMEM)] + [pl.BlockSpec(v.shape, lambda: (0, 0)) for v in blocks] + [anywhere] * len(given),
         out_specs=(anywhere, pl.BlockSpec((8, 128), lambda: (0, 0))),
         scratch_shapes=[pltpu.SemaphoreType.DMA((len(blocks),))],
         input_output_aliases={len(blocks) + 1: 0} if given else {},
         compiler_params=pltpu.CompilerParams(vmem_limit_bytes=VMEM_BYTES),
-        cost_estimate=pl.CostEstimate(flops=0, bytes_accessed=4 * len(blocks) * blocks[0].size, transcendentals=0),
+        cost_estimate=pl.CostEstimate(flops=0, bytes_accessed=0, transcendentals=0),
     )(at, *blocks, *given)
 
 
@@ -354,12 +360,12 @@
     one = after(one, state)
     two = along_y(one)
     one_swapped = to_other_core(one)
-    other_swapped = to_other_core(one_other)
-    near = ((0, False), (0, True), (1, False), (1, True), (-1, True), (-1, False))
-    weights, filled = fill(at, near, (low, other, one, one_other, one_swapped, other_swapped))
+    halves = [to_other_core(one_other[row : row + PART]) for row in (0, PART)]
+    near = ((0, False, 0), (0, True, 0), (1, False, 0), (1, True, 0), (-1, True, 0), (-1, False, 0), (-1, False, PART))
+    weights, filled = fill(at, near, (low, other, one, one_other, one_swapped, *halves))
     two = after(two, filled)
     two_swapped = to_other_core(two)
-    return fill(at, ((2, False), (2, True)), (two, two_swapped), weights)[0]
+    return fill(at, ((2, False, 0), (2, True, 0)), (two, two_swapped), weights)[0]
 
 
 def on_device(grad_shards, hadamard_signs, scale_index, scale_table, master, mean_moment, var_moment):
@@ -368,13 +374,14 @@
     place = (lax.axis_index("dp") * 2 + (lax.axis_index("fsdp") & 1)).reshape(1)
     sign = in_hbm(hadamard_signs.reshape(1, WIDTH))
     hmat = in_hbm(jnp.asarray(hadamard(TILE)))
-    *state, staged = stage(master, mean_moment, var_moment)
+    *state, staged = stage(master, mean_moment)
+    state.append(var_moment)
     terms = reduce_scatter(place, scale_table, sign, grad, scale_index, hmat, staged)
     plain, square = decode(place, scale_table, sign, terms, scale_index, hmat, lax.axis_size("fsdp"))
     square = total_squares(square)
-    low = adamw(weights_kernel, jax.ShapeDtypeStruct((BLOCK, WIDTH), jnp.bfloat16), square, plain, *state)
-    new_state = adamw(state_kernel, (jax.ShapeDtypeStruct(master.shape, jnp.float32),) * 3, square, plain, *state)
-    return *new_state, gather(low, new_state[0])
+    low = adamw(weights_kernel, jax.ShapeDtypeStruct((BLOCK, WIDTH), jnp.bfloat16), square, in_hbm(plain), *state)
+    new_state = adamw(state_kernel, (jax.ShapeDtypeStruct(master.shape, jnp.float32),) * 3, square, in_hbm(plain), *state)
+    return *new_state, gather(low, in_hbm(new_state[0]))
 
 
 def solution(mesh):

time: 163 us -> 146 us (0.90)
  blocking collectives: 31.9 us -> 22.3 us
  local copies, waits for them, and re-layouts: 8.67 us -> 1.33 us
  waiting for transfers between devices: 60.2 us -> 55.4 us
  Pallas kernels: 34.1 us -> 38.9 us
    all_to_all x1, blocking collectives: 19.4 us -> 10.3 us  [total_squares(): square = jnp.sum(lax.all_to_all(square, 'fsdp', 0, 0), axis=0)]
    unnamed x16 -> x0, local copies, waits for them, and re-layouts: 7.38 us -> none
    ppermute x3, waiting for transfers between devices: 17.3 us -> 11.7 us  [along_y(): return lax.ppermute(value, 'fsdp', pairs)]
    pallas_call x2, Pallas kernels: 4.71 us -> 8.61 us  [adamw(): pl.pallas_call(kernel, out_shape=out_shape, grid=(BLOCK // STEP,), in_spe...]
    pallas_call x6 -> x7, Pallas kernels: 19 us -> 20.6 us  [encode(): pl.pallas_call(functools.partial(encode_kernel, [len(job[2]) for job in j...]
    ppermute x4 -> x5, starting transfers between devices: 8.58 us -> 8.83 us  [to_other_core(): return lax.ppermute(value, 'fsdp', [(i, i ^ 1) for i in range(8)])]
    ppermute x4 -> x5, waiting for transfers between devices: 4.85 us -> 4.75 us  [to_other_core(): return lax.ppermute(value, 'fsdp', [(i, i ^ 1) for i in range(8)])]
  transfers between devices with their start and end apart: 18 -> 19, of which waited for: 13 -> 14; matrix products, arithmetic and copies ran while one was open for 0% -> 0% of each run, Pallas kernels for 14% -> 18%
where the time goes in v4:
time: 146 us; the launch traced here: 145 us
  waiting for transfers between devices  55.4 us (38%)
  Pallas kernels  38.9 us (27%)
  starting transfers between devices  26.8 us (18%)
  blocking collectives  22.3 us (15%)
    ppermute x11, waiting for transfers between devices, hop(): return lax.ppermute(value, ('dp', 'fsdp'), pairs)  39 us
    pallas_call x7, Pallas kernels, encode(): pl.pallas_call(functools.partial(encode_kernel, [len(job[2]) for job in j...  20.6 us
    ppermute x11, starting transfers between devices, hop(): return lax.ppermute(value, ('dp', 'fsdp'), pairs)  16.2 us
    all_to_all x1, blocking collectives, total_squares(): return lax.all_to_all(copies, 'dp', 0, 0)  11.9 us
    ppermute x3, waiting for transfers between devices, along_y(): return lax.ppermute(value, 'fsdp', pairs)  11.7 us
    all_to_all x1, blocking collectives, total_squares(): square = jnp.sum(lax.all_to_all(square, 'fsdp', 0, 0), axis=0)  10.3 us
    ppermute x5, starting transfers between devices, to_other_core(): return lax.ppermute(value, 'fsdp', [(i, i ^ 1) for i in range(8)])  8.83 us
    pallas_call x2, Pallas kernels, adamw(): pl.pallas_call(kernel, out_shape=out_shape, grid=(BLOCK // STEP,), in_spe...  8.61 us
  transfers between devices with their start and end apart: 19, of which 14 were waited for; matrix products, arithmetic and copies ran while one was open for 0% of the time, Pallas kernels for 18%

profile of v4, /device:TPU:1, one launch (start us, length us, event | category | flops | bytes accessed | tf_op | source)
XLA Modules:
  0.0 145.5 jit_solution(11458584320207905596)
XLA Ops:
  1.9 4.1 %shard_map.112 = (bf16[2,512,768]{2,1,0:T(8,128)(2,1)S(1)}, bf16[2,512,768]{2,1,0:T(8,128)(2,1)S(1)}) custom-call(s32[1]{0:T(128)} %bitcast.place_ref, f32[16]{0:T(128)} %table_ref.15, s32[1,768]{1,0:T(1,128)} %reshape.18.sign_ref, bf16[256,256]{1,0:T(8,128)(2,1)} %constant.17.clone.hmat_ref, bf16[8192,768]{1,0:T(8,128)(2,1)} %bitcast.3, ...), custom_call_target="tpu_custom_call" | custom-call | tf_op jit(solution)/shard_map/pallas_call | solution.py:121
  6.1 2.5 %collective-permute-start = (bf16[2,512,768]{2,1,0:T(8,128)(2,1)S(1)}, bf16[2,512,768]{2,1,0:T(8,128)(2,1)S(1)}, u32[]{:S(2)}, u32[]{:S(2)}) collective-permute-start(bf16[2,512,768]{2,1,0:T(8,128)(2,1)S(1)} %get-tuple-element.26), channel_id=1, source_target_pairs={{0,32},{1,9},{2,34},{3,11},{4,36},{5,13},{6,38},{7,15},{8,40},{9,1... | collective-permute-start | bytes 4718600 | tf_op jit(solution)/shard_map/ppermute | solution.py:45
  8.6 2.2 %collective-permute-start.1 = (bf16[2,512,768]{2,1,0:T(8,128)(2,1)S(1)}, bf16[2,512,768]{2,1,0:T(8,128)(2,1)S(1)}, u32[]{:S(2)}, u32[]{:S(2)}) collective-permute-start(bf16[2,512,768]{2,1,0:T(8,128)(2,1)S(1)} %get-tuple-element.27), channel_id=1, source_target_pairs={{0,96},{1,25},{2,98},{3,27},{4,100},{5,29},{6,102},{7,31},{8,104},... | collective-permute-start | bytes 4718600 | tf_op jit(solution)/shard_map/ppermute | solution.py:45
  10.8 4.1 %shard_map.114 = (bf16[2,512,768]{2,1,0:T(8,128)(2,1)S(1)}, bf16[2,512,768]{2,1,0:T(8,128)(2,1)S(1)}) custom-call(s32[1]{0:T(128)} %bitcast.place_ref, f32[16]{0:T(128)} %table_ref.15, s32[1,768]{1,0:T(1,128)} %reshape.18.sign_ref, bf16[256,256]{1,0:T(8,128)(2,1)} %constant.17.clone.hmat_ref, bf16[8192,768]{1,0:T(8,128)(2,1)} %bitcast.5, ...), custom_call_target="tpu_custom_call" | custom-call | tf_op jit(solution)/shard_map/pallas_call | solution.py:121
  15.0 2.7 %collective-permute-start.5 = (bf16[2,512,768]{2,1,0:T(8,128)(2,1)S(1)}, bf16[2,512,768]{2,1,0:T(8,128)(2,1)S(1)}, u32[]{:S(2)}, u32[]{:S(2)}) collective-permute-start(bf16[2,512,768]{2,1,0:T(8,128)(2,1)S(1)} %get-tuple-element.31), channel_id=1, source_target_pairs={{0,96},{1,25},{2,98},{3,27},{4,100},{5,29},{6,102},{7,31},{8,104},... | collective-permute-start | bytes 4718600 | tf_op jit(solution)/shard_map/ppermute | solution.py:45
  17.7 2.6 %shard_map.111 = (f32[512,768]{1,0:T(8,128)S(1)}, f32[512,768]{1,0:T(8,128)S(1)}, f32[8,128]{1,0:T(8,128)S(1)}) custom-call(f32[512,768]{1,0:T(8,128)} %refs_0_.1, f32[512,768]{1,0:T(8,128)} %refs_1_.6), custom_call_target="tpu_custom_call" | custom-call | tf_op jit(solution)/shard_map/pallas_call | solution.py:291
  20.3 8.5 %collective-permute-done.refs_3_ = bf16[2,512,768]{2,1,0:T(8,128)(2,1)S(1)} collective-permute-done((bf16[2,512,768]{2,1,0:T(8,128)(2,1)S(1)}, bf16[2,512,768]{2,1,0:T(8,128)(2,1)S(1)}, u32[]{:S(2)}, u32[]{:S(2)}) %collective-permute-start) | collective-permute-done | bytes 1572896 | tf_op jit(solution)/shard_map/ppermute | solution.py:45
  28.8 2.6 %shard_map.116 = (bf16[512,768]{1,0:T(8,128)(2,1)S(1)}, bf16[512,768]{1,0:T(8,128)(2,1)S(1)}) custom-call(s32[1]{0:T(128)} %bitcast.place_ref, f32[16]{0:T(128)} %table_ref.15, s32[1,768]{1,0:T(1,128)} %reshape.18.sign_ref, bf16[256,256]{1,0:T(8,128)(2,1)} %constant.17.clone.hmat_ref, f32[8,128]{1,0:T(8,128)S(1)} %get-tuple-element.25.refs_0_, ...), custom_call_target="tpu_custom_call" | custom-call | tf_op jit(solution)/shard_map/pallas_call | solution.py:121
  34.3 2.6 %shard_map.113 = (bf16[512,768]{1,0:T(8,128)(2,1)S(1)}, bf16[512,768]{1,0:T(8,128)(2,1)S(1)}) custom-call(s32[1]{0:T(128)} %bitcast.place_ref, f32[16]{0:T(128)} %table_ref.15, s32[1,768]{1,0:T(1,128)} %reshape.18.sign_ref, bf16[256,256]{1,0:T(8,128)(2,1)} %constant.17.clone.hmat_ref, f32[8,128]{1,0:T(8,128)S(1)} %get-tuple-element.25.refs_0_, ...), custom_call_target="tpu_custom_call" | custom-call | tf_op jit(solution)/shard_map/pallas_call | solution.py:121
  36.9 8.7 %collective-permute-done.3.refs_3_.refs_7_ = bf16[2,512,768]{2,1,0:T(8,128)(2,1)S(1)} collective-permute-done((bf16[2,512,768]{2,1,0:T(8,128)(2,1)S(1)}, bf16[2,512,768]{2,1,0:T(8,128)(2,1)S(1)}, u32[]{:S(2)}, u32[]{:S(2)}) %collective-permute-start.3) | collective-permute-done | bytes 1572896 | tf_op jit(solution)/shard_map/ppermute | solution.py:45
  47.1 7.0 %collective-permute-done.4.refs_2_ = bf16[512,768]{1,0:T(8,128)(2,1)S(1)} collective-permute-done((bf16[512,768]{1,0:T(8,128)(2,1)S(1)}, bf16[512,768]{1,0:T(8,128)(2,1)S(1)}, u32[]{:S(2)}, u32[]{:S(2)}) %collective-permute-start.4) | collective-permute-done | bytes 786464 | tf_op jit(solution)/shard_map/ppermute | solution.py:45
  54.1 2.8 %shard_map.117 = (bf16[512,768]{1,0:T(8,128)(2,1)S(1)}, bf16[512,768]{1,0:T(8,128)(2,1)S(1)}) custom-call(s32[1]{0:T(128)} %bitcast.place_ref, f32[16]{0:T(128)} %table_ref.15, s32[1,768]{1,0:T(1,128)} %reshape.18.sign_ref, bf16[256,256]{1,0:T(8,128)(2,1)} %constant.17.clone.hmat_ref, bf16[8192,768]{1,0:T(8,128)(2,1)} %bitcast.11, s32[3,8192]{1,0:T(4,128)} %index_ref.1, ...), custom_call_target="tpu_custom_call" | custom-call | tf_op jit(solution)/shard_map/pallas_call | solution.py:121
  56.9 2.5 %collective-permute-start.7 = (bf16[512,768]{1,0:T(8,128)(2,1)S(1)}, bf16[512,768]{1,0:T(8,128)(2,1)S(1)}, u32[]{:S(2)}, u32[]{:S(2)}) collective-permute-start(bf16[512,768]{1,0:T(8,128)(2,1)S(1)} %get-tuple-element.33), channel_id=1, source_target_pairs={{0,16},{1,65},{2,18},{3,67},{4,20},{5,69},{6,22},{7,71},{8,24},{9,... | collective-permute-start | bytes 2359304 | tf_op jit(solution)/shard_map/ppermute | solution.py:45
  60.3 2.2 %collective-permute-done.8.refs_2_ = bf16[512,768]{1,0:T(8,128)(2,1)S(1)} collective-permute-done((bf16[512,768]{1,0:T(8,128)(2,1)S(1)}, bf16[512,768]{1,0:T(8,128)(2,1)S(1)}, u32[]{:S(2)}, u32[]{:S(2)}) %collective-permute-start.8) | collective-permute-done | bytes 786464 | tf_op jit(solution)/shard_map/ppermute | solution.py:45
  62.5 2.2 %shard_map.118 = bf16[512,768]{1,0:T(8,128)(2,1)S(1)} custom-call(s32[1]{0:T(128)} %bitcast.place_ref, f32[16]{0:T(128)} %table_ref.15, s32[1,768]{1,0:T(1,128)} %reshape.18.sign_ref, bf16[256,256]{1,0:T(8,128)(2,1)} %constant.17.clone.hmat_ref, bf16[8192,768]{1,0:T(8,128)(2,1)} %bitcast.13, s32[3,8192]{1,0:T(4,128)} %index_ref.1, ...), custom_call_target="tpu_custom_call" | custom-call | tf_op jit(solution)/shard_map/pallas_call | solution.py:121
  65.7 2.1 %shard_map.115.own_ref = f32[512,768]{1,0:T(8,128)S(1)} custom-call(s32[1]{0:T(128)} %bitcast.place_ref, f32[16]{0:T(128)} %table_ref.15, s32[1,768]{1,0:T(1,128)} %reshape.18.sign_ref, bf16[256,256]{1,0:T(8,128)(2,1)} %constant.17.clone.hmat_ref, bf16[8192,768]{1,0:T(8,128)(2,1)} %bitcast.14, s32[3,8192]{1,0:T(4,128)} %index_ref.1, ...), custom_call_target="tpu_custom_call" | custom-call | tf_op jit(solution)/shard_map/pallas_call | solution.py:121
  67.8 4.2 %collective-permute-done.7.two_ref = bf16[512,768]{1,0:T(8,128)(2,1)S(1)} collective-permute-done((bf16[512,768]{1,0:T(8,128)(2,1)S(1)}, bf16[512,768]{1,0:T(8,128)(2,1)S(1)}, u32[]{:S(2)}, u32[]{:S(2)}) %collective-permute-start.7) | collective-permute-done | bytes 786464 | tf_op jit(solution)/shard_map/ppermute | solution.py:45
  72.0 7.7 %collective-permute-done.10.three_ref = bf16[512,768]{1,0:T(8,128)(2,1)S(1)} collective-permute-done((bf16[512,768]{1,0:T(8,128)(2,1)S(1)}, bf16[512,768]{1,0:T(8,128)(2,1)S(1)}, u32[]{:S(2)}, u32[]{:S(2)}) %collective-permute-start.10) | collective-permute-done | bytes 786464 | tf_op jit(solution)/shard_map/ppermute | solution.py:45
  80.4 3.1 %shard_map.119 = (f32[512,768]{1,0:T(8,128)}, f32[8,8,128]{2,1,0:T(8,128)}) custom-call(s32[1]{0:T(128)} %bitcast.place_ref, f32[16]{0:T(128)} %table_ref.15, s32[1,768]{1,0:T(1,128)} %reshape.18.sign_ref, bf16[256,256]{1,0:T(8,128)(2,1)} %constant.17.clone.hmat_ref, f32[512,768]{1,0:T(8,128)S(1)} %shard_map.115.own_ref, ...), custom_call_target="tpu_custom_call" | custom-call | tf_op jit(solution)/shard_map/pallas_call | solution.py:205
  83.5 10.3 %all_to_all.10 = f32[8,8,128]{2,1,0:T(8,128)S(1)} all-to-all(f32[8,8,128]{2,1,0:T(8,128)} %get-tuple-element.36), channel_id=1, replica_groups=mesh['dp'=16,'fsdp'=8] {'fsdp'}, dimensions={0} | all-to-all | bytes 65536 | tf_op jit(solution)/shard_map/all_to_all | solution.py:233
  93.9 11.9 %all_to_all.11.square_ref = f32[16,8,128]{2,1,0:T(8,128)S(1)} all-to-all(f32[16,8,128]{2,1,0:T(8,128)S(1)} %broadcast_in_dim.3), channel_id=1, replica_groups=mesh['dp'=16,'fsdp'=8] {'dp'}, dimensions={0} | all-to-all | bytes 131072 | tf_op jit(solution)/shard_map/all_to_all | solution.py:235
  105.8 3.7 %shard_map.121.refs_0_ = bf16[512,768]{1,0:T(8,128)(2,1)S(1)} custom-call(f32[16,8,128]{2,1,0:T(8,128)S(1)} %all_to_all.11.square_ref, f32[512,768]{1,0:T(8,128)} %get-tuple-element.37.plain_ref, f32[512,768]{1,0:T(8,128)S(1)} %get-tuple-element.38.master_ref, f32[512,768]{1,0:T(8,128)S(1)} %get-tuple-element.39.mean_ref, f32[512,768]{1,0:T(8,128)} %var_ref.3), custom_call_target="tpu_custom_call" | custom-call | tf_op jit(solution)/shard_map/pallas_call | solution.py:272
  109.5 2.2 %collective-permute-start.13 = (bf16[512,768]{1,0:T(8,128)(2,1)S(1)}, bf16[512,768]{1,0:T(8,128)(2,1)S(1)}, u32[]{:S(2)}, u32[]{:S(2)}) collective-permute-start(bf16[512,768]{1,0:T(8,128)(2,1)S(1)} %shard_map.121.refs_0_), channel_id=1, source_target_pairs={{0,1},{1,0},{2,3},{3,2},{4,5},{5,4},{6,7},{7,6},{8,9},{9,8},{10,11... | collective-permute-start | bytes 2359304 | tf_op jit(solution)/shard_map/ppermute | solution.py:352
  114.5 4.9 %shard_map.120 = (f32[512,768]{1,0:T(8,128)}, f32[512,768]{1,0:T(8,128)}, f32[512,768]{1,0:T(8,128)}) custom-call(f32[16,8,128]{2,1,0:T(8,128)S(1)} %all_to_all.11.square_ref, f32[512,768]{1,0:T(8,128)} %get-tuple-element.37.plain_ref, f32[512,768]{1,0:T(8,128)S(1)} %get-tuple-element.38.master_ref, f32[512,768]{1,0:T(8,128)S(1)} %get-tuple-element.39.mean_ref, ...), custom_call_target="tpu_custom_call" | custom-call | tf_op jit(solution)/shard_map/pallas_call | solution.py:272
  119.5 3.4 %collective-permute-done.11.__0_ = bf16[512,768]{1,0:T(8,128)(2,1)S(1)} collective-permute-done((bf16[512,768]{1,0:T(8,128)(2,1)S(1)}, bf16[512,768]{1,0:T(8,128)(2,1)S(1)}, u32[]{:S(2)}, u32[]{:S(2)}) %collective-permute-start.11) | collective-permute-done | bytes 786464 | tf_op jit(solution)/shard_map/ppermute | solution.py:348
  122.8 2.1 %collective-permute-start.15 = (bf16[512,768]{1,0:T(8,128)(2,1)S(1)}, bf16[512,768]{1,0:T(8,128)(2,1)S(1)}, u32[]{:S(2)}, u32[]{:S(2)}) collective-permute-start(bf16[512,768]{1,0:T(8,128)(2,1)S(1)} %shard_map.122.refs_2_), channel_id=1, source_target_pairs={{0,1},{1,0},{2,3},{3,2},{4,5},{5,4},{6,7},{7,6},{8,9},{9,8},{10,11... | collective-permute-start | bytes 2359304 | tf_op jit(solution)/shard_map/ppermute | solution.py:352
  125.0 6.3 %collective-permute-done.14.refs_3_ = bf16[512,768]{1,0:T(8,128)(2,1)S(1)} collective-permute-done((bf16[512,768]{1,0:T(8,128)(2,1)S(1)}, bf16[512,768]{1,0:T(8,128)(2,1)S(1)}, u32[]{:S(2)}, u32[]{:S(2)}) %collective-permute-start.14) | collective-permute-done | bytes 786464 | tf_op jit(solution)/shard_map/ppermute | solution.py:348
  131.3 2.2 %collective-permute-start.17 = (bf16[256,768]{1,0:T(8,128)(2,1)S(1)}, bf16[256,768]{1,0:T(8,128)(2,1)S(1)}, u32[]{:S(2)}, u32[]{:S(2)}) collective-permute-start(bf16[256,768]{1,0:T(8,128)(2,1)S(1)} %get-tuple-element.46), channel_id=1, source_target_pairs={{0,1},{1,0},{2,3},{3,2},{4,5},{5,4},{6,7},{7,6},{8,9},{9,8},{10,11... | collective-permute-start | bytes 1179656 | tf_op jit(solution)/shard_map/ppermute | solution.py:352
  135.5 2.2 %shard_map.123 = (bf16[512,6144]{1,0:T(8,128)(2,1)}, f32[8,128]{1,0:T(8,128)S(1)}) custom-call(s32[1]{0:T(128)} %bitcast.2.at_ref, bf16[512,768]{1,0:T(8,128)(2,1)S(1)} %shard_map.121.refs_0_, bf16[512,768]{1,0:T(8,128)(2,1)S(1)} %collective-permute-done.13.refs_1_, bf16[512,768]{1,0:T(8,128)(2,1)S(1)} %shard_map.122.refs_2_, ...), custom_call_target="tpu_custom_call" | custom-call | tf_op jit(solution)/shard_map/pallas_call | solution.py:334
  137.7 2.0 %collective-permute-done.12.__0_ = bf16[512,768]{1,0:T(8,128)(2,1)S(1)} collective-permute-done((bf16[512,768]{1,0:T(8,128)(2,1)S(1)}, bf16[512,768]{1,0:T(8,128)(2,1)S(1)}, u32[]{:S(2)}, u32[]{:S(2)}) %collective-permute-start.12) | collective-permute-done | bytes 786464 | tf_op jit(solution)/shard_map/ppermute | solution.py:348
  139.7 2.1 %collective-permute-start.18 = (bf16[512,768]{1,0:T(8,128)(2,1)S(1)}, bf16[512,768]{1,0:T(8,128)(2,1)S(1)}, u32[]{:S(2)}, u32[]{:S(2)}) collective-permute-start(bf16[512,768]{1,0:T(8,128)(2,1)S(1)} %shard_map.124.refs_0_), channel_id=1, source_target_pairs={{0,1},{1,0},{2,3},{3,2},{4,5},{5,4},{6,7},{7,6},{8,9},{9,8},{10,11... | collective-permute-start | bytes 2359304 | tf_op jit(solution)/shard_map/ppermute | solution.py:352
  141.8 1.9 %collective-permute-done.18.refs_1_ = bf16[512,768]{1,0:T(8,128)(2,1)S(1)} collective-permute-done((bf16[512,768]{1,0:T(8,128)(2,1)S(1)}, bf16[512,768]{1,0:T(8,128)(2,1)S(1)}, u32[]{:S(2)}, u32[]{:S(2)}) %collective-permute-start.18) | collective-permute-done | bytes 786464 | tf_op jit(solution)/shard_map/ppermute | solution.py:352
  (27 shorter events, 14.7 us)
Async XLA Ops:
  6.1 22.8 %collective-permute-start = (bf16[2,512,768]{2,1,0:T(8,128)(2,1)S(1)}, bf16[2,512,768]{2,1,0:T(8,128)(2,1)S(1)}, u32[]{:S(2)}, u32[]{:S(2)}) collective-permute-start(bf16[2,512,768]{2,1,0:T(8,128)(2,1)S(1)} %get-tuple-element.26), channel_id=1, source_target_pairs={{0,32},{1,9},{2,34},{3,11},{4,36},{5,13},{6,38},{7,15},{8,40},{9,1... | collective-permute-start | bytes 4718600 | tf_op jit(solution)/shard_map/ppermute | solution.py:45
  8.6 20.2 %collective-permute-start.1 = (bf16[2,512,768]{2,1,0:T(8,128)(2,1)S(1)}, bf16[2,512,768]{2,1,0:T(8,128)(2,1)S(1)}, u32[]{:S(2)}, u32[]{:S(2)}) collective-permute-start(bf16[2,512,768]{2,1,0:T(8,128)(2,1)S(1)} %get-tuple-element.27), channel_id=1, source_target_pairs={{0,96},{1,25},{2,98},{3,27},{4,100},{5,29},{6,102},{7,31},{8,104},... | collective-permute-start | bytes 4718600 | tf_op jit(solution)/shard_map/ppermute | solution.py:45
  14.9 30.7 %collective-permute-start.3 = (bf16[2,512,768]{2,1,0:T(8,128)(2,1)S(1)}, bf16[2,512,768]{2,1,0:T(8,128)(2,1)S(1)}, u32[]{:S(2)}, u32[]{:S(2)}) collective-permute-start(bf16[2,512,768]{2,1,0:T(8,128)(2,1)S(1)} %get-tuple-element.29), channel_id=1, source_target_pairs={{0,32},{1,9},{2,34},{3,11},{4,36},{5,13},{6,38},{7,15},{8,40},{9,1... | collective-permute-start | bytes 4718600 | tf_op jit(solution)/shard_map/ppermute | solution.py:45
  15.0 32.1 %collective-permute-start.5 = (bf16[2,512,768]{2,1,0:T(8,128)(2,1)S(1)}, bf16[2,512,768]{2,1,0:T(8,128)(2,1)S(1)}, u32[]{:S(2)}, u32[]{:S(2)}) collective-permute-start(bf16[2,512,768]{2,1,0:T(8,128)(2,1)S(1)} %get-tuple-element.31), channel_id=1, source_target_pairs={{0,96},{1,25},{2,98},{3,27},{4,100},{5,29},{6,102},{7,31},{8,104},... | collective-permute-start | bytes 4718600 | tf_op jit(solution)/shard_map/ppermute | solution.py:45
  31.5 22.6 %collective-permute-start.4 = (bf16[512,768]{1,0:T(8,128)(2,1)S(1)}, bf16[512,768]{1,0:T(8,128)(2,1)S(1)}, u32[]{:S(2)}, u32[]{:S(2)}) collective-permute-start(bf16[512,768]{1,0:T(8,128)(2,1)S(1)} %get-tuple-element.30), channel_id=1, source_target_pairs={{0,32},{1,9},{2,34},{3,11},{4,36},{5,13},{6,38},{7,15},{8,40},{9,1... | collective-permute-start | bytes 2359304 | tf_op jit(solution)/shard_map/ppermute | solution.py:45
  32.4 21.7 %collective-permute-start.6 = (bf16[512,768]{1,0:T(8,128)(2,1)S(1)}, bf16[512,768]{1,0:T(8,128)(2,1)S(1)}, u32[]{:S(2)}, u32[]{:S(2)}) collective-permute-start(bf16[512,768]{1,0:T(8,128)(2,1)S(1)} %get-tuple-element.32), channel_id=1, source_target_pairs={{0,96},{1,25},{2,98},{3,27},{4,100},{5,29},{6,102},{7,31},{8,104},... | collective-permute-start | bytes 2359304 | tf_op jit(solution)/shard_map/ppermute | solution.py:45
  36.8 25.7 %collective-permute-start.8 = (bf16[512,768]{1,0:T(8,128)(2,1)S(1)}, bf16[512,768]{1,0:T(8,128)(2,1)S(1)}, u32[]{:S(2)}, u32[]{:S(2)}) collective-permute-start(bf16[512,768]{1,0:T(8,128)(2,1)S(1)} %get-tuple-element.34), channel_id=1, source_target_pairs={{0,32},{1,9},{2,34},{3,11},{4,36},{5,13},{6,38},{7,15},{8,40},{9,1... | collective-permute-start | bytes 2359304 | tf_op jit(solution)/shard_map/ppermute | solution.py:45
  45.7 20.0 %collective-permute-start.2 = (bf16[512,768]{1,0:T(8,128)(2,1)S(1)}, bf16[512,768]{1,0:T(8,128)(2,1)S(1)}, u32[]{:S(2)}, u32[]{:S(2)}) collective-permute-start(bf16[512,768]{1,0:T(8,128)(2,1)S(1)} %get-tuple-element.28), channel_id=1, source_target_pairs={{0,96},{1,25},{2,98},{3,27},{4,100},{5,29},{6,102},{7,31},{8,104},... | collective-permute-start | bytes 2359304 | tf_op jit(solution)/shard_map/ppermute | solution.py:45
  56.9 15.1 %collective-permute-start.7 = (bf16[512,768]{1,0:T(8,128)(2,1)S(1)}, bf16[512,768]{1,0:T(8,128)(2,1)S(1)}, u32[]{:S(2)}, u32[]{:S(2)}) collective-permute-start(bf16[512,768]{1,0:T(8,128)(2,1)S(1)} %get-tuple-element.33), channel_id=1, source_target_pairs={{0,16},{1,65},{2,18},{3,67},{4,20},{5,69},{6,22},{7,71},{8,24},{9,... | collective-permute-start | bytes 2359304 | tf_op jit(solution)/shard_map/ppermute | solution.py:45
  59.5 20.3 %collective-permute-start.10 = (bf16[512,768]{1,0:T(8,128)(2,1)S(1)}, bf16[512,768]{1,0:T(8,128)(2,1)S(1)}, u32[]{:S(2)}, u32[]{:S(2)}) collective-permute-start(bf16[512,768]{1,0:T(8,128)(2,1)S(1)} %get-tuple-element.35), channel_id=1, source_target_pairs={{0,24},{1,97},{2,26},{3,99},{4,28},{5,101},{6,30},{7,103},{8,0},{9... | collective-permute-start | bytes 2359304 | tf_op jit(solution)/shard_map/ppermute | solution.py:45
  64.7 15.7 %collective-permute-start.9 = (bf16[512,768]{1,0:T(8,128)(2,1)S(1)}, bf16[512,768]{1,0:T(8,128)(2,1)S(1)}, u32[]{:S(2)}, u32[]{:S(2)}) collective-permute-start(bf16[512,768]{1,0:T(8,128)(2,1)S(1)} %shard_map.118), channel_id=1, source_target_pairs={{0,8},{1,33},{2,10},{3,35},{4,12},{5,37},{6,14},{7,39},{8,16},{9,4... | collective-permute-start | bytes 2359304 | tf_op jit(solution)/shard_map/ppermute | solution.py:45
  109.5 4.1 %collective-permute-start.13 = (bf16[512,768]{1,0:T(8,128)(2,1)S(1)}, bf16[512,768]{1,0:T(8,128)(2,1)S(1)}, u32[]{:S(2)}, u32[]{:S(2)}) collective-permute-start(bf16[512,768]{1,0:T(8,128)(2,1)S(1)} %shard_map.121.refs_0_), channel_id=1, source_target_pairs={{0,1},{1,0},{2,3},{3,2},{4,5},{5,4},{6,7},{7,6},{8,9},{9,8},{10,11... | collective-permute-start | bytes 2359304 | tf_op jit(solution)/shard_map/ppermute | solution.py:352
  111.7 11.1 %collective-permute-start.11 = (bf16[512,768]{1,0:T(8,128)(2,1)S(1)}, bf16[512,768]{1,0:T(8,128)(2,1)S(1)}, u32[]{:S(2)}, u32[]{:S(2)}) collective-permute-start(bf16[512,768]{1,0:T(8,128)(2,1)S(1)} %shard_map.121.refs_0_), channel_id=1, source_target_pairs={{0,2},{1,7},{2,4},{3,1},{4,6},{5,3},{6,0},{7,5},{8,10},{9,15},{10,... | collective-permute-start | bytes 2359304 | tf_op jit(solution)/shard_map/ppermute | solution.py:348
  113.6 17.6 %collective-permute-start.14 = (bf16[512,768]{1,0:T(8,128)(2,1)S(1)}, bf16[512,768]{1,0:T(8,128)(2,1)S(1)}, u32[]{:S(2)}, u32[]{:S(2)}) collective-permute-start(bf16[512,768]{1,0:T(8,128)(2,1)S(1)} %collective-permute-done.13.refs_1_), channel_id=1, source_target_pairs={{0,2},{1,7},{2,4},{3,1},{4,6},{5,3},{6,0},{7,5},{8,10},{9,15},{10,... | collective-permute-start | bytes 2359304 | tf_op jit(solution)/shard_map/ppermute | solution.py:348
  122.8 10.8 %collective-permute-start.15 = (bf16[512,768]{1,0:T(8,128)(2,1)S(1)}, bf16[512,768]{1,0:T(8,128)(2,1)S(1)}, u32[]{:S(2)}, u32[]{:S(2)}) collective-permute-start(bf16[512,768]{1,0:T(8,128)(2,1)S(1)} %shard_map.122.refs_2_), channel_id=1, source_target_pairs={{0,1},{1,0},{2,3},{3,2},{4,5},{5,4},{6,7},{7,6},{8,9},{9,8},{10,11... | collective-permute-start | bytes 2359304 | tf_op jit(solution)/shard_map/ppermute | solution.py:352
  125.0 14.7 %collective-permute-start.12 = (bf16[512,768]{1,0:T(8,128)(2,1)S(1)}, bf16[512,768]{1,0:T(8,128)(2,1)S(1)}, u32[]{:S(2)}, u32[]{:S(2)}) collective-permute-start(bf16[512,768]{1,0:T(8,128)(2,1)S(1)} %shard_map.122.refs_2_), channel_id=1, source_target_pairs={{0,2},{1,7},{2,4},{3,1},{4,6},{5,3},{6,0},{7,5},{8,10},{9,15},{10,... | collective-permute-start | bytes 2359304 | tf_op jit(solution)/shard_map/ppermute | solution.py:348
  131.3 3.6 %collective-permute-start.17 = (bf16[256,768]{1,0:T(8,128)(2,1)S(1)}, bf16[256,768]{1,0:T(8,128)(2,1)S(1)}, u32[]{:S(2)}, u32[]{:S(2)}) collective-permute-start(bf16[256,768]{1,0:T(8,128)(2,1)S(1)} %get-tuple-element.46), channel_id=1, source_target_pairs={{0,1},{1,0},{2,3},{3,2},{4,5},{5,4},{6,7},{7,6},{8,9},{9,8},{10,11... | collective-permute-start | bytes 1179656 | tf_op jit(solution)/shard_map/ppermute | solution.py:352
  133.6 1.9 %collective-permute-start.16 = (bf16[256,768]{1,0:T(8,128)(2,1)S(1)}, bf16[256,768]{1,0:T(8,128)(2,1)S(1)}, u32[]{:S(2)}, u32[]{:S(2)}) collective-permute-start(bf16[256,768]{1,0:T(8,128)(2,1)S(1)} %get-tuple-element.47), channel_id=1, source_target_pairs={{0,1},{1,0},{2,3},{3,2},{4,5},{5,4},{6,7},{7,6},{8,9},{9,8},{10,11... | collective-permute-start | bytes 1179656 | tf_op jit(solution)/shard_map/ppermute | solution.py:352
  139.7 4.1 %collective-permute-start.18 = (bf16[512,768]{1,0:T(8,128)(2,1)S(1)}, bf16[512,768]{1,0:T(8,128)(2,1)S(1)}, u32[]{:S(2)}, u32[]{:S(2)}) collective-permute-start(bf16[512,768]{1,0:T(8,128)(2,1)S(1)} %shard_map.124.refs_0_), channel_id=1, source_target_pairs={{0,1},{1,0},{2,3},{3,2},{4,5},{5,4},{6,7},{7,6},{8,9},{9,8},{10,11... | collective-permute-start | bytes 2359304 | tf_op jit(solution)/shard_map/ppermute | solution.py:352

commit v5 on v4

--- a/solution.py
+++ b/solution.py
@@ -73,7 +73,7 @@
         index_refs.append(next(inputs))
         arrived_refs.append([next(inputs) for _ in range(count)])
     steps = row_scales(index_refs, table_ref, True)
-    sign = (2 * sign_ref[...] - 1).astype(jnp.bfloat16)
+    sign = (2 * sign_ref[...] - 1).reshape(1, WIDTH).astype(jnp.bfloat16)
     for tile in range(TILES):
         cols = slice(tile * TILE, (tile + 1) * TILE)
         signed = jnp.concatenate([ref[:, cols] for ref in grad_refs], axis=0) * sign[:, cols]
@@ -99,7 +99,7 @@
 def encode(place, table, sign, grad, index, hmat, grid, jobs, after=None):
     in_specs = [
         pl.BlockSpec(memory_space=pltpu.SMEM),
-        pl.BlockSpec((1, WIDTH), lambda *_: (0, 0)),
+        pl.BlockSpec((WIDTH,), lambda *_: (0,)),
         pl.BlockSpec((TILE, TILE), lambda *_: (0, 0)),
     ]
     operands, out_specs, out_shape = [table, sign, hmat], [], []
@@ -181,7 +181,7 @@
         sum_ref[...] = jnp.zeros_like(sum_ref)
 
     scales = row_scales([index_ref], table_ref, False) * (1.0 / math.sqrt(TILE))
-    sign = (2 * sign_ref[...] - 1).astype(f32)
+    sign = (2 * sign_ref[...] - 1).reshape(1, WIDTH).astype(f32)
     square = sum_ref[...]
     for tile in range(TILES):
         cols = slice(tile * TILE, (tile + 1) * TILE)
@@ -196,7 +196,7 @@
         parts = jnp.sum((plain * plain).reshape(-1, 8, TILE), axis=0)
         square = square + parts[:, :128] + parts[:, 128:]
     sum_ref[...] = square
-    square_ref[...] = jnp.broadcast_to(square, square_ref.shape)
+    square_ref[...] = jnp.broadcast_to(jnp.sum(square, axis=0, keepdims=True), square_ref.shape)
 
 
 def decode(place, table, sign, terms, index, hmat, copies):
@@ -205,22 +205,22 @@
     return pl.pallas_call(
         decode_kernel,
         out_shape=(
-            pltpu.HBM((BLOCK, WIDTH), jnp.float32),
-            pltpu.HBM((copies, 8, 128), jnp.float32),
+            pltpu.VMEM((BLOCK, WIDTH), jnp.float32),
+            pltpu.HBM((copies, 128), jnp.float32),
         ),
         grid_spec=pltpu.PrefetchScalarGridSpec(
             num_scalar_prefetch=1,
             grid=(parts,),
             in_specs=[
                 pl.BlockSpec(memory_space=pltpu.SMEM),
-                pl.BlockSpec((1, WIDTH), lambda j, place_ref: (0, 0)),
+                pl.BlockSpec((WIDTH,), lambda j, place_ref: (0,)),
                 pl.BlockSpec((TILE, TILE), lambda j, place_ref: (0, 0)),
                 *[single] * 4,
                 pl.BlockSpec((TILES, PART), lambda j, place_ref: (0, block_at(place_ref, 0, 0) * parts + j)),
             ],
             out_specs=(
                 single,
-                pl.BlockSpec((copies, 8, 128), lambda j, place_ref: (0, 0, 0)),
+                pl.BlockSpec((copies, 128), lambda j, place_ref: (0, 0)),
             ),
             scratch_shapes=[pltpu.VMEM((8, 128), jnp.float32)],
         ),
@@ -229,19 +229,12 @@
     )(place, table, sign, hmat, *terms, index)
 
 
-def total_squares(square):
-    square = jnp.sum(lax.all_to_all(square, "fsdp", 0, 0), axis=0)
-    copies = jnp.broadcast_to(square, (lax.axis_size("dp"), *square.shape))
-    return lax.all_to_all(copies, "dp", 0, 0)
-
-
 MEAN_SCALE = 0.02 / (1.0 - 0.9**10)
 VAR_SCALE = 1.0 / (1.0 - 0.95**10)
 
 
 def clip_factor(square_ref):
-    square = jnp.sum(square_ref[...], axis=0)
-    square = jnp.sum(jnp.sum(square, axis=0, keepdims=True), axis=1, keepdims=True)
+    square = jnp.sum(jnp.sum(square_ref[...], axis=0, keepdims=True), axis=1, keepdims=True)
     return LIMIT / jnp.maximum(jnp.sqrt(square), LIMIT)
 
 
@@ -273,7 +266,7 @@
         kernel,
         out_shape=out_shape,
         grid=(BLOCK // STEP,),
-        in_specs=[pl.BlockSpec(square.shape, lambda j: (0, 0, 0))] + [rows] * 4,
+        in_specs=[pl.BlockSpec(square.shape, lambda j: (0, 0))] + [rows] * 4,
         out_specs=jax.tree.map(lambda _: rows, out_shape),
         compiler_params=pltpu.CompilerParams(vmem_limit_bytes=VMEM_BYTES),
         cost_estimate=pl.CostEstimate(flops=0, bytes_accessed=0, transcendentals=0),
@@ -281,9 +274,9 @@
 
 
 def stage_kernel(*refs):
-    for source, target in zip(refs[:2], refs[2:4], strict=True):
+    for source, target in zip(refs[:3], refs[3:6], strict=True):
         target[...] = source[...]
-    refs[4][...] = jnp.zeros_like(refs[4])
+    refs[6][...] = jnp.zeros_like(refs[6])
 
 
 def stage(*state):
@@ -292,8 +285,8 @@
         stage_kernel,
         out_shape=[pltpu.VMEM(v.shape, v.dtype) for v in state] + [jax.ShapeDtypeStruct((8, 128), jnp.float32)],
         grid=(BLOCK // STEP,),
-        in_specs=[rows] * 2,
-        out_specs=[rows] * 2 + [pl.BlockSpec((8, 128), lambda j: (0, 0))],
+        in_specs=[rows] * 3,
+        out_specs=[rows] * 3 + [pl.BlockSpec((8, 128), lambda j: (0, 0))],
         compiler_params=pltpu.CompilerParams(vmem_limit_bytes=VMEM_BYTES),
         cost_estimate=pl.CostEstimate(flops=0, bytes_accessed=0, transcendentals=0),
     )(*state)
@@ -372,15 +365,15 @@
     grad, scale_index, master, mean_moment, var_moment = map(in_hbm, (grad_shards[0], scale_index, master, mean_moment, var_moment))
     scale_table = in_hbm(scale_table)
     place = (lax.axis_index("dp") * 2 + (lax.axis_index("fsdp") & 1)).reshape(1)
-    sign = in_hbm(hadamard_signs.reshape(1, WIDTH))
+    sign = in_hbm(hadamard_signs)
     hmat = in_hbm(jnp.asarray(hadamard(TILE)))
-    *state, staged = stage(master, mean_moment)
-    state.append(var_moment)
+    *state, staged = stage(master, mean_moment, var_moment)
     terms = reduce_scatter(place, scale_table, sign, grad, scale_index, hmat, staged)
-    plain, square = decode(place, scale_table, sign, terms, scale_index, hmat, lax.axis_size("fsdp"))
-    square = total_squares(square)
-    low = adamw(weights_kernel, jax.ShapeDtypeStruct((BLOCK, WIDTH), jnp.bfloat16), square, in_hbm(plain), *state)
-    new_state = adamw(state_kernel, (jax.ShapeDtypeStruct(master.shape, jnp.float32),) * 3, square, in_hbm(plain), *state)
+    plain, square = decode(place, scale_table, sign, terms, scale_index, hmat, lax.axis_size(("dp", "fsdp")))
+    square = lax.all_to_all(square, ("dp", "fsdp"), 0, 0, tiled=True)
+    state = [in_vmem(v) for v in (plain, *state)]
+    low = adamw(weights_kernel, jax.ShapeDtypeStruct((BLOCK, WIDTH), jnp.bfloat16), square, *state)
+    new_state = adamw(state_kernel, (jax.ShapeDtypeStruct(master.shape, jnp.float32),) * 3, square, *state)
     return *new_state, gather(low, in_hbm(new_state[0]))
 
 

time: 146 us -> 138 us (0.945)
  blocking collectives: 22.3 us -> 18.5 us
  Pallas kernels: 38.9 us -> 35.4 us
  waiting for transfers between devices: 55.4 us -> 57.1 us
    pallas_call x2, Pallas kernels: 8.61 us -> 4.76 us  [adamw(): pl.pallas_call(kernel, out_shape=out_shape, grid=(BLOCK // STEP,), in_spe...]
    all_to_all x2 -> x1, blocking collectives: 22.3 us -> 18.5 us  [on_device(): square = lax.all_to_all(square, ('dp', 'fsdp'), 0, 0, tiled=True)]
    ppermute x3, waiting for transfers between devices: 11.7 us -> 13.7 us  [along_y(): return lax.ppermute(value, 'fsdp', pairs)]
where the time goes in v5:
time: 138 us; the launch traced here: 137 us
  waiting for transfers between devices  57.1 us (41%)
  Pallas kernels  35.4 us (26%)
  starting transfers between devices  25.5 us (18%)
  blocking collectives  18.5 us (13%)
    ppermute x11, waiting for transfers between devices, hop(): return lax.ppermute(value, ('dp', 'fsdp'), pairs)  38.5 us
    pallas_call x7, Pallas kernels, encode(): pl.pallas_call(functools.partial(encode_kernel, [len(job[2]) for job in j...  20.7 us
    all_to_all x1, blocking collectives, on_device(): square = lax.all_to_all(square, ('dp', 'fsdp'), 0, 0, tiled=True)  18.5 us
    ppermute x11, starting transfers between devices, hop(): return lax.ppermute(value, ('dp', 'fsdp'), pairs)  16.2 us
    ppermute x3, waiting for transfers between devices, along_y(): return lax.ppermute(value, 'fsdp', pairs)  13.7 us
    ppermute x5, starting transfers between devices, to_other_core(): return lax.ppermute(value, 'fsdp', [(i, i ^ 1) for i in range(8)])  7.58 us
    ppermute x5, waiting for transfers between devices, to_other_core(): return lax.ppermute(value, 'fsdp', [(i, i ^ 1) for i in range(8)])  4.81 us
    pallas_call x2, Pallas kernels, adamw(): pl.pallas_call(kernel, out_shape=out_shape, grid=(BLOCK // STEP,), in_spe...  4.76 us
  transfers between devices with their start and end apart: 19, of which 14 were waited for; matrix products, arithmetic and copies ran while one was open for 0% of the time, Pallas kernels for 18%

profile of v5, /device:TPU:1, one launch (start us, length us, event | category | flops | bytes accessed | tf_op | source)
XLA Modules:
  0.0 137.3 jit_solution(1112640010340232565)
XLA Ops:
  0.6 4.3 %shard_map.112 = (bf16[2,512,768]{2,1,0:T(8,128)(2,1)S(1)}, bf16[2,512,768]{2,1,0:T(8,128)(2,1)S(1)}) custom-call(s32[1]{0:T(128)} %bitcast.place_ref, f32[16]{0:T(128)} %table_ref.15, s32[768]{0:T(1024)} %sign_ref.15, bf16[256,256]{1,0:T(8,128)(2,1)} %constant.15.clone.hmat_ref, bf16[8192,768]{1,0:T(8,128)(2,1)} %bitcast.9, s32[3,8192]{1,0:T(4,128)} %index_ref.1, ...), custom_call_target="tpu_custom_call" | custom-call | tf_op jit(solution)/shard_map/pallas_call | solution.py:121
  4.9 2.5 %collective-permute-start = (bf16[2,512,768]{2,1,0:T(8,128)(2,1)S(1)}, bf16[2,512,768]{2,1,0:T(8,128)(2,1)S(1)}, u32[]{:S(2)}, u32[]{:S(2)}) collective-permute-start(bf16[2,512,768]{2,1,0:T(8,128)(2,1)S(1)} %get-tuple-element.27), channel_id=1, source_target_pairs={{0,32},{1,9},{2,34},{3,11},{4,36},{5,13},{6,38},{7,15},{8,40},{9,1... | collective-permute-start | bytes 4718600 | tf_op jit(solution)/shard_map/ppermute | solution.py:45
  7.5 2.2 %collective-permute-start.1 = (bf16[2,512,768]{2,1,0:T(8,128)(2,1)S(1)}, bf16[2,512,768]{2,1,0:T(8,128)(2,1)S(1)}, u32[]{:S(2)}, u32[]{:S(2)}) collective-permute-start(bf16[2,512,768]{2,1,0:T(8,128)(2,1)S(1)} %get-tuple-element.28), channel_id=1, source_target_pairs={{0,96},{1,25},{2,98},{3,27},{4,100},{5,29},{6,102},{7,31},{8,104},... | collective-permute-start | bytes 4718600 | tf_op jit(solution)/shard_map/ppermute | solution.py:45
  9.7 4.1 %shard_map.114 = (bf16[2,512,768]{2,1,0:T(8,128)(2,1)S(1)}, bf16[2,512,768]{2,1,0:T(8,128)(2,1)S(1)}) custom-call(s32[1]{0:T(128)} %bitcast.place_ref, f32[16]{0:T(128)} %table_ref.15, s32[768]{0:T(1024)} %sign_ref.15, bf16[256,256]{1,0:T(8,128)(2,1)} %constant.15.clone.hmat_ref, bf16[8192,768]{1,0:T(8,128)(2,1)} %bitcast.11, s32[3,8192]{1,0:T(4,128)} %index_ref.1, ...), custom_call_target="tpu_custom_call" | custom-call | tf_op jit(solution)/shard_map/pallas_call | solution.py:121
  13.9 2.7 %collective-permute-start.5 = (bf16[2,512,768]{2,1,0:T(8,128)(2,1)S(1)}, bf16[2,512,768]{2,1,0:T(8,128)(2,1)S(1)}, u32[]{:S(2)}, u32[]{:S(2)}) collective-permute-start(bf16[2,512,768]{2,1,0:T(8,128)(2,1)S(1)} %get-tuple-element.32), channel_id=1, source_target_pairs={{0,96},{1,25},{2,98},{3,27},{4,100},{5,29},{6,102},{7,31},{8,104},... | collective-permute-start | bytes 4718600 | tf_op jit(solution)/shard_map/ppermute | solution.py:45
  16.6 3.1 %shard_map.111 = (f32[512,768]{1,0:T(8,128)S(1)}, f32[512,768]{1,0:T(8,128)S(1)}, f32[512,768]{1,0:T(8,128)S(1)}, f32[8,128]{1,0:T(8,128)S(1)}) custom-call(f32[512,768]{1,0:T(8,128)} %refs_0_.1, f32[512,768]{1,0:T(8,128)} %refs_1_.6, f32[512,768]{1,0:T(8,128)} %refs_2_.3), custom_call_target="tpu_custom_call" | custom-call | tf_op jit(solution)/shard_map/pallas_call | solution.py:284
  19.6 8.0 %collective-permute-done.refs_3_ = bf16[2,512,768]{2,1,0:T(8,128)(2,1)S(1)} collective-permute-done((bf16[2,512,768]{2,1,0:T(8,128)(2,1)S(1)}, bf16[2,512,768]{2,1,0:T(8,128)(2,1)S(1)}, u32[]{:S(2)}, u32[]{:S(2)}) %collective-permute-start) | collective-permute-done | bytes 1572896 | tf_op jit(solution)/shard_map/ppermute | solution.py:45
  27.7 2.6 %shard_map.116 = (bf16[512,768]{1,0:T(8,128)(2,1)S(1)}, bf16[512,768]{1,0:T(8,128)(2,1)S(1)}) custom-call(s32[1]{0:T(128)} %bitcast.place_ref, f32[16]{0:T(128)} %table_ref.15, s32[768]{0:T(1024)} %sign_ref.15, bf16[256,256]{1,0:T(8,128)(2,1)} %constant.15.clone.hmat_ref, f32[8,128]{1,0:T(8,128)S(1)} %get-tuple-element.26.refs_0_, ...), custom_call_target="tpu_custom_call" | custom-call | tf_op jit(solution)/shard_map/pallas_call | solution.py:121
  31.3 1.9 %collective-permute-start.6 = (bf16[512,768]{1,0:T(8,128)(2,1)S(1)}, bf16[512,768]{1,0:T(8,128)(2,1)S(1)}, u32[]{:S(2)}, u32[]{:S(2)}) collective-permute-start(bf16[512,768]{1,0:T(8,128)(2,1)S(1)} %get-tuple-element.33), channel_id=1, source_target_pairs={{0,96},{1,25},{2,98},{3,27},{4,100},{5,29},{6,102},{7,31},{8,104},... | collective-permute-start | bytes 2359304 | tf_op jit(solution)/shard_map/ppermute | solution.py:45
  33.1 2.6 %shard_map.113 = (bf16[512,768]{1,0:T(8,128)(2,1)S(1)}, bf16[512,768]{1,0:T(8,128)(2,1)S(1)}) custom-call(s32[1]{0:T(128)} %bitcast.place_ref, f32[16]{0:T(128)} %table_ref.15, s32[768]{0:T(1024)} %sign_ref.15, bf16[256,256]{1,0:T(8,128)(2,1)} %constant.15.clone.hmat_ref, f32[8,128]{1,0:T(8,128)S(1)} %get-tuple-element.26.refs_0_, ...), custom_call_target="tpu_custom_call" | custom-call | tf_op jit(solution)/shard_map/pallas_call | solution.py:121
  35.8 8.7 %collective-permute-done.3.refs_3_.refs_7_ = bf16[2,512,768]{2,1,0:T(8,128)(2,1)S(1)} collective-permute-done((bf16[2,512,768]{2,1,0:T(8,128)(2,1)S(1)}, bf16[2,512,768]{2,1,0:T(8,128)(2,1)S(1)}, u32[]{:S(2)}, u32[]{:S(2)}) %collective-permute-start.3) | collective-permute-done | bytes 1572896 | tf_op jit(solution)/shard_map/ppermute | solution.py:45
  46.0 7.0 %collective-permute-done.4.refs_2_ = bf16[512,768]{1,0:T(8,128)(2,1)S(1)} collective-permute-done((bf16[512,768]{1,0:T(8,128)(2,1)S(1)}, bf16[512,768]{1,0:T(8,128)(2,1)S(1)}, u32[]{:S(2)}, u32[]{:S(2)}) %collective-permute-start.4) | collective-permute-done | bytes 786464 | tf_op jit(solution)/shard_map/ppermute | solution.py:45
  53.0 2.8 %shard_map.117 = (bf16[512,768]{1,0:T(8,128)(2,1)S(1)}, bf16[512,768]{1,0:T(8,128)(2,1)S(1)}) custom-call(s32[1]{0:T(128)} %bitcast.place_ref, f32[16]{0:T(128)} %table_ref.15, s32[768]{0:T(1024)} %sign_ref.15, bf16[256,256]{1,0:T(8,128)(2,1)} %constant.15.clone.hmat_ref, bf16[8192,768]{1,0:T(8,128)(2,1)} %bitcast.17, s32[3,8192]{1,0:T(4,128)} %index_ref.1, ...), custom_call_target="tpu_custom_call" | custom-call | tf_op jit(solution)/shard_map/pallas_call | solution.py:121
  55.8 2.5 %collective-permute-start.7 = (bf16[512,768]{1,0:T(8,128)(2,1)S(1)}, bf16[512,768]{1,0:T(8,128)(2,1)S(1)}, u32[]{:S(2)}, u32[]{:S(2)}) collective-permute-start(bf16[512,768]{1,0:T(8,128)(2,1)S(1)} %get-tuple-element.34), channel_id=1, source_target_pairs={{0,16},{1,65},{2,18},{3,67},{4,20},{5,69},{6,22},{7,71},{8,24},{9,... | collective-permute-start | bytes 2359304 | tf_op jit(solution)/shard_map/ppermute | solution.py:45
  59.2 2.2 %collective-permute-done.8.refs_2_ = bf16[512,768]{1,0:T(8,128)(2,1)S(1)} collective-permute-done((bf16[512,768]{1,0:T(8,128)(2,1)S(1)}, bf16[512,768]{1,0:T(8,128)(2,1)S(1)}, u32[]{:S(2)}, u32[]{:S(2)}) %collective-permute-start.8) | collective-permute-done | bytes 786464 | tf_op jit(solution)/shard_map/ppermute | solution.py:45
  61.4 2.2 %shard_map.118 = bf16[512,768]{1,0:T(8,128)(2,1)S(1)} custom-call(s32[1]{0:T(128)} %bitcast.place_ref, f32[16]{0:T(128)} %table_ref.15, s32[768]{0:T(1024)} %sign_ref.15, bf16[256,256]{1,0:T(8,128)(2,1)} %constant.15.clone.hmat_ref, bf16[8192,768]{1,0:T(8,128)(2,1)} %bitcast.19, s32[3,8192]{1,0:T(4,128)} %index_ref.1, ...), custom_call_target="tpu_custom_call" | custom-call | tf_op jit(solution)/shard_map/pallas_call | solution.py:121
  64.5 2.1 %shard_map.115.own_ref = f32[512,768]{1,0:T(8,128)S(1)} custom-call(s32[1]{0:T(128)} %bitcast.place_ref, f32[16]{0:T(128)} %table_ref.15, s32[768]{0:T(1024)} %sign_ref.15, bf16[256,256]{1,0:T(8,128)(2,1)} %constant.15.clone.hmat_ref, bf16[8192,768]{1,0:T(8,128)(2,1)} %bitcast.20, s32[3,8192]{1,0:T(4,128)} %index_ref.1, ...), custom_call_target="tpu_custom_call" | custom-call | tf_op jit(solution)/shard_map/pallas_call | solution.py:121
  66.7 4.2 %collective-permute-done.7.two_ref = bf16[512,768]{1,0:T(8,128)(2,1)S(1)} collective-permute-done((bf16[512,768]{1,0:T(8,128)(2,1)S(1)}, bf16[512,768]{1,0:T(8,128)(2,1)S(1)}, u32[]{:S(2)}, u32[]{:S(2)}) %collective-permute-start.7) | collective-permute-done | bytes 786464 | tf_op jit(solution)/shard_map/ppermute | solution.py:45
  70.9 7.7 %collective-permute-done.10.three_ref = bf16[512,768]{1,0:T(8,128)(2,1)S(1)} collective-permute-done((bf16[512,768]{1,0:T(8,128)(2,1)S(1)}, bf16[512,768]{1,0:T(8,128)(2,1)S(1)}, u32[]{:S(2)}, u32[]{:S(2)}) %collective-permute-start.10) | collective-permute-done | bytes 786464 | tf_op jit(solution)/shard_map/ppermute | solution.py:45
  79.3 2.9 %shard_map.119 = (f32[512,768]{1,0:T(8,128)S(1)}, f32[128,128]{1,0:T(8,128)}) custom-call(s32[1]{0:T(128)} %bitcast.place_ref, f32[16]{0:T(128)} %table_ref.15, s32[768]{0:T(1024)} %sign_ref.15, bf16[256,256]{1,0:T(8,128)(2,1)} %constant.15.clone.hmat_ref, f32[512,768]{1,0:T(8,128)S(1)} %shard_map.115.own_ref, ...), custom_call_target="tpu_custom_call" | custom-call | tf_op jit(solution)/shard_map/pallas_call | solution.py:205
  82.1 18.5 %all_to_all.11 = f32[128,1,128]{2,1,0:T(1,128)S(1)} all-to-all(f32[128,1,128]{2,1,0:T(1,128)} %bitcast.21), channel_id=1, replica_groups=mesh['dp'=16,'fsdp'=8] {'dp','fsdp'}, dimensions={0} | all-to-all | bytes 131072 | tf_op jit(solution)/shard_map/all_to_all | solution.py:373
  100.7 1.8 %shard_map.121.refs_0_ = bf16[512,768]{1,0:T(8,128)(2,1)S(1)} custom-call(f32[128,128]{1,0:T(8,128)S(1)} %bitcast.7, f32[512,768]{1,0:T(8,128)S(1)} %get-tuple-element.38.plain_ref, f32[512,768]{1,0:T(8,128)S(1)} %get-tuple-element.39.master_ref, f32[512,768]{1,0:T(8,128)S(1)} %get-tuple-element.40.mean_ref, f32[512,768]{1,0:T(8,128)S(1)} %get-tuple-element.41.var_ref), custom_call_target="tpu_custom_call" | custom-call | tf_op jit(solution)/shard_map/pallas_call | solution.py:265
  106.2 2.9 %shard_map.120 = (f32[512,768]{1,0:T(8,128)}, f32[512,768]{1,0:T(8,128)}, f32[512,768]{1,0:T(8,128)}) custom-call(f32[128,128]{1,0:T(8,128)S(1)} %bitcast.8, f32[512,768]{1,0:T(8,128)S(1)} %get-tuple-element.38.plain_ref, f32[512,768]{1,0:T(8,128)S(1)} %get-tuple-element.39.master_ref, f32[512,768]{1,0:T(8,128)S(1)} %get-tuple-element.40.mean_ref, ...), custom_call_target="tpu_custom_call" | custom-call | tf_op jit(solution)/shard_map/pallas_call | solution.py:265
  109.1 5.5 %collective-permute-done.11.__0_ = bf16[512,768]{1,0:T(8,128)(2,1)S(1)} collective-permute-done((bf16[512,768]{1,0:T(8,128)(2,1)S(1)}, bf16[512,768]{1,0:T(8,128)(2,1)S(1)}, u32[]{:S(2)}, u32[]{:S(2)}) %collective-permute-start.11) | collective-permute-done | bytes 786464 | tf_op jit(solution)/shard_map/ppermute | solution.py:341
  114.6 2.1 %collective-permute-start.15 = (bf16[512,768]{1,0:T(8,128)(2,1)S(1)}, bf16[512,768]{1,0:T(8,128)(2,1)S(1)}, u32[]{:S(2)}, u32[]{:S(2)}) collective-permute-start(bf16[512,768]{1,0:T(8,128)(2,1)S(1)} %shard_map.122.refs_2_), channel_id=1, source_target_pairs={{0,1},{1,0},{2,3},{3,2},{4,5},{5,4},{6,7},{7,6},{8,9},{9,8},{10,11... | collective-permute-start | bytes 2359304 | tf_op jit(solution)/shard_map/ppermute | solution.py:345
  116.7 6.3 %collective-permute-done.14.refs_3_ = bf16[512,768]{1,0:T(8,128)(2,1)S(1)} collective-permute-done((bf16[512,768]{1,0:T(8,128)(2,1)S(1)}, bf16[512,768]{1,0:T(8,128)(2,1)S(1)}, u32[]{:S(2)}, u32[]{:S(2)}) %collective-permute-start.14) | collective-permute-done | bytes 786464 | tf_op jit(solution)/shard_map/ppermute | solution.py:341
  123.1 2.2 %collective-permute-start.17 = (bf16[256,768]{1,0:T(8,128)(2,1)S(1)}, bf16[256,768]{1,0:T(8,128)(2,1)S(1)}, u32[]{:S(2)}, u32[]{:S(2)}) collective-permute-start(bf16[256,768]{1,0:T(8,128)(2,1)S(1)} %get-tuple-element.48), channel_id=1, source_target_pairs={{0,1},{1,0},{2,3},{3,2},{4,5},{5,4},{6,7},{7,6},{8,9},{9,8},{10,11... | collective-permute-start | bytes 1179656 | tf_op jit(solution)/shard_map/ppermute | solution.py:345
  127.2 2.2 %shard_map.123 = (bf16[512,6144]{1,0:T(8,128)(2,1)}, f32[8,128]{1,0:T(8,128)S(1)}) custom-call(s32[1]{0:T(128)} %bitcast.5.at_ref, bf16[512,768]{1,0:T(8,128)(2,1)S(1)} %shard_map.121.refs_0_, bf16[512,768]{1,0:T(8,128)(2,1)S(1)} %collective-permute-done.13.refs_1_, bf16[512,768]{1,0:T(8,128)(2,1)S(1)} %shard_map.122.refs_2_, ...), custom_call_target="tpu_custom_call" | custom-call | tf_op jit(solution)/shard_map/pallas_call | solution.py:327
  129.5 2.0 %collective-permute-done.12.__0_ = bf16[512,768]{1,0:T(8,128)(2,1)S(1)} collective-permute-done((bf16[512,768]{1,0:T(8,128)(2,1)S(1)}, bf16[512,768]{1,0:T(8,128)(2,1)S(1)}, u32[]{:S(2)}, u32[]{:S(2)}) %collective-permute-start.12) | collective-permute-done | bytes 786464 | tf_op jit(solution)/shard_map/ppermute | solution.py:341
  131.4 2.1 %collective-permute-start.18 = (bf16[512,768]{1,0:T(8,128)(2,1)S(1)}, bf16[512,768]{1,0:T(8,128)(2,1)S(1)}, u32[]{:S(2)}, u32[]{:S(2)}) collective-permute-start(bf16[512,768]{1,0:T(8,128)(2,1)S(1)} %shard_map.124.refs_0_), channel_id=1, source_target_pairs={{0,1},{1,0},{2,3},{3,2},{4,5},{5,4},{6,7},{7,6},{8,9},{9,8},{10,11... | collective-permute-start | bytes 2359304 | tf_op jit(solution)/shard_map/ppermute | solution.py:345
  133.6 1.9 %collective-permute-done.18.refs_1_ = bf16[512,768]{1,0:T(8,128)(2,1)S(1)} collective-permute-done((bf16[512,768]{1,0:T(8,128)(2,1)S(1)}, bf16[512,768]{1,0:T(8,128)(2,1)S(1)}, u32[]{:S(2)}, u32[]{:S(2)}) %collective-permute-start.18) | collective-permute-done | bytes 786464 | tf_op jit(solution)/shard_map/ppermute | solution.py:345
  135.5 1.7 %shard_map.125 = (bf16[512,6144]{1,0:T(8,128)(2,1)}, f32[8,128]{1,0:T(8,128)}) custom-call(s32[1]{0:T(128)} %bitcast.5.at_ref, bf16[512,768]{1,0:T(8,128)(2,1)S(1)} %shard_map.124.refs_0_, bf16[512,768]{1,0:T(8,128)(2,1)S(1)} %collective-permute-done.18.refs_1_, bf16[512,6144]{1,0:T(8,128)(2,1)} %get-tuple-element.46.refs_2_), custom_call_target="tpu_custom_call", output_to_operand_aliasing={{0}: (3, {})} | custom-call | tf_op jit(solution)/shard_map/pallas_call | solution.py:327
  (23 shorter events, 10.8 us)
Async XLA Ops:
  4.9 22.8 %collective-permute-start = (bf16[2,512,768]{2,1,0:T(8,128)(2,1)S(1)}, bf16[2,512,768]{2,1,0:T(8,128)(2,1)S(1)}, u32[]{:S(2)}, u32[]{:S(2)}) collective-permute-start(bf16[2,512,768]{2,1,0:T(8,128)(2,1)S(1)} %get-tuple-element.27), channel_id=1, source_target_pairs={{0,32},{1,9},{2,34},{3,11},{4,36},{5,13},{6,38},{7,15},{8,40},{9,1... | collective-permute-start | bytes 4718600 | tf_op jit(solution)/shard_map/ppermute | solution.py:45
  7.5 20.2 %collective-permute-start.1 = (bf16[2,512,768]{2,1,0:T(8,128)(2,1)S(1)}, bf16[2,512,768]{2,1,0:T(8,128)(2,1)S(1)}, u32[]{:S(2)}, u32[]{:S(2)}) collective-permute-start(bf16[2,512,768]{2,1,0:T(8,128)(2,1)S(1)} %get-tuple-element.28), channel_id=1, source_target_pairs={{0,96},{1,25},{2,98},{3,27},{4,100},{5,29},{6,102},{7,31},{8,104},... | collective-permute-start | bytes 4718600 | tf_op jit(solution)/shard_map/ppermute | solution.py:45
  13.8 30.7 %collective-permute-start.3 = (bf16[2,512,768]{2,1,0:T(8,128)(2,1)S(1)}, bf16[2,512,768]{2,1,0:T(8,128)(2,1)S(1)}, u32[]{:S(2)}, u32[]{:S(2)}) collective-permute-start(bf16[2,512,768]{2,1,0:T(8,128)(2,1)S(1)} %get-tuple-element.30), channel_id=1, source_target_pairs={{0,32},{1,9},{2,34},{3,11},{4,36},{5,13},{6,38},{7,15},{8,40},{9,1... | collective-permute-start | bytes 4718600 | tf_op jit(solution)/shard_map/ppermute | solution.py:45
  13.9 32.1 %collective-permute-start.5 = (bf16[2,512,768]{2,1,0:T(8,128)(2,1)S(1)}, bf16[2,512,768]{2,1,0:T(8,128)(2,1)S(1)}, u32[]{:S(2)}, u32[]{:S(2)}) collective-permute-start(bf16[2,512,768]{2,1,0:T(8,128)(2,1)S(1)} %get-tuple-element.32), channel_id=1, source_target_pairs={{0,96},{1,25},{2,98},{3,27},{4,100},{5,29},{6,102},{7,31},{8,104},... | collective-permute-start | bytes 4718600 | tf_op jit(solution)/shard_map/ppermute | solution.py:45
  30.3 22.6 %collective-permute-start.4 = (bf16[512,768]{1,0:T(8,128)(2,1)S(1)}, bf16[512,768]{1,0:T(8,128)(2,1)S(1)}, u32[]{:S(2)}, u32[]{:S(2)}) collective-permute-start(bf16[512,768]{1,0:T(8,128)(2,1)S(1)} %get-tuple-element.31), channel_id=1, source_target_pairs={{0,32},{1,9},{2,34},{3,11},{4,36},{5,13},{6,38},{7,15},{8,40},{9,1... | collective-permute-start | bytes 2359304 | tf_op jit(solution)/shard_map/ppermute | solution.py:45
  31.3 21.7 %collective-permute-start.6 = (bf16[512,768]{1,0:T(8,128)(2,1)S(1)}, bf16[512,768]{1,0:T(8,128)(2,1)S(1)}, u32[]{:S(2)}, u32[]{:S(2)}) collective-permute-start(bf16[512,768]{1,0:T(8,128)(2,1)S(1)} %get-tuple-element.33), channel_id=1, source_target_pairs={{0,96},{1,25},{2,98},{3,27},{4,100},{5,29},{6,102},{7,31},{8,104},... | collective-permute-start | bytes 2359304 | tf_op jit(solution)/shard_map/ppermute | solution.py:45
  35.7 25.7 %collective-permute-start.8 = (bf16[512,768]{1,0:T(8,128)(2,1)S(1)}, bf16[512,768]{1,0:T(8,128)(2,1)S(1)}, u32[]{:S(2)}, u32[]{:S(2)}) collective-permute-start(bf16[512,768]{1,0:T(8,128)(2,1)S(1)} %get-tuple-element.35), channel_id=1, source_target_pairs={{0,32},{1,9},{2,34},{3,11},{4,36},{5,13},{6,38},{7,15},{8,40},{9,1... | collective-permute-start | bytes 2359304 | tf_op jit(solution)/shard_map/ppermute | solution.py:45
  44.5 20.0 %collective-permute-start.2 = (bf16[512,768]{1,0:T(8,128)(2,1)S(1)}, bf16[512,768]{1,0:T(8,128)(2,1)S(1)}, u32[]{:S(2)}, u32[]{:S(2)}) collective-permute-start(bf16[512,768]{1,0:T(8,128)(2,1)S(1)} %get-tuple-element.29), channel_id=1, source_target_pairs={{0,96},{1,25},{2,98},{3,27},{4,100},{5,29},{6,102},{7,31},{8,104},... | collective-permute-start | bytes 2359304 | tf_op jit(solution)/shard_map/ppermute | solution.py:45
  55.8 15.1 %collective-permute-start.7 = (bf16[512,768]{1,0:T(8,128)(2,1)S(1)}, bf16[512,768]{1,0:T(8,128)(2,1)S(1)}, u32[]{:S(2)}, u32[]{:S(2)}) collective-permute-start(bf16[512,768]{1,0:T(8,128)(2,1)S(1)} %get-tuple-element.34), channel_id=1, source_target_pairs={{0,16},{1,65},{2,18},{3,67},{4,20},{5,69},{6,22},{7,71},{8,24},{9,... | collective-permute-start | bytes 2359304 | tf_op jit(solution)/shard_map/ppermute | solution.py:45
  58.3 20.3 %collective-permute-start.10 = (bf16[512,768]{1,0:T(8,128)(2,1)S(1)}, bf16[512,768]{1,0:T(8,128)(2,1)S(1)}, u32[]{:S(2)}, u32[]{:S(2)}) collective-permute-start(bf16[512,768]{1,0:T(8,128)(2,1)S(1)} %get-tuple-element.36), channel_id=1, source_target_pairs={{0,24},{1,97},{2,26},{3,99},{4,28},{5,101},{6,30},{7,103},{8,0},{9... | collective-permute-start | bytes 2359304 | tf_op jit(solution)/shard_map/ppermute | solution.py:45
  63.5 15.7 %collective-permute-start.9 = (bf16[512,768]{1,0:T(8,128)(2,1)S(1)}, bf16[512,768]{1,0:T(8,128)(2,1)S(1)}, u32[]{:S(2)}, u32[]{:S(2)}) collective-permute-start(bf16[512,768]{1,0:T(8,128)(2,1)S(1)} %shard_map.118), channel_id=1, source_target_pairs={{0,8},{1,33},{2,10},{3,35},{4,12},{5,37},{6,14},{7,39},{8,16},{9,4... | collective-permute-start | bytes 2359304 | tf_op jit(solution)/shard_map/ppermute | solution.py:45
  102.5 2.9 %collective-permute-start.13 = (bf16[512,768]{1,0:T(8,128)(2,1)S(1)}, bf16[512,768]{1,0:T(8,128)(2,1)S(1)}, u32[]{:S(2)}, u32[]{:S(2)}) collective-permute-start(bf16[512,768]{1,0:T(8,128)(2,1)S(1)} %shard_map.121.refs_0_), channel_id=1, source_target_pairs={{0,1},{1,0},{2,3},{3,2},{4,5},{5,4},{6,7},{7,6},{8,9},{9,8},{10,11... | collective-permute-start | bytes 2359304 | tf_op jit(solution)/shard_map/ppermute | solution.py:345
  103.5 11.1 %collective-permute-start.11 = (bf16[512,768]{1,0:T(8,128)(2,1)S(1)}, bf16[512,768]{1,0:T(8,128)(2,1)S(1)}, u32[]{:S(2)}, u32[]{:S(2)}) collective-permute-start(bf16[512,768]{1,0:T(8,128)(2,1)S(1)} %shard_map.121.refs_0_), channel_id=1, source_target_pairs={{0,2},{1,7},{2,4},{3,1},{4,6},{5,3},{6,0},{7,5},{8,10},{9,15},{10,... | collective-permute-start | bytes 2359304 | tf_op jit(solution)/shard_map/ppermute | solution.py:341
  105.4 17.6 %collective-permute-start.14 = (bf16[512,768]{1,0:T(8,128)(2,1)S(1)}, bf16[512,768]{1,0:T(8,128)(2,1)S(1)}, u32[]{:S(2)}, u32[]{:S(2)}) collective-permute-start(bf16[512,768]{1,0:T(8,128)(2,1)S(1)} %collective-permute-done.13.refs_1_), channel_id=1, source_target_pairs={{0,2},{1,7},{2,4},{3,1},{4,6},{5,3},{6,0},{7,5},{8,10},{9,15},{10,... | collective-permute-start | bytes 2359304 | tf_op jit(solution)/shard_map/ppermute | solution.py:341
  114.6 10.8 %collective-permute-start.15 = (bf16[512,768]{1,0:T(8,128)(2,1)S(1)}, bf16[512,768]{1,0:T(8,128)(2,1)S(1)}, u32[]{:S(2)}, u32[]{:S(2)}) collective-permute-start(bf16[512,768]{1,0:T(8,128)(2,1)S(1)} %shard_map.122.refs_2_), channel_id=1, source_target_pairs={{0,1},{1,0},{2,3},{3,2},{4,5},{5,4},{6,7},{7,6},{8,9},{9,8},{10,11... | collective-permute-start | bytes 2359304 | tf_op jit(solution)/shard_map/ppermute | solution.py:345
  116.7 14.7 %collective-permute-start.12 = (bf16[512,768]{1,0:T(8,128)(2,1)S(1)}, bf16[512,768]{1,0:T(8,128)(2,1)S(1)}, u32[]{:S(2)}, u32[]{:S(2)}) collective-permute-start(bf16[512,768]{1,0:T(8,128)(2,1)S(1)} %shard_map.122.refs_2_), channel_id=1, source_target_pairs={{0,2},{1,7},{2,4},{3,1},{4,6},{5,3},{6,0},{7,5},{8,10},{9,15},{10,... | collective-permute-start | bytes 2359304 | tf_op jit(solution)/shard_map/ppermute | solution.py:341
  123.1 3.6 %collective-permute-start.17 = (bf16[256,768]{1,0:T(8,128)(2,1)S(1)}, bf16[256,768]{1,0:T(8,128)(2,1)S(1)}, u32[]{:S(2)}, u32[]{:S(2)}) collective-permute-start(bf16[256,768]{1,0:T(8,128)(2,1)S(1)} %get-tuple-element.48), channel_id=1, source_target_pairs={{0,1},{1,0},{2,3},{3,2},{4,5},{5,4},{6,7},{7,6},{8,9},{9,8},{10,11... | collective-permute-start | bytes 1179656 | tf_op jit(solution)/shard_map/ppermute | solution.py:345
  125.3 1.9 %collective-permute-start.16 = (bf16[256,768]{1,0:T(8,128)(2,1)S(1)}, bf16[256,768]{1,0:T(8,128)(2,1)S(1)}, u32[]{:S(2)}, u32[]{:S(2)}) collective-permute-start(bf16[256,768]{1,0:T(8,128)(2,1)S(1)} %get-tuple-element.49), channel_id=1, source_target_pairs={{0,1},{1,0},{2,3},{3,2},{4,5},{5,4},{6,7},{7,6},{8,9},{9,8},{10,11... | collective-permute-start | bytes 1179656 | tf_op jit(solution)/shard_map/ppermute | solution.py:345
  131.4 4.1 %collective-permute-start.18 = (bf16[512,768]{1,0:T(8,128)(2,1)S(1)}, bf16[512,768]{1,0:T(8,128)(2,1)S(1)}, u32[]{:S(2)}, u32[]{:S(2)}) collective-permute-start(bf16[512,768]{1,0:T(8,128)(2,1)S(1)} %shard_map.124.refs_0_), channel_id=1, source_target_pairs={{0,1},{1,0},{2,3},{3,2},{4,5},{5,4},{6,7},{7,6},{8,9},{9,8},{10,11... | collective-permute-start | bytes 2359304 | tf_op jit(solution)/shard_map/ppermute | solution.py:345

commit v6 on v5

--- a/solution.py
+++ b/solution.py
@@ -19,6 +19,7 @@
 BLOCK = 512
 PART = 256
 STEP = 128
+CUTS = 4
 RING0, RING1 = (2, 1), (3, 0)
 LIMIT = 4.0 * math.sqrt(ROWS * D)
 VMEM_BYTES = 14 * 1024 * 1024
@@ -200,8 +201,8 @@
 
 
 def decode(place, table, sign, terms, index, hmat, copies):
-    parts = BLOCK // PART
-    single = pl.BlockSpec((PART, WIDTH), lambda j, place_ref: (j, 0))
+    parts = BLOCK // BLOCK
+    single = pl.BlockSpec((BLOCK, WIDTH), lambda j, place_ref: (j, 0))
     return pl.pallas_call(
         decode_kernel,
         out_shape=(
@@ -216,7 +217,7 @@
                 pl.BlockSpec((WIDTH,), lambda j, place_ref: (0,)),
                 pl.BlockSpec((TILE, TILE), lambda j, place_ref: (0, 0)),
                 *[single] * 4,
-                pl.BlockSpec((TILES, PART), lambda j, place_ref: (0, block_at(place_ref, 0, 0) * parts + j)),
+                pl.BlockSpec((TILES, BLOCK), lambda j, place_ref: (0, block_at(place_ref, 0, 0) * parts + j)),
             ],
             out_specs=(
                 single,
@@ -304,36 +305,40 @@
     )(value, first)
 
 
-def fill_kernel(places, at_ref, *refs):
-    count = len(places)
-    out_ref, tile_ref, sems = refs[-3:]
-    tile_ref[...] = jnp.zeros_like(tile_ref)
-    chip, core = at_ref[0] // 2, at_ref[0] % 2
+def fill_kernel(places, out_at, *refs):
+    out_ref, sems = refs[out_at], refs[-1]
+    for tile_ref in refs[out_at + 1 : -1]:
+        tile_ref[...] = jnp.zeros_like(tile_ref)
+    at = lax.axis_index("fsdp")
+    chip, core = at // 2, at % 2
     copies = []
     for j, (step, swapped, row) in enumerate(places):
-        source = (chip + SIDE - step + 2 * step * core) % SIDE
-        column = pl.multiple_of((source * 2 + (1 - core if swapped else core)) * WIDTH, WIDTH)
-        target = out_ref.at[pl.ds(row, refs[j].shape[0]), pl.ds(column, WIDTH)]
-        copies.append(pltpu.make_async_copy(refs[j], target, sems.at[j]))
+        sender = (chip + SIDE - step + 2 * step * core) % SIDE
+        column = pl.multiple_of((sender * 2 + (1 - core if swapped else core)) * WIDTH, WIDTH)
+        height = refs[j].shape[0] // CUTS
+        for cut in range(CUTS):
+            source = refs[j].at[pl.ds(cut * height, height), :]
+            target = out_ref.at[pl.ds(row + cut * height, height), pl.ds(column, WIDTH)]
+            copies.append(pltpu.make_async_copy(source, target, sems.at[len(copies)]))
     for copy in copies:
         copy.start()
     for copy in copies:
         copy.wait()
 
 
-def fill(at, places, blocks, weights=None):
+def fill(places, blocks, weights=None, tile=False):
     anywhere = pl.BlockSpec(memory_space=pl.ANY)
     given = [] if weights is None else [weights]
     return pl.pallas_call(
-        functools.partial(fill_kernel, places),
-        out_shape=(pltpu.HBM((BLOCK, D), jnp.bfloat16), jax.ShapeDtypeStruct((8, 128), jnp.float32)),
-        in_specs=[pl.BlockSpec(memory_space=pltpu.SMEM)] + [pl.BlockSpec(v.shape, lambda: (0, 0)) for v in blocks] + [anywhere] * len(given),
-        out_specs=(anywhere, pl.BlockSpec((8, 128), lambda: (0, 0))),
-        scratch_shapes=[pltpu.SemaphoreType.DMA((len(blocks),))],
-        input_output_aliases={len(blocks) + 1: 0} if given else {},
+        functools.partial(fill_kernel, places, len(blocks) + len(given)),
+        out_shape=[pltpu.HBM((BLOCK, D), jnp.bfloat16)] + [jax.ShapeDtypeStruct((8, 128), jnp.float32)] * tile,
+        in_specs=[anywhere] * len(blocks) + [anywhere] * len(given),
+        out_specs=[anywhere] + [pl.BlockSpec((8, 128), lambda: (0, 0))] * tile,
+        scratch_shapes=[pltpu.SemaphoreType.DMA((CUTS * len(blocks),))],
+        input_output_aliases={len(blocks): 0} if given else {},
         compiler_params=pltpu.CompilerParams(vmem_limit_bytes=VMEM_BYTES),
         cost_estimate=pl.CostEstimate(flops=0, bytes_accessed=0, transcendentals=0),
-    )(at, *blocks, *given)
+    )(*map(in_vmem, blocks), *given)
 
 
 def along_y(value):
@@ -346,7 +351,6 @@
 
 
 def gather(low, state):
-    at = lax.axis_index("fsdp").reshape(1)
     one = along_y(low)
     other = to_other_core(low)
     one_other = along_y(other)
@@ -355,10 +359,11 @@
     one_swapped = to_other_core(one)
     halves = [to_other_core(one_other[row : row + PART]) for row in (0, PART)]
     near = ((0, False, 0), (0, True, 0), (1, False, 0), (1, True, 0), (-1, True, 0), (-1, False, 0), (-1, False, PART))
-    weights, filled = fill(at, near, (low, other, one, one_other, one_swapped, *halves))
+    weights, filled = fill(near, (low, other, one, one_other, one_swapped, *halves), tile=True)
     two = after(two, filled)
     two_swapped = to_other_core(two)
-    return fill(at, ((2, False, 0), (2, True, 0)), (two, two_swapped), weights)[0]
+    weights = fill(((2, False, 0),), (two,), weights)[0]
+    return fill(((2, True, 0),), (two_swapped,), weights)[0]
 
 
 def on_device(grad_shards, hadamard_signs, scale_index, scale_table, master, mean_moment, var_moment):

time: 138 us -> 137 us (level)
    pallas_call x2 -> x3, Pallas kernels: 3.97 us -> 4.19 us  [fill(): pl.pallas_call(functools.partial(fill_kernel, places, len(blocks) + len(g...]
  transfers between devices with their start and end apart: 19 -> 19, of which waited for: 14 -> 14; matrix products, arithmetic and copies ran while one was open for 0% -> 0% of each run, Pallas kernels for 18% -> 19%
where the time goes in v6:
time: 137 us; the launch traced here: 136 us
  waiting for transfers between devices  56 us (41%)
  Pallas kernels  35.4 us (26%)
  starting transfers between devices  25.5 us (19%)
  blocking collectives  18.5 us (14%)
    ppermute x11, waiting for transfers between devices, hop(): return lax.ppermute(value, ('dp', 'fsdp'), pairs)  38.5 us
    pallas_call x7, Pallas kernels, encode(): pl.pallas_call(functools.partial(encode_kernel, [len(job[2]) for job in j...  20.7 us
    all_to_all x1, blocking collectives, on_device(): square = lax.all_to_all(square, ('dp', 'fsdp'), 0, 0, tiled=True)  18.5 us
    ppermute x11, starting transfers between devices, hop(): return lax.ppermute(value, ('dp', 'fsdp'), pairs)  16.2 us
    ppermute x3, waiting for transfers between devices, along_y(): return lax.ppermute(value, 'fsdp', pairs)  13.6 us
    ppermute x5, starting transfers between devices, to_other_core(): return lax.ppermute(value, 'fsdp', [(i, i ^ 1) for i in range(8)])  7.58 us
    pallas_call x2, Pallas kernels, adamw(): pl.pallas_call(kernel, out_shape=out_shape, grid=(BLOCK // STEP,), in_spe...  4.76 us
    pallas_call x3, Pallas kernels, fill(): pl.pallas_call(functools.partial(fill_kernel, places, len(blocks) + len(g...  4.19 us
  transfers between devices with their start and end apart: 19, of which 14 were waited for; matrix products, arithmetic and copies ran while one was open for 0% of the time, Pallas kernels for 19%

profile of v6, /device:TPU:1, one launch (start us, length us, event | category | flops | bytes accessed | tf_op | source)
XLA Modules:
  0.0 136.2 jit_solution(12232713423334097413)
XLA Ops:
  0.6 4.3 %shard_map.112 = (bf16[2,512,768]{2,1,0:T(8,128)(2,1)S(1)}, bf16[2,512,768]{2,1,0:T(8,128)(2,1)S(1)}) custom-call(s32[1]{0:T(128)} %bitcast.place_ref, f32[16]{0:T(128)} %table_ref.15, s32[768]{0:T(1024)} %sign_ref.15, bf16[256,256]{1,0:T(8,128)(2,1)} %constant.15.clone.hmat_ref, bf16[8192,768]{1,0:T(8,128)(2,1)} %bitcast.8, s32[3,8192]{1,0:T(4,128)} %index_ref.1, ...), custom_call_target="tpu_custom_call" | custom-call | tf_op jit(solution)/shard_map/pallas_call | solution.py:122
  4.9 2.5 %collective-permute-start = (bf16[2,512,768]{2,1,0:T(8,128)(2,1)S(1)}, bf16[2,512,768]{2,1,0:T(8,128)(2,1)S(1)}, u32[]{:S(2)}, u32[]{:S(2)}) collective-permute-start(bf16[2,512,768]{2,1,0:T(8,128)(2,1)S(1)} %get-tuple-element.26), channel_id=1, source_target_pairs={{0,32},{1,9},{2,34},{3,11},{4,36},{5,13},{6,38},{7,15},{8,40},{9,1... | collective-permute-start | bytes 4718600 | tf_op jit(solution)/shard_map/ppermute | solution.py:46
  7.5 2.2 %collective-permute-start.1 = (bf16[2,512,768]{2,1,0:T(8,128)(2,1)S(1)}, bf16[2,512,768]{2,1,0:T(8,128)(2,1)S(1)}, u32[]{:S(2)}, u32[]{:S(2)}) collective-permute-start(bf16[2,512,768]{2,1,0:T(8,128)(2,1)S(1)} %get-tuple-element.27), channel_id=1, source_target_pairs={{0,96},{1,25},{2,98},{3,27},{4,100},{5,29},{6,102},{7,31},{8,104},... | collective-permute-start | bytes 4718600 | tf_op jit(solution)/shard_map/ppermute | solution.py:46
  9.7 4.1 %shard_map.114 = (bf16[2,512,768]{2,1,0:T(8,128)(2,1)S(1)}, bf16[2,512,768]{2,1,0:T(8,128)(2,1)S(1)}) custom-call(s32[1]{0:T(128)} %bitcast.place_ref, f32[16]{0:T(128)} %table_ref.15, s32[768]{0:T(1024)} %sign_ref.15, bf16[256,256]{1,0:T(8,128)(2,1)} %constant.15.clone.hmat_ref, bf16[8192,768]{1,0:T(8,128)(2,1)} %bitcast.10, s32[3,8192]{1,0:T(4,128)} %index_ref.1, ...), custom_call_target="tpu_custom_call" | custom-call | tf_op jit(solution)/shard_map/pallas_call | solution.py:122
  13.9 2.7 %collective-permute-start.5 = (bf16[2,512,768]{2,1,0:T(8,128)(2,1)S(1)}, bf16[2,512,768]{2,1,0:T(8,128)(2,1)S(1)}, u32[]{:S(2)}, u32[]{:S(2)}) collective-permute-start(bf16[2,512,768]{2,1,0:T(8,128)(2,1)S(1)} %get-tuple-element.31), channel_id=1, source_target_pairs={{0,96},{1,25},{2,98},{3,27},{4,100},{5,29},{6,102},{7,31},{8,104},... | collective-permute-start | bytes 4718600 | tf_op jit(solution)/shard_map/ppermute | solution.py:46
  16.5 3.1 %shard_map.111 = (f32[512,768]{1,0:T(8,128)S(1)}, f32[512,768]{1,0:T(8,128)S(1)}, f32[512,768]{1,0:T(8,128)S(1)}, f32[8,128]{1,0:T(8,128)S(1)}) custom-call(f32[512,768]{1,0:T(8,128)} %refs_0_.1, f32[512,768]{1,0:T(8,128)} %refs_1_.6, f32[512,768]{1,0:T(8,128)} %refs_2_.3), custom_call_target="tpu_custom_call" | custom-call | tf_op jit(solution)/shard_map/pallas_call | solution.py:285
  19.6 8.0 %collective-permute-done.refs_3_ = bf16[2,512,768]{2,1,0:T(8,128)(2,1)S(1)} collective-permute-done((bf16[2,512,768]{2,1,0:T(8,128)(2,1)S(1)}, bf16[2,512,768]{2,1,0:T(8,128)(2,1)S(1)}, u32[]{:S(2)}, u32[]{:S(2)}) %collective-permute-start) | collective-permute-done | bytes 1572896 | tf_op jit(solution)/shard_map/ppermute | solution.py:46
  27.7 2.6 %shard_map.116 = (bf16[512,768]{1,0:T(8,128)(2,1)S(1)}, bf16[512,768]{1,0:T(8,128)(2,1)S(1)}) custom-call(s32[1]{0:T(128)} %bitcast.place_ref, f32[16]{0:T(128)} %table_ref.15, s32[768]{0:T(1024)} %sign_ref.15, bf16[256,256]{1,0:T(8,128)(2,1)} %constant.15.clone.hmat_ref, f32[8,128]{1,0:T(8,128)S(1)} %get-tuple-element.25.refs_0_, ...), custom_call_target="tpu_custom_call" | custom-call | tf_op jit(solution)/shard_map/pallas_call | solution.py:122
  31.3 1.9 %collective-permute-start.6 = (bf16[512,768]{1,0:T(8,128)(2,1)S(1)}, bf16[512,768]{1,0:T(8,128)(2,1)S(1)}, u32[]{:S(2)}, u32[]{:S(2)}) collective-permute-start(bf16[512,768]{1,0:T(8,128)(2,1)S(1)} %get-tuple-element.32), channel_id=1, source_target_pairs={{0,96},{1,25},{2,98},{3,27},{4,100},{5,29},{6,102},{7,31},{8,104},... | collective-permute-start | bytes 2359304 | tf_op jit(solution)/shard_map/ppermute | solution.py:46
  33.1 2.6 %shard_map.113 = (bf16[512,768]{1,0:T(8,128)(2,1)S(1)}, bf16[512,768]{1,0:T(8,128)(2,1)S(1)}) custom-call(s32[1]{0:T(128)} %bitcast.place_ref, f32[16]{0:T(128)} %table_ref.15, s32[768]{0:T(1024)} %sign_ref.15, bf16[256,256]{1,0:T(8,128)(2,1)} %constant.15.clone.hmat_ref, f32[8,128]{1,0:T(8,128)S(1)} %get-tuple-element.25.refs_0_, ...), custom_call_target="tpu_custom_call" | custom-call | tf_op jit(solution)/shard_map/pallas_call | solution.py:122
  35.8 8.7 %collective-permute-done.3.refs_3_.refs_7_ = bf16[2,512,768]{2,1,0:T(8,128)(2,1)S(1)} collective-permute-done((bf16[2,512,768]{2,1,0:T(8,128)(2,1)S(1)}, bf16[2,512,768]{2,1,0:T(8,128)(2,1)S(1)}, u32[]{:S(2)}, u32[]{:S(2)}) %collective-permute-start.3) | collective-permute-done | bytes 1572896 | tf_op jit(solution)/shard_map/ppermute | solution.py:46
  44.5 1.5 %collective-permute-start.2 = (bf16[512,768]{1,0:T(8,128)(2,1)S(1)}, bf16[512,768]{1,0:T(8,128)(2,1)S(1)}, u32[]{:S(2)}, u32[]{:S(2)}) collective-permute-start(bf16[512,768]{1,0:T(8,128)(2,1)S(1)} %get-tuple-element.28), channel_id=1, source_target_pairs={{0,96},{1,25},{2,98},{3,27},{4,100},{5,29},{6,102},{7,31},{8,104},... | collective-permute-start | bytes 2359304 | tf_op jit(solution)/shard_map/ppermute | solution.py:46
  46.0 7.0 %collective-permute-done.4.refs_2_ = bf16[512,768]{1,0:T(8,128)(2,1)S(1)} collective-permute-done((bf16[512,768]{1,0:T(8,128)(2,1)S(1)}, bf16[512,768]{1,0:T(8,128)(2,1)S(1)}, u32[]{:S(2)}, u32[]{:S(2)}) %collective-permute-start.4) | collective-permute-done | bytes 786464 | tf_op jit(solution)/shard_map/ppermute | solution.py:46
  53.0 2.8 %shard_map.117 = (bf16[512,768]{1,0:T(8,128)(2,1)S(1)}, bf16[512,768]{1,0:T(8,128)(2,1)S(1)}) custom-call(s32[1]{0:T(128)} %bitcast.place_ref, f32[16]{0:T(128)} %table_ref.15, s32[768]{0:T(1024)} %sign_ref.15, bf16[256,256]{1,0:T(8,128)(2,1)} %constant.15.clone.hmat_ref, bf16[8192,768]{1,0:T(8,128)(2,1)} %bitcast.16, s32[3,8192]{1,0:T(4,128)} %index_ref.1, ...), custom_call_target="tpu_custom_call" | custom-call | tf_op jit(solution)/shard_map/pallas_call | solution.py:122
  55.8 2.5 %collective-permute-start.7 = (bf16[512,768]{1,0:T(8,128)(2,1)S(1)}, bf16[512,768]{1,0:T(8,128)(2,1)S(1)}, u32[]{:S(2)}, u32[]{:S(2)}) collective-permute-start(bf16[512,768]{1,0:T(8,128)(2,1)S(1)} %get-tuple-element.33), channel_id=1, source_target_pairs={{0,16},{1,65},{2,18},{3,67},{4,20},{5,69},{6,22},{7,71},{8,24},{9,... | collective-permute-start | bytes 2359304 | tf_op jit(solution)/shard_map/ppermute | solution.py:46
  59.2 2.2 %collective-permute-done.8.refs_2_ = bf16[512,768]{1,0:T(8,128)(2,1)S(1)} collective-permute-done((bf16[512,768]{1,0:T(8,128)(2,1)S(1)}, bf16[512,768]{1,0:T(8,128)(2,1)S(1)}, u32[]{:S(2)}, u32[]{:S(2)}) %collective-permute-start.8) | collective-permute-done | bytes 786464 | tf_op jit(solution)/shard_map/ppermute | solution.py:46
  61.4 2.2 %shard_map.118 = bf16[512,768]{1,0:T(8,128)(2,1)S(1)} custom-call(s32[1]{0:T(128)} %bitcast.place_ref, f32[16]{0:T(128)} %table_ref.15, s32[768]{0:T(1024)} %sign_ref.15, bf16[256,256]{1,0:T(8,128)(2,1)} %constant.15.clone.hmat_ref, bf16[8192,768]{1,0:T(8,128)(2,1)} %bitcast.18, s32[3,8192]{1,0:T(4,128)} %index_ref.1, ...), custom_call_target="tpu_custom_call" | custom-call | tf_op jit(solution)/shard_map/pallas_call | solution.py:122
  64.5 2.1 %shard_map.115.own_ref = f32[512,768]{1,0:T(8,128)S(1)} custom-call(s32[1]{0:T(128)} %bitcast.place_ref, f32[16]{0:T(128)} %table_ref.15, s32[768]{0:T(1024)} %sign_ref.15, bf16[256,256]{1,0:T(8,128)(2,1)} %constant.15.clone.hmat_ref, bf16[8192,768]{1,0:T(8,128)(2,1)} %bitcast.19, s32[3,8192]{1,0:T(4,128)} %index_ref.1, ...), custom_call_target="tpu_custom_call" | custom-call | tf_op jit(solution)/shard_map/pallas_call | solution.py:122
  66.7 4.2 %collective-permute-done.7.two_ref = bf16[512,768]{1,0:T(8,128)(2,1)S(1)} collective-permute-done((bf16[512,768]{1,0:T(8,128)(2,1)S(1)}, bf16[512,768]{1,0:T(8,128)(2,1)S(1)}, u32[]{:S(2)}, u32[]{:S(2)}) %collective-permute-start.7) | collective-permute-done | bytes 786464 | tf_op jit(solution)/shard_map/ppermute | solution.py:46
  70.9 7.7 %collective-permute-done.10.three_ref = bf16[512,768]{1,0:T(8,128)(2,1)S(1)} collective-permute-done((bf16[512,768]{1,0:T(8,128)(2,1)S(1)}, bf16[512,768]{1,0:T(8,128)(2,1)S(1)}, u32[]{:S(2)}, u32[]{:S(2)}) %collective-permute-start.10) | collective-permute-done | bytes 786464 | tf_op jit(solution)/shard_map/ppermute | solution.py:46
  79.3 2.6 %shard_map.119 = (f32[512,768]{1,0:T(8,128)S(1)}, f32[128,128]{1,0:T(8,128)}) custom-call(s32[1]{0:T(128)} %bitcast.place_ref, f32[16]{0:T(128)} %table_ref.15, s32[768]{0:T(1024)} %sign_ref.15, bf16[256,256]{1,0:T(8,128)(2,1)} %constant.15.clone.hmat_ref, f32[512,768]{1,0:T(8,128)S(1)} %shard_map.115.own_ref, ...), custom_call_target="tpu_custom_call" | custom-call | tf_op jit(solution)/shard_map/pallas_call | solution.py:206
  81.9 18.5 %all_to_all.11 = f32[128,1,128]{2,1,0:T(1,128)S(1)} all-to-all(f32[128,1,128]{2,1,0:T(1,128)} %bitcast.20), channel_id=1, replica_groups=mesh['dp'=16,'fsdp'=8] {'dp','fsdp'}, dimensions={0} | all-to-all | bytes 131072 | tf_op jit(solution)/shard_map/all_to_all | solution.py:378
  100.4 1.8 %shard_map.121.refs_0_ = bf16[512,768]{1,0:T(8,128)(2,1)S(1)} custom-call(f32[128,128]{1,0:T(8,128)S(1)} %bitcast.6, f32[512,768]{1,0:T(8,128)S(1)} %get-tuple-element.37.plain_ref, f32[512,768]{1,0:T(8,128)S(1)} %get-tuple-element.38.master_ref, f32[512,768]{1,0:T(8,128)S(1)} %get-tuple-element.39.mean_ref, f32[512,768]{1,0:T(8,128)S(1)} %get-tuple-element.40.var_ref), custom_call_target="tpu_custom_call" | custom-call | tf_op jit(solution)/shard_map/pallas_call | solution.py:266
  106.0 2.9 %shard_map.120 = (f32[512,768]{1,0:T(8,128)}, f32[512,768]{1,0:T(8,128)}, f32[512,768]{1,0:T(8,128)}) custom-call(f32[128,128]{1,0:T(8,128)S(1)} %bitcast.7, f32[512,768]{1,0:T(8,128)S(1)} %get-tuple-element.37.plain_ref, f32[512,768]{1,0:T(8,128)S(1)} %get-tuple-element.38.master_ref, f32[512,768]{1,0:T(8,128)S(1)} %get-tuple-element.39.mean_ref, ...), custom_call_target="tpu_custom_call" | custom-call | tf_op jit(solution)/shard_map/pallas_call | solution.py:266
  108.9 5.5 %collective-permute-done.11.__0_ = bf16[512,768]{1,0:T(8,128)(2,1)S(1)} collective-permute-done((bf16[512,768]{1,0:T(8,128)(2,1)S(1)}, bf16[512,768]{1,0:T(8,128)(2,1)S(1)}, u32[]{:S(2)}, u32[]{:S(2)}) %collective-permute-start.11) | collective-permute-done | bytes 786464 | tf_op jit(solution)/shard_map/ppermute | solution.py:346
  114.4 2.1 %collective-permute-start.15 = (bf16[512,768]{1,0:T(8,128)(2,1)S(1)}, bf16[512,768]{1,0:T(8,128)(2,1)S(1)}, u32[]{:S(2)}, u32[]{:S(2)}) collective-permute-start(bf16[512,768]{1,0:T(8,128)(2,1)S(1)} %shard_map.122.refs_2_), channel_id=1, source_target_pairs={{0,1},{1,0},{2,3},{3,2},{4,5},{5,4},{6,7},{7,6},{8,9},{9,8},{10,11... | collective-permute-start | bytes 2359304 | tf_op jit(solution)/shard_map/ppermute | solution.py:350
  116.5 6.3 %collective-permute-done.14.refs_3_ = bf16[512,768]{1,0:T(8,128)(2,1)S(1)} collective-permute-done((bf16[512,768]{1,0:T(8,128)(2,1)S(1)}, bf16[512,768]{1,0:T(8,128)(2,1)S(1)}, u32[]{:S(2)}, u32[]{:S(2)}) %collective-permute-start.14) | collective-permute-done | bytes 786464 | tf_op jit(solution)/shard_map/ppermute | solution.py:346
  122.9 2.2 %collective-permute-start.17 = (bf16[256,768]{1,0:T(8,128)(2,1)S(1)}, bf16[256,768]{1,0:T(8,128)(2,1)S(1)}, u32[]{:S(2)}, u32[]{:S(2)}) collective-permute-start(bf16[256,768]{1,0:T(8,128)(2,1)S(1)} %get-tuple-element.46), channel_id=1, source_target_pairs={{0,1},{1,0},{2,3},{3,2},{4,5},{5,4},{6,7},{7,6},{8,9},{9,8},{10,11... | collective-permute-start | bytes 1179656 | tf_op jit(solution)/shard_map/ppermute | solution.py:350
  125.2 1.3 collective-permute-done.17.refs_6_
  127.0 2.4 %shard_map.123 = (bf16[512,6144]{1,0:T(8,128)(2,1)}, f32[8,128]{1,0:T(8,128)S(1)}) custom-call(bf16[512,768]{1,0:T(8,128)(2,1)S(1)} %shard_map.121.refs_0_, bf16[512,768]{1,0:T(8,128)(2,1)S(1)} %collective-permute-done.13.refs_1_, bf16[512,768]{1,0:T(8,128)(2,1)S(1)} %shard_map.122.refs_2_, bf16[512,768]{1,0:T(8,128)(2,1)S(1)} %collective-permute-done.14.refs_3_, ...), custom_call_target="tpu_custom_call" | custom-call | tf_op jit(solution)/shard_map/pallas_call | solution.py:332
  129.4 1.8 %collective-permute-done.12.__0_ = bf16[512,768]{1,0:T(8,128)(2,1)S(1)} collective-permute-done((bf16[512,768]{1,0:T(8,128)(2,1)S(1)}, bf16[512,768]{1,0:T(8,128)(2,1)S(1)}, u32[]{:S(2)}, u32[]{:S(2)}) %collective-permute-start.12) | collective-permute-done | bytes 786464 | tf_op jit(solution)/shard_map/ppermute | solution.py:346
  131.2 2.1 %collective-permute-start.18 = (bf16[512,768]{1,0:T(8,128)(2,1)S(1)}, bf16[512,768]{1,0:T(8,128)(2,1)S(1)}, u32[]{:S(2)}, u32[]{:S(2)}) collective-permute-start(bf16[512,768]{1,0:T(8,128)(2,1)S(1)} %shard_map.124.refs_0_), channel_id=1, source_target_pairs={{0,1},{1,0},{2,3},{3,2},{4,5},{5,4},{6,7},{7,6},{8,9},{9,8},{10,11... | collective-permute-start | bytes 2359304 | tf_op jit(solution)/shard_map/ppermute | solution.py:350
  (24 shorter events, 10.9 us)
Async XLA Ops:
  4.9 22.8 %collective-permute-start = (bf16[2,512,768]{2,1,0:T(8,128)(2,1)S(1)}, bf16[2,512,768]{2,1,0:T(8,128)(2,1)S(1)}, u32[]{:S(2)}, u32[]{:S(2)}) collective-permute-start(bf16[2,512,768]{2,1,0:T(8,128)(2,1)S(1)} %get-tuple-element.26), channel_id=1, source_target_pairs={{0,32},{1,9},{2,34},{3,11},{4,36},{5,13},{6,38},{7,15},{8,40},{9,1... | collective-permute-start | bytes 4718600 | tf_op jit(solution)/shard_map/ppermute | solution.py:46
  7.5 20.2 %collective-permute-start.1 = (bf16[2,512,768]{2,1,0:T(8,128)(2,1)S(1)}, bf16[2,512,768]{2,1,0:T(8,128)(2,1)S(1)}, u32[]{:S(2)}, u32[]{:S(2)}) collective-permute-start(bf16[2,512,768]{2,1,0:T(8,128)(2,1)S(1)} %get-tuple-element.27), channel_id=1, source_target_pairs={{0,96},{1,25},{2,98},{3,27},{4,100},{5,29},{6,102},{7,31},{8,104},... | collective-permute-start | bytes 4718600 | tf_op jit(solution)/shard_map/ppermute | solution.py:46
  13.8 30.7 %collective-permute-start.3 = (bf16[2,512,768]{2,1,0:T(8,128)(2,1)S(1)}, bf16[2,512,768]{2,1,0:T(8,128)(2,1)S(1)}, u32[]{:S(2)}, u32[]{:S(2)}) collective-permute-start(bf16[2,512,768]{2,1,0:T(8,128)(2,1)S(1)} %get-tuple-element.29), channel_id=1, source_target_pairs={{0,32},{1,9},{2,34},{3,11},{4,36},{5,13},{6,38},{7,15},{8,40},{9,1... | collective-permute-start | bytes 4718600 | tf_op jit(solution)/shard_map/ppermute | solution.py:46
  13.9 32.1 %collective-permute-start.5 = (bf16[2,512,768]{2,1,0:T(8,128)(2,1)S(1)}, bf16[2,512,768]{2,1,0:T(8,128)(2,1)S(1)}, u32[]{:S(2)}, u32[]{:S(2)}) collective-permute-start(bf16[2,512,768]{2,1,0:T(8,128)(2,1)S(1)} %get-tuple-element.31), channel_id=1, source_target_pairs={{0,96},{1,25},{2,98},{3,27},{4,100},{5,29},{6,102},{7,31},{8,104},... | collective-permute-start | bytes 4718600 | tf_op jit(solution)/shard_map/ppermute | solution.py:46
  30.3 22.6 %collective-permute-start.4 = (bf16[512,768]{1,0:T(8,128)(2,1)S(1)}, bf16[512,768]{1,0:T(8,128)(2,1)S(1)}, u32[]{:S(2)}, u32[]{:S(2)}) collective-permute-start(bf16[512,768]{1,0:T(8,128)(2,1)S(1)} %get-tuple-element.30), channel_id=1, source_target_pairs={{0,32},{1,9},{2,34},{3,11},{4,36},{5,13},{6,38},{7,15},{8,40},{9,1... | collective-permute-start | bytes 2359304 | tf_op jit(solution)/shard_map/ppermute | solution.py:46
  31.3 21.7 %collective-permute-start.6 = (bf16[512,768]{1,0:T(8,128)(2,1)S(1)}, bf16[512,768]{1,0:T(8,128)(2,1)S(1)}, u32[]{:S(2)}, u32[]{:S(2)}) collective-permute-start(bf16[512,768]{1,0:T(8,128)(2,1)S(1)} %get-tuple-element.32), channel_id=1, source_target_pairs={{0,96},{1,25},{2,98},{3,27},{4,100},{5,29},{6,102},{7,31},{8,104},... | collective-permute-start | bytes 2359304 | tf_op jit(solution)/shard_map/ppermute | solution.py:46
  35.7 25.7 %collective-permute-start.8 = (bf16[512,768]{1,0:T(8,128)(2,1)S(1)}, bf16[512,768]{1,0:T(8,128)(2,1)S(1)}, u32[]{:S(2)}, u32[]{:S(2)}) collective-permute-start(bf16[512,768]{1,0:T(8,128)(2,1)S(1)} %get-tuple-element.34), channel_id=1, source_target_pairs={{0,32},{1,9},{2,34},{3,11},{4,36},{5,13},{6,38},{7,15},{8,40},{9,1... | collective-permute-start | bytes 2359304 | tf_op jit(solution)/shard_map/ppermute | solution.py:46
  44.5 20.0 %collective-permute-start.2 = (bf16[512,768]{1,0:T(8,128)(2,1)S(1)}, bf16[512,768]{1,0:T(8,128)(2,1)S(1)}, u32[]{:S(2)}, u32[]{:S(2)}) collective-permute-start(bf16[512,768]{1,0:T(8,128)(2,1)S(1)} %get-tuple-element.28), channel_id=1, source_target_pairs={{0,96},{1,25},{2,98},{3,27},{4,100},{5,29},{6,102},{7,31},{8,104},... | collective-permute-start | bytes 2359304 | tf_op jit(solution)/shard_map/ppermute | solution.py:46
  55.8 15.1 %collective-permute-start.7 = (bf16[512,768]{1,0:T(8,128)(2,1)S(1)}, bf16[512,768]{1,0:T(8,128)(2,1)S(1)}, u32[]{:S(2)}, u32[]{:S(2)}) collective-permute-start(bf16[512,768]{1,0:T(8,128)(2,1)S(1)} %get-tuple-element.33), channel_id=1, source_target_pairs={{0,16},{1,65},{2,18},{3,67},{4,20},{5,69},{6,22},{7,71},{8,24},{9,... | collective-permute-start | bytes 2359304 | tf_op jit(solution)/shard_map/ppermute | solution.py:46
  58.3 20.3 %collective-permute-start.10 = (bf16[512,768]{1,0:T(8,128)(2,1)S(1)}, bf16[512,768]{1,0:T(8,128)(2,1)S(1)}, u32[]{:S(2)}, u32[]{:S(2)}) collective-permute-start(bf16[512,768]{1,0:T(8,128)(2,1)S(1)} %get-tuple-element.35), channel_id=1, source_target_pairs={{0,24},{1,97},{2,26},{3,99},{4,28},{5,101},{6,30},{7,103},{8,0},{9... | collective-permute-start | bytes 2359304 | tf_op jit(solution)/shard_map/ppermute | solution.py:46
  63.5 15.7 %collective-permute-start.9 = (bf16[512,768]{1,0:T(8,128)(2,1)S(1)}, bf16[512,768]{1,0:T(8,128)(2,1)S(1)}, u32[]{:S(2)}, u32[]{:S(2)}) collective-permute-start(bf16[512,768]{1,0:T(8,128)(2,1)S(1)} %shard_map.118), channel_id=1, source_target_pairs={{0,8},{1,33},{2,10},{3,35},{4,12},{5,37},{6,14},{7,39},{8,16},{9,4... | collective-permute-start | bytes 2359304 | tf_op jit(solution)/shard_map/ppermute | solution.py:46
  102.3 2.9 %collective-permute-start.13 = (bf16[512,768]{1,0:T(8,128)(2,1)S(1)}, bf16[512,768]{1,0:T(8,128)(2,1)S(1)}, u32[]{:S(2)}, u32[]{:S(2)}) collective-permute-start(bf16[512,768]{1,0:T(8,128)(2,1)S(1)} %shard_map.121.refs_0_), channel_id=1, source_target_pairs={{0,1},{1,0},{2,3},{3,2},{4,5},{5,4},{6,7},{7,6},{8,9},{9,8},{10,11... | collective-permute-start | bytes 2359304 | tf_op jit(solution)/shard_map/ppermute | solution.py:350
  103.3 11.1 %collective-permute-start.11 = (bf16[512,768]{1,0:T(8,128)(2,1)S(1)}, bf16[512,768]{1,0:T(8,128)(2,1)S(1)}, u32[]{:S(2)}, u32[]{:S(2)}) collective-permute-start(bf16[512,768]{1,0:T(8,128)(2,1)S(1)} %shard_map.121.refs_0_), channel_id=1, source_target_pairs={{0,2},{1,7},{2,4},{3,1},{4,6},{5,3},{6,0},{7,5},{8,10},{9,15},{10,... | collective-permute-start | bytes 2359304 | tf_op jit(solution)/shard_map/ppermute | solution.py:346
  105.2 17.6 %collective-permute-start.14 = (bf16[512,768]{1,0:T(8,128)(2,1)S(1)}, bf16[512,768]{1,0:T(8,128)(2,1)S(1)}, u32[]{:S(2)}, u32[]{:S(2)}) collective-permute-start(bf16[512,768]{1,0:T(8,128)(2,1)S(1)} %collective-permute-done.13.refs_1_), channel_id=1, source_target_pairs={{0,2},{1,7},{2,4},{3,1},{4,6},{5,3},{6,0},{7,5},{8,10},{9,15},{10,... | collective-permute-start | bytes 2359304 | tf_op jit(solution)/shard_map/ppermute | solution.py:346
  114.4 10.8 %collective-permute-start.15 = (bf16[512,768]{1,0:T(8,128)(2,1)S(1)}, bf16[512,768]{1,0:T(8,128)(2,1)S(1)}, u32[]{:S(2)}, u32[]{:S(2)}) collective-permute-start(bf16[512,768]{1,0:T(8,128)(2,1)S(1)} %shard_map.122.refs_2_), channel_id=1, source_target_pairs={{0,1},{1,0},{2,3},{3,2},{4,5},{5,4},{6,7},{7,6},{8,9},{9,8},{10,11... | collective-permute-start | bytes 2359304 | tf_op jit(solution)/shard_map/ppermute | solution.py:350
  116.5 14.7 %collective-permute-start.12 = (bf16[512,768]{1,0:T(8,128)(2,1)S(1)}, bf16[512,768]{1,0:T(8,128)(2,1)S(1)}, u32[]{:S(2)}, u32[]{:S(2)}) collective-permute-start(bf16[512,768]{1,0:T(8,128)(2,1)S(1)} %shard_map.122.refs_2_), channel_id=1, source_target_pairs={{0,2},{1,7},{2,4},{3,1},{4,6},{5,3},{6,0},{7,5},{8,10},{9,15},{10,... | collective-permute-start | bytes 2359304 | tf_op jit(solution)/shard_map/ppermute | solution.py:346
  122.9 3.6 %collective-permute-start.17 = (bf16[256,768]{1,0:T(8,128)(2,1)S(1)}, bf16[256,768]{1,0:T(8,128)(2,1)S(1)}, u32[]{:S(2)}, u32[]{:S(2)}) collective-permute-start(bf16[256,768]{1,0:T(8,128)(2,1)S(1)} %get-tuple-element.46), channel_id=1, source_target_pairs={{0,1},{1,0},{2,3},{3,2},{4,5},{5,4},{6,7},{7,6},{8,9},{9,8},{10,11... | collective-permute-start | bytes 1179656 | tf_op jit(solution)/shard_map/ppermute | solution.py:350
  125.1 1.9 %collective-permute-start.16 = (bf16[256,768]{1,0:T(8,128)(2,1)S(1)}, bf16[256,768]{1,0:T(8,128)(2,1)S(1)}, u32[]{:S(2)}, u32[]{:S(2)}) collective-permute-start(bf16[256,768]{1,0:T(8,128)(2,1)S(1)} %get-tuple-element.47), channel_id=1, source_target_pairs={{0,1},{1,0},{2,3},{3,2},{4,5},{5,4},{6,7},{7,6},{8,9},{9,8},{10,11... | collective-permute-start | bytes 1179656 | tf_op jit(solution)/shard_map/ppermute | solution.py:350
  131.2 4.1 %collective-permute-start.18 = (bf16[512,768]{1,0:T(8,128)(2,1)S(1)}, bf16[512,768]{1,0:T(8,128)(2,1)S(1)}, u32[]{:S(2)}, u32[]{:S(2)}) collective-permute-start(bf16[512,768]{1,0:T(8,128)(2,1)S(1)} %shard_map.124.refs_0_), channel_id=1, source_target_pairs={{0,1},{1,0},{2,3},{3,2},{4,5},{5,4},{6,7},{7,6},{8,9},{9,8},{10,11... | collective-permute-start | bytes 2359304 | tf_op jit(solution)/shard_map/ppermute | solution.py:350

commit v7 on v6

--- a/solution.py
+++ b/solution.py
@@ -65,9 +65,11 @@
     return jnp.concatenate([scale, ones], axis=0).T
 
 
-def encode_kernel(counts, ordered, place_ref, table_ref, sign_ref, hmat_ref, *refs):
+def encode_kernel(counts, targets, ordered, place_ref, table_ref, sign_ref, hmat_ref, *refs):
     jobs = len(counts)
-    inputs, out_refs = iter(refs[int(ordered) : -jobs]), refs[-jobs:]
+    outs = max(out for out, _ in targets) + 1
+    inputs, outs = iter(refs[int(ordered) : -outs]), refs[-outs:]
+    out_refs = [outs[out] if slot is None else outs[out].at[slot] for out, slot in targets]
     grad_refs, index_refs, arrived_refs = [], [], []
     for count in counts:
         grad_refs.append(next(inputs))
@@ -107,7 +109,7 @@
     if after is not None:
         in_specs.append(pl.BlockSpec((8, 128), lambda *_: (0, 0)))
         operands.append(after)
-    parts = BLOCK // PART
+    parts, targets = BLOCK // PART, []
     for near, far, arrived, spec, shape, dtype in jobs:
         rows = functools.partial(lambda near, far, i, j, place_ref: block_at(place_ref, near, far(i)) * parts + j, near, far)
         in_specs.append(pl.BlockSpec((PART, WIDTH), functools.partial(lambda rows, *at: (rows(*at), 0), rows)))
@@ -116,35 +118,33 @@
         for value, its_spec in arrived:
             in_specs.append(its_spec)
             operands.append(value)
-        out_specs.append(spec)
-        out_shape.append(jax.ShapeDtypeStruct(shape, dtype))
+        if spec is not None:
+            out_specs.append(spec)
+            out_shape.append(jax.ShapeDtypeStruct(shape, dtype))
+        targets.append((len(out_specs) - 1, None if len(shape) == 2 else int(spec is None)))
     blocks = len(jobs) * grid[0] * parts
     return pl.pallas_call(
-        functools.partial(encode_kernel, [len(job[2]) for job in jobs], after is not None),
+        functools.partial(encode_kernel, [len(job[2]) for job in jobs], targets, after is not None),
         out_shape=out_shape,
         grid_spec=pltpu.PrefetchScalarGridSpec(num_scalar_prefetch=1, grid=grid, in_specs=in_specs, out_specs=out_specs),
         compiler_params=pltpu.CompilerParams(vmem_limit_bytes=VMEM_BYTES),
         cost_estimate=pl.CostEstimate(flops=0, bytes_accessed=0, transcendentals=0),
     )(place, *operands)
-
-
-def paired(ring):
-    return lambda i: ring[0] + i * (ring[1] - ring[0])
 
 
 def reduce_scatter(place, table, sign, grad, index, hmat, staged):
     code = functools.partial(encode, place, table, sign, grad, index, hmat)
     pair = ((2, BLOCK, WIDTH), jnp.bfloat16)
-    both = pl.BlockSpec((None, PART, WIDTH), lambda i, j, place_ref: (i, j, 0))
-    grid = (2, BLOCK // PART)
+    both = pl.BlockSpec((2, PART, WIDTH), lambda i, j, place_ref: (0, j, 0))
 
     def round_of(*plan):
-        jobs = [(near, paired(ring), [(v, both) for v in arrived], both, *pair) for _, near, ring, arrived in plan]
-        codes = code(grid, jobs)
-        return [hop(v, "first", step) for v, (step, *_) in zip(codes, plan, strict=True)]
-
-    up_far, down_far = round_of((1, 2, RING0, ()), (-1, 2, RING1, ()))
-    up_own, down_own = round_of((1, 1, RING1, ()), (-1, 3, RING0, ()))
+        jobs = []
+        for _, near, ring in plan:
+            jobs += [(near, lambda i, far=far: far, (), spec, *pair) for far, spec in zip(ring, (both, None), strict=True)]
+        return [hop(v, "first", step) for v, (step, *_) in zip(code((1, BLOCK // PART), jobs), plan, strict=True)]
+
+    up_far, down_far = round_of((1, 2, RING0), (-1, 2, RING1))
+    up_own, down_own = round_of((1, 1, RING1), (-1, 3, RING0))
     single = pl.BlockSpec((PART, WIDTH), lambda i, j, place_ref: (j, 0))
     low = ((BLOCK, WIDTH), jnp.bfloat16)
 

time: 137 us -> 136 us (level)
  transfers between devices with their start and end apart: 19 -> 19, of which waited for: 14 -> 14; matrix products, arithmetic and copies ran while one was open for 0% -> 0% of each run, Pallas kernels for 19% -> 18%
where the time goes in v7:
time: 136 us
  waiting for transfers between devices  56.3 us (41%)
  Pallas kernels  34.1 us (25%)
  starting transfers between devices  26 us (19%)
  blocking collectives  18.6 us (14%)
    ppermute x11, waiting for transfers between devices, hop(): return lax.ppermute(value, ('dp', 'fsdp'), pairs)  39.2 us
    pallas_call x7, Pallas kernels, encode(): pl.pallas_call(functools.partial(encode_kernel, [len(job[2]) for job in j...  19.5 us
    all_to_all x1, blocking collectives, on_device(): square = lax.all_to_all(square, ('dp', 'fsdp'), 0, 0, tiled=True)  18.6 us
    ppermute x11, starting transfers between devices, hop(): return lax.ppermute(value, ('dp', 'fsdp'), pairs)  16.2 us
    ppermute x3, waiting for transfers between devices, along_y(): return lax.ppermute(value, 'fsdp', pairs)  13.2 us
    ppermute x5, starting transfers between devices, to_other_core(): return lax.ppermute(value, 'fsdp', [(i, i ^ 1) for i in range(8)])  8.12 us
    pallas_call x2, Pallas kernels, adamw(): pl.pallas_call(kernel, out_shape=out_shape, grid=(BLOCK // STEP,), in_spe...  4.76 us
    pallas_call x3, Pallas kernels, fill(): pl.pallas_call(functools.partial(fill_kernel, places, len(blocks) + len(g...  4.19 us
  transfers between devices with their start and end apart: 19, of which 14 were waited for; matrix products, arithmetic and copies ran while one was open for 0% of the time, Pallas kernels for 18%

profile of v7, /device:TPU:1, one launch (start us, length us, event | category | flops | bytes accessed | tf_op | source)
XLA Modules:
  0.0 136.0 jit_solution(4939401370476111777)
XLA Ops:
  0.6 3.7 %shard_map.112 = (bf16[2,512,768]{2,1,0:T(8,128)(2,1)S(1)}, bf16[2,512,768]{2,1,0:T(8,128)(2,1)S(1)}) custom-call(s32[1]{0:T(128)} %bitcast.place_ref, f32[16]{0:T(128)} %table_ref.15, s32[768]{0:T(1024)} %sign_ref.15, bf16[256,256]{1,0:T(8,128)(2,1)} %constant.15.clone.hmat_ref, bf16[8192,768]{1,0:T(8,128)(2,1)} %bitcast.8, s32[3,8192]{1,0:T(4,128)} %index_ref.1, ...), custom_call_target="tpu_custom_call" | custom-call | tf_op jit(solution)/shard_map/pallas_call | solution.py:126
  4.3 2.5 %collective-permute-start = (bf16[2,512,768]{2,1,0:T(8,128)(2,1)S(1)}, bf16[2,512,768]{2,1,0:T(8,128)(2,1)S(1)}, u32[]{:S(2)}, u32[]{:S(2)}) collective-permute-start(bf16[2,512,768]{2,1,0:T(8,128)(2,1)S(1)} %get-tuple-element.26), channel_id=1, source_target_pairs={{0,32},{1,9},{2,34},{3,11},{4,36},{5,13},{6,38},{7,15},{8,40},{9,1... | collective-permute-start | bytes 4718600 | tf_op jit(solution)/shard_map/ppermute | solution.py:46
  6.8 2.2 %collective-permute-start.1 = (bf16[2,512,768]{2,1,0:T(8,128)(2,1)S(1)}, bf16[2,512,768]{2,1,0:T(8,128)(2,1)S(1)}, u32[]{:S(2)}, u32[]{:S(2)}) collective-permute-start(bf16[2,512,768]{2,1,0:T(8,128)(2,1)S(1)} %get-tuple-element.27), channel_id=1, source_target_pairs={{0,96},{1,25},{2,98},{3,27},{4,100},{5,29},{6,102},{7,31},{8,104},... | collective-permute-start | bytes 4718600 | tf_op jit(solution)/shard_map/ppermute | solution.py:46
  9.1 3.5 %shard_map.114 = (bf16[2,512,768]{2,1,0:T(8,128)(2,1)S(1)}, bf16[2,512,768]{2,1,0:T(8,128)(2,1)S(1)}) custom-call(s32[1]{0:T(128)} %bitcast.place_ref, f32[16]{0:T(128)} %table_ref.15, s32[768]{0:T(1024)} %sign_ref.15, bf16[256,256]{1,0:T(8,128)(2,1)} %constant.15.clone.hmat_ref, bf16[8192,768]{1,0:T(8,128)(2,1)} %bitcast.12, s32[3,8192]{1,0:T(4,128)} %index_ref.1, ...), custom_call_target="tpu_custom_call" | custom-call | tf_op jit(solution)/shard_map/pallas_call | solution.py:126
  12.6 2.7 %collective-permute-start.5 = (bf16[2,512,768]{2,1,0:T(8,128)(2,1)S(1)}, bf16[2,512,768]{2,1,0:T(8,128)(2,1)S(1)}, u32[]{:S(2)}, u32[]{:S(2)}) collective-permute-start(bf16[2,512,768]{2,1,0:T(8,128)(2,1)S(1)} %get-tuple-element.31), channel_id=1, source_target_pairs={{0,96},{1,25},{2,98},{3,27},{4,100},{5,29},{6,102},{7,31},{8,104},... | collective-permute-start | bytes 4718600 | tf_op jit(solution)/shard_map/ppermute | solution.py:46
  15.3 3.1 %shard_map.111 = (f32[512,768]{1,0:T(8,128)S(1)}, f32[512,768]{1,0:T(8,128)S(1)}, f32[512,768]{1,0:T(8,128)S(1)}, f32[8,128]{1,0:T(8,128)S(1)}) custom-call(f32[512,768]{1,0:T(8,128)} %refs_0_.1, f32[512,768]{1,0:T(8,128)} %refs_1_.6, f32[512,768]{1,0:T(8,128)} %refs_2_.3), custom_call_target="tpu_custom_call" | custom-call | tf_op jit(solution)/shard_map/pallas_call | solution.py:285
  18.4 8.7 %collective-permute-done.refs_3_ = bf16[2,512,768]{2,1,0:T(8,128)(2,1)S(1)} collective-permute-done((bf16[2,512,768]{2,1,0:T(8,128)(2,1)S(1)}, bf16[2,512,768]{2,1,0:T(8,128)(2,1)S(1)}, u32[]{:S(2)}, u32[]{:S(2)}) %collective-permute-start) | collective-permute-done | bytes 1572896 | tf_op jit(solution)/shard_map/ppermute | solution.py:46
  27.1 2.6 %shard_map.116 = (bf16[512,768]{1,0:T(8,128)(2,1)S(1)}, bf16[512,768]{1,0:T(8,128)(2,1)S(1)}) custom-call(s32[1]{0:T(128)} %bitcast.place_ref, f32[16]{0:T(128)} %table_ref.15, s32[768]{0:T(1024)} %sign_ref.15, bf16[256,256]{1,0:T(8,128)(2,1)} %constant.15.clone.hmat_ref, f32[8,128]{1,0:T(8,128)S(1)} %get-tuple-element.25.refs_0_, ...), custom_call_target="tpu_custom_call" | custom-call | tf_op jit(solution)/shard_map/pallas_call | solution.py:126
  30.7 1.8 %collective-permute-start.6 = (bf16[512,768]{1,0:T(8,128)(2,1)S(1)}, bf16[512,768]{1,0:T(8,128)(2,1)S(1)}, u32[]{:S(2)}, u32[]{:S(2)}) collective-permute-start(bf16[512,768]{1,0:T(8,128)(2,1)S(1)} %get-tuple-element.32), channel_id=1, source_target_pairs={{0,96},{1,25},{2,98},{3,27},{4,100},{5,29},{6,102},{7,31},{8,104},... | collective-permute-start | bytes 2359304 | tf_op jit(solution)/shard_map/ppermute | solution.py:46
  32.5 2.6 %shard_map.113 = (bf16[512,768]{1,0:T(8,128)(2,1)S(1)}, bf16[512,768]{1,0:T(8,128)(2,1)S(1)}) custom-call(s32[1]{0:T(128)} %bitcast.place_ref, f32[16]{0:T(128)} %table_ref.15, s32[768]{0:T(1024)} %sign_ref.15, bf16[256,256]{1,0:T(8,128)(2,1)} %constant.15.clone.hmat_ref, f32[8,128]{1,0:T(8,128)S(1)} %get-tuple-element.25.refs_0_, ...), custom_call_target="tpu_custom_call" | custom-call | tf_op jit(solution)/shard_map/pallas_call | solution.py:126
  35.2 8.7 %collective-permute-done.3.refs_3_.refs_7_ = bf16[2,512,768]{2,1,0:T(8,128)(2,1)S(1)} collective-permute-done((bf16[2,512,768]{2,1,0:T(8,128)(2,1)S(1)}, bf16[2,512,768]{2,1,0:T(8,128)(2,1)S(1)}, u32[]{:S(2)}, u32[]{:S(2)}) %collective-permute-start.3) | collective-permute-done | bytes 1572896 | tf_op jit(solution)/shard_map/ppermute | solution.py:46
  43.9 1.5 %collective-permute-start.2 = (bf16[512,768]{1,0:T(8,128)(2,1)S(1)}, bf16[512,768]{1,0:T(8,128)(2,1)S(1)}, u32[]{:S(2)}, u32[]{:S(2)}) collective-permute-start(bf16[512,768]{1,0:T(8,128)(2,1)S(1)} %get-tuple-element.28), channel_id=1, source_target_pairs={{0,96},{1,25},{2,98},{3,27},{4,100},{5,29},{6,102},{7,31},{8,104},... | collective-permute-start | bytes 2359304 | tf_op jit(solution)/shard_map/ppermute | solution.py:46
  45.4 7.0 %collective-permute-done.4.refs_2_ = bf16[512,768]{1,0:T(8,128)(2,1)S(1)} collective-permute-done((bf16[512,768]{1,0:T(8,128)(2,1)S(1)}, bf16[512,768]{1,0:T(8,128)(2,1)S(1)}, u32[]{:S(2)}, u32[]{:S(2)}) %collective-permute-start.4) | collective-permute-done | bytes 786464 | tf_op jit(solution)/shard_map/ppermute | solution.py:46
  52.4 2.8 %shard_map.117 = (bf16[512,768]{1,0:T(8,128)(2,1)S(1)}, bf16[512,768]{1,0:T(8,128)(2,1)S(1)}) custom-call(s32[1]{0:T(128)} %bitcast.place_ref, f32[16]{0:T(128)} %table_ref.15, s32[768]{0:T(1024)} %sign_ref.15, bf16[256,256]{1,0:T(8,128)(2,1)} %constant.15.clone.hmat_ref, bf16[8192,768]{1,0:T(8,128)(2,1)} %bitcast.20, s32[3,8192]{1,0:T(4,128)} %index_ref.1, ...), custom_call_target="tpu_custom_call" | custom-call | tf_op jit(solution)/shard_map/pallas_call | solution.py:126
  55.2 2.5 %collective-permute-start.7 = (bf16[512,768]{1,0:T(8,128)(2,1)S(1)}, bf16[512,768]{1,0:T(8,128)(2,1)S(1)}, u32[]{:S(2)}, u32[]{:S(2)}) collective-permute-start(bf16[512,768]{1,0:T(8,128)(2,1)S(1)} %get-tuple-element.33), channel_id=1, source_target_pairs={{0,16},{1,65},{2,18},{3,67},{4,20},{5,69},{6,22},{7,71},{8,24},{9,... | collective-permute-start | bytes 2359304 | tf_op jit(solution)/shard_map/ppermute | solution.py:46
  58.6 2.2 %collective-permute-done.8.refs_2_ = bf16[512,768]{1,0:T(8,128)(2,1)S(1)} collective-permute-done((bf16[512,768]{1,0:T(8,128)(2,1)S(1)}, bf16[512,768]{1,0:T(8,128)(2,1)S(1)}, u32[]{:S(2)}, u32[]{:S(2)}) %collective-permute-start.8) | collective-permute-done | bytes 786464 | tf_op jit(solution)/shard_map/ppermute | solution.py:46
  60.8 2.2 %shard_map.118 = bf16[512,768]{1,0:T(8,128)(2,1)S(1)} custom-call(s32[1]{0:T(128)} %bitcast.place_ref, f32[16]{0:T(128)} %table_ref.15, s32[768]{0:T(1024)} %sign_ref.15, bf16[256,256]{1,0:T(8,128)(2,1)} %constant.15.clone.hmat_ref, bf16[8192,768]{1,0:T(8,128)(2,1)} %bitcast.22, s32[3,8192]{1,0:T(4,128)} %index_ref.1, ...), custom_call_target="tpu_custom_call" | custom-call | tf_op jit(solution)/shard_map/pallas_call | solution.py:126
  63.9 2.1 %shard_map.115.own_ref = f32[512,768]{1,0:T(8,128)S(1)} custom-call(s32[1]{0:T(128)} %bitcast.place_ref, f32[16]{0:T(128)} %table_ref.15, s32[768]{0:T(1024)} %sign_ref.15, bf16[256,256]{1,0:T(8,128)(2,1)} %constant.15.clone.hmat_ref, bf16[8192,768]{1,0:T(8,128)(2,1)} %bitcast.23, s32[3,8192]{1,0:T(4,128)} %index_ref.1, ...), custom_call_target="tpu_custom_call" | custom-call | tf_op jit(solution)/shard_map/pallas_call | solution.py:126
  66.1 4.2 %collective-permute-done.7.two_ref = bf16[512,768]{1,0:T(8,128)(2,1)S(1)} collective-permute-done((bf16[512,768]{1,0:T(8,128)(2,1)S(1)}, bf16[512,768]{1,0:T(8,128)(2,1)S(1)}, u32[]{:S(2)}, u32[]{:S(2)}) %collective-permute-start.7) | collective-permute-done | bytes 786464 | tf_op jit(solution)/shard_map/ppermute | solution.py:46
  70.3 7.8 %collective-permute-done.10.three_ref = bf16[512,768]{1,0:T(8,128)(2,1)S(1)} collective-permute-done((bf16[512,768]{1,0:T(8,128)(2,1)S(1)}, bf16[512,768]{1,0:T(8,128)(2,1)S(1)}, u32[]{:S(2)}, u32[]{:S(2)}) %collective-permute-start.10) | collective-permute-done | bytes 786464 | tf_op jit(solution)/shard_map/ppermute | solution.py:46
  78.6 2.6 %shard_map.119 = (f32[512,768]{1,0:T(8,128)S(1)}, f32[128,128]{1,0:T(8,128)}) custom-call(s32[1]{0:T(128)} %bitcast.place_ref, f32[16]{0:T(128)} %table_ref.15, s32[768]{0:T(1024)} %sign_ref.15, bf16[256,256]{1,0:T(8,128)(2,1)} %constant.15.clone.hmat_ref, f32[512,768]{1,0:T(8,128)S(1)} %shard_map.115.own_ref, ...), custom_call_target="tpu_custom_call" | custom-call | tf_op jit(solution)/shard_map/pallas_call | solution.py:206
  81.3 18.6 %all_to_all.11 = f32[128,1,128]{2,1,0:T(1,128)S(1)} all-to-all(f32[128,1,128]{2,1,0:T(1,128)} %bitcast.24), channel_id=1, replica_groups=mesh['dp'=16,'fsdp'=8] {'dp','fsdp'}, dimensions={0} | all-to-all | bytes 131072 | tf_op jit(solution)/shard_map/all_to_all | solution.py:378
  99.9 1.8 %shard_map.121.refs_0_ = bf16[512,768]{1,0:T(8,128)(2,1)S(1)} custom-call(f32[128,128]{1,0:T(8,128)S(1)} %bitcast.6, f32[512,768]{1,0:T(8,128)S(1)} %get-tuple-element.37.plain_ref, f32[512,768]{1,0:T(8,128)S(1)} %get-tuple-element.38.master_ref, f32[512,768]{1,0:T(8,128)S(1)} %get-tuple-element.39.mean_ref, f32[512,768]{1,0:T(8,128)S(1)} %get-tuple-element.40.var_ref), custom_call_target="tpu_custom_call" | custom-call | tf_op jit(solution)/shard_map/pallas_call | solution.py:266
  105.4 2.9 %shard_map.120 = (f32[512,768]{1,0:T(8,128)}, f32[512,768]{1,0:T(8,128)}, f32[512,768]{1,0:T(8,128)}) custom-call(f32[128,128]{1,0:T(8,128)S(1)} %bitcast.7, f32[512,768]{1,0:T(8,128)S(1)} %get-tuple-element.37.plain_ref, f32[512,768]{1,0:T(8,128)S(1)} %get-tuple-element.38.master_ref, f32[512,768]{1,0:T(8,128)S(1)} %get-tuple-element.39.mean_ref, ...), custom_call_target="tpu_custom_call" | custom-call | tf_op jit(solution)/shard_map/pallas_call | solution.py:266
  108.3 5.5 %collective-permute-done.11.__0_ = bf16[512,768]{1,0:T(8,128)(2,1)S(1)} collective-permute-done((bf16[512,768]{1,0:T(8,128)(2,1)S(1)}, bf16[512,768]{1,0:T(8,128)(2,1)S(1)}, u32[]{:S(2)}, u32[]{:S(2)}) %collective-permute-start.11) | collective-permute-done | bytes 786464 | tf_op jit(solution)/shard_map/ppermute | solution.py:346
  113.8 2.3 %collective-permute-start.15 = (bf16[512,768]{1,0:T(8,128)(2,1)S(1)}, bf16[512,768]{1,0:T(8,128)(2,1)S(1)}, u32[]{:S(2)}, u32[]{:S(2)}) collective-permute-start(bf16[512,768]{1,0:T(8,128)(2,1)S(1)} %shard_map.122.refs_2_), channel_id=1, source_target_pairs={{0,1},{1,0},{2,3},{3,2},{4,5},{5,4},{6,7},{7,6},{8,9},{9,8},{10,11... | collective-permute-start | bytes 2359304 | tf_op jit(solution)/shard_map/ppermute | solution.py:350
  116.1 6.1 %collective-permute-done.14.refs_3_ = bf16[512,768]{1,0:T(8,128)(2,1)S(1)} collective-permute-done((bf16[512,768]{1,0:T(8,128)(2,1)S(1)}, bf16[512,768]{1,0:T(8,128)(2,1)S(1)}, u32[]{:S(2)}, u32[]{:S(2)}) %collective-permute-start.14) | collective-permute-done | bytes 786464 | tf_op jit(solution)/shard_map/ppermute | solution.py:346
  122.3 2.4 %collective-permute-start.17 = (bf16[256,768]{1,0:T(8,128)(2,1)S(1)}, bf16[256,768]{1,0:T(8,128)(2,1)S(1)}, u32[]{:S(2)}, u32[]{:S(2)}) collective-permute-start(bf16[256,768]{1,0:T(8,128)(2,1)S(1)} %get-tuple-element.46), channel_id=1, source_target_pairs={{0,1},{1,0},{2,3},{3,2},{4,5},{5,4},{6,7},{7,6},{8,9},{9,8},{10,11... | collective-permute-start | bytes 1179656 | tf_op jit(solution)/shard_map/ppermute | solution.py:350
  124.8 1.3 collective-permute-done.17.refs_6_
  126.6 2.4 %shard_map.123 = (bf16[512,6144]{1,0:T(8,128)(2,1)}, f32[8,128]{1,0:T(8,128)S(1)}) custom-call(bf16[512,768]{1,0:T(8,128)(2,1)S(1)} %shard_map.121.refs_0_, bf16[512,768]{1,0:T(8,128)(2,1)S(1)} %collective-permute-done.13.refs_1_, bf16[512,768]{1,0:T(8,128)(2,1)S(1)} %shard_map.122.refs_2_, bf16[512,768]{1,0:T(8,128)(2,1)S(1)} %collective-permute-done.14.refs_3_, ...), custom_call_target="tpu_custom_call" | custom-call | tf_op jit(solution)/shard_map/pallas_call | solution.py:332
  129.0 1.7 %collective-permute-done.12.__0_ = bf16[512,768]{1,0:T(8,128)(2,1)S(1)} collective-permute-done((bf16[512,768]{1,0:T(8,128)(2,1)S(1)}, bf16[512,768]{1,0:T(8,128)(2,1)S(1)}, u32[]{:S(2)}, u32[]{:S(2)}) %collective-permute-start.12) | collective-permute-done | bytes 786464 | tf_op jit(solution)/shard_map/ppermute | solution.py:346
  130.6 2.3 %collective-permute-start.18 = (bf16[512,768]{1,0:T(8,128)(2,1)S(1)}, bf16[512,768]{1,0:T(8,128)(2,1)S(1)}, u32[]{:S(2)}, u32[]{:S(2)}) collective-permute-start(bf16[512,768]{1,0:T(8,128)(2,1)S(1)} %shard_map.124.refs_0_), channel_id=1, source_target_pairs={{0,1},{1,0},{2,3},{3,2},{4,5},{5,4},{6,7},{7,6},{8,9},{9,8},{10,11... | collective-permute-start | bytes 2359304 | tf_op jit(solution)/shard_map/ppermute | solution.py:350
  (24 shorter events, 10.8 us)
Async XLA Ops:
  4.3 22.8 %collective-permute-start = (bf16[2,512,768]{2,1,0:T(8,128)(2,1)S(1)}, bf16[2,512,768]{2,1,0:T(8,128)(2,1)S(1)}, u32[]{:S(2)}, u32[]{:S(2)}) collective-permute-start(bf16[2,512,768]{2,1,0:T(8,128)(2,1)S(1)} %get-tuple-element.26), channel_id=1, source_target_pairs={{0,32},{1,9},{2,34},{3,11},{4,36},{5,13},{6,38},{7,15},{8,40},{9,1... | collective-permute-start | bytes 4718600 | tf_op jit(solution)/shard_map/ppermute | solution.py:46
  6.8 20.2 %collective-permute-start.1 = (bf16[2,512,768]{2,1,0:T(8,128)(2,1)S(1)}, bf16[2,512,768]{2,1,0:T(8,128)(2,1)S(1)}, u32[]{:S(2)}, u32[]{:S(2)}) collective-permute-start(bf16[2,512,768]{2,1,0:T(8,128)(2,1)S(1)} %get-tuple-element.27), channel_id=1, source_target_pairs={{0,96},{1,25},{2,98},{3,27},{4,100},{5,29},{6,102},{7,31},{8,104},... | collective-permute-start | bytes 4718600 | tf_op jit(solution)/shard_map/ppermute | solution.py:46
  12.5 31.4 %collective-permute-start.3 = (bf16[2,512,768]{2,1,0:T(8,128)(2,1)S(1)}, bf16[2,512,768]{2,1,0:T(8,128)(2,1)S(1)}, u32[]{:S(2)}, u32[]{:S(2)}) collective-permute-start(bf16[2,512,768]{2,1,0:T(8,128)(2,1)S(1)} %get-tuple-element.29), channel_id=1, source_target_pairs={{0,32},{1,9},{2,34},{3,11},{4,36},{5,13},{6,38},{7,15},{8,40},{9,1... | collective-permute-start | bytes 4718600 | tf_op jit(solution)/shard_map/ppermute | solution.py:46
  12.6 32.8 %collective-permute-start.5 = (bf16[2,512,768]{2,1,0:T(8,128)(2,1)S(1)}, bf16[2,512,768]{2,1,0:T(8,128)(2,1)S(1)}, u32[]{:S(2)}, u32[]{:S(2)}) collective-permute-start(bf16[2,512,768]{2,1,0:T(8,128)(2,1)S(1)} %get-tuple-element.31), channel_id=1, source_target_pairs={{0,96},{1,25},{2,98},{3,27},{4,100},{5,29},{6,102},{7,31},{8,104},... | collective-permute-start | bytes 4718600 | tf_op jit(solution)/shard_map/ppermute | solution.py:46
  29.7 22.6 %collective-permute-start.4 = (bf16[512,768]{1,0:T(8,128)(2,1)S(1)}, bf16[512,768]{1,0:T(8,128)(2,1)S(1)}, u32[]{:S(2)}, u32[]{:S(2)}) collective-permute-start(bf16[512,768]{1,0:T(8,128)(2,1)S(1)} %get-tuple-element.30), channel_id=1, source_target_pairs={{0,32},{1,9},{2,34},{3,11},{4,36},{5,13},{6,38},{7,15},{8,40},{9,1... | collective-permute-start | bytes 2359304 | tf_op jit(solution)/shard_map/ppermute | solution.py:46
  30.7 21.7 %collective-permute-start.6 = (bf16[512,768]{1,0:T(8,128)(2,1)S(1)}, bf16[512,768]{1,0:T(8,128)(2,1)S(1)}, u32[]{:S(2)}, u32[]{:S(2)}) collective-permute-start(bf16[512,768]{1,0:T(8,128)(2,1)S(1)} %get-tuple-element.32), channel_id=1, source_target_pairs={{0,96},{1,25},{2,98},{3,27},{4,100},{5,29},{6,102},{7,31},{8,104},... | collective-permute-start | bytes 2359304 | tf_op jit(solution)/shard_map/ppermute | solution.py:46
  35.1 25.7 %collective-permute-start.8 = (bf16[512,768]{1,0:T(8,128)(2,1)S(1)}, bf16[512,768]{1,0:T(8,128)(2,1)S(1)}, u32[]{:S(2)}, u32[]{:S(2)}) collective-permute-start(bf16[512,768]{1,0:T(8,128)(2,1)S(1)} %get-tuple-element.34), channel_id=1, source_target_pairs={{0,32},{1,9},{2,34},{3,11},{4,36},{5,13},{6,38},{7,15},{8,40},{9,1... | collective-permute-start | bytes 2359304 | tf_op jit(solution)/shard_map/ppermute | solution.py:46
  43.9 20.0 %collective-permute-start.2 = (bf16[512,768]{1,0:T(8,128)(2,1)S(1)}, bf16[512,768]{1,0:T(8,128)(2,1)S(1)}, u32[]{:S(2)}, u32[]{:S(2)}) collective-permute-start(bf16[512,768]{1,0:T(8,128)(2,1)S(1)} %get-tuple-element.28), channel_id=1, source_target_pairs={{0,96},{1,25},{2,98},{3,27},{4,100},{5,29},{6,102},{7,31},{8,104},... | collective-permute-start | bytes 2359304 | tf_op jit(solution)/shard_map/ppermute | solution.py:46
  55.2 15.1 %collective-permute-start.7 = (bf16[512,768]{1,0:T(8,128)(2,1)S(1)}, bf16[512,768]{1,0:T(8,128)(2,1)S(1)}, u32[]{:S(2)}, u32[]{:S(2)}) collective-permute-start(bf16[512,768]{1,0:T(8,128)(2,1)S(1)} %get-tuple-element.33), channel_id=1, source_target_pairs={{0,16},{1,65},{2,18},{3,67},{4,20},{5,69},{6,22},{7,71},{8,24},{9,... | collective-permute-start | bytes 2359304 | tf_op jit(solution)/shard_map/ppermute | solution.py:46
  57.7 20.3 %collective-permute-start.10 = (bf16[512,768]{1,0:T(8,128)(2,1)S(1)}, bf16[512,768]{1,0:T(8,128)(2,1)S(1)}, u32[]{:S(2)}, u32[]{:S(2)}) collective-permute-start(bf16[512,768]{1,0:T(8,128)(2,1)S(1)} %get-tuple-element.35), channel_id=1, source_target_pairs={{0,24},{1,97},{2,26},{3,99},{4,28},{5,101},{6,30},{7,103},{8,0},{9... | collective-permute-start | bytes 2359304 | tf_op jit(solution)/shard_map/ppermute | solution.py:46
  62.9 15.7 %collective-permute-start.9 = (bf16[512,768]{1,0:T(8,128)(2,1)S(1)}, bf16[512,768]{1,0:T(8,128)(2,1)S(1)}, u32[]{:S(2)}, u32[]{:S(2)}) collective-permute-start(bf16[512,768]{1,0:T(8,128)(2,1)S(1)} %shard_map.118), channel_id=1, source_target_pairs={{0,8},{1,33},{2,10},{3,35},{4,12},{5,37},{6,14},{7,39},{8,16},{9,4... | collective-permute-start | bytes 2359304 | tf_op jit(solution)/shard_map/ppermute | solution.py:46
  101.7 2.9 %collective-permute-start.13 = (bf16[512,768]{1,0:T(8,128)(2,1)S(1)}, bf16[512,768]{1,0:T(8,128)(2,1)S(1)}, u32[]{:S(2)}, u32[]{:S(2)}) collective-permute-start(bf16[512,768]{1,0:T(8,128)(2,1)S(1)} %shard_map.121.refs_0_), channel_id=1, source_target_pairs={{0,1},{1,0},{2,3},{3,2},{4,5},{5,4},{6,7},{7,6},{8,9},{9,8},{10,11... | collective-permute-start | bytes 2359304 | tf_op jit(solution)/shard_map/ppermute | solution.py:350
  102.7 11.1 %collective-permute-start.11 = (bf16[512,768]{1,0:T(8,128)(2,1)S(1)}, bf16[512,768]{1,0:T(8,128)(2,1)S(1)}, u32[]{:S(2)}, u32[]{:S(2)}) collective-permute-start(bf16[512,768]{1,0:T(8,128)(2,1)S(1)} %shard_map.121.refs_0_), channel_id=1, source_target_pairs={{0,2},{1,7},{2,4},{3,1},{4,6},{5,3},{6,0},{7,5},{8,10},{9,15},{10,... | collective-permute-start | bytes 2359304 | tf_op jit(solution)/shard_map/ppermute | solution.py:346
  104.6 17.6 %collective-permute-start.14 = (bf16[512,768]{1,0:T(8,128)(2,1)S(1)}, bf16[512,768]{1,0:T(8,128)(2,1)S(1)}, u32[]{:S(2)}, u32[]{:S(2)}) collective-permute-start(bf16[512,768]{1,0:T(8,128)(2,1)S(1)} %collective-permute-done.13.refs_1_), channel_id=1, source_target_pairs={{0,2},{1,7},{2,4},{3,1},{4,6},{5,3},{6,0},{7,5},{8,10},{9,15},{10,... | collective-permute-start | bytes 2359304 | tf_op jit(solution)/shard_map/ppermute | solution.py:346
  113.8 11.0 %collective-permute-start.15 = (bf16[512,768]{1,0:T(8,128)(2,1)S(1)}, bf16[512,768]{1,0:T(8,128)(2,1)S(1)}, u32[]{:S(2)}, u32[]{:S(2)}) collective-permute-start(bf16[512,768]{1,0:T(8,128)(2,1)S(1)} %shard_map.122.refs_2_), channel_id=1, source_target_pairs={{0,1},{1,0},{2,3},{3,2},{4,5},{5,4},{6,7},{7,6},{8,9},{9,8},{10,11... | collective-permute-start | bytes 2359304 | tf_op jit(solution)/shard_map/ppermute | solution.py:350
  116.1 14.5 %collective-permute-start.12 = (bf16[512,768]{1,0:T(8,128)(2,1)S(1)}, bf16[512,768]{1,0:T(8,128)(2,1)S(1)}, u32[]{:S(2)}, u32[]{:S(2)}) collective-permute-start(bf16[512,768]{1,0:T(8,128)(2,1)S(1)} %shard_map.122.refs_2_), channel_id=1, source_target_pairs={{0,2},{1,7},{2,4},{3,1},{4,6},{5,3},{6,0},{7,5},{8,10},{9,15},{10,... | collective-permute-start | bytes 2359304 | tf_op jit(solution)/shard_map/ppermute | solution.py:346
  122.3 3.8 %collective-permute-start.17 = (bf16[256,768]{1,0:T(8,128)(2,1)S(1)}, bf16[256,768]{1,0:T(8,128)(2,1)S(1)}, u32[]{:S(2)}, u32[]{:S(2)}) collective-permute-start(bf16[256,768]{1,0:T(8,128)(2,1)S(1)} %get-tuple-element.46), channel_id=1, source_target_pairs={{0,1},{1,0},{2,3},{3,2},{4,5},{5,4},{6,7},{7,6},{8,9},{9,8},{10,11... | collective-permute-start | bytes 1179656 | tf_op jit(solution)/shard_map/ppermute | solution.py:350
  124.7 1.9 %collective-permute-start.16 = (bf16[256,768]{1,0:T(8,128)(2,1)S(1)}, bf16[256,768]{1,0:T(8,128)(2,1)S(1)}, u32[]{:S(2)}, u32[]{:S(2)}) collective-permute-start(bf16[256,768]{1,0:T(8,128)(2,1)S(1)} %get-tuple-element.47), channel_id=1, source_target_pairs={{0,1},{1,0},{2,3},{3,2},{4,5},{5,4},{6,7},{7,6},{8,9},{9,8},{10,11... | collective-permute-start | bytes 1179656 | tf_op jit(solution)/shard_map/ppermute | solution.py:350
  130.6 4.2 %collective-permute-start.18 = (bf16[512,768]{1,0:T(8,128)(2,1)S(1)}, bf16[512,768]{1,0:T(8,128)(2,1)S(1)}, u32[]{:S(2)}, u32[]{:S(2)}) collective-permute-start(bf16[512,768]{1,0:T(8,128)(2,1)S(1)} %shard_map.124.refs_0_), channel_id=1, source_target_pairs={{0,1},{1,0},{2,3},{3,2},{4,5},{5,4},{6,7},{7,6},{8,9},{9,8},{10,11... | collective-permute-start | bytes 2359304 | tf_op jit(solution)/shard_map/ppermute | solution.py:350

commit v8 on v7

--- a/solution.py
+++ b/solution.py
@@ -19,6 +19,7 @@
 BLOCK = 512
 PART = 256
 STEP = 128
+ROOT_STEPS = 1450.0
 CUTS = 4
 RING0, RING1 = (2, 1), (3, 0)
 LIMIT = 4.0 * math.sqrt(ROWS * D)
@@ -63,6 +64,16 @@
         scale = 1.0 / (math.sqrt(TILE) * scale)
     ones = jnp.ones((8 - index.shape[0], index.shape[1]), jnp.float32)
     return jnp.concatenate([scale, ones], axis=0).T
+
+
+def to_root(value):
+    root = value * lax.rsqrt(jnp.maximum(jnp.abs(value), 1e-30)) * ROOT_STEPS
+    return (root + jnp.where(root < 0, -0.5, 0.5)).astype(jnp.int32).astype(jnp.int16)
+
+
+def from_root(root):
+    root = root.astype(jnp.int32).astype(jnp.float32)
+    return root * jnp.abs(root) * (1.0 / ROOT_STEPS**2)
 
 
 def encode_kernel(counts, targets, ordered, place_ref, table_ref, sign_ref, hmat_ref, *refs):
@@ -88,7 +99,7 @@
                 total = code.astype(jnp.float32)
                 for ref in arrived_refs[job]:
                     total = total + ref[:, cols].astype(jnp.float32)
-                code = total.astype(out_refs[job].dtype)
+                code = to_root(total) if out_refs[job].dtype == jnp.int16 else total.astype(out_refs[job].dtype)
             out_refs[job][:, cols] = code
 
 
@@ -160,7 +171,7 @@
         plan, jobs = [], []
         for ring, whole in rings:
             far, part = (RING0[slot], down_own) if ring == 0 else (RING1[slot], up_own)
-            shape = low if far else ((BLOCK, WIDTH), jnp.float32)
+            shape = ((BLOCK, WIDTH), jnp.int16 if far else jnp.float32)
             jobs.append((0, lambda i, far=far: far, [(whole, single), (part, of_slot(slot))], single, *shape))
             plan.append(far)
         values = code((1, BLOCK // PART), jobs)
@@ -186,7 +197,7 @@
     square = sum_ref[...]
     for tile in range(TILES):
         cols = slice(tile * TILE, (tile + 1) * TILE)
-        value = own_ref[:, cols] + two_ref[:, cols].astype(f32) + one_ref[:, cols].astype(f32) + three_ref[:, cols].astype(f32)
+        value = own_ref[:, cols] + from_root(two_ref[:, cols]) + from_root(one_ref[:, cols]) + from_root(three_ref[:, cols])
         plain = jnp.zeros(value.shape, f32)
         for _ in range(3):
             piece = value.astype(jnp.bfloat16)

time: 136 us -> 138 us (1.015)
  Pallas kernels: 34.1 us -> 36.3 us
    pallas_call x7, Pallas kernels: 19.5 us -> 21 us  [encode(): pl.pallas_call(functools.partial(encode_kernel, [len(job[2]) for job in j...]
    ppermute x11, waiting for transfers between devices: 39.2 us -> 37.7 us  [hop(): return lax.ppermute(value, ('dp', 'fsdp'), pairs)]
  transfers between devices with their start and end apart: 19 -> 19, of which waited for: 14 -> 14; matrix products, arithmetic and copies ran while one was open for 0% -> 0% of each run, Pallas kernels for 18% -> 19%
where the time goes in v8:
time: 138 us; the launch traced here: 137 us
  waiting for transfers between devices  55.1 us (40%)
  Pallas kernels  36.3 us (26%)
  starting transfers between devices  25.5 us (18%)
  blocking collectives  19.6 us (14%)
    ppermute x11, waiting for transfers between devices, hop(): return lax.ppermute(value, ('dp', 'fsdp'), pairs)  37.7 us
    pallas_call x7, Pallas kernels, encode(): pl.pallas_call(functools.partial(encode_kernel, [len(job[2]) for job in j...  21 us
    all_to_all x1, blocking collectives, on_device(): square = lax.all_to_all(square, ('dp', 'fsdp'), 0, 0, tiled=True)  19.6 us
    ppermute x11, starting transfers between devices, hop(): return lax.ppermute(value, ('dp', 'fsdp'), pairs)  16.2 us
    ppermute x3, waiting for transfers between devices, along_y(): return lax.ppermute(value, 'fsdp', pairs)  13.6 us
    ppermute x5, starting transfers between devices, to_other_core(): return lax.ppermute(value, 'fsdp', [(i, i ^ 1) for i in range(8)])  7.58 us
    pallas_call x2, Pallas kernels, adamw(): pl.pallas_call(kernel, out_shape=out_shape, grid=(BLOCK // STEP,), in_spe...  4.76 us
    pallas_call x3, Pallas kernels, fill(): pl.pallas_call(functools.partial(fill_kernel, places, len(blocks) + len(g...  4.19 us
  transfers between devices with their start and end apart: 19, of which 14 were waited for; matrix products, arithmetic and copies ran while one was open for 0% of the time, Pallas kernels for 19%

profile of v8, /device:TPU:1, one launch (start us, length us, event | category | flops | bytes accessed | tf_op | source)
XLA Modules:
  0.0 137.4 jit_solution(353036522957531038)
XLA Ops:
  0.6 3.7 %shard_map.112 = (bf16[2,512,768]{2,1,0:T(8,128)(2,1)S(1)}, bf16[2,512,768]{2,1,0:T(8,128)(2,1)S(1)}) custom-call(s32[1]{0:T(128)} %bitcast.place_ref, f32[16]{0:T(128)} %table_ref.15, s32[768]{0:T(1024)} %sign_ref.15, bf16[256,256]{1,0:T(8,128)(2,1)} %constant.15.clone.hmat_ref, bf16[8192,768]{1,0:T(8,128)(2,1)} %bitcast.8, s32[3,8192]{1,0:T(4,128)} %index_ref.1, ...), custom_call_target="tpu_custom_call" | custom-call | tf_op jit(solution)/shard_map/pallas_call | solution.py:137
  4.3 2.5 %collective-permute-start = (bf16[2,512,768]{2,1,0:T(8,128)(2,1)S(1)}, bf16[2,512,768]{2,1,0:T(8,128)(2,1)S(1)}, u32[]{:S(2)}, u32[]{:S(2)}) collective-permute-start(bf16[2,512,768]{2,1,0:T(8,128)(2,1)S(1)} %get-tuple-element.26), channel_id=1, source_target_pairs={{0,32},{1,9},{2,34},{3,11},{4,36},{5,13},{6,38},{7,15},{8,40},{9,1... | collective-permute-start | bytes 4718600 | tf_op jit(solution)/shard_map/ppermute | solution.py:47
  6.8 2.2 %collective-permute-start.1 = (bf16[2,512,768]{2,1,0:T(8,128)(2,1)S(1)}, bf16[2,512,768]{2,1,0:T(8,128)(2,1)S(1)}, u32[]{:S(2)}, u32[]{:S(2)}) collective-permute-start(bf16[2,512,768]{2,1,0:T(8,128)(2,1)S(1)} %get-tuple-element.27), channel_id=1, source_target_pairs={{0,96},{1,25},{2,98},{3,27},{4,100},{5,29},{6,102},{7,31},{8,104},... | collective-permute-start | bytes 4718600 | tf_op jit(solution)/shard_map/ppermute | solution.py:47
  9.1 3.5 %shard_map.114 = (bf16[2,512,768]{2,1,0:T(8,128)(2,1)S(1)}, bf16[2,512,768]{2,1,0:T(8,128)(2,1)S(1)}) custom-call(s32[1]{0:T(128)} %bitcast.place_ref, f32[16]{0:T(128)} %table_ref.15, s32[768]{0:T(1024)} %sign_ref.15, bf16[256,256]{1,0:T(8,128)(2,1)} %constant.15.clone.hmat_ref, bf16[8192,768]{1,0:T(8,128)(2,1)} %bitcast.12, s32[3,8192]{1,0:T(4,128)} %index_ref.1, ...), custom_call_target="tpu_custom_call" | custom-call | tf_op jit(solution)/shard_map/pallas_call | solution.py:137
  12.6 2.7 %collective-permute-start.5 = (bf16[2,512,768]{2,1,0:T(8,128)(2,1)S(1)}, bf16[2,512,768]{2,1,0:T(8,128)(2,1)S(1)}, u32[]{:S(2)}, u32[]{:S(2)}) collective-permute-start(bf16[2,512,768]{2,1,0:T(8,128)(2,1)S(1)} %get-tuple-element.31), channel_id=1, source_target_pairs={{0,96},{1,25},{2,98},{3,27},{4,100},{5,29},{6,102},{7,31},{8,104},... | collective-permute-start | bytes 4718600 | tf_op jit(solution)/shard_map/ppermute | solution.py:47
  15.3 3.1 %shard_map.111 = (f32[512,768]{1,0:T(8,128)S(1)}, f32[512,768]{1,0:T(8,128)S(1)}, f32[512,768]{1,0:T(8,128)S(1)}, f32[8,128]{1,0:T(8,128)S(1)}) custom-call(f32[512,768]{1,0:T(8,128)} %refs_0_.1, f32[512,768]{1,0:T(8,128)} %refs_1_.6, f32[512,768]{1,0:T(8,128)} %refs_2_.3), custom_call_target="tpu_custom_call" | custom-call | tf_op jit(solution)/shard_map/pallas_call | solution.py:296
  18.4 8.7 %collective-permute-done.refs_3_ = bf16[2,512,768]{2,1,0:T(8,128)(2,1)S(1)} collective-permute-done((bf16[2,512,768]{2,1,0:T(8,128)(2,1)S(1)}, bf16[2,512,768]{2,1,0:T(8,128)(2,1)S(1)}, u32[]{:S(2)}, u32[]{:S(2)}) %collective-permute-start) | collective-permute-done | bytes 1572896 | tf_op jit(solution)/shard_map/ppermute | solution.py:47
  27.1 2.6 %shard_map.116 = (bf16[512,768]{1,0:T(8,128)(2,1)S(1)}, bf16[512,768]{1,0:T(8,128)(2,1)S(1)}) custom-call(s32[1]{0:T(128)} %bitcast.place_ref, f32[16]{0:T(128)} %table_ref.15, s32[768]{0:T(1024)} %sign_ref.15, bf16[256,256]{1,0:T(8,128)(2,1)} %constant.15.clone.hmat_ref, f32[8,128]{1,0:T(8,128)S(1)} %get-tuple-element.25.refs_0_, ...), custom_call_target="tpu_custom_call" | custom-call | tf_op jit(solution)/shard_map/pallas_call | solution.py:137
  30.7 1.8 %collective-permute-start.6 = (bf16[512,768]{1,0:T(8,128)(2,1)S(1)}, bf16[512,768]{1,0:T(8,128)(2,1)S(1)}, u32[]{:S(2)}, u32[]{:S(2)}) collective-permute-start(bf16[512,768]{1,0:T(8,128)(2,1)S(1)} %get-tuple-element.32), channel_id=1, source_target_pairs={{0,96},{1,25},{2,98},{3,27},{4,100},{5,29},{6,102},{7,31},{8,104},... | collective-permute-start | bytes 2359304 | tf_op jit(solution)/shard_map/ppermute | solution.py:47
  32.5 2.6 %shard_map.113 = (bf16[512,768]{1,0:T(8,128)(2,1)S(1)}, bf16[512,768]{1,0:T(8,128)(2,1)S(1)}) custom-call(s32[1]{0:T(128)} %bitcast.place_ref, f32[16]{0:T(128)} %table_ref.15, s32[768]{0:T(1024)} %sign_ref.15, bf16[256,256]{1,0:T(8,128)(2,1)} %constant.15.clone.hmat_ref, f32[8,128]{1,0:T(8,128)S(1)} %get-tuple-element.25.refs_0_, ...), custom_call_target="tpu_custom_call" | custom-call | tf_op jit(solution)/shard_map/pallas_call | solution.py:137
  35.2 8.7 %collective-permute-done.3.refs_3_.refs_7_ = bf16[2,512,768]{2,1,0:T(8,128)(2,1)S(1)} collective-permute-done((bf16[2,512,768]{2,1,0:T(8,128)(2,1)S(1)}, bf16[2,512,768]{2,1,0:T(8,128)(2,1)S(1)}, u32[]{:S(2)}, u32[]{:S(2)}) %collective-permute-start.3) | collective-permute-done | bytes 1572896 | tf_op jit(solution)/shard_map/ppermute | solution.py:47
  43.9 1.5 %collective-permute-start.2 = (bf16[512,768]{1,0:T(8,128)(2,1)S(1)}, bf16[512,768]{1,0:T(8,128)(2,1)S(1)}, u32[]{:S(2)}, u32[]{:S(2)}) collective-permute-start(bf16[512,768]{1,0:T(8,128)(2,1)S(1)} %get-tuple-element.28), channel_id=1, source_target_pairs={{0,96},{1,25},{2,98},{3,27},{4,100},{5,29},{6,102},{7,31},{8,104},... | collective-permute-start | bytes 2359304 | tf_op jit(solution)/shard_map/ppermute | solution.py:47
  45.4 7.0 %collective-permute-done.4.refs_2_ = bf16[512,768]{1,0:T(8,128)(2,1)S(1)} collective-permute-done((bf16[512,768]{1,0:T(8,128)(2,1)S(1)}, bf16[512,768]{1,0:T(8,128)(2,1)S(1)}, u32[]{:S(2)}, u32[]{:S(2)}) %collective-permute-start.4) | collective-permute-done | bytes 786464 | tf_op jit(solution)/shard_map/ppermute | solution.py:47
  52.4 3.8 %shard_map.117 = (s16[512,768]{1,0:T(8,128)(2,1)S(1)}, s16[512,768]{1,0:T(8,128)(2,1)S(1)}) custom-call(s32[1]{0:T(128)} %bitcast.place_ref, f32[16]{0:T(128)} %table_ref.15, s32[768]{0:T(1024)} %sign_ref.15, bf16[256,256]{1,0:T(8,128)(2,1)} %constant.15.clone.hmat_ref, bf16[8192,768]{1,0:T(8,128)(2,1)} %bitcast.20, s32[3,8192]{1,0:T(4,128)} %index_ref.1, ...), custom_call_target="tpu_custom_call" | custom-call | tf_op jit(solution)/shard_map/pallas_call | solution.py:137
  56.2 2.5 %collective-permute-start.7 = (s16[512,768]{1,0:T(8,128)(2,1)S(1)}, s16[512,768]{1,0:T(8,128)(2,1)S(1)}, u32[]{:S(2)}, u32[]{:S(2)}) collective-permute-start(s16[512,768]{1,0:T(8,128)(2,1)S(1)} %get-tuple-element.33), channel_id=1, source_target_pairs={{0,16},{1,65},{2,18},{3,67},{4,20},{5,69},{6,22},{7,71},{8,24},{9,... | collective-permute-start | bytes 2359304 | tf_op jit(solution)/shard_map/ppermute | solution.py:47
  59.6 1.2 collective-permute-done.8.refs_2_
  60.8 2.7 %shard_map.118 = s16[512,768]{1,0:T(8,128)(2,1)S(1)} custom-call(s32[1]{0:T(128)} %bitcast.place_ref, f32[16]{0:T(128)} %table_ref.15, s32[768]{0:T(1024)} %sign_ref.15, bf16[256,256]{1,0:T(8,128)(2,1)} %constant.15.clone.hmat_ref, bf16[8192,768]{1,0:T(8,128)(2,1)} %bitcast.22, s32[3,8192]{1,0:T(4,128)} %index_ref.1, ...), custom_call_target="tpu_custom_call" | custom-call | tf_op jit(solution)/shard_map/pallas_call | solution.py:137
  64.4 2.1 %shard_map.115.own_ref = f32[512,768]{1,0:T(8,128)S(1)} custom-call(s32[1]{0:T(128)} %bitcast.place_ref, f32[16]{0:T(128)} %table_ref.15, s32[768]{0:T(1024)} %sign_ref.15, bf16[256,256]{1,0:T(8,128)(2,1)} %constant.15.clone.hmat_ref, bf16[8192,768]{1,0:T(8,128)(2,1)} %bitcast.23, s32[3,8192]{1,0:T(4,128)} %index_ref.1, ...), custom_call_target="tpu_custom_call" | custom-call | tf_op jit(solution)/shard_map/pallas_call | solution.py:137
  66.6 3.7 %collective-permute-done.7.two_ref = s16[512,768]{1,0:T(8,128)(2,1)S(1)} collective-permute-done((s16[512,768]{1,0:T(8,128)(2,1)S(1)}, s16[512,768]{1,0:T(8,128)(2,1)S(1)}, u32[]{:S(2)}, u32[]{:S(2)}) %collective-permute-start.7) | collective-permute-done | bytes 786464 | tf_op jit(solution)/shard_map/ppermute | solution.py:47
  70.3 7.8 %collective-permute-done.10.three_ref = s16[512,768]{1,0:T(8,128)(2,1)S(1)} collective-permute-done((s16[512,768]{1,0:T(8,128)(2,1)S(1)}, s16[512,768]{1,0:T(8,128)(2,1)S(1)}, u32[]{:S(2)}, u32[]{:S(2)}) %collective-permute-start.10) | collective-permute-done | bytes 786464 | tf_op jit(solution)/shard_map/ppermute | solution.py:47
  78.6 3.3 %shard_map.119 = (f32[512,768]{1,0:T(8,128)S(1)}, f32[128,128]{1,0:T(8,128)}) custom-call(s32[1]{0:T(128)} %bitcast.place_ref, f32[16]{0:T(128)} %table_ref.15, s32[768]{0:T(1024)} %sign_ref.15, bf16[256,256]{1,0:T(8,128)(2,1)} %constant.15.clone.hmat_ref, f32[512,768]{1,0:T(8,128)S(1)} %shard_map.115.own_ref, ...), custom_call_target="tpu_custom_call" | custom-call | tf_op jit(solution)/shard_map/pallas_call | solution.py:217
  81.9 19.6 %all_to_all.11 = f32[128,1,128]{2,1,0:T(1,128)S(1)} all-to-all(f32[128,1,128]{2,1,0:T(1,128)} %bitcast.24), channel_id=1, replica_groups=mesh['dp'=16,'fsdp'=8] {'dp','fsdp'}, dimensions={0} | all-to-all | bytes 131072 | tf_op jit(solution)/shard_map/all_to_all | solution.py:389
  101.5 1.8 %shard_map.121.refs_0_ = bf16[512,768]{1,0:T(8,128)(2,1)S(1)} custom-call(f32[128,128]{1,0:T(8,128)S(1)} %bitcast.6, f32[512,768]{1,0:T(8,128)S(1)} %get-tuple-element.37.plain_ref, f32[512,768]{1,0:T(8,128)S(1)} %get-tuple-element.38.master_ref, f32[512,768]{1,0:T(8,128)S(1)} %get-tuple-element.39.mean_ref, f32[512,768]{1,0:T(8,128)S(1)} %get-tuple-element.40.var_ref), custom_call_target="tpu_custom_call" | custom-call | tf_op jit(solution)/shard_map/pallas_call | solution.py:277
  107.0 2.9 %shard_map.120 = (f32[512,768]{1,0:T(8,128)}, f32[512,768]{1,0:T(8,128)}, f32[512,768]{1,0:T(8,128)}) custom-call(f32[128,128]{1,0:T(8,128)S(1)} %bitcast.7, f32[512,768]{1,0:T(8,128)S(1)} %get-tuple-element.37.plain_ref, f32[512,768]{1,0:T(8,128)S(1)} %get-tuple-element.38.master_ref, f32[512,768]{1,0:T(8,128)S(1)} %get-tuple-element.39.mean_ref, ...), custom_call_target="tpu_custom_call" | custom-call | tf_op jit(solution)/shard_map/pallas_call | solution.py:277
  109.9 5.5 %collective-permute-done.11.__0_ = bf16[512,768]{1,0:T(8,128)(2,1)S(1)} collective-permute-done((bf16[512,768]{1,0:T(8,128)(2,1)S(1)}, bf16[512,768]{1,0:T(8,128)(2,1)S(1)}, u32[]{:S(2)}, u32[]{:S(2)}) %collective-permute-start.11) | collective-permute-done | bytes 786464 | tf_op jit(solution)/shard_map/ppermute | solution.py:357
  115.4 2.1 %collective-permute-start.15 = (bf16[512,768]{1,0:T(8,128)(2,1)S(1)}, bf16[512,768]{1,0:T(8,128)(2,1)S(1)}, u32[]{:S(2)}, u32[]{:S(2)}) collective-permute-start(bf16[512,768]{1,0:T(8,128)(2,1)S(1)} %shard_map.122.refs_2_), channel_id=1, source_target_pairs={{0,1},{1,0},{2,3},{3,2},{4,5},{5,4},{6,7},{7,6},{8,9},{9,8},{10,11... | collective-permute-start | bytes 2359304 | tf_op jit(solution)/shard_map/ppermute | solution.py:361
  117.6 6.3 %collective-permute-done.14.refs_3_ = bf16[512,768]{1,0:T(8,128)(2,1)S(1)} collective-permute-done((bf16[512,768]{1,0:T(8,128)(2,1)S(1)}, bf16[512,768]{1,0:T(8,128)(2,1)S(1)}, u32[]{:S(2)}, u32[]{:S(2)}) %collective-permute-start.14) | collective-permute-done | bytes 786464 | tf_op jit(solution)/shard_map/ppermute | solution.py:357
  123.9 2.2 %collective-permute-start.17 = (bf16[256,768]{1,0:T(8,128)(2,1)S(1)}, bf16[256,768]{1,0:T(8,128)(2,1)S(1)}, u32[]{:S(2)}, u32[]{:S(2)}) collective-permute-start(bf16[256,768]{1,0:T(8,128)(2,1)S(1)} %get-tuple-element.46), channel_id=1, source_target_pairs={{0,1},{1,0},{2,3},{3,2},{4,5},{5,4},{6,7},{7,6},{8,9},{9,8},{10,11... | collective-permute-start | bytes 1179656 | tf_op jit(solution)/shard_map/ppermute | solution.py:361
  126.2 1.3 collective-permute-done.17.refs_6_
  128.0 2.4 %shard_map.123 = (bf16[512,6144]{1,0:T(8,128)(2,1)}, f32[8,128]{1,0:T(8,128)S(1)}) custom-call(bf16[512,768]{1,0:T(8,128)(2,1)S(1)} %shard_map.121.refs_0_, bf16[512,768]{1,0:T(8,128)(2,1)S(1)} %collective-permute-done.13.refs_1_, bf16[512,768]{1,0:T(8,128)(2,1)S(1)} %shard_map.122.refs_2_, bf16[512,768]{1,0:T(8,128)(2,1)S(1)} %collective-permute-done.14.refs_3_, ...), custom_call_target="tpu_custom_call" | custom-call | tf_op jit(solution)/shard_map/pallas_call | solution.py:343
  130.4 1.8 %collective-permute-done.12.__0_ = bf16[512,768]{1,0:T(8,128)(2,1)S(1)} collective-permute-done((bf16[512,768]{1,0:T(8,128)(2,1)S(1)}, bf16[512,768]{1,0:T(8,128)(2,1)S(1)}, u32[]{:S(2)}, u32[]{:S(2)}) %collective-permute-start.12) | collective-permute-done | bytes 786464 | tf_op jit(solution)/shard_map/ppermute | solution.py:357
  132.3 2.1 %collective-permute-start.18 = (bf16[512,768]{1,0:T(8,128)(2,1)S(1)}, bf16[512,768]{1,0:T(8,128)(2,1)S(1)}, u32[]{:S(2)}, u32[]{:S(2)}) collective-permute-start(bf16[512,768]{1,0:T(8,128)(2,1)S(1)} %shard_map.124.refs_0_), channel_id=1, source_target_pairs={{0,1},{1,0},{2,3},{3,2},{4,5},{5,4},{6,7},{7,6},{8,9},{9,8},{10,11... | collective-permute-start | bytes 2359304 | tf_op jit(solution)/shard_map/ppermute | solution.py:361
  (24 shorter events, 10.8 us)
Async XLA Ops:
  4.3 22.8 %collective-permute-start = (bf16[2,512,768]{2,1,0:T(8,128)(2,1)S(1)}, bf16[2,512,768]{2,1,0:T(8,128)(2,1)S(1)}, u32[]{:S(2)}, u32[]{:S(2)}) collective-permute-start(bf16[2,512,768]{2,1,0:T(8,128)(2,1)S(1)} %get-tuple-element.26), channel_id=1, source_target_pairs={{0,32},{1,9},{2,34},{3,11},{4,36},{5,13},{6,38},{7,15},{8,40},{9,1... | collective-permute-start | bytes 4718600 | tf_op jit(solution)/shard_map/ppermute | solution.py:47
  6.8 20.2 %collective-permute-start.1 = (bf16[2,512,768]{2,1,0:T(8,128)(2,1)S(1)}, bf16[2,512,768]{2,1,0:T(8,128)(2,1)S(1)}, u32[]{:S(2)}, u32[]{:S(2)}) collective-permute-start(bf16[2,512,768]{2,1,0:T(8,128)(2,1)S(1)} %get-tuple-element.27), channel_id=1, source_target_pairs={{0,96},{1,25},{2,98},{3,27},{4,100},{5,29},{6,102},{7,31},{8,104},... | collective-permute-start | bytes 4718600 | tf_op jit(solution)/shard_map/ppermute | solution.py:47
  12.5 31.4 %collective-permute-start.3 = (bf16[2,512,768]{2,1,0:T(8,128)(2,1)S(1)}, bf16[2,512,768]{2,1,0:T(8,128)(2,1)S(1)}, u32[]{:S(2)}, u32[]{:S(2)}) collective-permute-start(bf16[2,512,768]{2,1,0:T(8,128)(2,1)S(1)} %get-tuple-element.29), channel_id=1, source_target_pairs={{0,32},{1,9},{2,34},{3,11},{4,36},{5,13},{6,38},{7,15},{8,40},{9,1... | collective-permute-start | bytes 4718600 | tf_op jit(solution)/shard_map/ppermute | solution.py:47
  12.6 32.8 %collective-permute-start.5 = (bf16[2,512,768]{2,1,0:T(8,128)(2,1)S(1)}, bf16[2,512,768]{2,1,0:T(8,128)(2,1)S(1)}, u32[]{:S(2)}, u32[]{:S(2)}) collective-permute-start(bf16[2,512,768]{2,1,0:T(8,128)(2,1)S(1)} %get-tuple-element.31), channel_id=1, source_target_pairs={{0,96},{1,25},{2,98},{3,27},{4,100},{5,29},{6,102},{7,31},{8,104},... | collective-permute-start | bytes 4718600 | tf_op jit(solution)/shard_map/ppermute | solution.py:47
  29.7 22.6 %collective-permute-start.4 = (bf16[512,768]{1,0:T(8,128)(2,1)S(1)}, bf16[512,768]{1,0:T(8,128)(2,1)S(1)}, u32[]{:S(2)}, u32[]{:S(2)}) collective-permute-start(bf16[512,768]{1,0:T(8,128)(2,1)S(1)} %get-tuple-element.30), channel_id=1, source_target_pairs={{0,32},{1,9},{2,34},{3,11},{4,36},{5,13},{6,38},{7,15},{8,40},{9,1... | collective-permute-start | bytes 2359304 | tf_op jit(solution)/shard_map/ppermute | solution.py:47
  30.7 21.7 %collective-permute-start.6 = (bf16[512,768]{1,0:T(8,128)(2,1)S(1)}, bf16[512,768]{1,0:T(8,128)(2,1)S(1)}, u32[]{:S(2)}, u32[]{:S(2)}) collective-permute-start(bf16[512,768]{1,0:T(8,128)(2,1)S(1)} %get-tuple-element.32), channel_id=1, source_target_pairs={{0,96},{1,25},{2,98},{3,27},{4,100},{5,29},{6,102},{7,31},{8,104},... | collective-permute-start | bytes 2359304 | tf_op jit(solution)/shard_map/ppermute | solution.py:47
  35.1 25.7 %collective-permute-start.8 = (bf16[512,768]{1,0:T(8,128)(2,1)S(1)}, bf16[512,768]{1,0:T(8,128)(2,1)S(1)}, u32[]{:S(2)}, u32[]{:S(2)}) collective-permute-start(bf16[512,768]{1,0:T(8,128)(2,1)S(1)} %get-tuple-element.34), channel_id=1, source_target_pairs={{0,32},{1,9},{2,34},{3,11},{4,36},{5,13},{6,38},{7,15},{8,40},{9,1... | collective-permute-start | bytes 2359304 | tf_op jit(solution)/shard_map/ppermute | solution.py:47
  43.9 20.5 %collective-permute-start.2 = (bf16[512,768]{1,0:T(8,128)(2,1)S(1)}, bf16[512,768]{1,0:T(8,128)(2,1)S(1)}, u32[]{:S(2)}, u32[]{:S(2)}) collective-permute-start(bf16[512,768]{1,0:T(8,128)(2,1)S(1)} %get-tuple-element.28), channel_id=1, source_target_pairs={{0,96},{1,25},{2,98},{3,27},{4,100},{5,29},{6,102},{7,31},{8,104},... | collective-permute-start | bytes 2359304 | tf_op jit(solution)/shard_map/ppermute | solution.py:47
  56.2 14.0 %collective-permute-start.7 = (s16[512,768]{1,0:T(8,128)(2,1)S(1)}, s16[512,768]{1,0:T(8,128)(2,1)S(1)}, u32[]{:S(2)}, u32[]{:S(2)}) collective-permute-start(s16[512,768]{1,0:T(8,128)(2,1)S(1)} %get-tuple-element.33), channel_id=1, source_target_pairs={{0,16},{1,65},{2,18},{3,67},{4,20},{5,69},{6,22},{7,71},{8,24},{9,... | collective-permute-start | bytes 2359304 | tf_op jit(solution)/shard_map/ppermute | solution.py:47
  58.8 19.3 %collective-permute-start.10 = (s16[512,768]{1,0:T(8,128)(2,1)S(1)}, s16[512,768]{1,0:T(8,128)(2,1)S(1)}, u32[]{:S(2)}, u32[]{:S(2)}) collective-permute-start(s16[512,768]{1,0:T(8,128)(2,1)S(1)} %get-tuple-element.35), channel_id=1, source_target_pairs={{0,24},{1,97},{2,26},{3,99},{4,28},{5,101},{6,30},{7,103},{8,0},{9... | collective-permute-start | bytes 2359304 | tf_op jit(solution)/shard_map/ppermute | solution.py:47
  63.4 15.2 %collective-permute-start.9 = (s16[512,768]{1,0:T(8,128)(2,1)S(1)}, s16[512,768]{1,0:T(8,128)(2,1)S(1)}, u32[]{:S(2)}, u32[]{:S(2)}) collective-permute-start(s16[512,768]{1,0:T(8,128)(2,1)S(1)} %shard_map.118), channel_id=1, source_target_pairs={{0,8},{1,33},{2,10},{3,35},{4,12},{5,37},{6,14},{7,39},{8,16},{9,4... | collective-permute-start | bytes 2359304 | tf_op jit(solution)/shard_map/ppermute | solution.py:47
  103.3 2.9 %collective-permute-start.13 = (bf16[512,768]{1,0:T(8,128)(2,1)S(1)}, bf16[512,768]{1,0:T(8,128)(2,1)S(1)}, u32[]{:S(2)}, u32[]{:S(2)}) collective-permute-start(bf16[512,768]{1,0:T(8,128)(2,1)S(1)} %shard_map.121.refs_0_), channel_id=1, source_target_pairs={{0,1},{1,0},{2,3},{3,2},{4,5},{5,4},{6,7},{7,6},{8,9},{9,8},{10,11... | collective-permute-start | bytes 2359304 | tf_op jit(solution)/shard_map/ppermute | solution.py:361
  104.3 11.1 %collective-permute-start.11 = (bf16[512,768]{1,0:T(8,128)(2,1)S(1)}, bf16[512,768]{1,0:T(8,128)(2,1)S(1)}, u32[]{:S(2)}, u32[]{:S(2)}) collective-permute-start(bf16[512,768]{1,0:T(8,128)(2,1)S(1)} %shard_map.121.refs_0_), channel_id=1, source_target_pairs={{0,2},{1,7},{2,4},{3,1},{4,6},{5,3},{6,0},{7,5},{8,10},{9,15},{10,... | collective-permute-start | bytes 2359304 | tf_op jit(solution)/shard_map/ppermute | solution.py:357
  106.2 17.6 %collective-permute-start.14 = (bf16[512,768]{1,0:T(8,128)(2,1)S(1)}, bf16[512,768]{1,0:T(8,128)(2,1)S(1)}, u32[]{:S(2)}, u32[]{:S(2)}) collective-permute-start(bf16[512,768]{1,0:T(8,128)(2,1)S(1)} %collective-permute-done.13.refs_1_), channel_id=1, source_target_pairs={{0,2},{1,7},{2,4},{3,1},{4,6},{5,3},{6,0},{7,5},{8,10},{9,15},{10,... | collective-permute-start | bytes 2359304 | tf_op jit(solution)/shard_map/ppermute | solution.py:357
  115.4 10.8 %collective-permute-start.15 = (bf16[512,768]{1,0:T(8,128)(2,1)S(1)}, bf16[512,768]{1,0:T(8,128)(2,1)S(1)}, u32[]{:S(2)}, u32[]{:S(2)}) collective-permute-start(bf16[512,768]{1,0:T(8,128)(2,1)S(1)} %shard_map.122.refs_2_), channel_id=1, source_target_pairs={{0,1},{1,0},{2,3},{3,2},{4,5},{5,4},{6,7},{7,6},{8,9},{9,8},{10,11... | collective-permute-start | bytes 2359304 | tf_op jit(solution)/shard_map/ppermute | solution.py:361
  117.6 14.7 %collective-permute-start.12 = (bf16[512,768]{1,0:T(8,128)(2,1)S(1)}, bf16[512,768]{1,0:T(8,128)(2,1)S(1)}, u32[]{:S(2)}, u32[]{:S(2)}) collective-permute-start(bf16[512,768]{1,0:T(8,128)(2,1)S(1)} %shard_map.122.refs_2_), channel_id=1, source_target_pairs={{0,2},{1,7},{2,4},{3,1},{4,6},{5,3},{6,0},{7,5},{8,10},{9,15},{10,... | collective-permute-start | bytes 2359304 | tf_op jit(solution)/shard_map/ppermute | solution.py:357
  123.9 3.6 %collective-permute-start.17 = (bf16[256,768]{1,0:T(8,128)(2,1)S(1)}, bf16[256,768]{1,0:T(8,128)(2,1)S(1)}, u32[]{:S(2)}, u32[]{:S(2)}) collective-permute-start(bf16[256,768]{1,0:T(8,128)(2,1)S(1)} %get-tuple-element.46), channel_id=1, source_target_pairs={{0,1},{1,0},{2,3},{3,2},{4,5},{5,4},{6,7},{7,6},{8,9},{9,8},{10,11... | collective-permute-start | bytes 1179656 | tf_op jit(solution)/shard_map/ppermute | solution.py:361
  126.1 1.9 %collective-permute-start.16 = (bf16[256,768]{1,0:T(8,128)(2,1)S(1)}, bf16[256,768]{1,0:T(8,128)(2,1)S(1)}, u32[]{:S(2)}, u32[]{:S(2)}) collective-permute-start(bf16[256,768]{1,0:T(8,128)(2,1)S(1)} %get-tuple-element.47), channel_id=1, source_target_pairs={{0,1},{1,0},{2,3},{3,2},{4,5},{5,4},{6,7},{7,6},{8,9},{9,8},{10,11... | collective-permute-start | bytes 1179656 | tf_op jit(solution)/shard_map/ppermute | solution.py:361
  132.3 4.1 %collective-permute-start.18 = (bf16[512,768]{1,0:T(8,128)(2,1)S(1)}, bf16[512,768]{1,0:T(8,128)(2,1)S(1)}, u32[]{:S(2)}, u32[]{:S(2)}) collective-permute-start(bf16[512,768]{1,0:T(8,128)(2,1)S(1)} %shard_map.124.refs_0_), channel_id=1, source_target_pairs={{0,1},{1,0},{2,3},{3,2},{4,5},{5,4},{6,7},{7,6},{8,9},{9,8},{10,11... | collective-permute-start | bytes 2359304 | tf_op jit(solution)/shard_map/ppermute | solution.py:361

commit v9 on v8

--- a/solution.py
+++ b/solution.py
@@ -68,7 +68,7 @@
 
 def to_root(value):
     root = value * lax.rsqrt(jnp.maximum(jnp.abs(value), 1e-30)) * ROOT_STEPS
-    return (root + jnp.where(root < 0, -0.5, 0.5)).astype(jnp.int32).astype(jnp.int16)
+    return jnp.round(root).astype(jnp.int32).astype(jnp.int16)
 
 
 def from_root(root):

time: 138 us -> 137 us (level)
  no operation moved by 1% of the time
where the time goes in v9:
time: 137 us
  waiting for transfers between devices  55.8 us (41%)
  Pallas kernels  35.6 us (26%)
  starting transfers between devices  25.5 us (19%)
  blocking collectives  19.1 us (14%)
    ppermute x11, waiting for transfers between devices, hop(): return lax.ppermute(value, ('dp', 'fsdp'), pairs)  38.3 us
    pallas_call x7, Pallas kernels, encode(): pl.pallas_call(functools.partial(encode_kernel, [len(job[2]) for job in j...  20.3 us
    all_to_all x1, blocking collectives, on_device(): square = lax.all_to_all(square, ('dp', 'fsdp'), 0, 0, tiled=True)  19.1 us
    ppermute x11, starting transfers between devices, hop(): return lax.ppermute(value, ('dp', 'fsdp'), pairs)  16.2 us
    ppermute x3, waiting for transfers between devices, along_y(): return lax.ppermute(value, 'fsdp', pairs)  13.6 us
    ppermute x5, starting transfers between devices, to_other_core(): return lax.ppermute(value, 'fsdp', [(i, i ^ 1) for i in range(8)])  7.58 us
    pallas_call x2, Pallas kernels, adamw(): pl.pallas_call(kernel, out_shape=out_shape, grid=(BLOCK // STEP,), in_spe...  4.76 us
    pallas_call x3, Pallas kernels, fill(): pl.pallas_call(functools.partial(fill_kernel, places, len(blocks) + len(g...  4.19 us
  transfers between devices with their start and end apart: 19, of which 14 were waited for; matrix products, arithmetic and copies ran while one was open for 0% of the time, Pallas kernels for 19%

profile of v9, /device:TPU:1, one launch (start us, length us, event | category | flops | bytes accessed | tf_op | source)
XLA Modules:
  0.0 137.0 jit_solution(16109837370998785495)
XLA Ops:
  0.6 3.7 %shard_map.112 = (bf16[2,512,768]{2,1,0:T(8,128)(2,1)S(1)}, bf16[2,512,768]{2,1,0:T(8,128)(2,1)S(1)}) custom-call(s32[1]{0:T(128)} %bitcast.place_ref, f32[16]{0:T(128)} %table_ref.15, s32[768]{0:T(1024)} %sign_ref.15, bf16[256,256]{1,0:T(8,128)(2,1)} %constant.15.clone.hmat_ref, bf16[8192,768]{1,0:T(8,128)(2,1)} %bitcast.8, s32[3,8192]{1,0:T(4,128)} %index_ref.1, ...), custom_call_target="tpu_custom_call" | custom-call | tf_op jit(solution)/shard_map/pallas_call | solution.py:137
  4.3 2.5 %collective-permute-start = (bf16[2,512,768]{2,1,0:T(8,128)(2,1)S(1)}, bf16[2,512,768]{2,1,0:T(8,128)(2,1)S(1)}, u32[]{:S(2)}, u32[]{:S(2)}) collective-permute-start(bf16[2,512,768]{2,1,0:T(8,128)(2,1)S(1)} %get-tuple-element.26), channel_id=1, source_target_pairs={{0,32},{1,9},{2,34},{3,11},{4,36},{5,13},{6,38},{7,15},{8,40},{9,1... | collective-permute-start | bytes 4718600 | tf_op jit(solution)/shard_map/ppermute | solution.py:47
  6.8 2.2 %collective-permute-start.1 = (bf16[2,512,768]{2,1,0:T(8,128)(2,1)S(1)}, bf16[2,512,768]{2,1,0:T(8,128)(2,1)S(1)}, u32[]{:S(2)}, u32[]{:S(2)}) collective-permute-start(bf16[2,512,768]{2,1,0:T(8,128)(2,1)S(1)} %get-tuple-element.27), channel_id=1, source_target_pairs={{0,96},{1,25},{2,98},{3,27},{4,100},{5,29},{6,102},{7,31},{8,104},... | collective-permute-start | bytes 4718600 | tf_op jit(solution)/shard_map/ppermute | solution.py:47
  9.1 3.5 %shard_map.114 = (bf16[2,512,768]{2,1,0:T(8,128)(2,1)S(1)}, bf16[2,512,768]{2,1,0:T(8,128)(2,1)S(1)}) custom-call(s32[1]{0:T(128)} %bitcast.place_ref, f32[16]{0:T(128)} %table_ref.15, s32[768]{0:T(1024)} %sign_ref.15, bf16[256,256]{1,0:T(8,128)(2,1)} %constant.15.clone.hmat_ref, bf16[8192,768]{1,0:T(8,128)(2,1)} %bitcast.12, s32[3,8192]{1,0:T(4,128)} %index_ref.1, ...), custom_call_target="tpu_custom_call" | custom-call | tf_op jit(solution)/shard_map/pallas_call | solution.py:137
  12.6 2.7 %collective-permute-start.5 = (bf16[2,512,768]{2,1,0:T(8,128)(2,1)S(1)}, bf16[2,512,768]{2,1,0:T(8,128)(2,1)S(1)}, u32[]{:S(2)}, u32[]{:S(2)}) collective-permute-start(bf16[2,512,768]{2,1,0:T(8,128)(2,1)S(1)} %get-tuple-element.31), channel_id=1, source_target_pairs={{0,96},{1,25},{2,98},{3,27},{4,100},{5,29},{6,102},{7,31},{8,104},... | collective-permute-start | bytes 4718600 | tf_op jit(solution)/shard_map/ppermute | solution.py:47
  15.3 3.1 %shard_map.111 = (f32[512,768]{1,0:T(8,128)S(1)}, f32[512,768]{1,0:T(8,128)S(1)}, f32[512,768]{1,0:T(8,128)S(1)}, f32[8,128]{1,0:T(8,128)S(1)}) custom-call(f32[512,768]{1,0:T(8,128)} %refs_0_.1, f32[512,768]{1,0:T(8,128)} %refs_1_.6, f32[512,768]{1,0:T(8,128)} %refs_2_.3), custom_call_target="tpu_custom_call" | custom-call | tf_op jit(solution)/shard_map/pallas_call | solution.py:296
  18.4 8.7 %collective-permute-done.refs_3_ = bf16[2,512,768]{2,1,0:T(8,128)(2,1)S(1)} collective-permute-done((bf16[2,512,768]{2,1,0:T(8,128)(2,1)S(1)}, bf16[2,512,768]{2,1,0:T(8,128)(2,1)S(1)}, u32[]{:S(2)}, u32[]{:S(2)}) %collective-permute-start) | collective-permute-done | bytes 1572896 | tf_op jit(solution)/shard_map/ppermute | solution.py:47
  27.1 2.6 %shard_map.116 = (bf16[512,768]{1,0:T(8,128)(2,1)S(1)}, bf16[512,768]{1,0:T(8,128)(2,1)S(1)}) custom-call(s32[1]{0:T(128)} %bitcast.place_ref, f32[16]{0:T(128)} %table_ref.15, s32[768]{0:T(1024)} %sign_ref.15, bf16[256,256]{1,0:T(8,128)(2,1)} %constant.15.clone.hmat_ref, f32[8,128]{1,0:T(8,128)S(1)} %get-tuple-element.25.refs_0_, ...), custom_call_target="tpu_custom_call" | custom-call | tf_op jit(solution)/shard_map/pallas_call | solution.py:137
  30.7 1.8 %collective-permute-start.6 = (bf16[512,768]{1,0:T(8,128)(2,1)S(1)}, bf16[512,768]{1,0:T(8,128)(2,1)S(1)}, u32[]{:S(2)}, u32[]{:S(2)}) collective-permute-start(bf16[512,768]{1,0:T(8,128)(2,1)S(1)} %get-tuple-element.32), channel_id=1, source_target_pairs={{0,96},{1,25},{2,98},{3,27},{4,100},{5,29},{6,102},{7,31},{8,104},... | collective-permute-start | bytes 2359304 | tf_op jit(solution)/shard_map/ppermute | solution.py:47
  32.5 2.6 %shard_map.113 = (bf16[512,768]{1,0:T(8,128)(2,1)S(1)}, bf16[512,768]{1,0:T(8,128)(2,1)S(1)}) custom-call(s32[1]{0:T(128)} %bitcast.place_ref, f32[16]{0:T(128)} %table_ref.15, s32[768]{0:T(1024)} %sign_ref.15, bf16[256,256]{1,0:T(8,128)(2,1)} %constant.15.clone.hmat_ref, f32[8,128]{1,0:T(8,128)S(1)} %get-tuple-element.25.refs_0_, ...), custom_call_target="tpu_custom_call" | custom-call | tf_op jit(solution)/shard_map/pallas_call | solution.py:137
  35.2 8.7 %collective-permute-done.3.refs_3_.refs_7_ = bf16[2,512,768]{2,1,0:T(8,128)(2,1)S(1)} collective-permute-done((bf16[2,512,768]{2,1,0:T(8,128)(2,1)S(1)}, bf16[2,512,768]{2,1,0:T(8,128)(2,1)S(1)}, u32[]{:S(2)}, u32[]{:S(2)}) %collective-permute-start.3) | collective-permute-done | bytes 1572896 | tf_op jit(solution)/shard_map/ppermute | solution.py:47
  43.9 1.5 %collective-permute-start.2 = (bf16[512,768]{1,0:T(8,128)(2,1)S(1)}, bf16[512,768]{1,0:T(8,128)(2,1)S(1)}, u32[]{:S(2)}, u32[]{:S(2)}) collective-permute-start(bf16[512,768]{1,0:T(8,128)(2,1)S(1)} %get-tuple-element.28), channel_id=1, source_target_pairs={{0,96},{1,25},{2,98},{3,27},{4,100},{5,29},{6,102},{7,31},{8,104},... | collective-permute-start | bytes 2359304 | tf_op jit(solution)/shard_map/ppermute | solution.py:47
  45.4 7.0 %collective-permute-done.4.refs_2_ = bf16[512,768]{1,0:T(8,128)(2,1)S(1)} collective-permute-done((bf16[512,768]{1,0:T(8,128)(2,1)S(1)}, bf16[512,768]{1,0:T(8,128)(2,1)S(1)}, u32[]{:S(2)}, u32[]{:S(2)}) %collective-permute-start.4) | collective-permute-done | bytes 786464 | tf_op jit(solution)/shard_map/ppermute | solution.py:47
  52.4 3.4 %shard_map.117 = (s16[512,768]{1,0:T(8,128)(2,1)S(1)}, s16[512,768]{1,0:T(8,128)(2,1)S(1)}) custom-call(s32[1]{0:T(128)} %bitcast.place_ref, f32[16]{0:T(128)} %table_ref.15, s32[768]{0:T(1024)} %sign_ref.15, bf16[256,256]{1,0:T(8,128)(2,1)} %constant.15.clone.hmat_ref, bf16[8192,768]{1,0:T(8,128)(2,1)} %bitcast.20, s32[3,8192]{1,0:T(4,128)} %index_ref.1, ...), custom_call_target="tpu_custom_call" | custom-call | tf_op jit(solution)/shard_map/pallas_call | solution.py:137
  55.8 2.5 %collective-permute-start.7 = (s16[512,768]{1,0:T(8,128)(2,1)S(1)}, s16[512,768]{1,0:T(8,128)(2,1)S(1)}, u32[]{:S(2)}, u32[]{:S(2)}) collective-permute-start(s16[512,768]{1,0:T(8,128)(2,1)S(1)} %get-tuple-element.33), channel_id=1, source_target_pairs={{0,16},{1,65},{2,18},{3,67},{4,20},{5,69},{6,22},{7,71},{8,24},{9,... | collective-permute-start | bytes 2359304 | tf_op jit(solution)/shard_map/ppermute | solution.py:47
  59.2 1.6 %collective-permute-done.8.refs_2_ = bf16[512,768]{1,0:T(8,128)(2,1)S(1)} collective-permute-done((bf16[512,768]{1,0:T(8,128)(2,1)S(1)}, bf16[512,768]{1,0:T(8,128)(2,1)S(1)}, u32[]{:S(2)}, u32[]{:S(2)}) %collective-permute-start.8) | collective-permute-done | bytes 786464 | tf_op jit(solution)/shard_map/ppermute | solution.py:47
  60.8 2.5 %shard_map.118 = s16[512,768]{1,0:T(8,128)(2,1)S(1)} custom-call(s32[1]{0:T(128)} %bitcast.place_ref, f32[16]{0:T(128)} %table_ref.15, s32[768]{0:T(1024)} %sign_ref.15, bf16[256,256]{1,0:T(8,128)(2,1)} %constant.15.clone.hmat_ref, bf16[8192,768]{1,0:T(8,128)(2,1)} %bitcast.22, s32[3,8192]{1,0:T(4,128)} %index_ref.1, ...), custom_call_target="tpu_custom_call" | custom-call | tf_op jit(solution)/shard_map/pallas_call | solution.py:137
  64.2 2.1 %shard_map.115.own_ref = f32[512,768]{1,0:T(8,128)S(1)} custom-call(s32[1]{0:T(128)} %bitcast.place_ref, f32[16]{0:T(128)} %table_ref.15, s32[768]{0:T(1024)} %sign_ref.15, bf16[256,256]{1,0:T(8,128)(2,1)} %constant.15.clone.hmat_ref, bf16[8192,768]{1,0:T(8,128)(2,1)} %bitcast.23, s32[3,8192]{1,0:T(4,128)} %index_ref.1, ...), custom_call_target="tpu_custom_call" | custom-call | tf_op jit(solution)/shard_map/pallas_call | solution.py:137
  66.4 3.9 %collective-permute-done.7.two_ref = s16[512,768]{1,0:T(8,128)(2,1)S(1)} collective-permute-done((s16[512,768]{1,0:T(8,128)(2,1)S(1)}, s16[512,768]{1,0:T(8,128)(2,1)S(1)}, u32[]{:S(2)}, u32[]{:S(2)}) %collective-permute-start.7) | collective-permute-done | bytes 786464 | tf_op jit(solution)/shard_map/ppermute | solution.py:47
  70.3 7.8 %collective-permute-done.10.three_ref = s16[512,768]{1,0:T(8,128)(2,1)S(1)} collective-permute-done((s16[512,768]{1,0:T(8,128)(2,1)S(1)}, s16[512,768]{1,0:T(8,128)(2,1)S(1)}, u32[]{:S(2)}, u32[]{:S(2)}) %collective-permute-start.10) | collective-permute-done | bytes 786464 | tf_op jit(solution)/shard_map/ppermute | solution.py:47
  78.6 3.3 %shard_map.119 = (f32[512,768]{1,0:T(8,128)S(1)}, f32[128,128]{1,0:T(8,128)}) custom-call(s32[1]{0:T(128)} %bitcast.place_ref, f32[16]{0:T(128)} %table_ref.15, s32[768]{0:T(1024)} %sign_ref.15, bf16[256,256]{1,0:T(8,128)(2,1)} %constant.15.clone.hmat_ref, f32[512,768]{1,0:T(8,128)S(1)} %shard_map.115.own_ref, ...), custom_call_target="tpu_custom_call" | custom-call | tf_op jit(solution)/shard_map/pallas_call | solution.py:217
  81.9 19.1 %all_to_all.11 = f32[128,1,128]{2,1,0:T(1,128)S(1)} all-to-all(f32[128,1,128]{2,1,0:T(1,128)} %bitcast.24), channel_id=1, replica_groups=mesh['dp'=16,'fsdp'=8] {'dp','fsdp'}, dimensions={0} | all-to-all | bytes 131072 | tf_op jit(solution)/shard_map/all_to_all | solution.py:389
  101.0 1.8 %shard_map.121.refs_0_ = bf16[512,768]{1,0:T(8,128)(2,1)S(1)} custom-call(f32[128,128]{1,0:T(8,128)S(1)} %bitcast.6, f32[512,768]{1,0:T(8,128)S(1)} %get-tuple-element.37.plain_ref, f32[512,768]{1,0:T(8,128)S(1)} %get-tuple-element.38.master_ref, f32[512,768]{1,0:T(8,128)S(1)} %get-tuple-element.39.mean_ref, f32[512,768]{1,0:T(8,128)S(1)} %get-tuple-element.40.var_ref), custom_call_target="tpu_custom_call" | custom-call | tf_op jit(solution)/shard_map/pallas_call | solution.py:277
  106.6 2.9 %shard_map.120 = (f32[512,768]{1,0:T(8,128)}, f32[512,768]{1,0:T(8,128)}, f32[512,768]{1,0:T(8,128)}) custom-call(f32[128,128]{1,0:T(8,128)S(1)} %bitcast.7, f32[512,768]{1,0:T(8,128)S(1)} %get-tuple-element.37.plain_ref, f32[512,768]{1,0:T(8,128)S(1)} %get-tuple-element.38.master_ref, f32[512,768]{1,0:T(8,128)S(1)} %get-tuple-element.39.mean_ref, ...), custom_call_target="tpu_custom_call" | custom-call | tf_op jit(solution)/shard_map/pallas_call | solution.py:277
  109.5 5.5 %collective-permute-done.11.__0_ = bf16[512,768]{1,0:T(8,128)(2,1)S(1)} collective-permute-done((bf16[512,768]{1,0:T(8,128)(2,1)S(1)}, bf16[512,768]{1,0:T(8,128)(2,1)S(1)}, u32[]{:S(2)}, u32[]{:S(2)}) %collective-permute-start.11) | collective-permute-done | bytes 786464 | tf_op jit(solution)/shard_map/ppermute | solution.py:357
  115.0 2.1 %collective-permute-start.15 = (bf16[512,768]{1,0:T(8,128)(2,1)S(1)}, bf16[512,768]{1,0:T(8,128)(2,1)S(1)}, u32[]{:S(2)}, u32[]{:S(2)}) collective-permute-start(bf16[512,768]{1,0:T(8,128)(2,1)S(1)} %shard_map.122.refs_2_), channel_id=1, source_target_pairs={{0,1},{1,0},{2,3},{3,2},{4,5},{5,4},{6,7},{7,6},{8,9},{9,8},{10,11... | collective-permute-start | bytes 2359304 | tf_op jit(solution)/shard_map/ppermute | solution.py:361
  117.1 6.3 %collective-permute-done.14.refs_3_ = bf16[512,768]{1,0:T(8,128)(2,1)S(1)} collective-permute-done((bf16[512,768]{1,0:T(8,128)(2,1)S(1)}, bf16[512,768]{1,0:T(8,128)(2,1)S(1)}, u32[]{:S(2)}, u32[]{:S(2)}) %collective-permute-start.14) | collective-permute-done | bytes 786464 | tf_op jit(solution)/shard_map/ppermute | solution.py:357
  123.5 2.2 %collective-permute-start.17 = (bf16[256,768]{1,0:T(8,128)(2,1)S(1)}, bf16[256,768]{1,0:T(8,128)(2,1)S(1)}, u32[]{:S(2)}, u32[]{:S(2)}) collective-permute-start(bf16[256,768]{1,0:T(8,128)(2,1)S(1)} %get-tuple-element.46), channel_id=1, source_target_pairs={{0,1},{1,0},{2,3},{3,2},{4,5},{5,4},{6,7},{7,6},{8,9},{9,8},{10,11... | collective-permute-start | bytes 1179656 | tf_op jit(solution)/shard_map/ppermute | solution.py:361
  125.8 1.3 collective-permute-done.17.refs_6_
  127.6 2.4 %shard_map.123 = (bf16[512,6144]{1,0:T(8,128)(2,1)}, f32[8,128]{1,0:T(8,128)S(1)}) custom-call(bf16[512,768]{1,0:T(8,128)(2,1)S(1)} %shard_map.121.refs_0_, bf16[512,768]{1,0:T(8,128)(2,1)S(1)} %collective-permute-done.13.refs_1_, bf16[512,768]{1,0:T(8,128)(2,1)S(1)} %shard_map.122.refs_2_, bf16[512,768]{1,0:T(8,128)(2,1)S(1)} %collective-permute-done.14.refs_3_, ...), custom_call_target="tpu_custom_call" | custom-call | tf_op jit(solution)/shard_map/pallas_call | solution.py:343
  130.0 1.8 %collective-permute-done.12.__0_ = bf16[512,768]{1,0:T(8,128)(2,1)S(1)} collective-permute-done((bf16[512,768]{1,0:T(8,128)(2,1)S(1)}, bf16[512,768]{1,0:T(8,128)(2,1)S(1)}, u32[]{:S(2)}, u32[]{:S(2)}) %collective-permute-start.12) | collective-permute-done | bytes 786464 | tf_op jit(solution)/shard_map/ppermute | solution.py:357
  131.8 2.1 %collective-permute-start.18 = (bf16[512,768]{1,0:T(8,128)(2,1)S(1)}, bf16[512,768]{1,0:T(8,128)(2,1)S(1)}, u32[]{:S(2)}, u32[]{:S(2)}) collective-permute-start(bf16[512,768]{1,0:T(8,128)(2,1)S(1)} %shard_map.124.refs_0_), channel_id=1, source_target_pairs={{0,1},{1,0},{2,3},{3,2},{4,5},{5,4},{6,7},{7,6},{8,9},{9,8},{10,11... | collective-permute-start | bytes 2359304 | tf_op jit(solution)/shard_map/ppermute | solution.py:361
  (24 shorter events, 10.8 us)
Async XLA Ops:
  4.3 22.8 %collective-permute-start = (bf16[2,512,768]{2,1,0:T(8,128)(2,1)S(1)}, bf16[2,512,768]{2,1,0:T(8,128)(2,1)S(1)}, u32[]{:S(2)}, u32[]{:S(2)}) collective-permute-start(bf16[2,512,768]{2,1,0:T(8,128)(2,1)S(1)} %get-tuple-element.26), channel_id=1, source_target_pairs={{0,32},{1,9},{2,34},{3,11},{4,36},{5,13},{6,38},{7,15},{8,40},{9,1... | collective-permute-start | bytes 4718600 | tf_op jit(solution)/shard_map/ppermute | solution.py:47
  6.8 20.2 %collective-permute-start.1 = (bf16[2,512,768]{2,1,0:T(8,128)(2,1)S(1)}, bf16[2,512,768]{2,1,0:T(8,128)(2,1)S(1)}, u32[]{:S(2)}, u32[]{:S(2)}) collective-permute-start(bf16[2,512,768]{2,1,0:T(8,128)(2,1)S(1)} %get-tuple-element.27), channel_id=1, source_target_pairs={{0,96},{1,25},{2,98},{3,27},{4,100},{5,29},{6,102},{7,31},{8,104},... | collective-permute-start | bytes 4718600 | tf_op jit(solution)/shard_map/ppermute | solution.py:47
  12.5 31.4 %collective-permute-start.3 = (bf16[2,512,768]{2,1,0:T(8,128)(2,1)S(1)}, bf16[2,512,768]{2,1,0:T(8,128)(2,1)S(1)}, u32[]{:S(2)}, u32[]{:S(2)}) collective-permute-start(bf16[2,512,768]{2,1,0:T(8,128)(2,1)S(1)} %get-tuple-element.29), channel_id=1, source_target_pairs={{0,32},{1,9},{2,34},{3,11},{4,36},{5,13},{6,38},{7,15},{8,40},{9,1... | collective-permute-start | bytes 4718600 | tf_op jit(solution)/shard_map/ppermute | solution.py:47
  12.6 32.8 %collective-permute-start.5 = (bf16[2,512,768]{2,1,0:T(8,128)(2,1)S(1)}, bf16[2,512,768]{2,1,0:T(8,128)(2,1)S(1)}, u32[]{:S(2)}, u32[]{:S(2)}) collective-permute-start(bf16[2,512,768]{2,1,0:T(8,128)(2,1)S(1)} %get-tuple-element.31), channel_id=1, source_target_pairs={{0,96},{1,25},{2,98},{3,27},{4,100},{5,29},{6,102},{7,31},{8,104},... | collective-permute-start | bytes 4718600 | tf_op jit(solution)/shard_map/ppermute | solution.py:47
  29.7 22.6 %collective-permute-start.4 = (bf16[512,768]{1,0:T(8,128)(2,1)S(1)}, bf16[512,768]{1,0:T(8,128)(2,1)S(1)}, u32[]{:S(2)}, u32[]{:S(2)}) collective-permute-start(bf16[512,768]{1,0:T(8,128)(2,1)S(1)} %get-tuple-element.30), channel_id=1, source_target_pairs={{0,32},{1,9},{2,34},{3,11},{4,36},{5,13},{6,38},{7,15},{8,40},{9,1... | collective-permute-start | bytes 2359304 | tf_op jit(solution)/shard_map/ppermute | solution.py:47
  30.7 21.7 %collective-permute-start.6 = (bf16[512,768]{1,0:T(8,128)(2,1)S(1)}, bf16[512,768]{1,0:T(8,128)(2,1)S(1)}, u32[]{:S(2)}, u32[]{:S(2)}) collective-permute-start(bf16[512,768]{1,0:T(8,128)(2,1)S(1)} %get-tuple-element.32), channel_id=1, source_target_pairs={{0,96},{1,25},{2,98},{3,27},{4,100},{5,29},{6,102},{7,31},{8,104},... | collective-permute-start | bytes 2359304 | tf_op jit(solution)/shard_map/ppermute | solution.py:47
  35.1 25.7 %collective-permute-start.8 = (bf16[512,768]{1,0:T(8,128)(2,1)S(1)}, bf16[512,768]{1,0:T(8,128)(2,1)S(1)}, u32[]{:S(2)}, u32[]{:S(2)}) collective-permute-start(bf16[512,768]{1,0:T(8,128)(2,1)S(1)} %get-tuple-element.34), channel_id=1, source_target_pairs={{0,32},{1,9},{2,34},{3,11},{4,36},{5,13},{6,38},{7,15},{8,40},{9,1... | collective-permute-start | bytes 2359304 | tf_op jit(solution)/shard_map/ppermute | solution.py:47
  43.9 20.3 %collective-permute-start.2 = (bf16[512,768]{1,0:T(8,128)(2,1)S(1)}, bf16[512,768]{1,0:T(8,128)(2,1)S(1)}, u32[]{:S(2)}, u32[]{:S(2)}) collective-permute-start(bf16[512,768]{1,0:T(8,128)(2,1)S(1)} %get-tuple-element.28), channel_id=1, source_target_pairs={{0,96},{1,25},{2,98},{3,27},{4,100},{5,29},{6,102},{7,31},{8,104},... | collective-permute-start | bytes 2359304 | tf_op jit(solution)/shard_map/ppermute | solution.py:47
  55.8 14.5 %collective-permute-start.7 = (s16[512,768]{1,0:T(8,128)(2,1)S(1)}, s16[512,768]{1,0:T(8,128)(2,1)S(1)}, u32[]{:S(2)}, u32[]{:S(2)}) collective-permute-start(s16[512,768]{1,0:T(8,128)(2,1)S(1)} %get-tuple-element.33), channel_id=1, source_target_pairs={{0,16},{1,65},{2,18},{3,67},{4,20},{5,69},{6,22},{7,71},{8,24},{9,... | collective-permute-start | bytes 2359304 | tf_op jit(solution)/shard_map/ppermute | solution.py:47
  58.3 19.7 %collective-permute-start.10 = (s16[512,768]{1,0:T(8,128)(2,1)S(1)}, s16[512,768]{1,0:T(8,128)(2,1)S(1)}, u32[]{:S(2)}, u32[]{:S(2)}) collective-permute-start(s16[512,768]{1,0:T(8,128)(2,1)S(1)} %get-tuple-element.35), channel_id=1, source_target_pairs={{0,24},{1,97},{2,26},{3,99},{4,28},{5,101},{6,30},{7,103},{8,0},{9... | collective-permute-start | bytes 2359304 | tf_op jit(solution)/shard_map/ppermute | solution.py:47
  63.2 15.4 %collective-permute-start.9 = (s16[512,768]{1,0:T(8,128)(2,1)S(1)}, s16[512,768]{1,0:T(8,128)(2,1)S(1)}, u32[]{:S(2)}, u32[]{:S(2)}) collective-permute-start(s16[512,768]{1,0:T(8,128)(2,1)S(1)} %shard_map.118), channel_id=1, source_target_pairs={{0,8},{1,33},{2,10},{3,35},{4,12},{5,37},{6,14},{7,39},{8,16},{9,4... | collective-permute-start | bytes 2359304 | tf_op jit(solution)/shard_map/ppermute | solution.py:47
  102.9 2.9 %collective-permute-start.13 = (bf16[512,768]{1,0:T(8,128)(2,1)S(1)}, bf16[512,768]{1,0:T(8,128)(2,1)S(1)}, u32[]{:S(2)}, u32[]{:S(2)}) collective-permute-start(bf16[512,768]{1,0:T(8,128)(2,1)S(1)} %shard_map.121.refs_0_), channel_id=1, source_target_pairs={{0,1},{1,0},{2,3},{3,2},{4,5},{5,4},{6,7},{7,6},{8,9},{9,8},{10,11... | collective-permute-start | bytes 2359304 | tf_op jit(solution)/shard_map/ppermute | solution.py:361
  103.8 11.1 %collective-permute-start.11 = (bf16[512,768]{1,0:T(8,128)(2,1)S(1)}, bf16[512,768]{1,0:T(8,128)(2,1)S(1)}, u32[]{:S(2)}, u32[]{:S(2)}) collective-permute-start(bf16[512,768]{1,0:T(8,128)(2,1)S(1)} %shard_map.121.refs_0_), channel_id=1, source_target_pairs={{0,2},{1,7},{2,4},{3,1},{4,6},{5,3},{6,0},{7,5},{8,10},{9,15},{10,... | collective-permute-start | bytes 2359304 | tf_op jit(solution)/shard_map/ppermute | solution.py:357
  105.7 17.6 %collective-permute-start.14 = (bf16[512,768]{1,0:T(8,128)(2,1)S(1)}, bf16[512,768]{1,0:T(8,128)(2,1)S(1)}, u32[]{:S(2)}, u32[]{:S(2)}) collective-permute-start(bf16[512,768]{1,0:T(8,128)(2,1)S(1)} %collective-permute-done.13.refs_1_), channel_id=1, source_target_pairs={{0,2},{1,7},{2,4},{3,1},{4,6},{5,3},{6,0},{7,5},{8,10},{9,15},{10,... | collective-permute-start | bytes 2359304 | tf_op jit(solution)/shard_map/ppermute | solution.py:357
  115.0 10.8 %collective-permute-start.15 = (bf16[512,768]{1,0:T(8,128)(2,1)S(1)}, bf16[512,768]{1,0:T(8,128)(2,1)S(1)}, u32[]{:S(2)}, u32[]{:S(2)}) collective-permute-start(bf16[512,768]{1,0:T(8,128)(2,1)S(1)} %shard_map.122.refs_2_), channel_id=1, source_target_pairs={{0,1},{1,0},{2,3},{3,2},{4,5},{5,4},{6,7},{7,6},{8,9},{9,8},{10,11... | collective-permute-start | bytes 2359304 | tf_op jit(solution)/shard_map/ppermute | solution.py:361
  117.1 14.7 %collective-permute-start.12 = (bf16[512,768]{1,0:T(8,128)(2,1)S(1)}, bf16[512,768]{1,0:T(8,128)(2,1)S(1)}, u32[]{:S(2)}, u32[]{:S(2)}) collective-permute-start(bf16[512,768]{1,0:T(8,128)(2,1)S(1)} %shard_map.122.refs_2_), channel_id=1, source_target_pairs={{0,2},{1,7},{2,4},{3,1},{4,6},{5,3},{6,0},{7,5},{8,10},{9,15},{10,... | collective-permute-start | bytes 2359304 | tf_op jit(solution)/shard_map/ppermute | solution.py:357
  123.5 3.6 %collective-permute-start.17 = (bf16[256,768]{1,0:T(8,128)(2,1)S(1)}, bf16[256,768]{1,0:T(8,128)(2,1)S(1)}, u32[]{:S(2)}, u32[]{:S(2)}) collective-permute-start(bf16[256,768]{1,0:T(8,128)(2,1)S(1)} %get-tuple-element.46), channel_id=1, source_target_pairs={{0,1},{1,0},{2,3},{3,2},{4,5},{5,4},{6,7},{7,6},{8,9},{9,8},{10,11... | collective-permute-start | bytes 1179656 | tf_op jit(solution)/shard_map/ppermute | solution.py:361
  125.7 1.9 %collective-permute-start.16 = (bf16[256,768]{1,0:T(8,128)(2,1)S(1)}, bf16[256,768]{1,0:T(8,128)(2,1)S(1)}, u32[]{:S(2)}, u32[]{:S(2)}) collective-permute-start(bf16[256,768]{1,0:T(8,128)(2,1)S(1)} %get-tuple-element.47), channel_id=1, source_target_pairs={{0,1},{1,0},{2,3},{3,2},{4,5},{5,4},{6,7},{7,6},{8,9},{9,8},{10,11... | collective-permute-start | bytes 1179656 | tf_op jit(solution)/shard_map/ppermute | solution.py:361
  131.8 4.1 %collective-permute-start.18 = (bf16[512,768]{1,0:T(8,128)(2,1)S(1)}, bf16[512,768]{1,0:T(8,128)(2,1)S(1)}, u32[]{:S(2)}, u32[]{:S(2)}) collective-permute-start(bf16[512,768]{1,0:T(8,128)(2,1)S(1)} %shard_map.124.refs_0_), channel_id=1, source_target_pairs={{0,1},{1,0},{2,3},{3,2},{4,5},{5,4},{6,7},{7,6},{8,9},{9,8},{10,11... | collective-permute-start | bytes 2359304 | tf_op jit(solution)/shard_map/ppermute | solution.py:361

commit v10 on v9

--- a/solution.py
+++ b/solution.py
@@ -245,9 +245,13 @@
 VAR_SCALE = 1.0 / (1.0 - 0.95**10)
 
 
-def clip_factor(square_ref):
-    square = jnp.sum(jnp.sum(square_ref[...], axis=0, keepdims=True), axis=1, keepdims=True)
-    return LIMIT / jnp.maximum(jnp.sqrt(square), LIMIT)
+def clip_factor(square_ref, factor_ref):
+    @pl.when(pl.program_id(0) == 0)
+    def _():
+        square = jnp.sum(jnp.sum(square_ref[...], axis=0, keepdims=True), axis=1, keepdims=True)
+        factor_ref[...] = jnp.broadcast_to(LIMIT / jnp.maximum(jnp.sqrt(square), LIMIT), factor_ref.shape)
+
+    return factor_ref[...]
 
 
 def stepped(master, new_mean, new_var):
@@ -256,15 +260,15 @@
     return 0.998 * master - new_mean * MEAN_SCALE / (spread + 1e-08)
 
 
-def weights_kernel(square_ref, plain_ref, master_ref, mean_ref, var_ref, out_ref):
-    grad = plain_ref[...] * clip_factor(square_ref)
+def weights_kernel(square_ref, plain_ref, master_ref, mean_ref, var_ref, out_ref, factor_ref):
+    grad = plain_ref[...] * clip_factor(square_ref, factor_ref)
     new_mean = 0.9 * mean_ref[...] + 0.1 * grad
     new_var = 0.95 * var_ref[...] + 0.05 * grad * grad
     out_ref[...] = stepped(master_ref[...], new_mean, new_var).astype(jnp.bfloat16)
 
 
-def state_kernel(square_ref, plain_ref, master_ref, mean_ref, var_ref, new_master_ref, new_mean_ref, new_var_ref):
-    grad = plain_ref[...] * clip_factor(square_ref)
+def state_kernel(square_ref, plain_ref, master_ref, mean_ref, var_ref, new_master_ref, new_mean_ref, new_var_ref, factor_ref):
+    grad = plain_ref[...] * clip_factor(square_ref, factor_ref)
     new_mean = 0.9 * mean_ref[...] + 0.1 * grad
     new_var = 0.95 * var_ref[...] + 0.05 * grad * grad
     new_mean_ref[...] = new_mean
@@ -280,6 +284,7 @@
         grid=(BLOCK // STEP,),
         in_specs=[pl.BlockSpec(square.shape, lambda j: (0, 0))] + [rows] * 4,
         out_specs=jax.tree.map(lambda _: rows, out_shape),
+        scratch_shapes=[pltpu.VMEM((1, WIDTH), jnp.float32)],
         compiler_params=pltpu.CompilerParams(vmem_limit_bytes=VMEM_BYTES),
         cost_estimate=pl.CostEstimate(flops=0, bytes_accessed=0, transcendentals=0),
     )(square, plain, master, mean, var)

time: 137 us -> 137 us (level)
  no operation moved by 1% of the time
where the time goes in v10:
time: 137 us; the launch traced here: 136 us
  waiting for transfers between devices  55.9 us (41%)
  Pallas kernels  34.9 us (25%)
  starting transfers between devices  25.5 us (19%)
  blocking collectives  19.1 us (14%)
    ppermute x11, waiting for transfers between devices, hop(): return lax.ppermute(value, ('dp', 'fsdp'), pairs)  38.3 us
    pallas_call x7, Pallas kernels, encode(): pl.pallas_call(functools.partial(encode_kernel, [len(job[2]) for job in j...  20.3 us
    all_to_all x1, blocking collectives, on_device(): square = lax.all_to_all(square, ('dp', 'fsdp'), 0, 0, tiled=True)  19.1 us
    ppermute x11, starting transfers between devices, hop(): return lax.ppermute(value, ('dp', 'fsdp'), pairs)  16.2 us
    ppermute x3, waiting for transfers between devices, along_y(): return lax.ppermute(value, 'fsdp', pairs)  13.7 us
    ppermute x5, starting transfers between devices, to_other_core(): return lax.ppermute(value, 'fsdp', [(i, i ^ 1) for i in range(8)])  7.58 us
    pallas_call x3, Pallas kernels, fill(): pl.pallas_call(functools.partial(fill_kernel, places, len(blocks) + len(g...  4.19 us
    pallas_call x2, Pallas kernels, adamw(): pl.pallas_call(kernel, out_shape=out_shape, grid=(BLOCK // STEP,), in_spe...  4 us
  transfers between devices with their start and end apart: 19, of which 14 were waited for; matrix products, arithmetic and copies ran while one was open for 0% of the time, Pallas kernels for 19%

profile of v10, /device:TPU:1, one launch (start us, length us, event | category | flops | bytes accessed | tf_op | source)
XLA Modules:
  0.0 136.4 jit_solution(13515111918975662100)
XLA Ops:
  0.6 3.7 %shard_map.112 = (bf16[2,512,768]{2,1,0:T(8,128)(2,1)S(1)}, bf16[2,512,768]{2,1,0:T(8,128)(2,1)S(1)}) custom-call(s32[1]{0:T(128)} %bitcast.place_ref, f32[16]{0:T(128)} %table_ref.15, s32[768]{0:T(1024)} %sign_ref.15, bf16[256,256]{1,0:T(8,128)(2,1)} %constant.15.clone.hmat_ref, bf16[8192,768]{1,0:T(8,128)(2,1)} %bitcast.8, s32[3,8192]{1,0:T(4,128)} %index_ref.1, ...), custom_call_target="tpu_custom_call" | custom-call | tf_op jit(solution)/shard_map/pallas_call | solution.py:137
  4.3 2.5 %collective-permute-start = (bf16[2,512,768]{2,1,0:T(8,128)(2,1)S(1)}, bf16[2,512,768]{2,1,0:T(8,128)(2,1)S(1)}, u32[]{:S(2)}, u32[]{:S(2)}) collective-permute-start(bf16[2,512,768]{2,1,0:T(8,128)(2,1)S(1)} %get-tuple-element.26), channel_id=1, source_target_pairs={{0,32},{1,9},{2,34},{3,11},{4,36},{5,13},{6,38},{7,15},{8,40},{9,1... | collective-permute-start | bytes 4718600 | tf_op jit(solution)/shard_map/ppermute | solution.py:47
  6.8 2.2 %collective-permute-start.1 = (bf16[2,512,768]{2,1,0:T(8,128)(2,1)S(1)}, bf16[2,512,768]{2,1,0:T(8,128)(2,1)S(1)}, u32[]{:S(2)}, u32[]{:S(2)}) collective-permute-start(bf16[2,512,768]{2,1,0:T(8,128)(2,1)S(1)} %get-tuple-element.27), channel_id=1, source_target_pairs={{0,96},{1,25},{2,98},{3,27},{4,100},{5,29},{6,102},{7,31},{8,104},... | collective-permute-start | bytes 4718600 | tf_op jit(solution)/shard_map/ppermute | solution.py:47
  9.1 3.5 %shard_map.114 = (bf16[2,512,768]{2,1,0:T(8,128)(2,1)S(1)}, bf16[2,512,768]{2,1,0:T(8,128)(2,1)S(1)}) custom-call(s32[1]{0:T(128)} %bitcast.place_ref, f32[16]{0:T(128)} %table_ref.15, s32[768]{0:T(1024)} %sign_ref.15, bf16[256,256]{1,0:T(8,128)(2,1)} %constant.15.clone.hmat_ref, bf16[8192,768]{1,0:T(8,128)(2,1)} %bitcast.12, s32[3,8192]{1,0:T(4,128)} %index_ref.1, ...), custom_call_target="tpu_custom_call" | custom-call | tf_op jit(solution)/shard_map/pallas_call | solution.py:137
  12.6 2.7 %collective-permute-start.5 = (bf16[2,512,768]{2,1,0:T(8,128)(2,1)S(1)}, bf16[2,512,768]{2,1,0:T(8,128)(2,1)S(1)}, u32[]{:S(2)}, u32[]{:S(2)}) collective-permute-start(bf16[2,512,768]{2,1,0:T(8,128)(2,1)S(1)} %get-tuple-element.31), channel_id=1, source_target_pairs={{0,96},{1,25},{2,98},{3,27},{4,100},{5,29},{6,102},{7,31},{8,104},... | collective-permute-start | bytes 4718600 | tf_op jit(solution)/shard_map/ppermute | solution.py:47
  15.3 3.1 %shard_map.111 = (f32[512,768]{1,0:T(8,128)S(1)}, f32[512,768]{1,0:T(8,128)S(1)}, f32[512,768]{1,0:T(8,128)S(1)}, f32[8,128]{1,0:T(8,128)S(1)}) custom-call(f32[512,768]{1,0:T(8,128)} %refs_0_.1, f32[512,768]{1,0:T(8,128)} %refs_1_.6, f32[512,768]{1,0:T(8,128)} %refs_2_.3), custom_call_target="tpu_custom_call" | custom-call | tf_op jit(solution)/shard_map/pallas_call | solution.py:301
  18.4 8.7 %collective-permute-done.refs_3_ = bf16[2,512,768]{2,1,0:T(8,128)(2,1)S(1)} collective-permute-done((bf16[2,512,768]{2,1,0:T(8,128)(2,1)S(1)}, bf16[2,512,768]{2,1,0:T(8,128)(2,1)S(1)}, u32[]{:S(2)}, u32[]{:S(2)}) %collective-permute-start) | collective-permute-done | bytes 1572896 | tf_op jit(solution)/shard_map/ppermute | solution.py:47
  27.1 2.6 %shard_map.116 = (bf16[512,768]{1,0:T(8,128)(2,1)S(1)}, bf16[512,768]{1,0:T(8,128)(2,1)S(1)}) custom-call(s32[1]{0:T(128)} %bitcast.place_ref, f32[16]{0:T(128)} %table_ref.15, s32[768]{0:T(1024)} %sign_ref.15, bf16[256,256]{1,0:T(8,128)(2,1)} %constant.15.clone.hmat_ref, f32[8,128]{1,0:T(8,128)S(1)} %get-tuple-element.25.refs_0_, ...), custom_call_target="tpu_custom_call" | custom-call | tf_op jit(solution)/shard_map/pallas_call | solution.py:137
  30.7 1.8 %collective-permute-start.6 = (bf16[512,768]{1,0:T(8,128)(2,1)S(1)}, bf16[512,768]{1,0:T(8,128)(2,1)S(1)}, u32[]{:S(2)}, u32[]{:S(2)}) collective-permute-start(bf16[512,768]{1,0:T(8,128)(2,1)S(1)} %get-tuple-element.32), channel_id=1, source_target_pairs={{0,96},{1,25},{2,98},{3,27},{4,100},{5,29},{6,102},{7,31},{8,104},... | collective-permute-start | bytes 2359304 | tf_op jit(solution)/shard_map/ppermute | solution.py:47
  32.5 2.6 %shard_map.113 = (bf16[512,768]{1,0:T(8,128)(2,1)S(1)}, bf16[512,768]{1,0:T(8,128)(2,1)S(1)}) custom-call(s32[1]{0:T(128)} %bitcast.place_ref, f32[16]{0:T(128)} %table_ref.15, s32[768]{0:T(1024)} %sign_ref.15, bf16[256,256]{1,0:T(8,128)(2,1)} %constant.15.clone.hmat_ref, f32[8,128]{1,0:T(8,128)S(1)} %get-tuple-element.25.refs_0_, ...), custom_call_target="tpu_custom_call" | custom-call | tf_op jit(solution)/shard_map/pallas_call | solution.py:137
  35.2 8.7 %collective-permute-done.3.refs_3_.refs_7_ = bf16[2,512,768]{2,1,0:T(8,128)(2,1)S(1)} collective-permute-done((bf16[2,512,768]{2,1,0:T(8,128)(2,1)S(1)}, bf16[2,512,768]{2,1,0:T(8,128)(2,1)S(1)}, u32[]{:S(2)}, u32[]{:S(2)}) %collective-permute-start.3) | collective-permute-done | bytes 1572896 | tf_op jit(solution)/shard_map/ppermute | solution.py:47
  43.9 1.5 %collective-permute-start.2 = (bf16[512,768]{1,0:T(8,128)(2,1)S(1)}, bf16[512,768]{1,0:T(8,128)(2,1)S(1)}, u32[]{:S(2)}, u32[]{:S(2)}) collective-permute-start(bf16[512,768]{1,0:T(8,128)(2,1)S(1)} %get-tuple-element.28), channel_id=1, source_target_pairs={{0,96},{1,25},{2,98},{3,27},{4,100},{5,29},{6,102},{7,31},{8,104},... | collective-permute-start | bytes 2359304 | tf_op jit(solution)/shard_map/ppermute | solution.py:47
  45.4 7.0 %collective-permute-done.4.refs_2_ = bf16[512,768]{1,0:T(8,128)(2,1)S(1)} collective-permute-done((bf16[512,768]{1,0:T(8,128)(2,1)S(1)}, bf16[512,768]{1,0:T(8,128)(2,1)S(1)}, u32[]{:S(2)}, u32[]{:S(2)}) %collective-permute-start.4) | collective-permute-done | bytes 786464 | tf_op jit(solution)/shard_map/ppermute | solution.py:47
  52.4 3.4 %shard_map.117 = (s16[512,768]{1,0:T(8,128)(2,1)S(1)}, s16[512,768]{1,0:T(8,128)(2,1)S(1)}) custom-call(s32[1]{0:T(128)} %bitcast.place_ref, f32[16]{0:T(128)} %table_ref.15, s32[768]{0:T(1024)} %sign_ref.15, bf16[256,256]{1,0:T(8,128)(2,1)} %constant.15.clone.hmat_ref, bf16[8192,768]{1,0:T(8,128)(2,1)} %bitcast.20, s32[3,8192]{1,0:T(4,128)} %index_ref.1, ...), custom_call_target="tpu_custom_call" | custom-call | tf_op jit(solution)/shard_map/pallas_call | solution.py:137
  55.8 2.5 %collective-permute-start.7 = (s16[512,768]{1,0:T(8,128)(2,1)S(1)}, s16[512,768]{1,0:T(8,128)(2,1)S(1)}, u32[]{:S(2)}, u32[]{:S(2)}) collective-permute-start(s16[512,768]{1,0:T(8,128)(2,1)S(1)} %get-tuple-element.33), channel_id=1, source_target_pairs={{0,16},{1,65},{2,18},{3,67},{4,20},{5,69},{6,22},{7,71},{8,24},{9,... | collective-permute-start | bytes 2359304 | tf_op jit(solution)/shard_map/ppermute | solution.py:47
  59.2 1.6 %collective-permute-done.8.refs_2_ = bf16[512,768]{1,0:T(8,128)(2,1)S(1)} collective-permute-done((bf16[512,768]{1,0:T(8,128)(2,1)S(1)}, bf16[512,768]{1,0:T(8,128)(2,1)S(1)}, u32[]{:S(2)}, u32[]{:S(2)}) %collective-permute-start.8) | collective-permute-done | bytes 786464 | tf_op jit(solution)/shard_map/ppermute | solution.py:47
  60.8 2.5 %shard_map.118 = s16[512,768]{1,0:T(8,128)(2,1)S(1)} custom-call(s32[1]{0:T(128)} %bitcast.place_ref, f32[16]{0:T(128)} %table_ref.15, s32[768]{0:T(1024)} %sign_ref.15, bf16[256,256]{1,0:T(8,128)(2,1)} %constant.15.clone.hmat_ref, bf16[8192,768]{1,0:T(8,128)(2,1)} %bitcast.22, s32[3,8192]{1,0:T(4,128)} %index_ref.1, ...), custom_call_target="tpu_custom_call" | custom-call | tf_op jit(solution)/shard_map/pallas_call | solution.py:137
  64.2 2.1 %shard_map.115.own_ref = f32[512,768]{1,0:T(8,128)S(1)} custom-call(s32[1]{0:T(128)} %bitcast.place_ref, f32[16]{0:T(128)} %table_ref.15, s32[768]{0:T(1024)} %sign_ref.15, bf16[256,256]{1,0:T(8,128)(2,1)} %constant.15.clone.hmat_ref, bf16[8192,768]{1,0:T(8,128)(2,1)} %bitcast.23, s32[3,8192]{1,0:T(4,128)} %index_ref.1, ...), custom_call_target="tpu_custom_call" | custom-call | tf_op jit(solution)/shard_map/pallas_call | solution.py:137
  66.4 3.9 %collective-permute-done.7.two_ref = s16[512,768]{1,0:T(8,128)(2,1)S(1)} collective-permute-done((s16[512,768]{1,0:T(8,128)(2,1)S(1)}, s16[512,768]{1,0:T(8,128)(2,1)S(1)}, u32[]{:S(2)}, u32[]{:S(2)}) %collective-permute-start.7) | collective-permute-done | bytes 786464 | tf_op jit(solution)/shard_map/ppermute | solution.py:47
  70.3 7.8 %collective-permute-done.10.three_ref = s16[512,768]{1,0:T(8,128)(2,1)S(1)} collective-permute-done((s16[512,768]{1,0:T(8,128)(2,1)S(1)}, s16[512,768]{1,0:T(8,128)(2,1)S(1)}, u32[]{:S(2)}, u32[]{:S(2)}) %collective-permute-start.10) | collective-permute-done | bytes 786464 | tf_op jit(solution)/shard_map/ppermute | solution.py:47
  78.6 3.3 %shard_map.119 = (f32[512,768]{1,0:T(8,128)S(1)}, f32[128,128]{1,0:T(8,128)}) custom-call(s32[1]{0:T(128)} %bitcast.place_ref, f32[16]{0:T(128)} %table_ref.15, s32[768]{0:T(1024)} %sign_ref.15, bf16[256,256]{1,0:T(8,128)(2,1)} %constant.15.clone.hmat_ref, f32[512,768]{1,0:T(8,128)S(1)} %shard_map.115.own_ref, ...), custom_call_target="tpu_custom_call" | custom-call | tf_op jit(solution)/shard_map/pallas_call | solution.py:217
  81.9 19.1 %all_to_all.11 = f32[128,1,128]{2,1,0:T(1,128)S(1)} all-to-all(f32[128,1,128]{2,1,0:T(1,128)} %bitcast.24), channel_id=1, replica_groups=mesh['dp'=16,'fsdp'=8] {'dp','fsdp'}, dimensions={0} | all-to-all | bytes 131072 | tf_op jit(solution)/shard_map/all_to_all | solution.py:394
  101.0 1.2 shard_map.121.refs_0_
  106.0 2.8 %shard_map.120 = (f32[512,768]{1,0:T(8,128)}, f32[512,768]{1,0:T(8,128)}, f32[512,768]{1,0:T(8,128)}) custom-call(f32[128,128]{1,0:T(8,128)S(1)} %bitcast.7, f32[512,768]{1,0:T(8,128)S(1)} %get-tuple-element.37.plain_ref, f32[512,768]{1,0:T(8,128)S(1)} %get-tuple-element.38.master_ref, f32[512,768]{1,0:T(8,128)S(1)} %get-tuple-element.39.mean_ref, ...), custom_call_target="tpu_custom_call" | custom-call | tf_op jit(solution)/shard_map/pallas_call | solution.py:281
  108.8 5.6 %collective-permute-done.11.__0_ = bf16[512,768]{1,0:T(8,128)(2,1)S(1)} collective-permute-done((bf16[512,768]{1,0:T(8,128)(2,1)S(1)}, bf16[512,768]{1,0:T(8,128)(2,1)S(1)}, u32[]{:S(2)}, u32[]{:S(2)}) %collective-permute-start.11) | collective-permute-done | bytes 786464 | tf_op jit(solution)/shard_map/ppermute | solution.py:362
  114.4 2.1 %collective-permute-start.15 = (bf16[512,768]{1,0:T(8,128)(2,1)S(1)}, bf16[512,768]{1,0:T(8,128)(2,1)S(1)}, u32[]{:S(2)}, u32[]{:S(2)}) collective-permute-start(bf16[512,768]{1,0:T(8,128)(2,1)S(1)} %shard_map.122.refs_2_), channel_id=1, source_target_pairs={{0,1},{1,0},{2,3},{3,2},{4,5},{5,4},{6,7},{7,6},{8,9},{9,8},{10,11... | collective-permute-start | bytes 2359304 | tf_op jit(solution)/shard_map/ppermute | solution.py:366
  116.5 6.3 %collective-permute-done.14.refs_3_ = bf16[512,768]{1,0:T(8,128)(2,1)S(1)} collective-permute-done((bf16[512,768]{1,0:T(8,128)(2,1)S(1)}, bf16[512,768]{1,0:T(8,128)(2,1)S(1)}, u32[]{:S(2)}, u32[]{:S(2)}) %collective-permute-start.14) | collective-permute-done | bytes 786464 | tf_op jit(solution)/shard_map/ppermute | solution.py:362
  122.9 2.2 %collective-permute-start.17 = (bf16[256,768]{1,0:T(8,128)(2,1)S(1)}, bf16[256,768]{1,0:T(8,128)(2,1)S(1)}, u32[]{:S(2)}, u32[]{:S(2)}) collective-permute-start(bf16[256,768]{1,0:T(8,128)(2,1)S(1)} %get-tuple-element.46), channel_id=1, source_target_pairs={{0,1},{1,0},{2,3},{3,2},{4,5},{5,4},{6,7},{7,6},{8,9},{9,8},{10,11... | collective-permute-start | bytes 1179656 | tf_op jit(solution)/shard_map/ppermute | solution.py:366
  125.2 1.3 collective-permute-done.17.refs_6_
  127.0 2.4 %shard_map.123 = (bf16[512,6144]{1,0:T(8,128)(2,1)}, f32[8,128]{1,0:T(8,128)S(1)}) custom-call(bf16[512,768]{1,0:T(8,128)(2,1)S(1)} %shard_map.121.refs_0_, bf16[512,768]{1,0:T(8,128)(2,1)S(1)} %collective-permute-done.13.refs_1_, bf16[512,768]{1,0:T(8,128)(2,1)S(1)} %shard_map.122.refs_2_, bf16[512,768]{1,0:T(8,128)(2,1)S(1)} %collective-permute-done.14.refs_3_, ...), custom_call_target="tpu_custom_call" | custom-call | tf_op jit(solution)/shard_map/pallas_call | solution.py:348
  129.4 1.8 %collective-permute-done.12.__0_ = bf16[512,768]{1,0:T(8,128)(2,1)S(1)} collective-permute-done((bf16[512,768]{1,0:T(8,128)(2,1)S(1)}, bf16[512,768]{1,0:T(8,128)(2,1)S(1)}, u32[]{:S(2)}, u32[]{:S(2)}) %collective-permute-start.12) | collective-permute-done | bytes 786464 | tf_op jit(solution)/shard_map/ppermute | solution.py:362
  131.2 2.1 %collective-permute-start.18 = (bf16[512,768]{1,0:T(8,128)(2,1)S(1)}, bf16[512,768]{1,0:T(8,128)(2,1)S(1)}, u32[]{:S(2)}, u32[]{:S(2)}) collective-permute-start(bf16[512,768]{1,0:T(8,128)(2,1)S(1)} %shard_map.124.refs_0_), channel_id=1, source_target_pairs={{0,1},{1,0},{2,3},{3,2},{4,5},{5,4},{6,7},{7,6},{8,9},{9,8},{10,11... | collective-permute-start | bytes 2359304 | tf_op jit(solution)/shard_map/ppermute | solution.py:366
  (24 shorter events, 10.8 us)
Async XLA Ops:
  4.3 22.8 %collective-permute-start = (bf16[2,512,768]{2,1,0:T(8,128)(2,1)S(1)}, bf16[2,512,768]{2,1,0:T(8,128)(2,1)S(1)}, u32[]{:S(2)}, u32[]{:S(2)}) collective-permute-start(bf16[2,512,768]{2,1,0:T(8,128)(2,1)S(1)} %get-tuple-element.26), channel_id=1, source_target_pairs={{0,32},{1,9},{2,34},{3,11},{4,36},{5,13},{6,38},{7,15},{8,40},{9,1... | collective-permute-start | bytes 4718600 | tf_op jit(solution)/shard_map/ppermute | solution.py:47
  6.8 20.2 %collective-permute-start.1 = (bf16[2,512,768]{2,1,0:T(8,128)(2,1)S(1)}, bf16[2,512,768]{2,1,0:T(8,128)(2,1)S(1)}, u32[]{:S(2)}, u32[]{:S(2)}) collective-permute-start(bf16[2,512,768]{2,1,0:T(8,128)(2,1)S(1)} %get-tuple-element.27), channel_id=1, source_target_pairs={{0,96},{1,25},{2,98},{3,27},{4,100},{5,29},{6,102},{7,31},{8,104},... | collective-permute-start | bytes 4718600 | tf_op jit(solution)/shard_map/ppermute | solution.py:47
  12.5 31.4 %collective-permute-start.3 = (bf16[2,512,768]{2,1,0:T(8,128)(2,1)S(1)}, bf16[2,512,768]{2,1,0:T(8,128)(2,1)S(1)}, u32[]{:S(2)}, u32[]{:S(2)}) collective-permute-start(bf16[2,512,768]{2,1,0:T(8,128)(2,1)S(1)} %get-tuple-element.29), channel_id=1, source_target_pairs={{0,32},{1,9},{2,34},{3,11},{4,36},{5,13},{6,38},{7,15},{8,40},{9,1... | collective-permute-start | bytes 4718600 | tf_op jit(solution)/shard_map/ppermute | solution.py:47
  12.6 32.8 %collective-permute-start.5 = (bf16[2,512,768]{2,1,0:T(8,128)(2,1)S(1)}, bf16[2,512,768]{2,1,0:T(8,128)(2,1)S(1)}, u32[]{:S(2)}, u32[]{:S(2)}) collective-permute-start(bf16[2,512,768]{2,1,0:T(8,128)(2,1)S(1)} %get-tuple-element.31), channel_id=1, source_target_pairs={{0,96},{1,25},{2,98},{3,27},{4,100},{5,29},{6,102},{7,31},{8,104},... | collective-permute-start | bytes 4718600 | tf_op jit(solution)/shard_map/ppermute | solution.py:47
  29.7 22.6 %collective-permute-start.4 = (bf16[512,768]{1,0:T(8,128)(2,1)S(1)}, bf16[512,768]{1,0:T(8,128)(2,1)S(1)}, u32[]{:S(2)}, u32[]{:S(2)}) collective-permute-start(bf16[512,768]{1,0:T(8,128)(2,1)S(1)} %get-tuple-element.30), channel_id=1, source_target_pairs={{0,32},{1,9},{2,34},{3,11},{4,36},{5,13},{6,38},{7,15},{8,40},{9,1... | collective-permute-start | bytes 2359304 | tf_op jit(solution)/shard_map/ppermute | solution.py:47
  30.7 21.7 %collective-permute-start.6 = (bf16[512,768]{1,0:T(8,128)(2,1)S(1)}, bf16[512,768]{1,0:T(8,128)(2,1)S(1)}, u32[]{:S(2)}, u32[]{:S(2)}) collective-permute-start(bf16[512,768]{1,0:T(8,128)(2,1)S(1)} %get-tuple-element.32), channel_id=1, source_target_pairs={{0,96},{1,25},{2,98},{3,27},{4,100},{5,29},{6,102},{7,31},{8,104},... | collective-permute-start | bytes 2359304 | tf_op jit(solution)/shard_map/ppermute | solution.py:47
  35.1 25.7 %collective-permute-start.8 = (bf16[512,768]{1,0:T(8,128)(2,1)S(1)}, bf16[512,768]{1,0:T(8,128)(2,1)S(1)}, u32[]{:S(2)}, u32[]{:S(2)}) collective-permute-start(bf16[512,768]{1,0:T(8,128)(2,1)S(1)} %get-tuple-element.34), channel_id=1, source_target_pairs={{0,32},{1,9},{2,34},{3,11},{4,36},{5,13},{6,38},{7,15},{8,40},{9,1... | collective-permute-start | bytes 2359304 | tf_op jit(solution)/shard_map/ppermute | solution.py:47
  43.9 20.3 %collective-permute-start.2 = (bf16[512,768]{1,0:T(8,128)(2,1)S(1)}, bf16[512,768]{1,0:T(8,128)(2,1)S(1)}, u32[]{:S(2)}, u32[]{:S(2)}) collective-permute-start(bf16[512,768]{1,0:T(8,128)(2,1)S(1)} %get-tuple-element.28), channel_id=1, source_target_pairs={{0,96},{1,25},{2,98},{3,27},{4,100},{5,29},{6,102},{7,31},{8,104},... | collective-permute-start | bytes 2359304 | tf_op jit(solution)/shard_map/ppermute | solution.py:47
  55.8 14.5 %collective-permute-start.7 = (s16[512,768]{1,0:T(8,128)(2,1)S(1)}, s16[512,768]{1,0:T(8,128)(2,1)S(1)}, u32[]{:S(2)}, u32[]{:S(2)}) collective-permute-start(s16[512,768]{1,0:T(8,128)(2,1)S(1)} %get-tuple-element.33), channel_id=1, source_target_pairs={{0,16},{1,65},{2,18},{3,67},{4,20},{5,69},{6,22},{7,71},{8,24},{9,... | collective-permute-start | bytes 2359304 | tf_op jit(solution)/shard_map/ppermute | solution.py:47
  58.3 19.7 %collective-permute-start.10 = (s16[512,768]{1,0:T(8,128)(2,1)S(1)}, s16[512,768]{1,0:T(8,128)(2,1)S(1)}, u32[]{:S(2)}, u32[]{:S(2)}) collective-permute-start(s16[512,768]{1,0:T(8,128)(2,1)S(1)} %get-tuple-element.35), channel_id=1, source_target_pairs={{0,24},{1,97},{2,26},{3,99},{4,28},{5,101},{6,30},{7,103},{8,0},{9... | collective-permute-start | bytes 2359304 | tf_op jit(solution)/shard_map/ppermute | solution.py:47
  63.2 15.4 %collective-permute-start.9 = (s16[512,768]{1,0:T(8,128)(2,1)S(1)}, s16[512,768]{1,0:T(8,128)(2,1)S(1)}, u32[]{:S(2)}, u32[]{:S(2)}) collective-permute-start(s16[512,768]{1,0:T(8,128)(2,1)S(1)} %shard_map.118), channel_id=1, source_target_pairs={{0,8},{1,33},{2,10},{3,35},{4,12},{5,37},{6,14},{7,39},{8,16},{9,4... | collective-permute-start | bytes 2359304 | tf_op jit(solution)/shard_map/ppermute | solution.py:47
  102.3 2.9 %collective-permute-start.13 = (bf16[512,768]{1,0:T(8,128)(2,1)S(1)}, bf16[512,768]{1,0:T(8,128)(2,1)S(1)}, u32[]{:S(2)}, u32[]{:S(2)}) collective-permute-start(bf16[512,768]{1,0:T(8,128)(2,1)S(1)} %shard_map.121.refs_0_), channel_id=1, source_target_pairs={{0,1},{1,0},{2,3},{3,2},{4,5},{5,4},{6,7},{7,6},{8,9},{9,8},{10,11... | collective-permute-start | bytes 2359304 | tf_op jit(solution)/shard_map/ppermute | solution.py:366
  103.2 11.1 %collective-permute-start.11 = (bf16[512,768]{1,0:T(8,128)(2,1)S(1)}, bf16[512,768]{1,0:T(8,128)(2,1)S(1)}, u32[]{:S(2)}, u32[]{:S(2)}) collective-permute-start(bf16[512,768]{1,0:T(8,128)(2,1)S(1)} %shard_map.121.refs_0_), channel_id=1, source_target_pairs={{0,2},{1,7},{2,4},{3,1},{4,6},{5,3},{6,0},{7,5},{8,10},{9,15},{10,... | collective-permute-start | bytes 2359304 | tf_op jit(solution)/shard_map/ppermute | solution.py:362
  105.2 17.6 %collective-permute-start.14 = (bf16[512,768]{1,0:T(8,128)(2,1)S(1)}, bf16[512,768]{1,0:T(8,128)(2,1)S(1)}, u32[]{:S(2)}, u32[]{:S(2)}) collective-permute-start(bf16[512,768]{1,0:T(8,128)(2,1)S(1)} %collective-permute-done.13.refs_1_), channel_id=1, source_target_pairs={{0,2},{1,7},{2,4},{3,1},{4,6},{5,3},{6,0},{7,5},{8,10},{9,15},{10,... | collective-permute-start | bytes 2359304 | tf_op jit(solution)/shard_map/ppermute | solution.py:362
  114.4 10.8 %collective-permute-start.15 = (bf16[512,768]{1,0:T(8,128)(2,1)S(1)}, bf16[512,768]{1,0:T(8,128)(2,1)S(1)}, u32[]{:S(2)}, u32[]{:S(2)}) collective-permute-start(bf16[512,768]{1,0:T(8,128)(2,1)S(1)} %shard_map.122.refs_2_), channel_id=1, source_target_pairs={{0,1},{1,0},{2,3},{3,2},{4,5},{5,4},{6,7},{7,6},{8,9},{9,8},{10,11... | collective-permute-start | bytes 2359304 | tf_op jit(solution)/shard_map/ppermute | solution.py:366
  116.5 14.7 %collective-permute-start.12 = (bf16[512,768]{1,0:T(8,128)(2,1)S(1)}, bf16[512,768]{1,0:T(8,128)(2,1)S(1)}, u32[]{:S(2)}, u32[]{:S(2)}) collective-permute-start(bf16[512,768]{1,0:T(8,128)(2,1)S(1)} %shard_map.122.refs_2_), channel_id=1, source_target_pairs={{0,2},{1,7},{2,4},{3,1},{4,6},{5,3},{6,0},{7,5},{8,10},{9,15},{10,... | collective-permute-start | bytes 2359304 | tf_op jit(solution)/shard_map/ppermute | solution.py:362
  122.9 3.6 %collective-permute-start.17 = (bf16[256,768]{1,0:T(8,128)(2,1)S(1)}, bf16[256,768]{1,0:T(8,128)(2,1)S(1)}, u32[]{:S(2)}, u32[]{:S(2)}) collective-permute-start(bf16[256,768]{1,0:T(8,128)(2,1)S(1)} %get-tuple-element.46), channel_id=1, source_target_pairs={{0,1},{1,0},{2,3},{3,2},{4,5},{5,4},{6,7},{7,6},{8,9},{9,8},{10,11... | collective-permute-start | bytes 1179656 | tf_op jit(solution)/shard_map/ppermute | solution.py:366
  125.1 1.9 %collective-permute-start.16 = (bf16[256,768]{1,0:T(8,128)(2,1)S(1)}, bf16[256,768]{1,0:T(8,128)(2,1)S(1)}, u32[]{:S(2)}, u32[]{:S(2)}) collective-permute-start(bf16[256,768]{1,0:T(8,128)(2,1)S(1)} %get-tuple-element.47), channel_id=1, source_target_pairs={{0,1},{1,0},{2,3},{3,2},{4,5},{5,4},{6,7},{7,6},{8,9},{9,8},{10,11... | collective-permute-start | bytes 1179656 | tf_op jit(solution)/shard_map/ppermute | solution.py:366
  131.2 4.1 %collective-permute-start.18 = (bf16[512,768]{1,0:T(8,128)(2,1)S(1)}, bf16[512,768]{1,0:T(8,128)(2,1)S(1)}, u32[]{:S(2)}, u32[]{:S(2)}) collective-permute-start(bf16[512,768]{1,0:T(8,128)(2,1)S(1)} %shard_map.124.refs_0_), channel_id=1, source_target_pairs={{0,1},{1,0},{2,3},{3,2},{4,5},{5,4},{6,7},{7,6},{8,9},{9,8},{10,11... | collective-permute-start | bytes 2359304 | tf_op jit(solution)/shard_map/ppermute | solution.py:366
